TPU v7x, 32 devices: a whole 2x2x4 slice. The times are simulated.
32 devices in a mesh: replica: 4 (over z), fsdp: 4 (over y, core), ctx: 2 (over x).
Axes of the slice: x: 2, y: 2, z: 4, core: 2. Of those that a mesh axis runs over, the one named last changes fastest.
Arguments:
- tokens: bfloat16 [16, 256, 1024], P(('replica', 'fsdp'), 'ctx'), may hold values from -6 to 6
- input_gain: bfloat16 [1024], P(('fsdp', 'ctx')), may hold values from 0.099609375 to 1.8984375
- qkv_weight: bfloat16 [1024, 3072], P(('fsdp', 'ctx')), may hold values from -0.1875 to 0.1875
- output_weight: bfloat16 [1024, 1024], P(('fsdp', 'ctx')), may hold values from -1.5 to 1.5
- mlp_gain: bfloat16 [1024], P(('fsdp', 'ctx')), may hold values from 0.099609375 to 1.8984375
- expand_weight: bfloat16 [1024, 5248], P(('fsdp', 'ctx')), may hold values from -0.1875 to 0.1875
- contract_weight: bfloat16 [1024, 2624], P(('fsdp', 'ctx')), may hold values from -0.125 to 0.125
- positions: int32 [16, 256], P(('replica', 'fsdp'), 'ctx'), may hold values from 0 to 199, as said below
- mask_bias: float32 [16, 256, 256], P(('replica', 'fsdp'), 'ctx'), may hold values from -1000000000 to 0, as said below
- cotangent: bfloat16 [16, 256, 1024], P(('replica', 'fsdp'), 'ctx'), may hold values from -6 to 6
Outputs:
- layer_out: bfloat16 [16, 256, 1024], P(('replica', 'fsdp'), 'ctx')
- input_grad: bfloat16 [16, 256, 1024], P(('replica', 'fsdp'), 'ctx')
- input_gain_grad: float32 [1024], P(('fsdp', 'ctx'))
- qkv_weight_grad: float32 [1024, 3072], P(('fsdp', 'ctx'))
- output_weight_grad: float32 [1024, 1024], P(('fsdp', 'ctx'))
- mlp_gain_grad: float32 [1024], P(('fsdp', 'ctx'))
- expand_weight_grad: float32 [1024, 5248], P(('fsdp', 'ctx'))
- contract_weight_grad: float32 [1024, 2624], P(('fsdp', 'ctx'))
Inputs may be any that keep to these rules, and one draw needn't show every extreme that they name: `positions`: each sequence is a pack of documents one after another; a token's position is its index inside its document, 0 at a document's first token and rising by one; every sequence holds one document of exactly 200 tokens and none longer. mask_bias[s, t, j] is 0 where the key token k = 128 * (t // 128) - 64 + j lies inside the sequence, |k - t| <= 64, and k is in the same document as t (as positions give the documents); else -1e9.
All inputs are finite; a program needn't handle non-finite values.
Results may differ from a plain program's by a relative error of at most 0.015.
Values may be sent and summed in bfloat16 or wider, within the bound.
No kernel may reach another device: no remote copies, remote signals or barrier semaphores. Data moves between devices by JAX's collectives and lax.ppermute only.
A program may use at most 256 MiB of HBM per device.

v0:
```python
import math

import jax
import jax.numpy as jnp
from jax import lax
from jax.sharding import PartitionSpec as P

HEAD_DIM = 64
HALF = 64


EPS = 1e-05
THETA = 10000.0


def extended_2(cells, sides, width):
    for axis, dim in sides:
        count = lax.axis_size(axis)
        ends = count - 1
        head = lax.slice_in_dim(cells, 0, width, axis=dim)
        tail = lax.slice_in_dim(cells, cells.shape[dim] - width, cells.shape[dim], axis=dim)
        cells = jnp.concatenate(
            [
                lax.ppermute(tail, axis, [(i, (i + 1) % count) for i in range(ends)]),
                cells,
                lax.ppermute(head, axis, [((i + 1) % count, i) for i in range(ends)]),
            ],
            axis=dim,
        )
    return cells


def from_behind(value, axis, steps):
    count = lax.axis_size(axis)
    first, last = (max(0, -steps), min(count, count - steps))
    return lax.ppermute(value, axis, [(source, source + steps) for source in range(first, last)])


def layer_norm(values, gain):
    center = values - jnp.mean(values, axis=-1, keepdims=True)
    variance = jnp.mean(center * center, axis=-1, keepdims=True)
    scaled = lax.rsqrt(variance + EPS)
    normed = center * scaled
    return (normed, scaled, (normed * gain.astype(jnp.float32)).astype(jnp.bfloat16))


def layer_norm_back(incoming, normed, scaled, gain):
    weighted = incoming * gain.astype(jnp.float32)
    gain_grad = jnp.sum(incoming * normed, axis=0)
    mean_one = jnp.mean(weighted, axis=-1, keepdims=True)
    mean_two = jnp.mean(weighted * normed, axis=-1, keepdims=True)
    return (scaled * (weighted - mean_one - normed * mean_two), gain_grad)


def rope_tables(positions, head_size):
    half_dim = head_size // 2
    exponent = jnp.arange(half_dim, dtype=jnp.float32) * (2.0 / head_size)
    frequency = jnp.exp(-math.log(THETA) * exponent)
    angles = positions.astype(jnp.float32)[:, None] * frequency[None, :]
    return (jnp.cos(angles)[:, None, :], jnp.sin(angles)[:, None, :])


def rotate(values, cosine, sine):
    half_dim = values.shape[-1] // 2
    lower_half, upper_half = (values[..., :half_dim], values[..., half_dim:])
    return jnp.concatenate(
        [lower_half * cosine - upper_half * sine, upper_half * cosine + lower_half * sine], axis=-1
    )


def rotate_back(values, cosine, sine):
    half_dim = values.shape[-1] // 2
    lower_half, upper_half = (values[..., :half_dim], values[..., half_dim:])
    return jnp.concatenate(
        [lower_half * cosine + upper_half * sine, upper_half * cosine - lower_half * sine], axis=-1
    )


def gelu_slope(values):
    cdf_part = 0.5 * (1.0 + jax.scipy.special.erf(values * (1.0 / math.sqrt(2.0))))
    density = jnp.exp(-0.5 * values * values) * (1.0 / math.sqrt(2.0 * math.pi))
    return cdf_part + values * density


def block_scores(queries, key_rows, additive):
    factor = 1.0 / math.sqrt(queries.shape[-1])
    scores = jnp.einsum("qhd,khd->hqk", queries, key_rows, preferred_element_type=jnp.float32)
    return scores * factor + additive[None]


def attend(queries, key_rows, value_rows, additive):
    scores = block_scores(queries, key_rows, additive)
    row_peak = jnp.max(scores, axis=-1, keepdims=True)
    exponent = jnp.exp(scores - row_peak)
    row_total = jnp.sum(exponent, axis=-1, keepdims=True)
    soft_weights = (exponent / row_total).astype(jnp.bfloat16)
    mixed = jnp.einsum("hqk,khd->qhd", soft_weights, value_rows, preferred_element_type=jnp.float32)
    return (mixed.astype(jnp.bfloat16), row_peak[..., 0] + jnp.log(row_total[..., 0]))


def attend_back(queries, key_rows, value_rows, additive, log_total, d_mixed):
    factor = 1.0 / math.sqrt(queries.shape[-1])
    scores = block_scores(queries, key_rows, additive)
    recomputed = jnp.exp(scores - log_total[..., None])
    d_soft = jnp.einsum("qhd,khd->hqk", d_mixed, value_rows, preferred_element_type=jnp.float32)
    center = jnp.sum(recomputed * d_soft, axis=-1, keepdims=True)
    d_scores = (recomputed * (d_soft - center) * factor).astype(jnp.bfloat16)
    d_queries = jnp.einsum("hqk,khd->qhd", d_scores, key_rows, preferred_element_type=jnp.float32)
    d_keys = jnp.einsum("hqk,qhd->khd", d_scores, queries, preferred_element_type=jnp.float32)
    d_values = jnp.einsum(
        "hqk,qhd->khd", recomputed.astype(jnp.bfloat16), d_mixed, preferred_element_type=jnp.float32
    )
    return (d_queries, d_keys, d_values)


def body(
    tokens,
    input_gain,
    qkv_weight,
    output_weight,
    mlp_gain,
    expand_weight,
    contract_weight,
    positions,
    mask_bias,
    cotangent,
):
    gathered = (
        lax.all_gather(input_gain, ("fsdp", "ctx"), axis=0, tiled=True),
        lax.all_gather(qkv_weight, ("fsdp", "ctx"), axis=0, tiled=True),
        lax.all_gather(output_weight, ("fsdp", "ctx"), axis=0, tiled=True),
        lax.all_gather(mlp_gain, ("fsdp", "ctx"), axis=0, tiled=True),
        lax.all_gather(expand_weight, ("fsdp", "ctx"), axis=0, tiled=True),
        lax.all_gather(contract_weight, ("fsdp", "ctx"), axis=0, tiled=True),
    )
    full_input_gain, full_qkv, full_output, full_mlp_gain, full_expand, full_contract = gathered
    residual = tokens[0].astype(jnp.float32)
    row_count, model_width = residual.shape
    head_count = model_width // HEAD_DIM
    cosine, sine = rope_tables(positions[0], HEAD_DIM)
    normed1, scaled1, xn1 = layer_norm(residual, full_input_gain)
    projected = jnp.dot(xn1, full_qkv, preferred_element_type=jnp.float32).reshape(
        row_count, 3, head_count, HEAD_DIM
    )
    queries = rotate(projected[:, 0], cosine, sine).astype(jnp.bfloat16)
    key_rows = rotate(projected[:, 1], cosine, sine).astype(jnp.bfloat16)
    value_rows = projected[:, 2].astype(jnp.bfloat16)
    packed = jnp.concatenate(
        [key_rows.reshape(row_count, model_width), value_rows.reshape(row_count, model_width)],
        axis=1,
    )
    extended = extended_2(packed, (("ctx", 0),), HALF)
    extent = extended.shape[0]
    key_ext = extended[:, :model_width].reshape(extent, head_count, HEAD_DIM)
    value_ext = extended[:, model_width:].reshape(extent, head_count, HEAD_DIM)
    additive = mask_bias[0]
    mixed, log_total = attend(queries, key_ext, value_ext, additive)
    attention = mixed.reshape(row_count, model_width)
    hidden = residual + jnp.dot(attention, full_output, preferred_element_type=jnp.float32)
    normed2, scaled2, xn2 = layer_norm(hidden, full_mlp_gain)
    lifted = jnp.dot(xn2, full_expand, preferred_element_type=jnp.float32)
    ff_width = lifted.shape[1] // 2
    gelu_input = lifted[:, :ff_width]
    gate_part = lifted[:, ff_width:]
    activated = jax.nn.gelu(gelu_input, approximate=False)
    gated = (activated * gate_part).astype(jnp.bfloat16)
    down_out = jnp.einsum("tf,jf->tj", gated, full_contract, preferred_element_type=jnp.float32)
    layer_out = (hidden + down_out).astype(jnp.bfloat16)
    back_input_gain, back_qkv, back_output, back_mlp_gain, back_expand, back_contract = gathered
    grad_out = cotangent[0]
    d_gated = jnp.dot(grad_out, back_contract, preferred_element_type=jnp.float32)
    d_lifted = jnp.concatenate(
        [d_gated * gate_part * gelu_slope(gelu_input), d_gated * activated], axis=1
    ).astype(jnp.bfloat16)
    d_xn2 = jnp.einsum("tc,dc->td", d_lifted, back_expand, preferred_element_type=jnp.float32)
    d_norm2, mlp_gain_term = layer_norm_back(d_xn2, normed2, scaled2, back_mlp_gain)
    d_hidden = grad_out.astype(jnp.float32) + d_norm2
    d_proj = d_hidden.astype(jnp.bfloat16)
    d_attention = jnp.einsum(
        "tj,ij->ti", d_proj, back_output, preferred_element_type=jnp.float32
    ).astype(jnp.bfloat16)
    d_queries, d_key_ext, d_value_ext = attend_back(
        queries,
        key_ext,
        value_ext,
        additive,
        log_total,
        d_attention.reshape(row_count, head_count, HEAD_DIM),
    )
    grad_ext = jnp.concatenate(
        [d_key_ext.reshape(extent, model_width), d_value_ext.reshape(extent, model_width)], axis=1
    )
    from_next = from_behind(grad_ext[:HALF], "ctx", -1)
    from_prev = from_behind(grad_ext[row_count + HALF :], "ctx", 1)
    grad_kv = grad_ext[HALF : HALF + row_count]
    grad_kv = grad_kv + jnp.pad(from_prev, ((0, row_count - HALF), (0, 0)))
    grad_kv = grad_kv + jnp.pad(from_next, ((row_count - HALF, 0), (0, 0)))
    d_keys = rotate_back(
        grad_kv[:, :model_width].reshape(row_count, head_count, HEAD_DIM), cosine, sine
    )
    d_values = grad_kv[:, model_width:]
    d_queries = rotate_back(d_queries, cosine, sine)
    d_projected = jnp.concatenate(
        [
            d_queries.reshape(row_count, model_width),
            d_keys.reshape(row_count, model_width),
            d_values,
        ],
        axis=1,
    ).astype(jnp.bfloat16)
    d_xn1 = jnp.einsum("tc,dc->td", d_projected, back_qkv, preferred_element_type=jnp.float32)
    d_norm1, input_gain_term = layer_norm_back(d_xn1, normed1, scaled1, back_input_gain)
    input_grad = (d_hidden + d_norm1).astype(jnp.bfloat16)
    left_one, left_two, left_three, left_four = (xn1, attention, xn2, grad_out)
    gain_one, gain_two = (input_gain_term, mlp_gain_term)
    qkv_term = jnp.einsum("ti,tj->ij", left_one, d_projected, preferred_element_type=jnp.float32)
    output_term = jnp.einsum("ti,tj->ij", left_two, d_proj, preferred_element_type=jnp.float32)
    expand_term = jnp.einsum("ti,tj->ij", left_three, d_lifted, preferred_element_type=jnp.float32)
    contract_term = jnp.einsum("ti,tj->ij", left_four, gated, preferred_element_type=jnp.float32)
    first_gain = gain_one[:, None]
    second_gain = gain_two[:, None]
    shares = lax.psum_scatter(
        jnp.concatenate(
            [qkv_term, output_term, expand_term, contract_term, first_gain, second_gain], axis=1
        ),
        ("fsdp", "ctx"),
        scatter_dimension=0,
        tiled=True,
    )
    result = lax.psum(shares, "replica")
    qkv_cols = 3 * model_width
    expand_cols = 2 * ff_width
    qkv_grad = result[:, :qkv_cols]
    output_grad = result[:, qkv_cols : qkv_cols + model_width]
    offset = qkv_cols + model_width
    expand_grad = result[:, offset : offset + expand_cols]
    offset = offset + expand_cols
    contract_grad = result[:, offset : offset + ff_width]
    offset = offset + ff_width
    input_gain_grad = result[:, offset]
    mlp_gain_grad = result[:, offset + 1]
    return (
        layer_out[None],
        input_grad[None],
        input_gain_grad,
        qkv_grad,
        output_grad,
        mlp_gain_grad,
        expand_grad,
        contract_grad,
    )


def solution(mesh):
    in_specs = (
        P(("replica", "fsdp"), "ctx", None),
        P(("fsdp", "ctx")),
        P(("fsdp", "ctx"), None),
        P(("fsdp", "ctx"), None),
        P(("fsdp", "ctx")),
        P(("fsdp", "ctx"), None),
        P(("fsdp", "ctx"), None),
        P(("replica", "fsdp"), "ctx"),
        P(("replica", "fsdp"), "ctx", None),
        P(("replica", "fsdp"), "ctx", None),
    )
    out_specs = (
        P(("replica", "fsdp"), "ctx", None),
        P(("replica", "fsdp"), "ctx", None),
        P(("fsdp", "ctx")),
        P(("fsdp", "ctx"), None),
        P(("fsdp", "ctx"), None),
        P(("fsdp", "ctx")),
        P(("fsdp", "ctx"), None),
        P(("fsdp", "ctx"), None),
    )
    return jax.shard_map(body, mesh=mesh, in_specs=in_specs, out_specs=out_specs, check_vma=False)
```

profile of v0, /device:TPU:0, one launch (start us, length us, event | category | flops | bytes accessed | tf_op | source)
XLA Modules:
  0.0 876.1 jit_solution(3466343634456219086)
XLA Ops:
  10.0 12.2 %all-gather = bf16[8,1,128]{2,1,0:T(2,128)(2,1)S(1)} all-gather(bf16[1,1,128]{2,1,0:T(2,128)(2,1)S(1)} %bitcast.140), channel_id=1, replica_groups=mesh['replica'=4,'fsdp'=4,'ctx'=2] {'fsdp','ctx'}, dimensions={0}, use_global_device_ids=true | all-gather | bytes 2304 | tf_op jit(solution)/shard_map/all_gather | solution.py:129
  22.9 35.3 %all-gather.7.cloned.1.call-done = bf16[1024,3072]{1,0:T(8,128)(2,1)} async-done(((bf16[128,3072]{1,0:T(8,128)(2,1)}), bf16[1024,3072]{1,0:T(8,128)(2,1)}) %all-gather.7.cloned.1.call-update) | async-done | bytes 6291472 | tf_op jit(solution)/shard_map/all_gather | solution.py:130
  58.2 8.6 copy.35
  66.8 4.9 fusion.68
  72.2 3.5 collective-permute-start
  77.0 25.0 %all-gather.1 = bf16[8,1,128]{2,1,0:T(2,128)(2,1)S(1)} all-gather(bf16[1,1,128]{2,1,0:T(2,128)(2,1)S(1)} %bitcast.141), channel_id=1, replica_groups=mesh['replica'=4,'fsdp'=4,'ctx'=2] {'fsdp','ctx'}, dimensions={0}, use_global_device_ids=true | all-gather | bytes 2304 | tf_op jit(solution)/shard_map/all_gather | solution.py:132
  105.9 2.2 fusion.98
  108.4 51.5 %all-gather.11.cloned.1.call-done = bf16[1024,5248]{1,0:T(8,128)(2,1)} async-done(((bf16[128,5248]{1,0:T(8,128)(2,1)}), bf16[1024,5248]{1,0:T(8,128)(2,1)}) %all-gather.11.cloned.1.call-update) | async-done | bytes 10747920 | tf_op jit(solution)/shard_map/all_gather | solution.py:133
  159.9 7.3 fusion.94
  167.2 37.1 %all-gather.13.cloned.1.call-done = bf16[1024,2624]{0,1:T(8,128)(2,1)} async-done(((bf16[128,2624]{0,1:T(8,128)(2,1)}), bf16[1024,2624]{0,1:T(8,128)(2,1)}) %all-gather.13.cloned.1.call-update) | async-done | bytes 5373968 | tf_op jit(solution)/shard_map/all_gather | solution.py:134
  204.3 8.3 multiply_convert_fusion.1
  212.7 4.2 multiply_reduce_fusion.1
  219.4 1.8 copy.38
  221.2 3.0 fusion.99
  225.7 14.5 %fusion.27 = f32[128,16,64]{0,2,1:T(8,128)} fusion(bf16[256,16,64]{0,2,1:T(8,128)(2,1)} %bitcast.121, f32[16,128,256]{2,1,0:T(8,128)} %fusion.99, f32[16,128,256]{2,1,0:T(8,128)S(1)} %get-tuple-element.66, f32[16,128]{1,0:T(8,128)S(1)} %log_add_fusion), kind=kOutput, calls=%fused_computation.45 | convolution fusion | flops 70781184 | bytes 5251072 | tf_op jit(solution)/shard_map/hqk,khd->qhd/dot_general | solution.py:108
  240.2 14.6 %fusion.6 = f32[16,64,256]{2,1,0:T(8,128)} fusion(f32[16,128,256]{2,1,0:T(8,128)} %fusion.99, f32[16,128,256]{2,1,0:T(8,128)S(1)} %get-tuple-element.66, f32[16,128]{1,0:T(8,128)S(1)} %log_add_fusion, bf16[128,16,32]{0,2,1:T(8,128)(2,1)} %copy-done.21, bf16[128,16,32]{0,2,1:T(8,128)(2,1)S(1)} %get-tuple-element.53), kind=kOutput, calls=%fused_computation.16 | convolution fusion | flops 71305472 | bytes 5513216 | tf_op jit(solution)/shard_map/hqk,qhd->khd/dot_general | solution.py:109
  254.8 3.7 fusion.81
  258.6 8.9 %fusion.44 = f32[1024,5248]{1,0:T(8,128)} fusion(bf16[128,2624]{1,0:T(8,128)(2,1)S(1)} %copy-done.17, bf16[128,2624]{1,0:T(8,128)(2,1)S(1)} %copy-done.19, f32[128,1024]{1,0:T(8,128)S(1)} %get-tuple-element.68, f32[1024]{0:T(1024)S(1)} %bitcast.132, f32[128]{0:T(128)S(1)} %copy-done.30, f32[128]{0:T(128)S(1)} %copy-done.28), kind=kOutput, calls=%fused_computation.62 | convolution fusion | flops 1378942976 | bytes 23368704 | tf_op jit(solution)/shard_map/ti,tj->ij/dot_general | solution.py:218
  271.8 3.5 collective-permute-start.2
  276.7 5.8 convolution_bitcast_fusion
  282.4 4.5 collective-permute-done.2
  286.9 4.1 collective-permute-done.3
  292.9 6.5 fusion.65
  299.4 5.2 fusion.59
  304.8 51.3 %concatenate.45 = f32[1024,11970]{1,0:T(8,128)} concatenate(f32[1024,3072]{1,0:T(8,128)} %fusion.65, f32[1024,1024]{1,0:T(8,128)} %fusion.81, f32[1024,5248]{1,0:T(8,128)} %fusion.44, f32[1024,2624]{1,0:T(8,128)} %convolution_bitcast_fusion, f32[1024,1]{1,0:T(8,128)S(1)} %copy.46, f32[1024,1]{1,0:T(8,128)S(1)} %copy-done.8), dimensions={1} | concatenate | bytes 98058240 | tf_op jit(solution)/shard_map/concatenate | solution.py:223
  356.2 279.7 %reduce-scatter.2.cloned.1.call-done = f32[128,11970]{1,0:T(8,128)} async-done(((f32[1024,11970]{1,0:T(8,128)}), f32[128,11970]{1,0:T(8,128)}) %reduce-scatter.2.cloned.1.call-update) | async-done | bytes 6128656 | tf_op jit(solution)/shard_map/reduce_scatter | solution.py:222
  637.0 4.1 fusion.31
  642.1 214.6 %all-reduce.4.cloned.1.call-done = f32[128,11970]{1,0:T(8,128)} async-done(((f32[128,11970]{1,0:T(8,128)}), f32[128,11970]{1,0:T(8,128)}) %all-reduce.4.cloned.1.call-update) | async-done | bytes 6128656 | tf_op jit(solution)/shard_map/psum | solution.py:230
  859.6 1.6 slice_reduce_fusion
  861.2 1.9 slice.139
  863.1 2.7 slice.138
  865.8 3.4 slice.141
  (143 shorter events, 25.8 us)
Async XLA Ops:
  7.2 15.1 %copy-start.1 = (bf16[1,128,1024]{2,1,0:T(8,128)(2,1)S(1)}, bf16[1,128,1024]{2,1,0:T(8,128)(2,1)}, u32[]{:S(2)}) copy-start(bf16[1,128,1024]{2,1,0:T(8,128)(2,1)} %param.10) | copy-start | bytes 786436
  7.2 51.0 %all-gather.7.cloned.1.call-start = ((), (), s32[]{:S(2)}) async-start(), calls=%async_computation.1 | async-start | bytes 7077888 | tf_op jit(solution)/shard_map/all_gather | solution.py:130
  7.9 14.7 %copy-start.38 = (s32[1,128]{1,0:T(1,128)S(1)}, s32[1,128]{1,0:T(1,128)}, u32[]{:S(2)}) copy-start(s32[1,128]{1,0:T(1,128)} %param.17) | copy-start | bytes 1540
  7.9 98.0 %all-gather.9.cloned.1.call-start = ((), (), s32[]{:S(2)}) async-start(), calls=%async_computation.2 | async-start | bytes 2359296 | tf_op jit(solution)/shard_map/all_gather | solution.py:131
  8.7 151.2 %all-gather.11.cloned.1.call-start = ((), (), s32[]{:S(2)}) async-start(), calls=%async_computation.3 | async-start | bytes 12091392 | tf_op jit(solution)/shard_map/all_gather | solution.py:133
  9.4 194.9 %all-gather.13.cloned.1.call-start = ((), (), s32[]{:S(2)}) async-start(), calls=%async_computation.4 | async-start | bytes 6045696 | tf_op jit(solution)/shard_map/all_gather | solution.py:134
  10.0 625.9 %reduce-scatter.2.cloned.1.call-start = ((), (), s32[]{:S(2)}) async-start(), calls=%async_computation.5 | async-start | bytes 55443456 | tf_op jit(solution)/shard_map/reduce_scatter | solution.py:222
  22.4 44.4 %copy-start.31 = (f32[128]{0:T(128)}, f32[128]{0:T(128)S(1)}, u32[]{:S(2)}) copy-start(f32[128]{0:T(128)S(1)} %broadcast_multiply_fusion.5) | copy-start | bytes 1540
  22.7 44.1 %copy-start.33 = (f32[128]{0:T(128)}, f32[128]{0:T(128)S(1)}, u32[]{:S(2)}) copy-start(f32[128]{0:T(128)S(1)} %add_rsqrt_fusion.1) | copy-start | bytes 1540
  22.8 48.9 %copy-start.22 = (f32[128,32]{0,1:T(8,128)}, f32[128,32]{0,1:T(8,128)S(1)}, u32[]{:S(2)}) copy-start(f32[128,32]{0,1:T(8,128)S(1)} %get-tuple-element.63) | copy-start | bytes 49156
  22.8 48.9 %copy-start.24 = (f32[128,32]{0,1:T(8,128)}, f32[128,32]{0,1:T(8,128)S(1)}, u32[]{:S(2)}) copy-start(f32[128,32]{0,1:T(8,128)S(1)} %get-tuple-element.64) | copy-start | bytes 49156
  71.8 5.2 copy-start.37
  72.0 30.8 %copy-start.21 = (bf16[128,16,32]{0,2,1:T(8,128)(2,1)}, bf16[128,16,32]{0,2,1:T(8,128)(2,1)S(1)}, u32[]{:S(2)}) copy-start(bf16[128,16,32]{0,2,1:T(8,128)(2,1)S(1)} %get-tuple-element.54) | copy-start | bytes 393220
  72.2 29.7 %collective-permute-start = (bf16[64,2048]{0,1:T(8,128)(2,1)S(1)}, bf16[64,2048]{0,1:T(8,128)(2,1)S(1)}, u32[]{:S(2)}, u32[]{:S(2)}) collective-permute-start(bf16[64,2048]{0,1:T(8,128)(2,1)S(1)} %get-tuple-element.57), channel_id=1, source_target_pairs={{0,1},{2,3},{4,5},{6,7},{8,9},{10,11},{12,13},{14,15},{16,17},{18,... | collective-permute-start | bytes 786440 | tf_op jit(solution)/shard_map/ppermute | solution.py:24
  75.7 26.3 %collective-permute-start.1 = (bf16[64,2048]{0,1:T(8,128)(2,1)S(1)}, bf16[64,2048]{0,1:T(8,128)(2,1)S(1)}, u32[]{:S(2)}, u32[]{:S(2)}) collective-permute-start(bf16[64,2048]{0,1:T(8,128)(2,1)S(1)} %get-tuple-element.58), channel_id=1, source_target_pairs={{1,0},{3,2},{5,4},{7,6},{9,8},{11,10},{13,12},{15,14},{17,16},{19,... | collective-permute-start | bytes 786440 | tf_op jit(solution)/shard_map/ppermute | solution.py:26
  108.1 104.5 %copy-start.27 = (f32[128]{0:T(128)}, f32[128]{0:T(128)S(1)}, u32[]{:S(2)}) copy-start(f32[128]{0:T(128)S(1)} %broadcast_multiply_fusion.4) | copy-start | bytes 1540
  108.4 104.3 %copy-start.29 = (f32[128]{0:T(128)}, f32[128]{0:T(128)S(1)}, u32[]{:S(2)}) copy-start(f32[128]{0:T(128)S(1)} %add_rsqrt_fusion) | copy-start | bytes 1540
  159.9 44.4 %copy-start.13 = (bf16[1,128,1024]{2,1,0:T(8,128)(2,1)S(1)}, bf16[1,128,1024]{2,1,0:T(8,128)(2,1)}, u32[]{:S(2)}) copy-start(bf16[1,128,1024]{2,1,0:T(8,128)(2,1)} %param.19) | copy-start | bytes 786436
  204.3 8.3 copy-start
  212.6 4.3 copy-start.16
  212.6 4.3 copy-start.18
  212.6 4.2 copy-start.14
  212.6 5.2 copy-start.2
  254.8 3.7 copy-start.30
  258.6 8.9 %copy-start.5 = (f32[128,5248]{1,0:T(8,128)S(1)}, f32[128,5248]{1,0:T(8,128)}, u32[]{:S(2)}) copy-start(f32[128,5248]{1,0:T(8,128)} %fusion.94) | copy-start | bytes 8060932
  258.6 8.9 %copy-start.11 = (f32[128,2624]{1,0:T(8,128)S(1)}, f32[128,2624]{1,0:T(8,128)}, u32[]{:S(2)}) copy-start(f32[128,2624]{1,0:T(8,128)} %get-tuple-element.41) | copy-start | bytes 4030468
  271.7 5.0 copy-start.3
  271.7 5.0 copy-start.15
  271.8 15.1 %collective-permute-start.2 = (f32[64,2048]{1,0:T(8,128)S(1)}, f32[64,2048]{1,0:T(8,128)S(1)}, u32[]{:S(2)}, u32[]{:S(2)}) collective-permute-start(f32[64,2048]{1,0:T(8,128)S(1)} %get-tuple-element.43), channel_id=1, source_target_pairs={{0,1},{2,3},{4,5},{6,7},{8,9},{10,11},{12,13},{14,15},{16,17},{18,... | collective-permute-start | bytes 1572872 | tf_op jit(solution)/shard_map/ppermute | solution.py:36
  275.4 15.7 %collective-permute-start.3 = (f32[64,2048]{1,0:T(8,128)S(1)}, f32[64,2048]{1,0:T(8,128)S(1)}, u32[]{:S(2)}, u32[]{:S(2)}) collective-permute-start(f32[64,2048]{1,0:T(8,128)S(1)} %get-tuple-element.44), channel_id=1, source_target_pairs={{1,0},{3,2},{5,4},{7,6},{9,8},{11,10},{13,12},{15,14},{17,16},{19,... | collective-permute-start | bytes 1572872 | tf_op jit(solution)/shard_map/ppermute | solution.py:36
  299.4 5.4 copy-start.8
  356.1 500.6 %all-reduce.4.cloned.1.call-start = ((), (), s32[]{:S(2)}) async-start(), calls=%async_computation.6 | async-start | bytes 12320768 | tf_op jit(solution)/shard_map/psum | solution.py:230
  (18 other events, 33.4 us)
Sparse Core Ops, SparseCore 0:
  9.9 48.2 all-gather.6
  60.0 33.4 all-gather.8
  95.4 64.5 all-gather.10
  161.7 42.6 all-gather.12
  356.3 279.5 reduce-scatter.1
  638.1 218.5 all-reduce.3
where the time goes:
time: 878 us; the launch traced here: 876 us
  waiting for transfers between devices  630 us (72%)
  matrix products  97.8 us (11%)
  local copies, waits for them, and re-layouts  81 us (9%)
  blocking collectives  37.2 us (4%)
  between operations  14.8 us (2%)
  starting transfers between devices  9.81 us (1%)
    reduce_scatter x1, waiting for transfers between devices, body(): lax.psum_scatter(jnp.concatenate([qkv_term, output_term, expand_term, con...  280 us
    psum x1, waiting for transfers between devices, body(): result = lax.psum(shares, 'replica')  215 us
    all_gather x1, waiting for transfers between devices, body(): lax.all_gather(expand_weight, ('fsdp', 'ctx'), axis=0, tiled=True)  51.5 us
    concatenate x1, local copies, waits for them, and re-layouts, body(): jnp.concatenate([qkv_term, output_term, expand_term, contract_term, first...  51.3 us
    all_gather x1, waiting for transfers between devices, body(): lax.all_gather(contract_weight, ('fsdp', 'ctx'), axis=0, tiled=True)  37.1 us
    all_gather x1, waiting for transfers between devices, body(): lax.all_gather(qkv_weight, ('fsdp', 'ctx'), axis=0, tiled=True)  35.3 us
    all_gather x1, blocking collectives, body(): lax.all_gather(mlp_gain, ('fsdp', 'ctx'), axis=0, tiled=True)  25 us
  transfers between devices with their start and end apart: 10, of which 7 were waited for; matrix products, arithmetic and copies ran while one was open for 4% of the time, Pallas kernels for 0%

commit v1 on v0

--- a/solution.py
+++ b/solution.py
@@ -113,7 +113,7 @@
     return (d_queries, d_keys, d_values)
 
 
-def body(
+def body_generic(
     tokens,
     input_gain,
     qkv_weight,
@@ -251,6 +251,216 @@
     )
 
 
+X_BIT, CORE_BIT, Y_BIT = (1, 2, 4)
+PLANE = ("fsdp", "ctx")
+PLANE_SIZE = 8
+
+
+def swap(value, bit):
+    return lax.ppermute(value, PLANE, [(i, i ^ bit) for i in range(PLANE_SIZE)])
+
+
+def reorder(values, me):
+    width = values.shape[1] // PLANE_SIZE
+    return jnp.concatenate(
+        [
+            lax.dynamic_slice_in_dim(values, (me ^ block) * width, width, axis=1)
+            for block in range(PLANE_SIZE)
+        ],
+        axis=1,
+    )
+
+
+def gather_rows(own, after=None):
+    if after is not None:
+        own, _ = lax.optimization_barrier((own, after))
+    half = own.shape[0] // 2
+    over_x = swap(own, X_BIT)
+    over_y = swap(own, Y_BIT)
+    corner = jnp.concatenate([swap(over_x[:half], Y_BIT), swap(over_y[half:], X_BIT)], axis=0)
+    first = [own, over_x, over_y, corner]
+    second = [swap(part, CORE_BIT) for part in first]
+    full = jnp.concatenate(
+        [first[0], first[1], second[0], second[1], first[2], first[3], second[2], second[3]], axis=0
+    )
+    return (full, (over_x, over_y))
+
+
+def line_sum(part):
+    first = lax.ppermute(part.astype(jnp.bfloat16), "replica", [(0, 1), (3, 2)])
+    pair = (part + first.astype(jnp.float32)).astype(jnp.bfloat16)
+    other = lax.ppermute(pair, "replica", [(1, 2), (2, 1)])
+    total = (pair.astype(jnp.float32) + other.astype(jnp.float32)).astype(jnp.bfloat16)
+    back = lax.ppermute(total, "replica", [(1, 0), (2, 3)])
+    place = lax.axis_index("replica")
+    middle = (place == 1) | (place == 2)
+    return jnp.where(middle, total, back).astype(jnp.float32)
+
+
+def grad_rows(left, right, gather_bit, sum_bit):
+    rows = left.shape[0]
+    width = left.shape[1] // PLANE_SIZE
+    cols = right.shape[1]
+    block = lambda values, o: values[:, o * width : (o + 1) * width]
+    keep = [0, CORE_BIT, sum_bit, CORE_BIT | sum_bit]
+    packed = jnp.concatenate([right] + [block(left, o | gather_bit) for o in keep], axis=1)
+    mine = jnp.concatenate([right] + [block(left, o) for o in keep], axis=1)
+    both = jnp.concatenate([mine, swap(packed, gather_bit)], axis=0)
+    tail = lambda k: both[:, cols + k * width : cols + (k + 1) * width]
+    other = swap(jnp.concatenate([both[:, :cols], tail(1), tail(3)], axis=1), CORE_BIT)
+    rights = jnp.concatenate([both[:, :cols], other[:, :cols]], axis=0)
+    lefts = [
+        jnp.concatenate([tail(0), other[:, cols : cols + width]], axis=0),
+        jnp.concatenate([tail(2), other[:, cols + width :]], axis=0),
+    ]
+    product = lambda one: jnp.einsum("ti,tj->ij", one, rights, preferred_element_type=jnp.float32)
+    sent = swap(product(lefts[1]).astype(jnp.bfloat16), sum_bit)
+    return line_sum(product(lefts[0]) + sent.astype(jnp.float32))
+
+
+def halo_rows(values):
+    place = lax.axis_index("ctx")
+    head, tail = (values[:HALF], values[values.shape[0] - HALF :])
+    got = swap(jnp.where(place == 0, tail, head), X_BIT)
+    none = jnp.zeros_like(got)
+    return jnp.concatenate(
+        [jnp.where(place == 0, none, got), values, jnp.where(place == 0, got, none)], axis=0
+    )
+
+
+def halo_sum(values, row_count):
+    place = lax.axis_index("ctx")
+    head, tail = (values[:HALF], values[row_count + HALF :])
+    got = swap(jnp.where(place == 0, tail, head), X_BIT)
+    none = jnp.zeros((row_count - HALF, values.shape[1]), values.dtype)
+    return values[HALF : HALF + row_count] + jnp.where(
+        place == 0, jnp.concatenate([none, got], axis=0), jnp.concatenate([got, none], axis=0)
+    )
+
+
+def body_plane(
+    tokens,
+    input_gain,
+    qkv_weight,
+    output_weight,
+    mlp_gain,
+    expand_weight,
+    contract_weight,
+    positions,
+    mask_bias,
+    cotangent,
+):
+    me = lax.axis_index(PLANE)
+    shard, qkv_cols = qkv_weight.shape
+    gains = jnp.stack([input_gain, mlp_gain], axis=1)
+    gains = jnp.pad(gains, ((0, 0), (0, 126)))
+    packed_one, arrived = gather_rows(jnp.concatenate([qkv_weight, output_weight, gains], axis=1))
+    full_expand, arrived = gather_rows(expand_weight, arrived)
+    full_contract, arrived = gather_rows(contract_weight, arrived)
+    residual = tokens[0].astype(jnp.float32)
+    row_count, model_width = residual.shape
+    full_qkv = packed_one[:, :qkv_cols]
+    full_output = packed_one[:, qkv_cols : qkv_cols + model_width]
+    both_gains = packed_one[:, qkv_cols + model_width :][:, :2].T
+    both_gains = reorder(both_gains, me)
+    full_input_gain, full_mlp_gain = (both_gains[0], both_gains[1])
+    head_count = model_width // HEAD_DIM
+    cosine, sine = rope_tables(positions[0], HEAD_DIM)
+    normed1, scaled1, xn1 = layer_norm(residual, full_input_gain)
+    xn1 = reorder(xn1, me)
+    projected = jnp.dot(xn1, full_qkv, preferred_element_type=jnp.float32).reshape(
+        row_count, 3, head_count, HEAD_DIM
+    )
+    queries = rotate(projected[:, 0], cosine, sine).astype(jnp.bfloat16)
+    key_rows = rotate(projected[:, 1], cosine, sine).astype(jnp.bfloat16)
+    value_rows = projected[:, 2].astype(jnp.bfloat16)
+    packed = jnp.concatenate(
+        [key_rows.reshape(row_count, model_width), value_rows.reshape(row_count, model_width)],
+        axis=1,
+    )
+    extended = halo_rows(packed)
+    extent = extended.shape[0]
+    key_ext = extended[:, :model_width].reshape(extent, head_count, HEAD_DIM)
+    value_ext = extended[:, model_width:].reshape(extent, head_count, HEAD_DIM)
+    additive = mask_bias[0]
+    mixed, log_total = attend(queries, key_ext, value_ext, additive)
+    attention = reorder(mixed.reshape(row_count, model_width), me)
+    hidden = residual + jnp.dot(attention, full_output, preferred_element_type=jnp.float32)
+    normed2, scaled2, xn2 = layer_norm(hidden, full_mlp_gain)
+    xn2 = reorder(xn2, me)
+    lifted = jnp.dot(xn2, full_expand, preferred_element_type=jnp.float32)
+    ff_width = lifted.shape[1] // 2
+    gelu_input = lifted[:, :ff_width]
+    gate_part = lifted[:, ff_width:]
+    activated = jax.nn.gelu(gelu_input, approximate=False)
+    gated = (activated * gate_part).astype(jnp.bfloat16)
+    grad_out = cotangent[0]
+    grad_local = reorder(grad_out, me)
+    contract_grad = grad_rows(grad_local, gated, X_BIT, Y_BIT)
+    down_out = jnp.einsum("tf,jf->tj", gated, full_contract, preferred_element_type=jnp.float32)
+    layer_out = (hidden + reorder(down_out, me)).astype(jnp.bfloat16)
+    d_gated = jnp.dot(grad_local, full_contract, preferred_element_type=jnp.float32)
+    d_first = (d_gated * gate_part * gelu_slope(gelu_input)).astype(jnp.bfloat16)
+    d_second = (d_gated * activated).astype(jnp.bfloat16)
+    expand_first = grad_rows(xn2, d_first, Y_BIT, X_BIT)
+    expand_second = grad_rows(xn2, d_second, X_BIT, Y_BIT)
+    d_xn2 = jnp.einsum(
+        "tc,dc->td",
+        jnp.concatenate([d_first, d_second], axis=1),
+        full_expand,
+        preferred_element_type=jnp.float32,
+    )
+    d_norm2, mlp_gain_term = layer_norm_back(reorder(d_xn2, me), normed2, scaled2, full_mlp_gain)
+    d_hidden = grad_out.astype(jnp.float32) + d_norm2
+    d_proj = d_hidden.astype(jnp.bfloat16)
+    output_grad = grad_rows(attention, d_proj, Y_BIT, X_BIT)
+    d_attention = jnp.einsum("tj,ij->ti", d_proj, full_output, preferred_element_type=jnp.float32)
+    d_attention = reorder(d_attention.astype(jnp.bfloat16), me)
+    d_queries, d_key_ext, d_value_ext = attend_back(
+        queries,
+        key_ext,
+        value_ext,
+        additive,
+        log_total,
+        d_attention.reshape(row_count, head_count, HEAD_DIM),
+    )
+    grad_ext = jnp.concatenate(
+        [d_key_ext.reshape(extent, model_width), d_value_ext.reshape(extent, model_width)], axis=1
+    )
+    grad_kv = halo_sum(grad_ext, row_count)
+    d_keys = rotate_back(
+        grad_kv[:, :model_width].reshape(row_count, head_count, HEAD_DIM), cosine, sine
+    )
+    d_values = grad_kv[:, model_width:]
+    d_queries = rotate_back(d_queries, cosine, sine)
+    d_projected = jnp.concatenate(
+        [
+            d_queries.reshape(row_count, model_width),
+            d_keys.reshape(row_count, model_width),
+            d_values,
+        ],
+        axis=1,
+    ).astype(jnp.bfloat16)
+    middle = d_projected.shape[1] // 2
+    qkv_first = grad_rows(xn1, d_projected[:, :middle], X_BIT, Y_BIT)
+    qkv_second = grad_rows(xn1, d_projected[:, middle:], Y_BIT, X_BIT)
+    d_xn1 = jnp.einsum("tc,dc->td", d_projected, full_qkv, preferred_element_type=jnp.float32)
+    d_norm1, input_gain_term = layer_norm_back(reorder(d_xn1, me), normed1, scaled1, full_input_gain)
+    input_grad = (d_hidden + d_norm1).astype(jnp.bfloat16)
+    gain_sums = lax.psum(jnp.stack([input_gain_term, mlp_gain_term]), ("replica", "fsdp", "ctx"))
+    gain_rows = lax.dynamic_slice_in_dim(gain_sums, me * shard, shard, axis=1)
+    return (
+        layer_out[None],
+        input_grad[None],
+        gain_rows[0],
+        jnp.concatenate([qkv_first, qkv_second], axis=1),
+        output_grad,
+        gain_rows[1],
+        jnp.concatenate([expand_first, expand_second], axis=1),
+        contract_grad,
+    )
+
+
 def solution(mesh):
     in_specs = (
         P(("replica", "fsdp"), "ctx", None),
@@ -274,4 +484,6 @@
         P(("fsdp", "ctx"), None),
         P(("fsdp", "ctx"), None),
     )
+    sizes = (mesh.shape["replica"], mesh.shape["fsdp"], mesh.shape["ctx"])
+    body = body_plane if sizes == (4, 4, 2) else body_generic
     return jax.shard_map(body, mesh=mesh, in_specs=in_specs, out_specs=out_specs, check_vma=False)

time: 878 us -> 605 us (0.69); the launches traced: 876 us -> 593 us
  waiting for transfers between devices: 630 us -> 147 us
  local copies, waits for them, and re-layouts: 81 us -> 176 us
  starting transfers between devices: 9.81 us -> 66.5 us
  other arithmetic: 5.94 us -> 45.4 us
  between operations: 14.8 us -> 3.51 us
  matrix products: 97.8 us -> 108 us
  blocking collectives: 37.2 us -> 46.3 us
    reduce_scatter x1 -> x0, waiting for transfers between devices: 280 us -> none  [body(): lax.psum_scatter(jnp.concatenate([qkv_term, output_term, expand_term, con...]
    psum x1 -> x0, waiting for transfers between devices: 215 us -> none  [body(): result = lax.psum(shares, 'replica')]
    ppermute x4 -> x62, waiting for transfers between devices: 8.61 us -> 147 us  [the longest x44 70.5 us: swap(): return lax.ppermute(value, PLANE, [(i, i ^ bit) for i in range(PLANE_SIZE)])]
    all_gather x4 -> x0, waiting for transfers between devices: 124 us -> none  [the longest x1 51.5 us: body(): lax.all_gather(expand_weight, ('fsdp', 'ctx'), axis=0, tiled=True)]
    unnamed x79 -> x372, local copies, waits for them, and re-layouts: 4.43 us -> 75.5 us
    ppermute x4 -> x62, starting transfers between devices: 9.58 us -> 66.5 us  [the longest x44 35 us: swap(): return lax.ppermute(value, PLANE, [(i, i ^ bit) for i in range(PLANE_SIZE)])]
    psum x0 -> x1, blocking collectives: none -> 46.3 us  [body_plane(): lax.psum(jnp.stack([input_gain_term, mlp_gain_term]), ('replica', 'fsdp',...]
    all_gather x2 -> x0, blocking collectives: 37.2 us -> none  [the longest x1 25 us: body(): lax.all_gather(mlp_gain, ('fsdp', 'ctx'), axis=0, tiled=True)]
  transfers between devices with their start and end apart: 10 -> 62, of which waited for: 7 -> 18; matrix products, arithmetic and copies ran while one was open for 4% -> 42% of each run, Pallas kernels for 0% -> 0%
where the time goes in v1:
time: 605 us; the launch traced here: 593 us
  local copies, waits for them, and re-layouts  176 us (29%)
  waiting for transfers between devices  147 us (24%)
  matrix products  108 us (18%)
  starting transfers between devices  66.5 us (11%)
  blocking collectives  46.3 us (8%)
  other arithmetic  45.4 us (8%)
    unnamed x372, local copies, waits for them, and re-layouts  75.5 us
    ppermute x44, waiting for transfers between devices, swap(): return lax.ppermute(value, PLANE, [(i, i ^ bit) for i in range(PLANE_SIZE)])  70.5 us
    ppermute x6, waiting for transfers between devices, line_sum(): back = lax.ppermute(total, 'replica', [(1, 0), (2, 3)])  56.2 us
    psum x1, blocking collectives, body_plane(): lax.psum(jnp.stack([input_gain_term, mlp_gain_term]), ('replica', 'fsdp',...  46.3 us
    ppermute x44, starting transfers between devices, swap(): return lax.ppermute(value, PLANE, [(i, i ^ bit) for i in range(PLANE_SIZE)])  35 us
    dot_general x12, matrix products, grad_rows(): jnp.einsum('ti,tj->ij', one, rights, preferred_element_type=jnp.float32)  29.4 us
    dot_general x1, matrix products, attend_back(): jnp.einsum('hqk,qhd->khd', d_scores, queries, preferred_element_type=jnp....  23.1 us
    ppermute x6, waiting for transfers between devices, line_sum(): first = lax.ppermute(part.astype(jnp.bfloat16), 'replica', [(0, 1), (3, 2)])  20.1 us
  transfers between devices with their start and end apart: 62, of which 18 were waited for; matrix products, arithmetic and copies ran while one was open for 42% of the time, Pallas kernels for 0%

profile of v1, /device:TPU:0, one launch (start us, length us, event | category | flops | bytes accessed | tf_op | source)
XLA Modules:
  0.0 593.1 jit_solution(12258495169733625339)
XLA Ops:
  4.2 2.9 collective-permute-start
  15.0 16.3 %collective-permute-done = bf16[128,4224]{1,0:T(8,128)(2,1)S(1)} collective-permute-done((bf16[128,4224]{1,0:T(8,128)(2,1)}, bf16[128,4224]{1,0:T(8,128)(2,1)S(1)}, u32[]{:S(2)}, u32[]{:S(2)}) %collective-permute-start) | collective-permute-done | bytes 1081376 | tf_op jit(solution)/shard_map/ppermute | solution.py:260
  41.1 6.8 %collective-permute-done.4 = bf16[64,4224]{1,0:T(8,128)(2,1)S(1)} collective-permute-done((bf16[64,4224]{1,0:T(8,128)(2,1)S(1)}, bf16[64,4224]{1,0:T(8,128)(2,1)S(1)}, u32[]{:S(2)}, u32[]{:S(2)}) %collective-permute-start.4) | collective-permute-done | bytes 540704 | tf_op jit(solution)/shard_map/ppermute | solution.py:260
  49.6 25.0 %collective-permute-done.5 = bf16[64,4224]{1,0:T(8,128)(2,1)S(1)} collective-permute-done((bf16[64,4224]{1,0:T(8,128)(2,1)S(1)}, bf16[64,4224]{1,0:T(8,128)(2,1)S(1)}, u32[]{:S(2)}, u32[]{:S(2)}) %collective-permute-start.5) | collective-permute-done | bytes 540704 | tf_op jit(solution)/shard_map/ppermute | solution.py:260
  98.3 5.4 fusion.3
  114.0 9.0 %collective-permute-done.8 = bf16[64,2048]{0,1:T(8,128)(2,1)S(1)} collective-permute-done((bf16[64,2048]{0,1:T(8,128)(2,1)S(1)}, bf16[64,2048]{0,1:T(8,128)(2,1)S(1)}, u32[]{:S(2)}, u32[]{:S(2)}) %collective-permute-start.8) | collective-permute-done | bytes 262176 | tf_op jit(solution)/shard_map/ppermute | solution.py:260
  153.0 6.1 %collective-permute-done.21 = bf16[64,2624]{1,0:T(8,128)(2,1)S(1)} collective-permute-done((bf16[64,2624]{1,0:T(8,128)(2,1)}, bf16[64,2624]{1,0:T(8,128)(2,1)S(1)}, u32[]{:S(2)}, u32[]{:S(2)}) %collective-permute-start.21) | collective-permute-done | bytes 335904 | tf_op jit(solution)/shard_map/ppermute | solution.py:260
  178.3 8.7 %concatenate.247 = bf16[1024,2624]{0,1:T(8,128)(2,1)} concatenate(bf16[128,2624]{0,1:T(8,128)(2,1)} %param.16, bf16[128,2624]{0,1:T(8,128)(2,1)} %collective-permute-done.17, bf16[128,2624]{0,1:T(8,128)(2,1)} %collective-permute-done.18, bf16[128,2624]{0,1:T(8,128)(2,1)} %collective-permute-done.19, bf16[128,2624]{0,1:T(8,128)(2,1)S(1)} %copy-done.42, bf16[64,2624]{0,1:T(8,128)(2,1)} %copy.158, ...), dimensions={0} | concatenate | bytes 10747904 | tf_op jit(solution)/shard_map/concatenate | solution.py:283
  189.6 5.8 fusion.189
  195.4 4.7 multiply_convert_fusion.1
  200.2 8.2 %fusion.39 = f32[128,1024]{1,0:T(8,128)S(1)} fusion(bf16[1024,5248]{1,0:T(8,128)(2,1)} %constant_dynamic-update-slice_fusion.41, bf16[128,2624]{1,0:T(8,128)(2,1)S(1)} %get-tuple-element.52, bf16[128,2624]{1,0:T(8,128)(2,1)S(1)} %get-tuple-element.102), kind=kOutput, calls=%fused_computation.90 | convolution fusion | flops 1378418688 | bytes 12615680 | tf_op jit(solution)/shard_map/tc,dc->td/dot_general | solution.py:407
  225.9 23.1 %fusion.15 = f32[16,64,256]{2,1,0:T(8,128)} fusion(f32[16,128,256]{2,1,0:T(8,128)} %fusion.191, f32[16,128,256]{2,1,0:T(8,128)S(1)} %get-tuple-element.189, f32[16,128]{1,0:T(8,128)S(1)} %copy-done.112, bf16[128,16,32]{0,2,1:T(8,128)(2,1)} %get-tuple-element.138, bf16[128,16,32]{0,2,1:T(8,128)(2,1)} %get-tuple-element.137), kind=kOutput, calls=%fused_computation.56 | convolution fusion | flops 71305472 | bytes 5513216 | tf_op jit(solution)/shard_map/hqk,qhd->khd/dot_general | solution.py:109
  257.3 14.5 %fusion.43 = f32[128,16,64]{0,2,1:T(8,128)} fusion(bf16[256,16,64]{0,2,1:T(8,128)(2,1)} %bitcast.151, f32[16,128,256]{2,1,0:T(8,128)} %fusion.191, f32[16,128,256]{2,1,0:T(8,128)S(1)} %get-tuple-element.189, f32[16,128]{1,0:T(8,128)S(1)} %copy-done.112), kind=kOutput, calls=%fused_computation.114 | convolution fusion | flops 70781184 | bytes 5251072 | tf_op jit(solution)/shard_map/hqk,khd->qhd/dot_general | solution.py:108
  298.4 5.0 fusion.1
  305.7 46.3 %psum.7 = f32[2,1024]{1,0:T(2,128)} all-reduce(f32[2,1024]{1,0:T(2,128)S(1)} %pad_maximum_fusion.47), channel_id=1, replica_groups=mesh['replica'=4,'fsdp'=4,'ctx'=2] {'replica','fsdp','ctx'}, use_global_device_ids=true, to_apply=%region_13.14 | all-reduce | flops 2048 | bytes 16384 | tf_op jit(solution)/shard_map/psum | solution.py:450
  366.5 3.3 concatenate.295
  377.2 3.3 concatenate.288
  396.7 4.6 collective-permute-done.40
  406.6 3.0 collective-permute-done.41
  412.2 3.3 concatenate.304
  439.9 3.9 convolution_convert_fusion.1
  451.9 3.9 convolution_convert_fusion.2
  466.5 3.3 fusion.183
  469.8 5.3 collective-permute-start.35
  485.1 5.6 collective-permute-done.29
  494.3 7.2 %collective-permute-start.53 = (bf16[128,2624]{0,1:T(8,128)(2,1)S(1)}, bf16[128,2624]{0,1:T(8,128)(2,1)S(1)}, u32[]{:S(2)}, u32[]{:S(2)}) collective-permute-start(bf16[128,2624]{0,1:T(8,128)(2,1)S(1)} %get-tuple-element.198), channel_id=1, source_target_pairs={{0,8},{24,16},{1,9},{25,17},{2,10},{26,18},{3,11},{27,19},{4,12},{... | collective-permute-start | bytes 2015240 | tf_op jit(solution)/shard_map/ppermute | solution.py:290
  511.9 11.2 %collective-permute-done.37 = bf16[128,1536]{1,0:T(8,128)(2,1)S(1)} collective-permute-done((bf16[128,1536]{1,0:T(8,128)(2,1)S(1)}, bf16[128,1536]{1,0:T(8,128)(2,1)S(1)}, u32[]{:S(2)}, u32[]{:S(2)}) %collective-permute-start.37) | collective-permute-done | bytes 393248 | tf_op jit(solution)/shard_map/ppermute | solution.py:294
  523.1 5.1 collective-permute-done.31
  532.2 10.5 %collective-permute-done.59 = bf16[128,2624]{0,1:T(8,128)(2,1)S(1)} collective-permute-done((bf16[128,2624]{0,1:T(8,128)(2,1)S(1)}, bf16[128,2624]{0,1:T(8,128)(2,1)S(1)}, u32[]{:S(2)}, u32[]{:S(2)}) %collective-permute-start.59) | collective-permute-done | bytes 671776 | tf_op jit(solution)/shard_map/ppermute | solution.py:290
  548.1 17.3 %collective-permute-done.55 = bf16[128,2624]{0,1:T(8,128)(2,1)S(1)} collective-permute-done((bf16[128,2624]{0,1:T(8,128)(2,1)S(1)}, bf16[128,2624]{0,1:T(8,128)(2,1)S(1)}, u32[]{:S(2)}, u32[]{:S(2)}) %collective-permute-start.55) | collective-permute-done | bytes 671776 | tf_op jit(solution)/shard_map/ppermute | solution.py:294
  565.5 14.3 %collective-permute-done.49 = bf16[128,2624]{0,1:T(8,128)(2,1)S(1)} collective-permute-done((bf16[128,2624]{0,1:T(8,128)(2,1)S(1)}, bf16[128,2624]{0,1:T(8,128)(2,1)S(1)}, u32[]{:S(2)}, u32[]{:S(2)}) %collective-permute-start.49) | collective-permute-done | bytes 671776 | tf_op jit(solution)/shard_map/ppermute | solution.py:294
  582.3 8.1 %collective-permute-done.61 = bf16[128,2624]{0,1:T(8,128)(2,1)} collective-permute-done((bf16[128,2624]{0,1:T(8,128)(2,1)S(1)}, bf16[128,2624]{0,1:T(8,128)(2,1)}, u32[]{:S(2)}, u32[]{:S(2)}) %collective-permute-start.61) | collective-permute-done | bytes 671776 | tf_op jit(solution)/shard_map/ppermute | solution.py:294
  (652 shorter events, 288.5 us)
Async XLA Ops:
  8.7 30.1 %collective-permute-start.1 = (bf16[128,4224]{1,0:T(8,128)(2,1)}, bf16[128,4224]{1,0:T(8,128)(2,1)}, u32[]{:S(2)}, u32[]{:S(2)}) collective-permute-start(bf16[128,4224]{1,0:T(8,128)(2,1)} %get-tuple-element.117), channel_id=1, source_target_pairs={{0,2},{1,3},{2,0},{3,1},{4,6},{5,7},{6,4},{7,5},{8,10},{9,11},{10,... | collective-permute-start | bytes 3244040 | tf_op jit(solution)/shard_map/ppermute | solution.py:260
  32.7 47.4 %collective-permute-start.9 = (bf16[128,5248]{1,0:T(8,128)(2,1)}, bf16[128,5248]{1,0:T(8,128)(2,1)}, u32[]{:S(2)}, u32[]{:S(2)}) collective-permute-start(bf16[128,5248]{1,0:T(8,128)(2,1)} %param.15), channel_id=1, source_target_pairs={{0,1},{1,0},{2,3},{3,2},{4,5},{5,4},{6,7},{7,6},{8,9},{9,8},{10,11... | collective-permute-start | bytes 4030472 | tf_op jit(solution)/shard_map/ppermute | solution.py:260
  33.1 72.0 %collective-permute-start.10 = (bf16[128,5248]{1,0:T(8,128)(2,1)}, bf16[128,5248]{1,0:T(8,128)(2,1)}, u32[]{:S(2)}, u32[]{:S(2)}) collective-permute-start(bf16[128,5248]{1,0:T(8,128)(2,1)} %param.15), channel_id=1, source_target_pairs={{0,2},{1,3},{2,0},{3,1},{4,6},{5,7},{6,4},{7,5},{8,10},{9,11},{10,... | collective-permute-start | bytes 4030472 | tf_op jit(solution)/shard_map/ppermute | solution.py:260
  34.9 39.6 %collective-permute-start.5 = (bf16[64,4224]{1,0:T(8,128)(2,1)S(1)}, bf16[64,4224]{1,0:T(8,128)(2,1)S(1)}, u32[]{:S(2)}, u32[]{:S(2)}) collective-permute-start(bf16[64,4224]{1,0:T(8,128)(2,1)S(1)} %slice.353), channel_id=1, source_target_pairs={{0,1},{1,0},{2,3},{3,2},{4,5},{5,4},{6,7},{7,6},{8,9},{9,8},{10,11... | collective-permute-start | bytes 1622024 | tf_op jit(solution)/shard_map/ppermute | solution.py:260
  38.8 35.9 %collective-permute-start.2 = (bf16[128,4224]{1,0:T(8,128)(2,1)S(1)}, bf16[128,4224]{1,0:T(8,128)(2,1)S(1)}, u32[]{:S(2)}, u32[]{:S(2)}) collective-permute-start(bf16[128,4224]{1,0:T(8,128)(2,1)S(1)} %collective-permute-done), channel_id=1, source_target_pairs={{0,2},{1,3},{2,0},{3,1},{4,6},{5,7},{6,4},{7,5},{8,10},{9,11},{10,... | collective-permute-start | bytes 3244040 | tf_op jit(solution)/shard_map/ppermute | solution.py:260
  47.9 32.2 %collective-permute-start.12 = (bf16[128,5248]{1,0:T(8,128)(2,1)S(1)}, bf16[128,5248]{1,0:T(8,128)(2,1)S(1)}, u32[]{:S(2)}, u32[]{:S(2)}) collective-permute-start(bf16[128,5248]{1,0:T(8,128)(2,1)S(1)} %copy-done.51), channel_id=1, source_target_pairs={{0,4},{1,5},{2,6},{3,7},{4,0},{5,1},{6,2},{7,3},{8,12},{9,13},{10,... | collective-permute-start | bytes 4030472 | tf_op jit(solution)/shard_map/ppermute | solution.py:260
  80.1 62.4 %collective-permute-start.17 = (bf16[128,2624]{0,1:T(8,128)(2,1)}, bf16[128,2624]{0,1:T(8,128)(2,1)}, u32[]{:S(2)}, u32[]{:S(2)}) collective-permute-start(bf16[128,2624]{0,1:T(8,128)(2,1)} %param.16), channel_id=1, source_target_pairs={{0,1},{1,0},{2,3},{3,2},{4,5},{5,4},{6,7},{7,6},{8,9},{9,8},{10,11... | collective-permute-start | bytes 2015240 | tf_op jit(solution)/shard_map/ppermute | solution.py:260
  80.8 64.4 %collective-permute-start.20 = (bf16[128,2624]{0,1:T(8,128)(2,1)}, bf16[128,2624]{0,1:T(8,128)(2,1)S(1)}, u32[]{:S(2)}, u32[]{:S(2)}) collective-permute-start(bf16[128,2624]{0,1:T(8,128)(2,1)} %param.16), channel_id=1, source_target_pairs={{0,4},{1,5},{2,6},{3,7},{4,0},{5,1},{6,2},{7,3},{8,12},{9,13},{10,... | collective-permute-start | bytes 2015240 | tf_op jit(solution)/shard_map/ppermute | solution.py:260
  84.3 64.1 %collective-permute-start.13 = (bf16[64,5248]{1,0:T(8,128)(2,1)}, bf16[64,5248]{1,0:T(8,128)(2,1)}, u32[]{:S(2)}, u32[]{:S(2)}) collective-permute-start(bf16[64,5248]{1,0:T(8,128)(2,1)} %slice.370), channel_id=1, source_target_pairs={{0,4},{1,5},{2,6},{3,7},{4,0},{5,1},{6,2},{7,3},{8,12},{9,13},{10,... | collective-permute-start | bytes 2015240 | tf_op jit(solution)/shard_map/ppermute | solution.py:260
  88.2 61.7 %collective-permute-start.14 = (bf16[64,5248]{1,0:T(8,128)(2,1)}, bf16[64,5248]{1,0:T(8,128)(2,1)}, u32[]{:S(2)}, u32[]{:S(2)}) collective-permute-start(bf16[64,5248]{1,0:T(8,128)(2,1)} %slice.371), channel_id=1, source_target_pairs={{0,1},{1,0},{2,3},{3,2},{4,5},{5,4},{6,7},{7,6},{8,9},{9,8},{10,11... | collective-permute-start | bytes 2015240 | tf_op jit(solution)/shard_map/ppermute | solution.py:260
  123.0 43.4 %collective-permute-start.11 = (bf16[128,5248]{1,0:T(8,128)(2,1)}, bf16[128,5248]{1,0:T(8,128)(2,1)}, u32[]{:S(2)}, u32[]{:S(2)}) collective-permute-start(bf16[128,5248]{1,0:T(8,128)(2,1)} %collective-permute-done.9), channel_id=1, source_target_pairs={{0,2},{1,3},{2,0},{3,1},{4,6},{5,7},{6,4},{7,5},{8,10},{9,11},{10,... | collective-permute-start | bytes 4030472 | tf_op jit(solution)/shard_map/ppermute | solution.py:260
  142.5 34.9 %collective-permute-start.18 = (bf16[128,2624]{0,1:T(8,128)(2,1)}, bf16[128,2624]{0,1:T(8,128)(2,1)}, u32[]{:S(2)}, u32[]{:S(2)}) collective-permute-start(bf16[128,2624]{0,1:T(8,128)(2,1)} %param.16), channel_id=1, source_target_pairs={{0,2},{1,3},{2,0},{3,1},{4,6},{5,7},{6,4},{7,5},{8,10},{9,11},{10,... | collective-permute-start | bytes 2015240 | tf_op jit(solution)/shard_map/ppermute | solution.py:260
  145.2 29.3 %collective-permute-start.15 = (bf16[128,5248]{1,0:T(8,128)(2,1)}, bf16[128,5248]{1,0:T(8,128)(2,1)}, u32[]{:S(2)}, u32[]{:S(2)}) collective-permute-start(bf16[128,5248]{1,0:T(8,128)(2,1)} %copy-done.39), channel_id=1, source_target_pairs={{0,2},{1,3},{2,0},{3,1},{4,6},{5,7},{6,4},{7,5},{8,10},{9,11},{10,... | collective-permute-start | bytes 4030472 | tf_op jit(solution)/shard_map/ppermute | solution.py:260
  254.2 38.1 %collective-permute-start.25 = (f32[64,2048]{1,0:T(8,128)}, f32[64,2048]{1,0:T(8,128)}, u32[]{:S(2)}, u32[]{:S(2)}) collective-permute-start(f32[64,2048]{1,0:T(8,128)} %copy.163), channel_id=1, source_target_pairs={{0,1},{1,0},{2,3},{3,2},{4,5},{5,4},{6,7},{7,6},{8,9},{9,8},{10,11... | collective-permute-start | bytes 1572872 | tf_op jit(solution)/shard_map/ppermute | solution.py:260
  256.7 32.1 %collective-permute-start.38 = (bf16[128,1536]{1,0:T(8,128)(2,1)}, bf16[128,1536]{1,0:T(8,128)(2,1)}, u32[]{:S(2)}, u32[]{:S(2)}) collective-permute-start(bf16[128,1536]{1,0:T(8,128)(2,1)} %constant_dynamic-update-slice_fusion.115), channel_id=1, source_target_pairs={{0,4},{1,5},{2,6},{3,7},{4,0},{5,1},{6,2},{7,3},{8,12},{9,13},{10,... | collective-permute-start | bytes 1179656 | tf_op jit(solution)/shard_map/ppermute | solution.py:260
  280.6 82.5 %collective-permute-start.50 = (bf16[128,3136]{0,1:T(8,128)(2,1)}, bf16[128,3136]{0,1:T(8,128)(2,1)}, u32[]{:S(2)}, u32[]{:S(2)}) collective-permute-start(bf16[128,3136]{0,1:T(8,128)(2,1)} %copy.188), channel_id=1, source_target_pairs={{0,1},{1,0},{2,3},{3,2},{4,5},{5,4},{6,7},{7,6},{8,9},{9,8},{10,11... | collective-permute-start | bytes 2408456 | tf_op jit(solution)/shard_map/ppermute | solution.py:260
  283.3 89.1 %collective-permute-start.44 = (bf16[128,3136]{0,1:T(8,128)(2,1)}, bf16[128,3136]{0,1:T(8,128)(2,1)}, u32[]{:S(2)}, u32[]{:S(2)}) collective-permute-start(bf16[128,3136]{0,1:T(8,128)(2,1)} %copy.182), channel_id=1, source_target_pairs={{0,4},{1,5},{2,6},{3,7},{4,0},{5,1},{6,2},{7,3},{8,12},{9,13},{10,... | collective-permute-start | bytes 2408456 | tf_op jit(solution)/shard_map/ppermute | solution.py:260
  287.1 96.0 %collective-permute-start.56 = (bf16[128,3136]{0,1:T(8,128)(2,1)}, bf16[128,3136]{0,1:T(8,128)(2,1)}, u32[]{:S(2)}, u32[]{:S(2)}) collective-permute-start(bf16[128,3136]{0,1:T(8,128)(2,1)} %copy.194), channel_id=1, source_target_pairs={{0,1},{1,0},{2,3},{3,2},{4,5},{5,4},{6,7},{7,6},{8,9},{9,8},{10,11... | collective-permute-start | bytes 2408456 | tf_op jit(solution)/shard_map/ppermute | solution.py:260
  292.3 97.3 %collective-permute-start.39 = (bf16[256,1280]{1,0:T(8,128)(2,1)}, bf16[256,1280]{1,0:T(8,128)(2,1)}, u32[]{:S(2)}, u32[]{:S(2)}) collective-permute-start(bf16[256,1280]{1,0:T(8,128)(2,1)} %pad_maximum_fusion.25), channel_id=1, source_target_pairs={{0,2},{1,3},{2,0},{3,1},{4,6},{5,7},{6,4},{7,5},{8,10},{9,11},{10,... | collective-permute-start | bytes 1966088 | tf_op jit(solution)/shard_map/ppermute | solution.py:260
  358.9 28.6 %collective-permute-start.32 = (bf16[128,2048]{0,1:T(8,128)(2,1)}, bf16[128,2048]{0,1:T(8,128)(2,1)}, u32[]{:S(2)}, u32[]{:S(2)}) collective-permute-start(bf16[128,2048]{0,1:T(8,128)(2,1)} %get-tuple-element.163), channel_id=1, source_target_pairs={{0,4},{1,5},{2,6},{3,7},{4,0},{5,1},{6,2},{7,3},{8,12},{9,13},{10,... | collective-permute-start | bytes 1572872 | tf_op jit(solution)/shard_map/ppermute | solution.py:260
  363.2 32.4 %collective-permute-start.26 = (bf16[128,2048]{0,1:T(8,128)(2,1)}, bf16[128,2048]{0,1:T(8,128)(2,1)}, u32[]{:S(2)}, u32[]{:S(2)}) collective-permute-start(bf16[128,2048]{0,1:T(8,128)(2,1)} %get-tuple-element.162), channel_id=1, source_target_pairs={{0,1},{1,0},{2,3},{3,2},{4,5},{5,4},{6,7},{7,6},{8,9},{9,8},{10,11... | collective-permute-start | bytes 1572872 | tf_op jit(solution)/shard_map/ppermute | solution.py:260
  372.4 60.9 %collective-permute-start.51 = (bf16[256,2880]{0,1:T(8,128)(2,1)}, bf16[256,2880]{0,1:T(8,128)(2,1)}, u32[]{:S(2)}, u32[]{:S(2)}) collective-permute-start(bf16[256,2880]{0,1:T(8,128)(2,1)} %copy.190), channel_id=1, source_target_pairs={{0,2},{1,3},{2,0},{3,1},{4,6},{5,7},{6,4},{7,5},{8,10},{9,11},{10,... | collective-permute-start | bytes 4423688 | tf_op jit(solution)/shard_map/ppermute | solution.py:260
  383.1 61.4 %collective-permute-start.45 = (bf16[256,2880]{0,1:T(8,128)(2,1)}, bf16[256,2880]{0,1:T(8,128)(2,1)}, u32[]{:S(2)}, u32[]{:S(2)}) collective-permute-start(bf16[256,2880]{0,1:T(8,128)(2,1)} %copy.184), channel_id=1, source_target_pairs={{0,2},{1,3},{2,0},{3,1},{4,6},{5,7},{6,4},{7,5},{8,10},{9,11},{10,... | collective-permute-start | bytes 4423688 | tf_op jit(solution)/shard_map/ppermute | solution.py:260
  418.2 40.2 %collective-permute-start.57 = (bf16[256,2880]{0,1:T(8,128)(2,1)}, bf16[256,2880]{0,1:T(8,128)(2,1)}, u32[]{:S(2)}, u32[]{:S(2)}) collective-permute-start(bf16[256,2880]{0,1:T(8,128)(2,1)} %copy.196), channel_id=1, source_target_pairs={{0,2},{1,3},{2,0},{3,1},{4,6},{5,7},{6,4},{7,5},{8,10},{9,11},{10,... | collective-permute-start | bytes 4423688 | tf_op jit(solution)/shard_map/ppermute | solution.py:260
  425.0 41.5 %collective-permute-start.34 = (bf16[128,1536]{1,0:T(8,128)(2,1)}, bf16[128,1536]{1,0:T(8,128)(2,1)}, u32[]{:S(2)}, u32[]{:S(2)}) collective-permute-start(bf16[128,1536]{1,0:T(8,128)(2,1)} %convolution_convert_fusion.3), channel_id=1, source_target_pairs={{0,1},{1,0},{2,3},{3,2},{4,5},{5,4},{6,7},{7,6},{8,9},{9,8},{10,11... | collective-permute-start | bytes 1179656 | tf_op jit(solution)/shard_map/ppermute | solution.py:260
  431.2 48.4 %collective-permute-start.28 = (bf16[128,1536]{1,0:T(8,128)(2,1)}, bf16[128,1536]{1,0:T(8,128)(2,1)}, u32[]{:S(2)}, u32[]{:S(2)}) collective-permute-start(bf16[128,1536]{1,0:T(8,128)(2,1)} %convolution_convert_fusion.4), channel_id=1, source_target_pairs={{0,4},{1,5},{2,6},{3,7},{4,0},{5,1},{6,2},{7,3},{8,12},{9,13},{10,... | collective-permute-start | bytes 1179656 | tf_op jit(solution)/shard_map/ppermute | solution.py:260
  443.8 47.9 %collective-permute-start.52 = (bf16[128,2624]{0,1:T(8,128)(2,1)}, bf16[128,2624]{0,1:T(8,128)(2,1)}, u32[]{:S(2)}, u32[]{:S(2)}) collective-permute-start(bf16[128,2624]{0,1:T(8,128)(2,1)} %convolution_convert_fusion.1), channel_id=1, source_target_pairs={{0,4},{1,5},{2,6},{3,7},{4,0},{5,1},{6,2},{7,3},{8,12},{9,13},{10,... | collective-permute-start | bytes 2015240 | tf_op jit(solution)/shard_map/ppermute | solution.py:260
  455.8 45.7 %collective-permute-start.46 = (bf16[128,2624]{0,1:T(8,128)(2,1)}, bf16[128,2624]{0,1:T(8,128)(2,1)}, u32[]{:S(2)}, u32[]{:S(2)}) collective-permute-start(bf16[128,2624]{0,1:T(8,128)(2,1)} %convolution_convert_fusion.2), channel_id=1, source_target_pairs={{0,1},{1,0},{2,3},{3,2},{4,5},{5,4},{6,7},{7,6},{8,9},{9,8},{10,11... | collective-permute-start | bytes 2015240 | tf_op jit(solution)/shard_map/ppermute | solution.py:260
  494.3 35.3 %collective-permute-start.53 = (bf16[128,2624]{0,1:T(8,128)(2,1)S(1)}, bf16[128,2624]{0,1:T(8,128)(2,1)S(1)}, u32[]{:S(2)}, u32[]{:S(2)}) collective-permute-start(bf16[128,2624]{0,1:T(8,128)(2,1)S(1)} %get-tuple-element.198), channel_id=1, source_target_pairs={{0,8},{24,16},{1,9},{25,17},{2,10},{26,18},{3,11},{27,19},{4,12},{... | collective-permute-start | bytes 2015240 | tf_op jit(solution)/shard_map/ppermute | solution.py:290
  507.7 35.1 %collective-permute-start.59 = (bf16[128,2624]{0,1:T(8,128)(2,1)S(1)}, bf16[128,2624]{0,1:T(8,128)(2,1)S(1)}, u32[]{:S(2)}, u32[]{:S(2)}) collective-permute-start(bf16[128,2624]{0,1:T(8,128)(2,1)S(1)} %get-tuple-element.202), channel_id=1, source_target_pairs={{0,8},{24,16},{1,9},{25,17},{2,10},{26,18},{3,11},{27,19},{4,12},{... | collective-permute-start | bytes 2015240 | tf_op jit(solution)/shard_map/ppermute | solution.py:290
  545.3 34.5 %collective-permute-start.49 = (bf16[128,2624]{0,1:T(8,128)(2,1)S(1)}, bf16[128,2624]{0,1:T(8,128)(2,1)S(1)}, u32[]{:S(2)}, u32[]{:S(2)}) collective-permute-start(bf16[128,2624]{0,1:T(8,128)(2,1)S(1)} %add_convert_fusion.4), channel_id=1, source_target_pairs={{8,0},{16,24},{9,1},{17,25},{10,2},{18,26},{11,3},{19,27},{12,4},{... | collective-permute-start | bytes 2015240 | tf_op jit(solution)/shard_map/ppermute | solution.py:294
  546.8 43.6 %collective-permute-start.61 = (bf16[128,2624]{0,1:T(8,128)(2,1)S(1)}, bf16[128,2624]{0,1:T(8,128)(2,1)}, u32[]{:S(2)}, u32[]{:S(2)}) collective-permute-start(bf16[128,2624]{0,1:T(8,128)(2,1)S(1)} %add_convert_fusion), channel_id=1, source_target_pairs={{8,0},{16,24},{9,1},{17,25},{10,2},{18,26},{11,3},{19,27},{12,4},{... | collective-permute-start | bytes 2015240 | tf_op jit(solution)/shard_map/ppermute | solution.py:294
  (160 other events, 1574.2 us)

commit v2 on v0

--- a/solution.py
+++ b/solution.py
@@ -3,6 +3,8 @@
 import jax
 import jax.numpy as jnp
 from jax import lax
+from jax.experimental import pallas as pl
+from jax.experimental.pallas import tpu as pltpu
 from jax.sharding import PartitionSpec as P
 
 HEAD_DIM = 64
@@ -113,7 +115,7 @@
     return (d_queries, d_keys, d_values)
 
 
-def body(
+def body_generic(
     tokens,
     input_gain,
     qkv_weight,
@@ -251,6 +253,495 @@
     )
 
 
+X_BIT, CORE_BIT, Y_BIT = (1, 2, 4)
+PLANE = ("fsdp", "ctx")
+PLANE_SIZE = 8
+PIECES = 10
+VMEM_BYTES = 50 * 1024 * 1024
+F32, BF16 = (jnp.float32, jnp.bfloat16)
+
+
+def swap(value, bit):
+    return lax.ppermute(value, PLANE, [(i, i ^ bit) for i in range(PLANE_SIZE)])
+
+
+def gather_pieces(own, after=None):
+    if after is not None:
+        own, _ = lax.optimization_barrier((own, after))
+    half = own.shape[0] // 2
+    over_x = swap(own, X_BIT)
+    over_y = swap(own, Y_BIT)
+    first = [own, over_x, over_y, swap(over_x[:half], Y_BIT), swap(over_y[half:], X_BIT)]
+    second = [swap(part, CORE_BIT) for part in first]
+    return (first + second, (over_x, over_y))
+
+
+def fill(pieces, target, sems, me, columns=None):
+    shard = target.shape[0] // PLANE_SIZE
+    half = shard // 2
+    corner = X_BIT | Y_BIT
+    places = [(0, 0, shard), (X_BIT, 0, shard), (Y_BIT, 0, shard), (corner, 0, half), (corner, half, half)]
+    places = places + [(offset | CORE_BIT, start, rows) for offset, start, rows in places]
+    copies = []
+    for index, (piece, (offset, start, rows)) in enumerate(zip(pieces, places)):
+        row = pl.multiple_of((me ^ offset) * shard + start, half)
+        source = piece if columns is None else piece.at[:, columns]
+        copies.append(pltpu.make_async_copy(source, target.at[pl.ds(row, rows)], sems.at[index]))
+    for copy in copies:
+        copy.start()
+    return copies
+
+
+def wait_all(copies):
+    for copy in copies:
+        copy.wait()
+
+
+def pack(keep, send, left, right, gather_bit, sum_bit, me):
+    width = left.shape[1] // PLANE_SIZE
+    for slot, offset in enumerate([0, CORE_BIT, sum_bit, CORE_BIT | sum_bit]):
+        for target, flip in ((keep, 0), (send, gather_bit)):
+            source = pl.multiple_of((me ^ (offset | flip)) * width, width)
+            target[:, slot * width : (slot + 1) * width] = left[:, pl.ds(source, width)]
+    keep[:, 4 * width :] = right
+    send[:, 4 * width :] = right
+
+
+def turn(values, cosine, sine):
+    lane = lax.broadcasted_iota(jnp.int32, values.shape, 1)
+    low = lane % HEAD_DIM < HEAD_DIM // 2
+    other = jnp.where(
+        low,
+        pltpu.roll(values, values.shape[1] - HEAD_DIM // 2, 1),
+        pltpu.roll(values, HEAD_DIM // 2, 1),
+    )
+    return values * cosine + other * sine
+
+
+def dot_tt(one, two):
+    return lax.dot_general(one, two, (((0,), (0,)), ((), ())), preferred_element_type=F32)
+
+
+def dot_nt(one, two):
+    return lax.dot_general(one, two, (((1,), (1,)), ((), ())), preferred_element_type=F32)
+
+
+def dot_nn(one, two):
+    return jnp.dot(one, two, preferred_element_type=F32)
+
+
+def norm_parts(values):
+    center = values - jnp.mean(values, axis=-1, keepdims=True)
+    variance = jnp.mean(center * center, axis=-1, keepdims=True)
+    scaled = lax.rsqrt(variance + EPS)
+    return (center * scaled, scaled)
+
+
+def norm_back(incoming, normed, scaled, gain):
+    weighted = incoming * gain
+    gain_grad = jnp.sum(incoming * normed, axis=0, keepdims=True)
+    mean_one = jnp.mean(weighted, axis=-1, keepdims=True)
+    mean_two = jnp.mean(weighted * normed, axis=-1, keepdims=True)
+    return (scaled * (weighted - mean_one - normed * mean_two), gain_grad)
+
+
+def front_kernel(place, tokens, cosine, sine, *refs):
+    pieces, (queries, keys_values, edge, xn1, gains, weight, sems) = (refs[:PIECES], refs[PIECES:])
+    me, along = (place[0], place[1])
+    copies = fill(pieces, weight, sems, me)
+    normed, _ = norm_parts(tokens[...].astype(F32))
+    width = tokens.shape[1]
+    wait_all(copies)
+    turned = weight[:, 4 * width :].astype(F32).T
+    gains[...] = turned[: gains.shape[0]]
+    rounded = (normed * gains[0:1, :]).astype(BF16)
+    xn1[...] = rounded
+    pair = cosine.shape[1]
+    projected = dot_nn(rounded, weight[:, : 3 * width])
+    for start in range(0, width, pair):
+        part = projected[:, start : start + pair]
+        queries[:, start : start + pair] = turn(part, cosine[...], sine[...]).astype(BF16)
+        part = projected[:, width + start : width + start + pair]
+        keys_values[:, start : start + pair] = turn(part, cosine[...], sine[...]).astype(BF16)
+    keys_values[:, width:] = projected[:, 2 * width :].astype(BF16)
+    rows = edge.shape[0]
+    edge[...] = keys_values[pl.ds(pl.multiple_of((1 - along) * rows, rows), rows), :]
+
+
+def head_masks(shape):
+    lane = lax.broadcasted_iota(jnp.int32, shape, 1)
+    return lane < HEAD_DIM
+
+
+def attend_kernel(place, queries, keys_values, edge, bias, tokens, gains, *refs):
+    pieces, (attention, totals, hidden, xn2, weight, sems) = (refs[:PIECES], refs[PIECES:])
+    width = tokens.shape[1]
+    copies = fill(pieces, weight, sems, place[0], pl.ds(3 * width, width))
+    pair = 2 * HEAD_DIM
+    factor = 1.0 / math.sqrt(HEAD_DIM)
+    rows = queries.shape[0]
+    is_first = head_masks((rows, pair))
+    lane = lax.broadcasted_iota(jnp.int32, totals.shape, 1)
+    logs = jnp.zeros(totals.shape, F32)
+    for start in range(0, width, pair):
+        two = queries[:, start : start + pair]
+        keys = jnp.concatenate([keys_values[:, start : start + pair], edge[:, start : start + pair]], axis=0)
+        vals = jnp.concatenate(
+            [keys_values[:, width + start : width + start + pair], edge[:, width + start : width + start + pair]],
+            axis=0,
+        )
+        outs = []
+        for which in range(2):
+            mask = is_first if which == 0 else jnp.logical_not(is_first)
+            one = jnp.where(mask, two, jnp.zeros_like(two))
+            scores = dot_nt(one, keys) * factor + bias[...]
+            peak = jnp.max(scores, axis=-1, keepdims=True)
+            exponent = jnp.exp(scores - peak)
+            total = jnp.sum(exponent, axis=-1, keepdims=True)
+            soft = (exponent / total).astype(BF16)
+            outs.append(dot_nn(soft, vals))
+            logs = jnp.where(lane == 2 * (start // pair) + which, peak + jnp.log(total), logs)
+        attention[:, start : start + pair] = jnp.where(is_first, outs[0], outs[1]).astype(BF16)
+    totals[...] = logs
+    wait_all(copies)
+    result = tokens[...].astype(F32) + dot_nn(attention[...], weight[...])
+    hidden[...] = result
+    normed, _ = norm_parts(result)
+    xn2[...] = (normed * gains[1:2, :]).astype(BF16)
+
+
+def lift_kernel(place, xn2, grad_out, *refs):
+    first, second, rest = (refs[:PIECES], refs[PIECES : 2 * PIECES], refs[2 * PIECES :])
+    keep, send, slope_gate, active, gelu_weight, gate_weight, sems_one, sems_two = rest
+    me = place[0]
+    copies = fill(first, gelu_weight, sems_one, me)
+    others = fill(second, gate_weight, sems_two, me)
+    wait_all(copies)
+    gelu_input = dot_nn(xn2[...], gelu_weight[...])
+    wait_all(others)
+    gate_part = dot_nn(xn2[...], gate_weight[...])
+    cdf_part = 0.5 * (1.0 + lax.erf(gelu_input * (1.0 / math.sqrt(2.0))))
+    density = jnp.exp(-0.5 * gelu_input * gelu_input) * (1.0 / math.sqrt(2.0 * math.pi))
+    activated = gelu_input * cdf_part
+    active[...] = activated
+    slope_gate[...] = gate_part * (cdf_part + gelu_input * density)
+    pack(keep, send, grad_out, (activated * gate_part).astype(BF16), X_BIT, Y_BIT, me)
+
+
+def contract_kernel(place, gated_pack, grad_out, xn2, hidden, slope_gate, active, *refs):
+    pieces, rest = (refs[:PIECES], refs[PIECES:])
+    layer_out, keep_one, send_one, keep_two, send_two, weight, sems = rest
+    me = place[0]
+    wait_all(fill(pieces, weight, sems, me))
+    d_gated = dot_nn(grad_out[...], weight[...])
+    pack(keep_one, send_one, xn2, (d_gated * slope_gate[...]).astype(BF16), Y_BIT, X_BIT, me)
+    pack(keep_two, send_two, xn2, (d_gated * active[...]).astype(BF16), X_BIT, Y_BIT, me)
+    gated = gated_pack[:, xn2.shape[1] // 2 :]
+    layer_out[...] = (hidden[...] + dot_nt(gated, weight[...])).astype(BF16)
+
+
+def hidden_back_kernel(place, pack_one, pack_two, grad_out, hidden, gains, attention, *refs):
+    first, second, third = (refs[:PIECES], refs[PIECES : 2 * PIECES], refs[2 * PIECES : 3 * PIECES])
+    keep, send, d_hidden, d_attention, gain_grad = refs[3 * PIECES : 3 * PIECES + 5]
+    gelu_weight, gate_weight, weight, sems_one, sems_two, sems_three = refs[3 * PIECES + 5 :]
+    me = place[0]
+    width = hidden.shape[1]
+    copies = fill(first, gelu_weight, sems_one, me)
+    others = fill(second, gate_weight, sems_two, me)
+    lasts = fill(third, weight, sems_three, me, pl.ds(3 * width, width))
+    normed, scaled = norm_parts(hidden[...])
+    wait_all(copies)
+    d_xn2 = dot_nt(pack_one[:, width // 2 :], gelu_weight[...])
+    wait_all(others)
+    d_xn2 = d_xn2 + dot_nt(pack_two[:, width // 2 :], gate_weight[...])
+    d_norm, gain_term = norm_back(d_xn2, normed, scaled, gains[1:2, :])
+    gain_grad[...] = gain_term
+    total = grad_out[...].astype(F32) + d_norm
+    d_hidden[...] = total
+    rounded = total.astype(BF16)
+    wait_all(lasts)
+    d_attention[...] = dot_nt(rounded, weight[...]).astype(BF16)
+    pack(keep, send, attention, rounded, Y_BIT, X_BIT, me)
+
+
+def attend_back_kernel(
+    place, queries, keys_values, edge, bias, totals, d_attention, cosine, sine, xn1, keep, send, d_keys_values, d_edge, d_turned
+):
+    width = queries.shape[1]
+    pair = 2 * HEAD_DIM
+    factor = 1.0 / math.sqrt(HEAD_DIM)
+    rows = queries.shape[0]
+    is_first = head_masks((rows, pair))
+    is_first_key = head_masks((rows + edge.shape[0], pair))
+    for start in range(0, width, pair):
+        here = slice(start, start + pair)
+        there = slice(width + start, width + start + pair)
+        two = queries[:, here]
+        d_two = d_attention[:, here]
+        keys = jnp.concatenate([keys_values[:, here], edge[:, here]], axis=0)
+        vals = jnp.concatenate([keys_values[:, there], edge[:, there]], axis=0)
+        d_queries, d_keys, d_vals = ([], [], [])
+        for which in range(2):
+            mask = is_first if which == 0 else jnp.logical_not(is_first)
+            one = jnp.where(mask, two, jnp.zeros_like(two))
+            d_one = jnp.where(mask, d_two, jnp.zeros_like(d_two))
+            head = 2 * (start // pair) + which
+            scores = dot_nt(one, keys) * factor + bias[...]
+            recomputed = jnp.exp(scores - totals[:, head : head + 1])
+            d_soft = dot_nt(d_one, vals)
+            center = jnp.sum(recomputed * d_soft, axis=-1, keepdims=True)
+            d_scores = (recomputed * (d_soft - center) * factor).astype(BF16)
+            d_queries.append(dot_nn(d_scores, keys))
+            d_keys.append(dot_tt(d_scores, two))
+            d_vals.append(dot_tt(recomputed.astype(BF16), d_two))
+        d_query = jnp.where(is_first, d_queries[0], d_queries[1])
+        d_turned[:, here] = turn(d_query, cosine[...], -sine[...]).astype(BF16)
+        d_key = jnp.where(is_first_key, d_keys[0], d_keys[1])
+        d_val = jnp.where(is_first_key, d_vals[0], d_vals[1])
+        d_keys_values[:, here] = d_key[:rows]
+        d_keys_values[:, there] = d_val[:rows]
+        d_edge[:, here] = d_key[rows:].astype(BF16)
+        d_edge[:, there] = d_val[rows:].astype(BF16)
+    pack(keep, send, xn1, d_turned[...], X_BIT, Y_BIT, place[0])
+
+
+def keys_back_kernel(
+    place, d_keys_values, arrived, cosine, sine, xn1, keep_one, send_one, keep_two, send_two, summed, d_turned
+):
+    me, along = (place[0], place[1])
+    width = xn1.shape[1]
+    pair = 2 * HEAD_DIM
+    rows = arrived.shape[0]
+    summed[...] = d_keys_values[...]
+    where = pl.ds(pl.multiple_of((1 - along) * rows, rows), rows)
+    summed[where, :] = summed[where, :] + arrived[...].astype(F32)
+    for start in range(0, width, pair):
+        here = slice(start, start + pair)
+        d_turned[:, here] = turn(summed[:, here], cosine[...], -sine[...]).astype(BF16)
+    pack(keep_one, send_one, xn1, d_turned[...], Y_BIT, X_BIT, me)
+    pack(keep_two, send_two, xn1, summed[:, width:].astype(BF16), X_BIT, Y_BIT, me)
+
+
+def tokens_back_kernel(place, pack_q, pack_k, pack_v, tokens, d_hidden, gains, *refs):
+    pieces, (input_grad, gain_grad, weight, sems) = (refs[:PIECES], refs[PIECES:])
+    width = tokens.shape[1]
+    copies = fill(pieces, weight, sems, place[0], pl.ds(0, 3 * width))
+    normed, scaled = norm_parts(tokens[...].astype(F32))
+    wait_all(copies)
+    d_xn1 = dot_nt(pack_q[:, width // 2 :], weight[:, :width])
+    d_xn1 = d_xn1 + dot_nt(pack_k[:, width // 2 :], weight[:, width : 2 * width])
+    d_xn1 = d_xn1 + dot_nt(pack_v[:, width // 2 :], weight[:, 2 * width :])
+    d_norm, gain_term = norm_back(d_xn1, normed, scaled, gains[0:1, :])
+    gain_grad[...] = gain_term
+    input_grad[...] = (d_hidden[...] + d_norm).astype(BF16)
+
+
+def product_kernel(width, mine, over_link, core_mine, core_link, own, sent, joined, sems):
+    rows = mine.shape[0]
+    copies = []
+    for index, part in enumerate((mine, over_link, core_mine, core_link)):
+        copies.append(pltpu.make_async_copy(part, joined.at[pl.ds(index * rows, rows)], sems.at[index]))
+    for copy in copies:
+        copy.start()
+    wait_all(copies)
+    block = lambda top, k: joined[2 * rows * top : 2 * rows * (top + 1), k * width : (k + 1) * width]
+    right = joined[:, 4 * width :]
+    left = jnp.concatenate([block(0, 2), block(1, 3)], axis=0)
+    sent[...] = dot_tt(left, right).astype(BF16)
+    left = jnp.concatenate([block(0, 0), block(1, 1)], axis=0)
+    own[...] = dot_tt(left, right)
+
+
+def call(kernel, outs, operands, scratch=(), smem=1, anywhere=(), flops=0, size=0):
+    specs = []
+    for index in range(len(operands)):
+        if index < smem:
+            specs.append(pl.BlockSpec(memory_space=pltpu.SMEM))
+        elif index in anywhere:
+            specs.append(pl.BlockSpec(memory_space=pl.ANY))
+        else:
+            specs.append(pl.BlockSpec(memory_space=pltpu.VMEM))
+    return pl.pallas_call(
+        kernel,
+        out_shape=[jax.ShapeDtypeStruct(shape, kind) for shape, kind in outs],
+        in_specs=specs,
+        out_specs=[pl.BlockSpec(memory_space=pltpu.VMEM)] * len(outs),
+        scratch_shapes=list(scratch),
+        cost_estimate=pl.CostEstimate(flops=flops, bytes_accessed=size, transcendentals=0),
+        compiler_params=pltpu.CompilerParams(vmem_limit_bytes=VMEM_BYTES),
+    )(*operands)
+
+
+def grad_rows(keep, send, gather_bit, sum_bit, width):
+    rows, cols = (keep.shape[0], keep.shape[1] - 4 * width)
+    over_link = swap(send, gather_bit)
+    core_mine = swap(keep, CORE_BIT)
+    core_link = swap(over_link, CORE_BIT)
+    own, sent = call(
+        lambda *refs: product_kernel(width, *refs),
+        [((width, cols), F32), ((width, cols), BF16)],
+        [keep, over_link, core_mine, core_link],
+        [pltpu.VMEM((4 * rows, 4 * width + cols), BF16), pltpu.SemaphoreType.DMA((4,))],
+        smem=0,
+        anywhere=(0, 1, 2, 3),
+        flops=16 * rows * width * cols,
+        size=4 * rows * (4 * width + cols) * 2 + 6 * width * cols,
+    )
+    return own + swap(sent, sum_bit).astype(F32)
+
+
+def line_sum(part):
+    first = lax.ppermute(part.astype(BF16), "replica", [(0, 1), (3, 2)])
+    pair = (part + first.astype(F32)).astype(BF16)
+    other = lax.ppermute(pair, "replica", [(1, 2), (2, 1)])
+    total = (pair.astype(F32) + other.astype(F32)).astype(BF16)
+    back = lax.ppermute(total, "replica", [(1, 0), (2, 3)])
+    place = lax.axis_index("replica")
+    middle = (place == 1) | (place == 2)
+    return jnp.where(middle, total, back).astype(F32)
+
+
+def sum_everywhere(values):
+    for bit in (CORE_BIT, X_BIT, Y_BIT):
+        values = values + swap(values, bit)
+    for bit in (1, 2):
+        values = values + lax.ppermute(values, "replica", [(i, i ^ bit) for i in range(4)])
+    return values
+
+
+def body_plane(
+    tokens,
+    input_gain,
+    qkv_weight,
+    output_weight,
+    mlp_gain,
+    expand_weight,
+    contract_weight,
+    positions,
+    mask_bias,
+    cotangent,
+):
+    me = lax.axis_index(PLANE)
+    along = lax.axis_index("ctx")
+    place = jnp.stack([me, along]).astype(jnp.int32)
+    shard = qkv_weight.shape[0]
+    ff_width = expand_weight.shape[1] // 2
+    source, grad_out = (tokens[0], cotangent[0])
+    rows, width = source.shape
+    gains = jnp.stack([input_gain, mlp_gain], axis=1)
+    gains = jnp.pad(gains, ((0, 0), (0, 126)))
+    front = jnp.concatenate([qkv_weight, output_weight, gains], axis=1)
+    packed, arrived = gather_pieces(front)
+    gelu_pieces, arrived = gather_pieces(expand_weight[:, :ff_width], arrived)
+    gate_pieces, arrived = gather_pieces(expand_weight[:, ff_width:], arrived)
+    contract_pieces, arrived = gather_pieces(contract_weight, arrived)
+    cosine, sine = rope_tables(positions[0], HEAD_DIM)
+    cosine = jnp.concatenate([cosine[:, 0]] * 4, axis=1)
+    sine = jnp.concatenate([-sine[:, 0], sine[:, 0]] * 2, axis=1)
+    bias = mask_bias[0]
+    bias = jnp.concatenate(
+        [bias[:, HALF : HALF + rows], jnp.where(along == 0, bias[:, HALF + rows :], bias[:, :HALF])], axis=1
+    )
+    sems = pltpu.SemaphoreType.DMA((PIECES,))
+    front_cols = front.shape[1]
+    queries, keys_values, edge, xn1, full_gains = call(
+        front_kernel,
+        [((rows, width), BF16), ((rows, 2 * width), BF16), ((HALF, 2 * width), BF16), ((rows, width), BF16), ((8, width), F32)],
+        [place, source, cosine, sine] + packed,
+        [pltpu.VMEM((width, front_cols), BF16), sems],
+        anywhere=range(4, 4 + PIECES),
+        flops=6 * rows * width * width,
+        size=2 * width * front_cols,
+    )
+    edge = swap(edge, X_BIT)
+    attention, totals, hidden, xn2 = call(
+        attend_kernel,
+        [((rows, width), BF16), ((rows, 128), F32), ((rows, width), F32), ((rows, width), BF16)],
+        [place, queries, keys_values, edge, bias, source, full_gains] + packed,
+        [pltpu.VMEM((width, width), BF16), sems],
+        anywhere=range(7, 7 + PIECES),
+        flops=12 * rows * width * width,
+        size=4 * width * width,
+    )
+    half = 4 * shard
+    keep_c, send_c, slope_gate, active = call(
+        lift_kernel,
+        [((rows, half + ff_width), BF16)] * 2 + [((rows, ff_width), F32)] * 2,
+        [place, xn2, grad_out] + gelu_pieces + gate_pieces,
+        [pltpu.VMEM((width, ff_width), BF16)] * 2 + [sems] * 2,
+        anywhere=range(3, 3 + 2 * PIECES),
+        flops=4 * rows * width * ff_width,
+        size=4 * width * ff_width,
+    )
+    contract_part = grad_rows(keep_c, send_c, X_BIT, Y_BIT, shard)
+    layer_out, keep_g, send_g, keep_u, send_u = call(
+        contract_kernel,
+        [((rows, width), BF16)] + [((rows, half + ff_width), BF16)] * 4,
+        [place, keep_c, grad_out, xn2, hidden, slope_gate, active] + contract_pieces,
+        [pltpu.VMEM((width, ff_width), BF16), sems],
+        anywhere=range(7, 7 + PIECES),
+        flops=4 * rows * width * ff_width,
+        size=2 * width * ff_width,
+    )
+    gelu_part = grad_rows(keep_g, send_g, Y_BIT, X_BIT, shard)
+    gate_part = grad_rows(keep_u, send_u, X_BIT, Y_BIT, shard)
+    keep_o, send_o, d_hidden, d_attention, mlp_term = call(
+        hidden_back_kernel,
+        [((rows, half + width), BF16)] * 2 + [((rows, width), F32), ((rows, width), BF16), ((1, width), F32)],
+        [place, keep_g, keep_u, grad_out, hidden, full_gains, attention] + gelu_pieces + gate_pieces + packed,
+        [pltpu.VMEM((width, ff_width), BF16)] * 2 + [pltpu.VMEM((width, width), BF16)] + [sems] * 3,
+        anywhere=range(7, 7 + 3 * PIECES),
+        flops=6 * rows * width * ff_width,
+        size=6 * width * ff_width,
+    )
+    output_part = grad_rows(keep_o, send_o, Y_BIT, X_BIT, shard)
+    keep_q, send_q, d_keys_values, d_edge = call(
+        attend_back_kernel,
+        [((rows, half + width), BF16)] * 2 + [((rows, 2 * width), F32), ((HALF, 2 * width), BF16)],
+        [place, queries, keys_values, edge, bias, totals, d_attention, cosine, sine, xn1],
+        [pltpu.VMEM((rows, width), BF16)],
+        flops=20 * rows * width * width,
+        size=4 * width * width,
+    )
+    query_part = grad_rows(keep_q, send_q, X_BIT, Y_BIT, shard)
+    keep_k, send_k, keep_v, send_v = call(
+        keys_back_kernel,
+        [((rows, half + width), BF16)] * 4,
+        [place, d_keys_values, swap(d_edge, X_BIT), cosine, sine, xn1],
+        [pltpu.VMEM((rows, 2 * width), F32), pltpu.VMEM((rows, width), BF16)],
+        flops=rows * width,
+        size=8 * rows * width,
+    )
+    key_part = grad_rows(keep_k, send_k, Y_BIT, X_BIT, shard)
+    value_part = grad_rows(keep_v, send_v, X_BIT, Y_BIT, shard)
+    input_grad, input_term = call(
+        tokens_back_kernel,
+        [((rows, width), BF16), ((1, width), F32)],
+        [place, keep_q, keep_k, keep_v, source, d_hidden, full_gains] + packed,
+        [pltpu.VMEM((width, 3 * width), BF16), sems],
+        anywhere=range(7, 7 + PIECES),
+        flops=6 * rows * width * width,
+        size=6 * width * width,
+    )
+    gain_sums = sum_everywhere(jnp.concatenate([input_term, mlp_term], axis=0))
+    gain_rows = lax.dynamic_slice_in_dim(gain_sums, me * shard, shard, axis=1)
+    contract_grad = line_sum(contract_part)
+    gelu_grad = line_sum(gelu_part)
+    gate_grad = line_sum(gate_part)
+    early_grad = line_sum(jnp.concatenate([output_part, query_part], axis=1))
+    late_grad = line_sum(jnp.concatenate([key_part, value_part], axis=1))
+    return (
+        layer_out[None],
+        input_grad[None],
+        gain_rows[0],
+        jnp.concatenate([early_grad[:, width:], late_grad], axis=1),
+        early_grad[:, :width],
+        gain_rows[1],
+        jnp.concatenate([gelu_grad, gate_grad], axis=1),
+        contract_grad,
+    )
+
+
 def solution(mesh):
     in_specs = (
         P(("replica", "fsdp"), "ctx", None),
@@ -274,4 +765,6 @@
         P(("fsdp", "ctx"), None),
         P(("fsdp", "ctx"), None),
     )
+    sizes = (mesh.shape["replica"], mesh.shape["fsdp"], mesh.shape["ctx"])
+    body = body_plane if sizes == (4, 4, 2) else body_generic
     return jax.shard_map(body, mesh=mesh, in_specs=in_specs, out_specs=out_specs, check_vma=False)

time: 878 us -> 526 us (0.60)
  waiting for transfers between devices: 630 us -> 170 us
  matrix products: 97.8 us -> 0 us
  Pallas kernels: 0 us -> 81.9 us
  local copies, waits for them, and re-layouts: 81 us -> 158 us
  starting transfers between devices: 9.81 us -> 80.9 us
  blocking collectives: 37.2 us -> 0 us
  other arithmetic: 5.94 us -> 30.3 us
  between operations: 14.8 us -> 1.96 us
    reduce_scatter x1 -> x0, waiting for transfers between devices: 280 us -> none  [body(): lax.psum_scatter(jnp.concatenate([qkv_term, output_term, expand_term, con...]
    psum x1 -> x0, waiting for transfers between devices: 215 us -> none  [body(): result = lax.psum(shares, 'replica')]
    ppermute x4 -> x86, waiting for transfers between devices: 8.61 us -> 170 us  [the longest x69 127 us: swap(): return lax.ppermute(value, PLANE, [(i, i ^ bit) for i in range(PLANE_SIZE)])]
    all_gather x4 -> x0, waiting for transfers between devices: 124 us -> none  [the longest x1 51.5 us: body(): lax.all_gather(expand_weight, ('fsdp', 'ctx'), axis=0, tiled=True)]
    dot_general x18 -> x0, matrix products: 97.8 us -> none  [the longest x1 14.6 us: attend_back(): jnp.einsum('hqk,qhd->khd', d_scores, queries, preferred_element_type=jnp....]
    pallas_call x0 -> x15, Pallas kernels: none -> 81.9 us  [call(): pl.pallas_call(kernel, out_shape=[jax.ShapeDtypeStruct(shape, kind) for s...]
    ppermute x4 -> x86, starting transfers between devices: 9.58 us -> 80.9 us  [the longest x69 41.3 us: swap(): return lax.ppermute(value, PLANE, [(i, i ^ bit) for i in range(PLANE_SIZE)])]
    ppermute x0 -> x36, local copies, waits for them, and re-layouts: none -> 68 us  [the longest x27 56.3 us: swap(): return lax.ppermute(value, PLANE, [(i, i ^ bit) for i in range(PLANE_SIZE)])]
  transfers between devices with their start and end apart: 10 -> 86, of which waited for: 7 -> 29; matrix products, arithmetic and copies ran while one was open for 4% -> 27% of each run, Pallas kernels for 0% -> 10%
where the time goes in v2:
time: 526 us; the launch traced here: 523 us
  waiting for transfers between devices  170 us (32%)
  local copies, waits for them, and re-layouts  158 us (30%)
  Pallas kernels  81.9 us (16%)
  starting transfers between devices  80.9 us (15%)
  other arithmetic  30.3 us (6%)
    ppermute x69, waiting for transfers between devices, swap(): return lax.ppermute(value, PLANE, [(i, i ^ bit) for i in range(PLANE_SIZE)])  127 us
    pallas_call x15, Pallas kernels, call(): pl.pallas_call(kernel, out_shape=[jax.ShapeDtypeStruct(shape, kind) for s...  81.9 us
    ppermute x27, local copies, waits for them, and re-layouts, swap(): return lax.ppermute(value, PLANE, [(i, i ^ bit) for i in range(PLANE_SIZE)])  56.3 us
    unnamed x221, local copies, waits for them, and re-layouts  44.9 us
    ppermute x69, starting transfers between devices, swap(): return lax.ppermute(value, PLANE, [(i, i ^ bit) for i in range(PLANE_SIZE)])  41.3 us
    ppermute x5, waiting for transfers between devices, line_sum(): back = lax.ppermute(total, 'replica', [(1, 0), (2, 3)])  38.4 us
    ppermute x5, starting transfers between devices, line_sum(): first = lax.ppermute(part.astype(BF16), 'replica', [(0, 1), (3, 2)])  21.3 us
    pallas_call x9, local copies, waits for them, and re-layouts, call(): pl.pallas_call(kernel, out_shape=[jax.ShapeDtypeStruct(shape, kind) for s...  16.6 us
  transfers between devices with their start and end apart: 86, of which 29 were waited for; matrix products, arithmetic and copies ran while one was open for 27% of the time, Pallas kernels for 10%

profile of v2, /device:TPU:0, one launch (start us, length us, event | category | flops | bytes accessed | tf_op | source)
XLA Modules:
  0.0 523.3 jit_solution(12585460470457400074)
XLA Ops:
  2.9 3.0 collective-permute-start.1
  7.4 22.4 %collective-permute-done.1.refs_2_.refs_22_ = bf16[128,4224]{1,0:T(8,128)(2,1)S(1)} collective-permute-done((bf16[128,4224]{1,0:T(8,128)(2,1)S(1)}, bf16[128,4224]{1,0:T(8,128)(2,1)S(1)}, u32[]{:S(2)}, u32[]{:S(2)}) %collective-permute-start.1) | collective-permute-done | bytes 1081376 | tf_op jit(solution)/shard_map/ppermute | solution.py:265
  39.4 6.9 %collective-permute-done.3.refs_4_.refs_24_ = bf16[64,4224]{1,0:T(8,128)(2,1)S(1)} collective-permute-done((bf16[64,4224]{1,0:T(8,128)(2,1)}, bf16[64,4224]{1,0:T(8,128)(2,1)S(1)}, u32[]{:S(2)}, u32[]{:S(2)}) %collective-permute-start.3) | collective-permute-done | bytes 540704 | tf_op jit(solution)/shard_map/ppermute | solution.py:265
  46.4 6.2 %collective-permute-done.2.refs_3_.refs_23_ = bf16[64,4224]{1,0:T(8,128)(2,1)S(1)} collective-permute-done((bf16[64,4224]{1,0:T(8,128)(2,1)S(1)}, bf16[64,4224]{1,0:T(8,128)(2,1)S(1)}, u32[]{:S(2)}, u32[]{:S(2)}) %collective-permute-start.2) | collective-permute-done | bytes 540704 | tf_op jit(solution)/shard_map/ppermute | solution.py:265
  52.6 6.5 %collective-permute-done.10 = bf16[128,2624]{0,1:T(8,128)(2,1)} collective-permute-done((bf16[128,2624]{0,1:T(8,128)(2,1)}, bf16[128,2624]{0,1:T(8,128)(2,1)}, u32[]{:S(2)}, u32[]{:S(2)}) %collective-permute-start.10) | collective-permute-done | bytes 671776 | tf_op jit(solution)/shard_map/ppermute | solution.py:265
  67.0 6.8 %collective-permute-done.12.refs_3_ = bf16[64,2624]{1,0:T(8,128)(2,1)S(1)} collective-permute-done((bf16[64,2624]{1,0:T(8,128)(2,1)}, bf16[64,2624]{1,0:T(8,128)(2,1)S(1)}, u32[]{:S(2)}, u32[]{:S(2)}) %collective-permute-start.12) | collective-permute-done | bytes 335904 | tf_op jit(solution)/shard_map/ppermute | solution.py:265
  84.1 6.7 %collective-permute-done.20 = bf16[128,2624]{0,1:T(8,128)(2,1)} collective-permute-done((bf16[128,2624]{0,1:T(8,128)(2,1)}, bf16[128,2624]{0,1:T(8,128)(2,1)}, u32[]{:S(2)}, u32[]{:S(2)}) %collective-permute-start.20) | collective-permute-done | bytes 671776 | tf_op jit(solution)/shard_map/ppermute | solution.py:265
  93.6 4.7 shard_map.161
  102.7 4.7 collective-permute-done.9.edge
  114.5 9.7 %collective-permute-done.21.refs_13_ = bf16[64,2624]{1,0:T(8,128)(2,1)} collective-permute-done((bf16[64,2624]{1,0:T(8,128)(2,1)S(1)}, bf16[64,2624]{1,0:T(8,128)(2,1)}, u32[]{:S(2)}, u32[]{:S(2)}) %collective-permute-start.21) | collective-permute-done | bytes 335904 | tf_op jit(solution)/shard_map/ppermute | solution.py:265
  136.0 2.9 collective-permute-done.22.refs_14_
  144.5 4.5 collective-permute-done.30.refs_3_
  164.7 7.7 %shard_map.162 = (bf16[128,1024]{1,0:T(8,128)(2,1)S(1)}, f32[128,128]{1,0:T(8,128)S(1)}, f32[128,1024]{1,0:T(8,128)S(1)}, bf16[128,1024]{1,0:T(8,128)(2,1)S(1)}) custom-call(s32[2]{0:T(128)S(1)} %copy-done.90, bf16[128,1024]{1,0:T(8,128)(2,1)S(1)} %copy-done.80, bf16[128,2048]{1,0:T(8,128)(2,1)S(1)} %copy-done.56, bf16[64,2048]{1,0:T(8,128)(2,1)S(1)} %copy-done.83, ...), custom_call_target="tpu_custom_call" | custom-call | flops 1610612736 | bytes 4194304 | tf_op jit(solution)/shard_map/pallas_call | solution.py:564
  186.0 17.4 %shard_map.163 = (bf16[128,3136]{1,0:T(8,128)(2,1)}, bf16[128,3136]{1,0:T(8,128)(2,1)}, f32[128,2624]{1,0:T(8,128)}, f32[128,2624]{1,0:T(8,128)}) custom-call(s32[2]{0:T(128)S(1)} %copy-done.90, bf16[128,1024]{1,0:T(8,128)(2,1)S(1)} %copy-done.42, bf16[128,1024]{1,0:T(8,128)(2,1)S(1)} %bitcast.15, bf16[128,2624]{1,0:T(8,128)(2,1)S(1)} %get-tuple-element.63.refs_0_, ...), custom_call_target="tpu_custom_call" | custom-call | flops 1375731712 | bytes 10747904 | tf_op jit(solution)/shard_map/pallas_call | solution.py:564
  208.9 9.2 %shard_map.164 = (bf16[128,1024]{1,0:T(8,128)(2,1)}, bf16[128,3136]{1,0:T(8,128)(2,1)}, bf16[128,3136]{1,0:T(8,128)(2,1)}, bf16[128,3136]{1,0:T(8,128)(2,1)}, bf16[128,3136]{1,0:T(8,128)(2,1)}) custom-call(s32[2]{0:T(128)S(1)} %copy-done.90, bf16[128,3136]{1,0:T(8,128)(2,1)} %get-tuple-element.65.gated_pack.refs_0_, bf16[128,1024]{1,0:T(8,128)(2,1)S(1)} %bitcast.16, ...), custom_call_target="tpu_custom_call" | custom-call | flops 1375731712 | bytes 5373952 | tf_op jit(solution)/shard_map/pallas_call | solution.py:564
  218.2 11.9 %shard_map.165 = (bf16[128,1536]{1,0:T(8,128)(2,1)S(1)}, bf16[128,1536]{1,0:T(8,128)(2,1)}, f32[128,1024]{1,0:T(8,128)}, bf16[128,1024]{1,0:T(8,128)(2,1)S(1)}, f32[1,1024]{1,0:T(1,128)S(1)}) custom-call(s32[2]{0:T(128)S(1)} %copy-done.90, bf16[128,3136]{1,0:T(8,128)(2,1)} %get-tuple-element.72.pack_one.refs_0_, ...), custom_call_target="tpu_custom_call" | custom-call | flops 2063597568 | bytes 16121856 | tf_op jit(solution)/shard_map/pallas_call | solution.py:564
  232.2 7.2 %shard_map.166 = (bf16[128,1536]{1,0:T(8,128)(2,1)}, bf16[128,1536]{1,0:T(8,128)(2,1)S(1)}, f32[128,2048]{1,0:T(8,128)S(1)}, bf16[64,2048]{1,0:T(8,128)(2,1)S(1)}) custom-call(s32[2]{0:T(128)S(1)} %copy-done.90, bf16[128,1024]{1,0:T(8,128)(2,1)S(1)} %copy-done.81, bf16[128,2048]{1,0:T(8,128)(2,1)S(1)} %copy-done.57, bf16[64,2048]{1,0:T(8,128)(2,1)S(1)} %copy-done.84, ...), custom_call_target="tpu_custom_call" | custom-call | flops 2684354560 | bytes 4194304 | tf_op jit(solution)/shard_map/pallas_call | solution.py:564
  246.9 3.1 collective-permute-done.37.arrived
  259.6 6.7 %shard_map.168 = (bf16[128,1024]{1,0:T(8,128)(2,1)}, f32[1,1024]{1,0:T(1,128)S(1)}) custom-call(s32[2]{0:T(128)S(1)} %copy-done.91, bf16[128,1536]{1,0:T(8,128)(2,1)} %get-tuple-element.77.pack_q.refs_0_, bf16[128,1536]{1,0:T(8,128)(2,1)S(1)} %get-tuple-element.80.pack_k.refs_0_, bf16[128,1536]{1,0:T(8,128)(2,1)S(1)} %get-tuple-element.81.pack_v.refs_0_, ...), custom_call_target="tpu_custom_call" | custom-call | flops 805306368 | bytes 6291456 | tf_op jit(solution)/shard_map/pallas_call | solution.py:564
  271.9 8.5 %collective-permute-done.40 = f32[2,1024]{1,0:T(2,128)S(1)} collective-permute-done((f32[2,1024]{1,0:T(2,128)S(1)}, f32[2,1024]{1,0:T(2,128)S(1)}, u32[]{:S(2)}, u32[]{:S(2)}) %collective-permute-start.40) | collective-permute-done | bytes 8224 | tf_op jit(solution)/shard_map/ppermute | solution.py:265
  308.6 14.9 %collective-permute-done.72 = bf16[128,3136]{0,1:T(8,128)(2,1)} collective-permute-done((bf16[128,3136]{0,1:T(8,128)(2,1)}, bf16[128,3136]{0,1:T(8,128)(2,1)}, u32[]{:S(2)}, u32[]{:S(2)}) %collective-permute-start.72) | collective-permute-done | bytes 802848 | tf_op jit(solution)/shard_map/ppermute | solution.py:265
  364.8 4.7 collective-permute-done.57
  369.5 3.5 collective-permute-start.51
  373.0 10.5 %collective-permute-done.61 = bf16[128,1024]{1,0:T(8,128)(2,1)S(1)} collective-permute-done((bf16[128,1024]{1,0:T(8,128)(2,1)S(1)}, bf16[128,1024]{1,0:T(8,128)(2,1)S(1)}, u32[]{:S(2)}, u32[]{:S(2)}) %collective-permute-start.61) | collective-permute-done | bytes 262176 | tf_op jit(solution)/shard_map/ppermute | solution.py:265
  384.6 4.4 collective-permute-start.62
  412.1 5.0 collective-permute-start.83
  428.2 6.2 %collective-permute-start.69 = (bf16[128,2624]{0,1:T(8,128)(2,1)}, bf16[128,2624]{0,1:T(8,128)(2,1)}, u32[]{:S(2)}, u32[]{:S(2)}) collective-permute-start(bf16[128,2624]{0,1:T(8,128)(2,1)} %copy.151), channel_id=1, source_target_pairs={{0,8},{24,16},{1,9},{25,17},{2,10},{26,18},{3,11},{27,19},{4,12},{... | collective-permute-start | bytes 2015240 | tf_op jit(solution)/shard_map/ppermute | solution.py:594
  450.9 10.1 %collective-permute-done.64 = bf16[128,2048]{1,0:T(8,128)(2,1)S(1)} collective-permute-done((bf16[128,2048]{1,0:T(8,128)(2,1)S(1)}, bf16[128,2048]{1,0:T(8,128)(2,1)S(1)}, u32[]{:S(2)}, u32[]{:S(2)}) %collective-permute-start.64) | collective-permute-done | bytes 524320 | tf_op jit(solution)/shard_map/ppermute | solution.py:598
  485.5 10.9 %collective-permute-done.85 = bf16[128,2624]{0,1:T(8,128)(2,1)} collective-permute-done((bf16[128,2624]{0,1:T(8,128)(2,1)}, bf16[128,2624]{0,1:T(8,128)(2,1)}, u32[]{:S(2)}, u32[]{:S(2)}) %collective-permute-start.85) | collective-permute-done | bytes 671776 | tf_op jit(solution)/shard_map/ppermute | solution.py:598
  499.0 2.8 copy.183
  501.8 9.0 %collective-permute-done.71 = bf16[128,2624]{0,1:T(8,128)(2,1)} collective-permute-done((bf16[128,2624]{0,1:T(8,128)(2,1)}, bf16[128,2624]{0,1:T(8,128)(2,1)}, u32[]{:S(2)}, u32[]{:S(2)}) %collective-permute-start.71) | collective-permute-done | bytes 671776 | tf_op jit(solution)/shard_map/ppermute | solution.py:598
  512.3 8.5 %collective-permute-done.78 = bf16[128,2624]{0,1:T(8,128)(2,1)S(1)} collective-permute-done((bf16[128,2624]{0,1:T(8,128)(2,1)}, bf16[128,2624]{0,1:T(8,128)(2,1)S(1)}, u32[]{:S(2)}, u32[]{:S(2)}) %collective-permute-start.78) | collective-permute-done | bytes 671776 | tf_op jit(solution)/shard_map/ppermute | solution.py:598
  (487 shorter events, 274.0 us)
Async XLA Ops:
  5.9 27.9 %collective-permute-start = (bf16[128,4224]{1,0:T(8,128)(2,1)S(1)}, bf16[128,4224]{1,0:T(8,128)(2,1)S(1)}, u32[]{:S(2)}, u32[]{:S(2)}) collective-permute-start(bf16[128,4224]{1,0:T(8,128)(2,1)S(1)} %fusion.1.refs_0_.refs_20_), channel_id=1, source_target_pairs={{0,1},{1,0},{2,3},{3,2},{4,5},{5,4},{6,7},{7,6},{8,9},{9,8},{10,11... | collective-permute-start | bytes 3244040 | tf_op jit(solution)/shard_map/ppermute | solution.py:265
  7.4 31.7 %collective-permute-start.4 = (bf16[128,4224]{1,0:T(8,128)(2,1)S(1)}, bf16[128,4224]{1,0:T(8,128)(2,1)}, u32[]{:S(2)}, u32[]{:S(2)}) collective-permute-start(bf16[128,4224]{1,0:T(8,128)(2,1)S(1)} %fusion.1.refs_0_.refs_20_), channel_id=1, source_target_pairs={{0,2},{1,3},{2,0},{3,1},{4,6},{5,7},{6,4},{7,5},{8,10},{9,11},{10,... | collective-permute-start | bytes 3244040 | tf_op jit(solution)/shard_map/ppermute | solution.py:265
  46.4 30.3 %collective-permute-start.6 = (bf16[128,4224]{1,0:T(8,128)(2,1)}, bf16[128,4224]{1,0:T(8,128)(2,1)}, u32[]{:S(2)}, u32[]{:S(2)}) collective-permute-start(bf16[128,4224]{1,0:T(8,128)(2,1)} %copy-done.98), channel_id=1, source_target_pairs={{0,2},{1,3},{2,0},{3,1},{4,6},{5,7},{6,4},{7,5},{8,10},{9,11},{10,... | collective-permute-start | bytes 3244040 | tf_op jit(solution)/shard_map/ppermute | solution.py:265
  76.7 35.2 %collective-permute-start.23 = (bf16[128,2624]{0,1:T(8,128)(2,1)}, bf16[128,2624]{0,1:T(8,128)(2,1)}, u32[]{:S(2)}, u32[]{:S(2)}) collective-permute-start(bf16[128,2624]{0,1:T(8,128)(2,1)} %copy.111), channel_id=1, source_target_pairs={{0,2},{1,3},{2,0},{3,1},{4,6},{5,7},{6,4},{7,5},{8,10},{9,11},{10,... | collective-permute-start | bytes 2015240 | tf_op jit(solution)/shard_map/ppermute | solution.py:265
  76.8 34.6 %collective-permute-start.16 = (bf16[128,2624]{0,1:T(8,128)(2,1)}, bf16[128,2624]{0,1:T(8,128)(2,1)}, u32[]{:S(2)}, u32[]{:S(2)}) collective-permute-start(bf16[128,2624]{0,1:T(8,128)(2,1)} %collective-permute-done.11), channel_id=1, source_target_pairs={{0,2},{1,3},{2,0},{3,1},{4,6},{5,7},{6,4},{7,5},{8,10},{9,11},{10,... | collective-permute-start | bytes 2015240 | tf_op jit(solution)/shard_map/ppermute | solution.py:265
  78.3 35.2 %collective-permute-start.15 = (bf16[128,2624]{0,1:T(8,128)(2,1)}, bf16[128,2624]{0,1:T(8,128)(2,1)}, u32[]{:S(2)}, u32[]{:S(2)}) collective-permute-start(bf16[128,2624]{0,1:T(8,128)(2,1)} %collective-permute-done.10), channel_id=1, source_target_pairs={{0,2},{1,3},{2,0},{3,1},{4,6},{5,7},{6,4},{7,5},{8,10},{9,11},{10,... | collective-permute-start | bytes 2015240 | tf_op jit(solution)/shard_map/ppermute | solution.py:265
  114.0 27.9 %collective-permute-start.32 = (bf16[128,2624]{0,1:T(8,128)(2,1)}, bf16[128,2624]{0,1:T(8,128)(2,1)}, u32[]{:S(2)}, u32[]{:S(2)}) collective-permute-start(bf16[128,2624]{0,1:T(8,128)(2,1)} %param.16), channel_id=1, source_target_pairs={{0,2},{1,3},{2,0},{3,1},{4,6},{5,7},{6,4},{7,5},{8,10},{9,11},{10,... | collective-permute-start | bytes 2015240 | tf_op jit(solution)/shard_map/ppermute | solution.py:265
  141.8 61.5 %collective-permute-start.34 = (bf16[128,2624]{0,1:T(8,128)(2,1)}, bf16[128,2624]{0,1:T(8,128)(2,1)}, u32[]{:S(2)}, u32[]{:S(2)}) collective-permute-start(bf16[128,2624]{0,1:T(8,128)(2,1)} %collective-permute-done.29), channel_id=1, source_target_pairs={{0,2},{1,3},{2,0},{3,1},{4,6},{5,7},{6,4},{7,5},{8,10},{9,11},{10,... | collective-permute-start | bytes 2015240 | tf_op jit(solution)/shard_map/ppermute | solution.py:265
  141.9 63.8 %collective-permute-start.33 = (bf16[128,2624]{0,1:T(8,128)(2,1)}, bf16[128,2624]{0,1:T(8,128)(2,1)}, u32[]{:S(2)}, u32[]{:S(2)}) collective-permute-start(bf16[128,2624]{0,1:T(8,128)(2,1)} %collective-permute-done.28), channel_id=1, source_target_pairs={{0,2},{1,3},{2,0},{3,1},{4,6},{5,7},{6,4},{7,5},{8,10},{9,11},{10,... | collective-permute-start | bytes 2015240 | tf_op jit(solution)/shard_map/ppermute | solution.py:265
  142.4 39.7 %collective-permute-start.27 = (bf16[64,2624]{1,0:T(8,128)(2,1)}, bf16[64,2624]{1,0:T(8,128)(2,1)}, u32[]{:S(2)}, u32[]{:S(2)}) collective-permute-start(bf16[64,2624]{1,0:T(8,128)(2,1)} %collective-permute-done.22.refs_14_), channel_id=1, source_target_pairs={{0,2},{1,3},{2,0},{3,1},{4,6},{5,7},{6,4},{7,5},{8,10},{9,11},{10,... | collective-permute-start | bytes 1007624 | tf_op jit(solution)/shard_map/ppermute | solution.py:265
  148.9 59.0 %collective-permute-start.35 = (bf16[64,2624]{1,0:T(8,128)(2,1)}, bf16[64,2624]{1,0:T(8,128)(2,1)}, u32[]{:S(2)}, u32[]{:S(2)}) collective-permute-start(bf16[64,2624]{1,0:T(8,128)(2,1)} %collective-permute-done.30.refs_3_), channel_id=1, source_target_pairs={{0,2},{1,3},{2,0},{3,1},{4,6},{5,7},{6,4},{7,5},{8,10},{9,11},{10,... | collective-permute-start | bytes 1007624 | tf_op jit(solution)/shard_map/ppermute | solution.py:265
  149.9 58.0 %collective-permute-start.36 = (bf16[64,2624]{1,0:T(8,128)(2,1)}, bf16[64,2624]{1,0:T(8,128)(2,1)}, u32[]{:S(2)}, u32[]{:S(2)}) collective-permute-start(bf16[64,2624]{1,0:T(8,128)(2,1)} %collective-permute-done.31.refs_4_), channel_id=1, source_target_pairs={{0,2},{1,3},{2,0},{3,1},{4,6},{5,7},{6,4},{7,5},{8,10},{9,11},{10,... | collective-permute-start | bytes 1007624 | tf_op jit(solution)/shard_map/ppermute | solution.py:265
  246.1 38.4 %collective-permute-start.80 = (bf16[128,3136]{0,1:T(8,128)(2,1)}, bf16[128,3136]{0,1:T(8,128)(2,1)S(1)}, u32[]{:S(2)}, u32[]{:S(2)}) collective-permute-start(bf16[128,3136]{0,1:T(8,128)(2,1)} %copy.171), channel_id=1, source_target_pairs={{0,2},{1,3},{2,0},{3,1},{4,6},{5,7},{6,4},{7,5},{8,10},{9,11},{10,... | collective-permute-start | bytes 2408456 | tf_op jit(solution)/shard_map/ppermute | solution.py:265
  246.4 40.8 %collective-permute-start.79 = (bf16[128,3136]{0,1:T(8,128)(2,1)}, bf16[128,3136]{0,1:T(8,128)(2,1)S(1)}, u32[]{:S(2)}, u32[]{:S(2)}) collective-permute-start(bf16[128,3136]{0,1:T(8,128)(2,1)} %copy.170), channel_id=1, source_target_pairs={{0,1},{1,0},{2,3},{3,2},{4,5},{5,4},{6,7},{7,6},{8,9},{9,8},{10,11... | collective-permute-start | bytes 2408456 | tf_op jit(solution)/shard_map/ppermute | solution.py:265
  308.0 46.9 %collective-permute-start.55 = (bf16[128,1536]{1,0:T(8,128)(2,1)S(1)}, bf16[128,1536]{1,0:T(8,128)(2,1)}, u32[]{:S(2)}, u32[]{:S(2)}) collective-permute-start(bf16[128,1536]{1,0:T(8,128)(2,1)S(1)} %copy-done.26), channel_id=1, source_target_pairs={{0,2},{1,3},{2,0},{3,1},{4,6},{5,7},{6,4},{7,5},{8,10},{9,11},{10,... | collective-permute-start | bytes 1179656 | tf_op jit(solution)/shard_map/ppermute | solution.py:265
  308.4 48.9 %collective-permute-start.59 = (bf16[128,1536]{1,0:T(8,128)(2,1)S(1)}, bf16[128,1536]{1,0:T(8,128)(2,1)}, u32[]{:S(2)}, u32[]{:S(2)}) collective-permute-start(bf16[128,1536]{1,0:T(8,128)(2,1)S(1)} %copy-done.24), channel_id=1, source_target_pairs={{0,2},{1,3},{2,0},{3,1},{4,6},{5,7},{6,4},{7,5},{8,10},{9,11},{10,... | collective-permute-start | bytes 1179656 | tf_op jit(solution)/shard_map/ppermute | solution.py:265
  323.4 31.9 %collective-permute-start.56 = (bf16[128,1536]{1,0:T(8,128)(2,1)}, bf16[128,1536]{1,0:T(8,128)(2,1)}, u32[]{:S(2)}, u32[]{:S(2)}) collective-permute-start(bf16[128,1536]{1,0:T(8,128)(2,1)} %collective-permute-done.54.refs_1_), channel_id=1, source_target_pairs={{0,2},{1,3},{2,0},{3,1},{4,6},{5,7},{6,4},{7,5},{8,10},{9,11},{10,... | collective-permute-start | bytes 1179656 | tf_op jit(solution)/shard_map/ppermute | solution.py:265
  323.5 34.3 %collective-permute-start.60 = (bf16[128,1536]{1,0:T(8,128)(2,1)}, bf16[128,1536]{1,0:T(8,128)(2,1)}, u32[]{:S(2)}, u32[]{:S(2)}) collective-permute-start(bf16[128,1536]{1,0:T(8,128)(2,1)} %collective-permute-done.58.refs_1_), channel_id=1, source_target_pairs={{0,2},{1,3},{2,0},{3,1},{4,6},{5,7},{6,4},{7,5},{8,10},{9,11},{10,... | collective-permute-start | bytes 1179656 | tf_op jit(solution)/shard_map/ppermute | solution.py:265
  329.8 31.6 %collective-permute-start.46 = (bf16[128,1024]{1,0:T(8,128)(2,1)S(1)}, bf16[128,1024]{1,0:T(8,128)(2,1)}, u32[]{:S(2)}, u32[]{:S(2)}) collective-permute-start(bf16[128,1024]{1,0:T(8,128)(2,1)S(1)} %get-tuple-element.89), channel_id=1, source_target_pairs={{0,1},{1,0},{2,3},{3,2},{4,5},{5,4},{6,7},{7,6},{8,9},{9,8},{10,11... | collective-permute-start | bytes 786440 | tf_op jit(solution)/shard_map/ppermute | solution.py:265
  355.3 44.5 %collective-permute-start.74 = (bf16[128,3136]{0,1:T(8,128)(2,1)}, bf16[128,3136]{0,1:T(8,128)(2,1)}, u32[]{:S(2)}, u32[]{:S(2)}) collective-permute-start(bf16[128,3136]{0,1:T(8,128)(2,1)} %collective-permute-done.72), channel_id=1, source_target_pairs={{0,2},{1,3},{2,0},{3,1},{4,6},{5,7},{6,4},{7,5},{8,10},{9,11},{10,... | collective-permute-start | bytes 2408456 | tf_op jit(solution)/shard_map/ppermute | solution.py:265
  357.3 34.1 %collective-permute-start.67 = (bf16[128,3136]{0,1:T(8,128)(2,1)}, bf16[128,3136]{0,1:T(8,128)(2,1)}, u32[]{:S(2)}, u32[]{:S(2)}) collective-permute-start(bf16[128,3136]{0,1:T(8,128)(2,1)} %collective-permute-done.65), channel_id=1, source_target_pairs={{0,2},{1,3},{2,0},{3,1},{4,6},{5,7},{6,4},{7,5},{8,10},{9,11},{10,... | collective-permute-start | bytes 2408456 | tf_op jit(solution)/shard_map/ppermute | solution.py:265
  357.9 49.6 %collective-permute-start.82 = (bf16[128,2624]{0,1:T(8,128)(2,1)}, bf16[128,2624]{0,1:T(8,128)(2,1)}, u32[]{:S(2)}, u32[]{:S(2)}) collective-permute-start(bf16[128,2624]{0,1:T(8,128)(2,1)} %copy.175), channel_id=1, source_target_pairs={{0,4},{1,5},{2,6},{3,7},{4,0},{5,1},{6,2},{7,3},{8,12},{9,13},{10,... | collective-permute-start | bytes 2015240 | tf_op jit(solution)/shard_map/ppermute | solution.py:265
  384.6 32.5 %collective-permute-start.62 = (bf16[128,2048]{1,0:T(8,128)(2,1)}, bf16[128,2048]{1,0:T(8,128)(2,1)}, u32[]{:S(2)}, u32[]{:S(2)}) collective-permute-start(bf16[128,2048]{1,0:T(8,128)(2,1)} %fusion.5), channel_id=1, source_target_pairs={{0,8},{24,16},{1,9},{25,17},{2,10},{26,18},{3,11},{27,19},{4,12},{... | collective-permute-start | bytes 1572872 | tf_op jit(solution)/shard_map/ppermute | solution.py:594
  389.9 30.7 %collective-permute-start.52 = (bf16[128,2048]{1,0:T(8,128)(2,1)}, bf16[128,2048]{1,0:T(8,128)(2,1)}, u32[]{:S(2)}, u32[]{:S(2)}) collective-permute-start(bf16[128,2048]{1,0:T(8,128)(2,1)} %add_convert_fusion.9), channel_id=1, source_target_pairs={{8,16},{16,8},{9,17},{17,9},{10,18},{18,10},{11,19},{19,11},{12,20... | collective-permute-start | bytes 1572872 | tf_op jit(solution)/shard_map/ppermute | solution.py:596
  407.0 27.4 %collective-permute-start.75 = (bf16[128,2624]{0,1:T(8,128)(2,1)}, bf16[128,2624]{0,1:T(8,128)(2,1)}, u32[]{:S(2)}, u32[]{:S(2)}) collective-permute-start(bf16[128,2624]{0,1:T(8,128)(2,1)} %copy.162), channel_id=1, source_target_pairs={{0,4},{1,5},{2,6},{3,7},{4,0},{5,1},{6,2},{7,3},{8,12},{9,13},{10,... | collective-permute-start | bytes 2015240 | tf_op jit(solution)/shard_map/ppermute | solution.py:265
  412.1 28.5 %collective-permute-start.83 = (bf16[128,2624]{0,1:T(8,128)(2,1)}, bf16[128,2624]{0,1:T(8,128)(2,1)}, u32[]{:S(2)}, u32[]{:S(2)}) collective-permute-start(bf16[128,2624]{0,1:T(8,128)(2,1)} %copy.177), channel_id=1, source_target_pairs={{0,8},{24,16},{1,9},{25,17},{2,10},{26,18},{3,11},{27,19},{4,12},{... | collective-permute-start | bytes 2015240 | tf_op jit(solution)/shard_map/ppermute | solution.py:594
  419.1 27.1 %collective-permute-start.63 = (bf16[128,2048]{1,0:T(8,128)(2,1)}, bf16[128,2048]{1,0:T(8,128)(2,1)}, u32[]{:S(2)}, u32[]{:S(2)}) collective-permute-start(bf16[128,2048]{1,0:T(8,128)(2,1)} %add_convert_fusion.7), channel_id=1, source_target_pairs={{8,16},{16,8},{9,17},{17,9},{10,18},{18,10},{11,19},{19,11},{12,20... | collective-permute-start | bytes 1572872 | tf_op jit(solution)/shard_map/ppermute | solution.py:596
  428.2 34.1 %collective-permute-start.69 = (bf16[128,2624]{0,1:T(8,128)(2,1)}, bf16[128,2624]{0,1:T(8,128)(2,1)}, u32[]{:S(2)}, u32[]{:S(2)}) collective-permute-start(bf16[128,2624]{0,1:T(8,128)(2,1)} %copy.151), channel_id=1, source_target_pairs={{0,8},{24,16},{1,9},{25,17},{2,10},{26,18},{3,11},{27,19},{4,12},{... | collective-permute-start | bytes 2015240 | tf_op jit(solution)/shard_map/ppermute | solution.py:594
  438.4 29.5 %collective-permute-start.76 = (bf16[128,2624]{0,1:T(8,128)(2,1)}, bf16[128,2624]{0,1:T(8,128)(2,1)}, u32[]{:S(2)}, u32[]{:S(2)}) collective-permute-start(bf16[128,2624]{0,1:T(8,128)(2,1)} %copy.164), channel_id=1, source_target_pairs={{0,8},{24,16},{1,9},{25,17},{2,10},{26,18},{3,11},{27,19},{4,12},{... | collective-permute-start | bytes 2015240 | tf_op jit(solution)/shard_map/ppermute | solution.py:594
  444.7 28.8 %collective-permute-start.84 = (bf16[128,2624]{0,1:T(8,128)(2,1)}, bf16[128,2624]{0,1:T(8,128)(2,1)}, u32[]{:S(2)}, u32[]{:S(2)}) collective-permute-start(bf16[128,2624]{0,1:T(8,128)(2,1)} %copy.179), channel_id=1, source_target_pairs={{8,16},{16,8},{9,17},{17,9},{10,18},{18,10},{11,19},{19,11},{12,20... | collective-permute-start | bytes 2015240 | tf_op jit(solution)/shard_map/ppermute | solution.py:596
  480.2 30.6 %collective-permute-start.71 = (bf16[128,2624]{0,1:T(8,128)(2,1)}, bf16[128,2624]{0,1:T(8,128)(2,1)}, u32[]{:S(2)}, u32[]{:S(2)}) collective-permute-start(bf16[128,2624]{0,1:T(8,128)(2,1)} %copy.155), channel_id=1, source_target_pairs={{8,0},{16,24},{9,1},{17,25},{10,2},{18,26},{11,3},{19,27},{12,4},{... | collective-permute-start | bytes 2015240 | tf_op jit(solution)/shard_map/ppermute | solution.py:598
  484.2 36.6 %collective-permute-start.78 = (bf16[128,2624]{0,1:T(8,128)(2,1)}, bf16[128,2624]{0,1:T(8,128)(2,1)S(1)}, u32[]{:S(2)}, u32[]{:S(2)}) collective-permute-start(bf16[128,2624]{0,1:T(8,128)(2,1)} %copy.168), channel_id=1, source_target_pairs={{8,0},{16,24},{9,1},{17,25},{10,2},{18,26},{11,3},{19,27},{12,4},{... | collective-permute-start | bytes 2015240 | tf_op jit(solution)/shard_map/ppermute | solution.py:598
  (164 other events, 2073.1 us)

commit v3 on v2

--- a/solution.py
+++ b/solution.py
@@ -411,15 +411,12 @@
 
 
 def lift_kernel(place, xn2, grad_out, *refs):
-    first, second, rest = (refs[:PIECES], refs[PIECES : 2 * PIECES], refs[2 * PIECES :])
-    keep, send, slope_gate, active, gelu_weight, gate_weight, sems_one, sems_two = rest
+    pieces, (keep, send, slope_gate, active, weight, sems) = (refs[:PIECES], refs[PIECES:])
     me = place[0]
-    copies = fill(first, gelu_weight, sems_one, me)
-    others = fill(second, gate_weight, sems_two, me)
-    wait_all(copies)
-    gelu_input = dot_nn(xn2[...], gelu_weight[...])
-    wait_all(others)
-    gate_part = dot_nn(xn2[...], gate_weight[...])
+    cols = active.shape[1]
+    wait_all(fill(pieces, weight, sems, me))
+    gelu_input = dot_nn(xn2[...], weight[:, :cols])
+    gate_part = dot_nn(xn2[...], weight[:, cols:])
     cdf_part = 0.5 * (1.0 + lax.erf(gelu_input * (1.0 / math.sqrt(2.0))))
     density = jnp.exp(-0.5 * gelu_input * gelu_input) * (1.0 / math.sqrt(2.0 * math.pi))
     activated = gelu_input * cdf_part
@@ -441,19 +438,17 @@
 
 
 def hidden_back_kernel(place, pack_one, pack_two, grad_out, hidden, gains, attention, *refs):
-    first, second, third = (refs[:PIECES], refs[PIECES : 2 * PIECES], refs[2 * PIECES : 3 * PIECES])
-    keep, send, d_hidden, d_attention, gain_grad = refs[3 * PIECES : 3 * PIECES + 5]
-    gelu_weight, gate_weight, weight, sems_one, sems_two, sems_three = refs[3 * PIECES + 5 :]
+    first, third = (refs[:PIECES], refs[PIECES : 2 * PIECES])
+    keep, send, d_hidden, d_attention, gain_grad, lift_weight, weight, sems, sems_three = refs[2 * PIECES :]
     me = place[0]
     width = hidden.shape[1]
-    copies = fill(first, gelu_weight, sems_one, me)
-    others = fill(second, gate_weight, sems_two, me)
+    copies = fill(first, lift_weight, sems, me)
     lasts = fill(third, weight, sems_three, me, pl.ds(3 * width, width))
     normed, scaled = norm_parts(hidden[...])
     wait_all(copies)
-    d_xn2 = dot_nt(pack_one[:, width // 2 :], gelu_weight[...])
-    wait_all(others)
-    d_xn2 = d_xn2 + dot_nt(pack_two[:, width // 2 :], gate_weight[...])
+    cols = lift_weight.shape[1] // 2
+    d_xn2 = dot_nt(pack_one[:, width // 2 :], lift_weight[:, :cols])
+    d_xn2 = d_xn2 + dot_nt(pack_two[:, width // 2 :], lift_weight[:, cols:])
     d_norm, gain_term = norm_back(d_xn2, normed, scaled, gains[1:2, :])
     gain_grad[...] = gain_term
     total = grad_out[...].astype(F32) + d_norm
@@ -558,7 +553,7 @@
         if index < smem:
             specs.append(pl.BlockSpec(memory_space=pltpu.SMEM))
         elif index in anywhere:
-            specs.append(pl.BlockSpec(memory_space=pl.ANY))
+            specs.append(pl.BlockSpec(memory_space=pltpu.HBM))
         else:
             specs.append(pl.BlockSpec(memory_space=pltpu.VMEM))
     return pl.pallas_call(
@@ -587,7 +582,7 @@
         flops=16 * rows * width * cols,
         size=4 * rows * (4 * width + cols) * 2 + 6 * width * cols,
     )
-    return own + swap(sent, sum_bit).astype(F32)
+    return (own + swap(sent, sum_bit).astype(F32), sent)
 
 
 def line_sum(part):
@@ -625,16 +620,21 @@
     along = lax.axis_index("ctx")
     place = jnp.stack([me, along]).astype(jnp.int32)
     shard = qkv_weight.shape[0]
-    ff_width = expand_weight.shape[1] // 2
+    true_width = expand_weight.shape[1] // 2
+    fill_cols = -true_width % 128
+    ff_width = true_width + fill_cols
     source, grad_out = (tokens[0], cotangent[0])
     rows, width = source.shape
     gains = jnp.stack([input_gain, mlp_gain], axis=1)
     gains = jnp.pad(gains, ((0, 0), (0, 126)))
     front = jnp.concatenate([qkv_weight, output_weight, gains], axis=1)
+    widened = lambda values: jnp.pad(values, ((0, 0), (0, fill_cols)))
+    lift = jnp.concatenate(
+        [widened(expand_weight[:, :true_width]), widened(expand_weight[:, true_width:])], axis=1
+    )
     packed, arrived = gather_pieces(front)
-    gelu_pieces, arrived = gather_pieces(expand_weight[:, :ff_width], arrived)
-    gate_pieces, arrived = gather_pieces(expand_weight[:, ff_width:], arrived)
-    contract_pieces, arrived = gather_pieces(contract_weight, arrived)
+    lift_pieces, arrived = gather_pieces(lift, arrived)
+    contract_pieces, arrived = gather_pieces(widened(contract_weight), arrived)
     cosine, sine = rope_tables(positions[0], HEAD_DIM)
     cosine = jnp.concatenate([cosine[:, 0]] * 4, axis=1)
     sine = jnp.concatenate([-sine[:, 0], sine[:, 0]] * 2, axis=1)
@@ -667,13 +667,13 @@
     keep_c, send_c, slope_gate, active = call(
         lift_kernel,
         [((rows, half + ff_width), BF16)] * 2 + [((rows, ff_width), F32)] * 2,
-        [place, xn2, grad_out] + gelu_pieces + gate_pieces,
-        [pltpu.VMEM((width, ff_width), BF16)] * 2 + [sems] * 2,
-        anywhere=range(3, 3 + 2 * PIECES),
+        [place, xn2, grad_out] + lift_pieces,
+        [pltpu.VMEM((width, 2 * ff_width), BF16), sems],
+        anywhere=range(3, 3 + PIECES),
         flops=4 * rows * width * ff_width,
         size=4 * width * ff_width,
     )
-    contract_part = grad_rows(keep_c, send_c, X_BIT, Y_BIT, shard)
+    contract_part, contract_sent = grad_rows(keep_c, send_c, X_BIT, Y_BIT, shard)
     layer_out, keep_g, send_g, keep_u, send_u = call(
         contract_kernel,
         [((rows, width), BF16)] + [((rows, half + ff_width), BF16)] * 4,
@@ -683,18 +683,19 @@
         flops=4 * rows * width * ff_width,
         size=2 * width * ff_width,
     )
-    gelu_part = grad_rows(keep_g, send_g, Y_BIT, X_BIT, shard)
-    gate_part = grad_rows(keep_u, send_u, X_BIT, Y_BIT, shard)
+    gelu_part, gelu_sent = grad_rows(keep_g, send_g, Y_BIT, X_BIT, shard)
+    gate_part, gate_sent = grad_rows(keep_u, send_u, X_BIT, Y_BIT, shard)
     keep_o, send_o, d_hidden, d_attention, mlp_term = call(
         hidden_back_kernel,
         [((rows, half + width), BF16)] * 2 + [((rows, width), F32), ((rows, width), BF16), ((1, width), F32)],
-        [place, keep_g, keep_u, grad_out, hidden, full_gains, attention] + gelu_pieces + gate_pieces + packed,
-        [pltpu.VMEM((width, ff_width), BF16)] * 2 + [pltpu.VMEM((width, width), BF16)] + [sems] * 3,
-        anywhere=range(7, 7 + 3 * PIECES),
+        [place, keep_g, keep_u, grad_out, hidden, full_gains, attention] + lift_pieces + packed,
+        [pltpu.VMEM((width, 2 * ff_width), BF16), pltpu.VMEM((width, width), BF16), sems, sems],
+        anywhere=range(7, 7 + 2 * PIECES),
         flops=6 * rows * width * ff_width,
         size=6 * width * ff_width,
     )
-    output_part = grad_rows(keep_o, send_o, Y_BIT, X_BIT, shard)
+    output_part, output_sent = grad_rows(keep_o, send_o, Y_BIT, X_BIT, shard)
+    d_attention, _ = lax.optimization_barrier((d_attention, contract_sent))
     keep_q, send_q, d_keys_values, d_edge = call(
         attend_back_kernel,
         [((rows, half + width), BF16)] * 2 + [((rows, 2 * width), F32), ((HALF, 2 * width), BF16)],
@@ -703,7 +704,8 @@
         flops=20 * rows * width * width,
         size=4 * width * width,
     )
-    query_part = grad_rows(keep_q, send_q, X_BIT, Y_BIT, shard)
+    d_keys_values, _ = lax.optimization_barrier((d_keys_values, (gelu_sent, gate_sent)))
+    query_part, query_sent = grad_rows(keep_q, send_q, X_BIT, Y_BIT, shard)
     keep_k, send_k, keep_v, send_v = call(
         keys_back_kernel,
         [((rows, half + width), BF16)] * 4,
@@ -712,8 +714,9 @@
         flops=rows * width,
         size=8 * rows * width,
     )
-    key_part = grad_rows(keep_k, send_k, Y_BIT, X_BIT, shard)
-    value_part = grad_rows(keep_v, send_v, X_BIT, Y_BIT, shard)
+    key_part, _ = grad_rows(keep_k, send_k, Y_BIT, X_BIT, shard)
+    value_part, _ = grad_rows(keep_v, send_v, X_BIT, Y_BIT, shard)
+    d_hidden, _ = lax.optimization_barrier((d_hidden, (contract_part, output_sent)))
     input_grad, input_term = call(
         tokens_back_kernel,
         [((rows, width), BF16), ((1, width), F32)],
@@ -737,8 +740,8 @@
         jnp.concatenate([early_grad[:, width:], late_grad], axis=1),
         early_grad[:, :width],
         gain_rows[1],
-        jnp.concatenate([gelu_grad, gate_grad], axis=1),
-        contract_grad,
+        jnp.concatenate([gelu_grad[:, :true_width], gate_grad[:, :true_width]], axis=1),
+        contract_grad[:, :true_width],
     )
 
 

time: 526 us -> 451 us (0.86)
  local copies, waits for them, and re-layouts: 158 us -> 30.1 us
  waiting for transfers between devices: 170 us -> 268 us
  starting transfers between devices: 80.9 us -> 62.7 us
  Pallas kernels: 81.9 us -> 68 us
  other arithmetic: 30.3 us -> 19.4 us
    ppermute x36 -> x0, local copies, waits for them, and re-layouts: 68 us -> none  [the longest x27 56.3 us: swap(): return lax.ppermute(value, PLANE, [(i, i ^ bit) for i in range(PLANE_SIZE)])]
    ppermute x5, waiting for transfers between devices: 0.01 us -> 45.8 us  [line_sum(): first = lax.ppermute(part.astype(BF16), 'replica', [(0, 1), (3, 2)])]
    ppermute x69 -> x60, waiting for transfers between devices: 127 us -> 162 us  [swap(): return lax.ppermute(value, PLANE, [(i, i ^ bit) for i in range(PLANE_SIZE)])]
    unnamed x221 -> x122, local copies, waits for them, and re-layouts: 44.9 us -> 20.5 us
    ppermute x5, waiting for transfers between devices: 38.4 us -> 59.9 us  [line_sum(): back = lax.ppermute(total, 'replica', [(1, 0), (2, 3)])]
    pallas_call x9 -> x0, local copies, waits for them, and re-layouts: 16.6 us -> none  [call(): pl.pallas_call(kernel, out_shape=[jax.ShapeDtypeStruct(shape, kind) for s...]
    pallas_call x15, Pallas kernels: 81.9 us -> 68 us  [call(): pl.pallas_call(kernel, out_shape=[jax.ShapeDtypeStruct(shape, kind) for s...]
    ppermute x5, starting transfers between devices: 21.3 us -> 8.13 us  [line_sum(): first = lax.ppermute(part.astype(BF16), 'replica', [(0, 1), (3, 2)])]
  transfers between devices with their start and end apart: 86 -> 77, of which waited for: 29 -> 26; matrix products, arithmetic and copies ran while one was open for 27% -> 6% of each run, Pallas kernels for 10% -> 14%
where the time goes in v3:
time: 451 us; the launch traced here: 450 us
  waiting for transfers between devices  268 us (59%)
  Pallas kernels  68 us (15%)
  starting transfers between devices  62.7 us (14%)
  local copies, waits for them, and re-layouts  30.1 us (7%)
  other arithmetic  19.4 us (4%)
    ppermute x60, waiting for transfers between devices, swap(): return lax.ppermute(value, PLANE, [(i, i ^ bit) for i in range(PLANE_SIZE)])  162 us
    pallas_call x15, Pallas kernels, call(): pl.pallas_call(kernel, out_shape=[jax.ShapeDtypeStruct(shape, kind) for s...  68 us
    ppermute x5, waiting for transfers between devices, line_sum(): back = lax.ppermute(total, 'replica', [(1, 0), (2, 3)])  59.9 us
    ppermute x5, waiting for transfers between devices, line_sum(): first = lax.ppermute(part.astype(BF16), 'replica', [(0, 1), (3, 2)])  45.8 us
    ppermute x60, starting transfers between devices, swap(): return lax.ppermute(value, PLANE, [(i, i ^ bit) for i in range(PLANE_SIZE)])  40.3 us
    unnamed x122, local copies, waits for them, and re-layouts  20.5 us
  transfers between devices with their start and end apart: 77, of which 26 were waited for; matrix products, arithmetic and copies ran while one was open for 6% of the time, Pallas kernels for 14%

profile of v3, /device:TPU:0, one launch (start us, length us, event | category | flops | bytes accessed | tf_op | source)
XLA Modules:
  0.0 450.0 jit_solution(17268984846579911380)
XLA Ops:
  2.9 3.0 collective-permute-start.1
  8.9 20.9 %collective-permute-done.1.refs_2_.refs_12_ = bf16[128,4224]{1,0:T(8,128)(2,1)} collective-permute-done((bf16[128,4224]{1,0:T(8,128)(2,1)S(1)}, bf16[128,4224]{1,0:T(8,128)(2,1)}, u32[]{:S(2)}, u32[]{:S(2)}) %collective-permute-start.1) | collective-permute-done | bytes 1081376 | tf_op jit(solution)/shard_map/ppermute | solution.py:265
  37.7 38.4 %collective-permute-done.3.refs_4_.refs_14_ = bf16[64,4224]{1,0:T(8,128)(2,1)S(1)} collective-permute-done((bf16[64,4224]{1,0:T(8,128)(2,1)S(1)}, bf16[64,4224]{1,0:T(8,128)(2,1)S(1)}, u32[]{:S(2)}, u32[]{:S(2)}) %collective-permute-start.3) | collective-permute-done | bytes 540704 | tf_op jit(solution)/shard_map/ppermute | solution.py:265
  84.8 4.7 %shard_map.161 = (bf16[128,1024]{1,0:T(8,128)(2,1)S(1)}, bf16[128,2048]{1,0:T(8,128)(2,1)S(1)}, bf16[64,2048]{1,0:T(8,128)(2,1)S(1)}, bf16[128,1024]{1,0:T(8,128)(2,1)S(1)}, f32[8,1024]{1,0:T(8,128)S(1)}) custom-call(s32[2]{0:T(128)S(1)} %pad_add_fusion.place, bf16[128,1024]{1,0:T(8,128)(2,1)S(1)} %bitcast.18, f32[128,128]{1,0:T(8,128)S(1)} %get-tuple-element.145.cosine, ...), custom_call_target="tpu_custom_call" | custom-call | flops 805306368 | bytes 8650752 | tf_op jit(solution)/shard_map/pallas_call | solution.py:559
  94.3 4.5 collective-permute-done.9.edge
  100.7 12.8 %collective-permute-done.13.refs_4_ = bf16[64,5376]{1,0:T(8,128)(2,1)S(1)} collective-permute-done((bf16[64,5376]{1,0:T(8,128)(2,1)S(1)}, bf16[64,5376]{1,0:T(8,128)(2,1)S(1)}, u32[]{:S(2)}, u32[]{:S(2)}) %collective-permute-start.13) | collective-permute-done | bytes 688160 | tf_op jit(solution)/shard_map/ppermute | solution.py:265
  115.0 13.3 %collective-permute-done.19.refs_1_ = bf16[128,2688]{1,0:T(8,128)(2,1)S(1)} collective-permute-done((bf16[128,2688]{1,0:T(8,128)(2,1)}, bf16[128,2688]{1,0:T(8,128)(2,1)S(1)}, u32[]{:S(2)}, u32[]{:S(2)}) %collective-permute-start.19) | collective-permute-done | bytes 688160 | tf_op jit(solution)/shard_map/ppermute | solution.py:265
  129.1 5.3 %collective-permute-done.22.refs_4_ = bf16[64,2688]{1,0:T(8,128)(2,1)S(1)} collective-permute-done((bf16[64,2688]{1,0:T(8,128)(2,1)S(1)}, bf16[64,2688]{1,0:T(8,128)(2,1)S(1)}, u32[]{:S(2)}, u32[]{:S(2)}) %collective-permute-start.22) | collective-permute-done | bytes 344096 | tf_op jit(solution)/shard_map/ppermute | solution.py:265
  135.2 3.8 collective-permute-done.21.refs_3_
  145.3 7.7 %shard_map.162 = (bf16[128,1024]{1,0:T(8,128)(2,1)S(1)}, f32[128,128]{1,0:T(8,128)S(1)}, f32[128,1024]{1,0:T(8,128)S(1)}, bf16[128,1024]{1,0:T(8,128)(2,1)S(1)}) custom-call(s32[2]{0:T(128)S(1)} %pad_add_fusion.place, bf16[128,1024]{1,0:T(8,128)(2,1)S(1)} %copy-done.35, bf16[128,2048]{1,0:T(8,128)(2,1)S(1)} %copy-done.15, bf16[64,2048]{1,0:T(8,128)(2,1)S(1)} %copy-done.38, ...), custom_call_target="tpu_custom_call" | custom-call | flops 1610612736 | bytes 4194304 | tf_op jit(solution)/shard_map/pallas_call | solution.py:559
  153.7 7.9 %shard_map.163 = (bf16[128,3200]{1,0:T(8,128)(2,1)S(1)}, bf16[128,3200]{1,0:T(8,128)(2,1)}, f32[128,2688]{1,0:T(8,128)}, f32[128,2688]{1,0:T(8,128)}) custom-call(s32[2]{0:T(128)S(1)} %pad_add_fusion.place, bf16[128,1024]{1,0:T(8,128)(2,1)S(1)} %get-tuple-element.64.xn2, bf16[128,1024]{1,0:T(8,128)(2,1)S(1)} %bitcast.15, bf16[128,5376]{1,0:T(8,128)(2,1)} %fusion.2.refs_0_, ...), custom_call_target="tpu_custom_call" | custom-call | flops 1409286144 | bytes 11010048 | tf_op jit(solution)/shard_map/pallas_call | solution.py:559
  165.1 8.6 %shard_map.164 = (bf16[128,1024]{1,0:T(8,128)(2,1)}, bf16[128,3200]{1,0:T(8,128)(2,1)}, bf16[128,3200]{1,0:T(8,128)(2,1)}, bf16[128,3200]{1,0:T(8,128)(2,1)}, bf16[128,3200]{1,0:T(8,128)(2,1)}) custom-call(s32[2]{0:T(128)S(1)} %pad_add_fusion.place, bf16[128,3200]{1,0:T(8,128)(2,1)} %copy-done.3, bf16[128,1024]{1,0:T(8,128)(2,1)S(1)} %bitcast.16, ...), custom_call_target="tpu_custom_call" | custom-call | flops 1409286144 | bytes 5505024 | tf_op jit(solution)/shard_map/pallas_call | solution.py:559
  174.4 10.8 %shard_map.165 = (bf16[128,1536]{1,0:T(8,128)(2,1)S(1)}, bf16[128,1536]{1,0:T(8,128)(2,1)S(1)}, f32[128,1024]{1,0:T(8,128)S(1)}, bf16[128,1024]{1,0:T(8,128)(2,1)S(1)}, f32[1,1024]{1,0:T(1,128)S(1)}) custom-call(s32[2]{0:T(128)S(1)} %pad_add_fusion.place, bf16[128,3200]{1,0:T(8,128)(2,1)} %get-tuple-element.73.pack_one.refs_0_, ...), custom_call_target="tpu_custom_call" | custom-call | flops 2113929216 | bytes 16515072 | tf_op jit(solution)/shard_map/pallas_call | solution.py:559
  189.3 13.5 %collective-permute-done.39.refs_1_ = bf16[128,1536]{1,0:T(8,128)(2,1)S(1)} collective-permute-done((bf16[128,1536]{1,0:T(8,128)(2,1)S(1)}, bf16[128,1536]{1,0:T(8,128)(2,1)S(1)}, u32[]{:S(2)}, u32[]{:S(2)}) %collective-permute-start.39) | collective-permute-done | bytes 393248 | tf_op jit(solution)/shard_map/ppermute | solution.py:265
  208.6 2.5 shard_map.166
  217.2 7.2 %shard_map.167 = (bf16[128,1536]{1,0:T(8,128)(2,1)S(1)}, bf16[128,1536]{1,0:T(8,128)(2,1)}, f32[128,2048]{1,0:T(8,128)S(1)}, bf16[64,2048]{1,0:T(8,128)(2,1)}) custom-call(s32[2]{0:T(128)S(1)} %pad_add_fusion.place, bf16[128,1024]{1,0:T(8,128)(2,1)S(1)} %copy-done.36, bf16[128,2048]{1,0:T(8,128)(2,1)S(1)} %copy-done.16, bf16[64,2048]{1,0:T(8,128)(2,1)S(1)} %copy-done.39, ...), custom_call_target="tpu_custom_call" | custom-call | flops 2684354560 | bytes 4194304 | tf_op jit(solution)/shard_map/pallas_call | solution.py:559
  227.6 2.5 shard_map.168
  230.1 2.5 shard_map.169
  234.8 2.8 fusion.11
  237.6 6.2 %shard_map.172 = (bf16[128,1024]{1,0:T(8,128)(2,1)}, f32[1,1024]{1,0:T(1,128)S(1)}) custom-call(s32[2]{0:T(128)S(1)} %pad_add_fusion.place, bf16[128,1536]{1,0:T(8,128)(2,1)S(1)} %get-tuple-element.81.pack_q.refs_0_, bf16[128,1536]{1,0:T(8,128)(2,1)S(1)} %get-tuple-element.89.pack_k.refs_0_, bf16[128,1536]{1,0:T(8,128)(2,1)S(1)} %get-tuple-element.90.pack_v.refs_0_, ...), custom_call_target="tpu_custom_call" | custom-call | flops 805306368 | bytes 6291456 | tf_op jit(solution)/shard_map/pallas_call | solution.py:559
  248.1 20.1 %collective-permute-done.43 = f32[2,1024]{1,0:T(2,128)S(1)} collective-permute-done((f32[2,1024]{1,0:T(2,128)S(1)}, f32[2,1024]{1,0:T(2,128)S(1)}, u32[]{:S(2)}, u32[]{:S(2)}) %collective-permute-start.43) | collective-permute-done | bytes 8224 | tf_op jit(solution)/shard_map/ppermute | solution.py:265
  278.5 2.6 collective-permute-start.46
  282.9 14.9 %collective-permute-done.55.refs_1_ = bf16[128,1536]{1,0:T(8,128)(2,1)S(1)} collective-permute-done((bf16[128,1536]{1,0:T(8,128)(2,1)S(1)}, bf16[128,1536]{1,0:T(8,128)(2,1)S(1)}, u32[]{:S(2)}, u32[]{:S(2)}) %collective-permute-start.55) | collective-permute-done | bytes 393248 | tf_op jit(solution)/shard_map/ppermute | solution.py:265
  303.5 2.4 collective-permute-start.67
  313.2 4.5 %collective-permute-done.58 = bf16[128,1024]{1,0:T(8,128)(2,1)S(1)} collective-permute-done((bf16[128,1024]{1,0:T(8,128)(2,1)S(1)}, bf16[128,1024]{1,0:T(8,128)(2,1)S(1)}, u32[]{:S(2)}, u32[]{:S(2)}) %collective-permute-start.58) | collective-permute-done | bytes 262176 | tf_op jit(solution)/shard_map/ppermute | solution.py:265
  324.1 12.4 %collective-permute-done.71 = bf16[128,2688]{1,0:T(8,128)(2,1)S(1)} collective-permute-done((bf16[128,2688]{1,0:T(8,128)(2,1)S(1)}, bf16[128,2688]{1,0:T(8,128)(2,1)S(1)}, u32[]{:S(2)}, u32[]{:S(2)}) %collective-permute-start.71) | collective-permute-done | bytes 688160 | tf_op jit(solution)/shard_map/ppermute | solution.py:589
  337.3 13.8 %collective-permute-done.74 = bf16[128,2688]{1,0:T(8,128)(2,1)S(1)} collective-permute-done((bf16[128,2688]{1,0:T(8,128)(2,1)S(1)}, bf16[128,2688]{1,0:T(8,128)(2,1)S(1)}, u32[]{:S(2)}, u32[]{:S(2)}) %collective-permute-start.74) | collective-permute-done | bytes 688160 | tf_op jit(solution)/shard_map/ppermute | solution.py:589
  352.0 10.4 %collective-permute-done.52 = bf16[128,2048]{1,0:T(8,128)(2,1)S(1)} collective-permute-done((bf16[128,2048]{1,0:T(8,128)(2,1)S(1)}, bf16[128,2048]{1,0:T(8,128)(2,1)S(1)}, u32[]{:S(2)}, u32[]{:S(2)}) %collective-permute-start.52) | collective-permute-done | bytes 524320 | tf_op jit(solution)/shard_map/ppermute | solution.py:589
  363.2 9.3 %collective-permute-done.63 = bf16[128,2048]{1,0:T(8,128)(2,1)S(1)} collective-permute-done((bf16[128,2048]{1,0:T(8,128)(2,1)S(1)}, bf16[128,2048]{1,0:T(8,128)(2,1)S(1)}, u32[]{:S(2)}, u32[]{:S(2)}) %collective-permute-start.63) | collective-permute-done | bytes 524320 | tf_op jit(solution)/shard_map/ppermute | solution.py:589
  380.7 42.8 %collective-permute-done.54 = bf16[128,2048]{1,0:T(8,128)(2,1)S(1)} collective-permute-done((bf16[128,2048]{1,0:T(8,128)(2,1)S(1)}, bf16[128,2048]{1,0:T(8,128)(2,1)S(1)}, u32[]{:S(2)}, u32[]{:S(2)}) %collective-permute-start.54) | collective-permute-done | bytes 524320 | tf_op jit(solution)/shard_map/ppermute | solution.py:593
  424.7 13.6 %collective-permute-done.76 = bf16[128,2688]{1,0:T(8,128)(2,1)S(1)} collective-permute-done((bf16[128,2688]{1,0:T(8,128)(2,1)S(1)}, bf16[128,2688]{1,0:T(8,128)(2,1)S(1)}, u32[]{:S(2)}, u32[]{:S(2)}) %collective-permute-start.76) | collective-permute-done | bytes 688160 | tf_op jit(solution)/shard_map/ppermute | solution.py:593
  444.0 3.5 collective-permute-done.65
  (314 shorter events, 119.1 us)
Async XLA Ops:
  2.9 27.0 %collective-permute-start.1 = (bf16[128,4224]{1,0:T(8,128)(2,1)S(1)}, bf16[128,4224]{1,0:T(8,128)(2,1)}, u32[]{:S(2)}, u32[]{:S(2)}) collective-permute-start(bf16[128,4224]{1,0:T(8,128)(2,1)S(1)} %fusion.3.refs_0_.refs_10_), channel_id=1, source_target_pairs={{0,4},{1,5},{2,6},{3,7},{4,0},{5,1},{6,2},{7,3},{8,12},{9,13},{10,... | collective-permute-start | bytes 3244040 | tf_op jit(solution)/shard_map/ppermute | solution.py:265
  5.9 25.4 %collective-permute-start = (bf16[128,4224]{1,0:T(8,128)(2,1)S(1)}, bf16[128,4224]{1,0:T(8,128)(2,1)}, u32[]{:S(2)}, u32[]{:S(2)}) collective-permute-start(bf16[128,4224]{1,0:T(8,128)(2,1)S(1)} %fusion.3.refs_0_.refs_10_), channel_id=1, source_target_pairs={{0,1},{1,0},{2,3},{3,2},{4,5},{5,4},{6,7},{7,6},{8,9},{9,8},{10,11... | collective-permute-start | bytes 3244040 | tf_op jit(solution)/shard_map/ppermute | solution.py:265
  31.4 45.3 %collective-permute-start.11 = (bf16[128,5376]{1,0:T(8,128)(2,1)}, bf16[128,5376]{1,0:T(8,128)(2,1)}, u32[]{:S(2)}, u32[]{:S(2)}) collective-permute-start(bf16[128,5376]{1,0:T(8,128)(2,1)} %fusion.2.refs_0_), channel_id=1, source_target_pairs={{0,4},{1,5},{2,6},{3,7},{4,0},{5,1},{6,2},{7,3},{8,12},{9,13},{10,... | collective-permute-start | bytes 4128776 | tf_op jit(solution)/shard_map/ppermute | solution.py:265
  31.7 49.3 %collective-permute-start.10 = (bf16[128,5376]{1,0:T(8,128)(2,1)}, bf16[128,5376]{1,0:T(8,128)(2,1)}, u32[]{:S(2)}, u32[]{:S(2)}) collective-permute-start(bf16[128,5376]{1,0:T(8,128)(2,1)} %fusion.2.refs_0_), channel_id=1, source_target_pairs={{0,1},{1,0},{2,3},{3,2},{4,5},{5,4},{6,7},{7,6},{8,9},{9,8},{10,11... | collective-permute-start | bytes 4128776 | tf_op jit(solution)/shard_map/ppermute | solution.py:265
  34.4 41.7 %collective-permute-start.3 = (bf16[64,4224]{1,0:T(8,128)(2,1)S(1)}, bf16[64,4224]{1,0:T(8,128)(2,1)S(1)}, u32[]{:S(2)}, u32[]{:S(2)}) collective-permute-start(bf16[64,4224]{1,0:T(8,128)(2,1)S(1)} %slice.80), channel_id=1, source_target_pairs={{0,1},{1,0},{2,3},{3,2},{4,5},{5,4},{6,7},{7,6},{8,9},{9,8},{10,11... | collective-permute-start | bytes 1622024 | tf_op jit(solution)/shard_map/ppermute | solution.py:265
  36.0 40.1 %collective-permute-start.2 = (bf16[64,4224]{1,0:T(8,128)(2,1)S(1)}, bf16[64,4224]{1,0:T(8,128)(2,1)S(1)}, u32[]{:S(2)}, u32[]{:S(2)}) collective-permute-start(bf16[64,4224]{1,0:T(8,128)(2,1)S(1)} %slice.79), channel_id=1, source_target_pairs={{0,4},{1,5},{2,6},{3,7},{4,0},{5,1},{6,2},{7,3},{8,12},{9,13},{10,... | collective-permute-start | bytes 1622024 | tf_op jit(solution)/shard_map/ppermute | solution.py:265
  37.7 46.0 %collective-permute-start.6 = (bf16[128,4224]{1,0:T(8,128)(2,1)}, bf16[128,4224]{1,0:T(8,128)(2,1)S(1)}, u32[]{:S(2)}, u32[]{:S(2)}) collective-permute-start(bf16[128,4224]{1,0:T(8,128)(2,1)} %collective-permute-done.1.refs_2_.refs_12_), channel_id=1, source_target_pairs={{0,2},{1,3},{2,0},{3,1},{4,6},{5,7},{6,4},{7,5},{8,10},{9,11},{10,... | collective-permute-start | bytes 3244040 | tf_op jit(solution)/shard_map/ppermute | solution.py:265
  76.1 24.0 %collective-permute-start.14 = (bf16[128,5376]{1,0:T(8,128)(2,1)}, bf16[128,5376]{1,0:T(8,128)(2,1)}, u32[]{:S(2)}, u32[]{:S(2)}) collective-permute-start(bf16[128,5376]{1,0:T(8,128)(2,1)} %fusion.2.refs_0_), channel_id=1, source_target_pairs={{0,2},{1,3},{2,0},{3,1},{4,6},{5,7},{6,4},{7,5},{8,10},{9,11},{10,... | collective-permute-start | bytes 4128776 | tf_op jit(solution)/shard_map/ppermute | solution.py:265
  92.8 35.5 %collective-permute-start.19 = (bf16[128,2688]{1,0:T(8,128)(2,1)}, bf16[128,2688]{1,0:T(8,128)(2,1)S(1)}, u32[]{:S(2)}, u32[]{:S(2)}) collective-permute-start(bf16[128,2688]{1,0:T(8,128)(2,1)} %pad.17.refs_0_), channel_id=1, source_target_pairs={{0,1},{1,0},{2,3},{3,2},{4,5},{5,4},{6,7},{7,6},{8,9},{9,8},{10,11... | collective-permute-start | bytes 2064392 | tf_op jit(solution)/shard_map/ppermute | solution.py:265
  98.8 42.7 %collective-permute-start.16 = (bf16[128,5376]{1,0:T(8,128)(2,1)}, bf16[128,5376]{1,0:T(8,128)(2,1)}, u32[]{:S(2)}, u32[]{:S(2)}) collective-permute-start(bf16[128,5376]{1,0:T(8,128)(2,1)} %collective-permute-done.11.refs_2_), channel_id=1, source_target_pairs={{0,2},{1,3},{2,0},{3,1},{4,6},{5,7},{6,4},{7,5},{8,10},{9,11},{10,... | collective-permute-start | bytes 4128776 | tf_op jit(solution)/shard_map/ppermute | solution.py:265
  100.1 28.2 %collective-permute-start.12 = (bf16[64,5376]{1,0:T(8,128)(2,1)S(1)}, bf16[64,5376]{1,0:T(8,128)(2,1)S(1)}, u32[]{:S(2)}, u32[]{:S(2)}) collective-permute-start(bf16[64,5376]{1,0:T(8,128)(2,1)S(1)} %slice.84), channel_id=1, source_target_pairs={{0,4},{1,5},{2,6},{3,7},{4,0},{5,1},{6,2},{7,3},{8,12},{9,13},{10,... | collective-permute-start | bytes 2064392 | tf_op jit(solution)/shard_map/ppermute | solution.py:265
  100.5 53.1 %collective-permute-start.15 = (bf16[128,5376]{1,0:T(8,128)(2,1)}, bf16[128,5376]{1,0:T(8,128)(2,1)}, u32[]{:S(2)}, u32[]{:S(2)}) collective-permute-start(bf16[128,5376]{1,0:T(8,128)(2,1)} %collective-permute-done.10.refs_1_), channel_id=1, source_target_pairs={{0,2},{1,3},{2,0},{3,1},{4,6},{5,7},{6,4},{7,5},{8,10},{9,11},{10,... | collective-permute-start | bytes 4128776 | tf_op jit(solution)/shard_map/ppermute | solution.py:265
  139.0 23.5 %collective-permute-start.23 = (bf16[128,2688]{1,0:T(8,128)(2,1)}, bf16[128,2688]{1,0:T(8,128)(2,1)}, u32[]{:S(2)}, u32[]{:S(2)}) collective-permute-start(bf16[128,2688]{1,0:T(8,128)(2,1)} %pad.17.refs_0_), channel_id=1, source_target_pairs={{0,2},{1,3},{2,0},{3,1},{4,6},{5,7},{6,4},{7,5},{8,10},{9,11},{10,... | collective-permute-start | bytes 2064392 | tf_op jit(solution)/shard_map/ppermute | solution.py:265
  141.0 23.1 %collective-permute-start.25 = (bf16[128,2688]{1,0:T(8,128)(2,1)}, bf16[128,2688]{1,0:T(8,128)(2,1)S(1)}, u32[]{:S(2)}, u32[]{:S(2)}) collective-permute-start(bf16[128,2688]{1,0:T(8,128)(2,1)} %copy-done.51), channel_id=1, source_target_pairs={{0,2},{1,3},{2,0},{3,1},{4,6},{5,7},{6,4},{7,5},{8,10},{9,11},{10,... | collective-permute-start | bytes 2064392 | tf_op jit(solution)/shard_map/ppermute | solution.py:265
  162.5 26.2 %collective-permute-start.28 = (bf16[128,3200]{1,0:T(8,128)(2,1)}, bf16[128,3200]{1,0:T(8,128)(2,1)S(1)}, u32[]{:S(2)}, u32[]{:S(2)}) collective-permute-start(bf16[128,3200]{1,0:T(8,128)(2,1)} %get-tuple-element.77), channel_id=1, source_target_pairs={{0,1},{1,0},{2,3},{3,2},{4,5},{5,4},{6,7},{7,6},{8,9},{9,8},{10,11... | collective-permute-start | bytes 2457608 | tf_op jit(solution)/shard_map/ppermute | solution.py:265
  173.8 31.6 %collective-permute-start.31 = (bf16[128,3200]{1,0:T(8,128)(2,1)}, bf16[128,3200]{1,0:T(8,128)(2,1)S(1)}, u32[]{:S(2)}, u32[]{:S(2)}) collective-permute-start(bf16[128,3200]{1,0:T(8,128)(2,1)} %get-tuple-element.83), channel_id=1, source_target_pairs={{0,4},{1,5},{2,6},{3,7},{4,0},{5,1},{6,2},{7,3},{8,12},{9,13},{10,... | collective-permute-start | bytes 2457608 | tf_op jit(solution)/shard_map/ppermute | solution.py:265
  243.9 29.6 %collective-permute-start.47 = (bf16[128,1024]{1,0:T(8,128)(2,1)}, bf16[128,1024]{1,0:T(8,128)(2,1)S(1)}, u32[]{:S(2)}, u32[]{:S(2)}) collective-permute-start(bf16[128,1024]{1,0:T(8,128)(2,1)} %get-tuple-element.95), channel_id=1, source_target_pairs={{0,1},{1,0},{2,3},{3,2},{4,5},{5,4},{6,7},{7,6},{8,9},{9,8},{10,11... | collective-permute-start | bytes 786440 | tf_op jit(solution)/shard_map/ppermute | solution.py:265
  245.3 33.2 %collective-permute-start.66 = (bf16[128,2688]{1,0:T(8,128)(2,1)}, bf16[128,2688]{1,0:T(8,128)(2,1)}, u32[]{:S(2)}, u32[]{:S(2)}) collective-permute-start(bf16[128,2688]{1,0:T(8,128)(2,1)} %get-tuple-element.84), channel_id=1, source_target_pairs={{0,1},{1,0},{2,3},{3,2},{4,5},{5,4},{6,7},{7,6},{8,9},{9,8},{10,11... | collective-permute-start | bytes 2064392 | tf_op jit(solution)/shard_map/ppermute | solution.py:265
  247.4 29.8 %collective-permute-start.48 = (bf16[128,1536]{1,0:T(8,128)(2,1)}, bf16[128,1536]{1,0:T(8,128)(2,1)S(1)}, u32[]{:S(2)}, u32[]{:S(2)}) collective-permute-start(bf16[128,1536]{1,0:T(8,128)(2,1)} %get-tuple-element.101), channel_id=1, source_target_pairs={{0,1},{1,0},{2,3},{3,2},{4,5},{5,4},{6,7},{7,6},{8,9},{9,8},{10,11... | collective-permute-start | bytes 1179656 | tf_op jit(solution)/shard_map/ppermute | solution.py:265
  273.6 24.7 %collective-permute-start.70 = (bf16[128,2688]{1,0:T(8,128)(2,1)}, bf16[128,2688]{1,0:T(8,128)(2,1)S(1)}, u32[]{:S(2)}, u32[]{:S(2)}) collective-permute-start(bf16[128,2688]{1,0:T(8,128)(2,1)} %get-tuple-element.86), channel_id=1, source_target_pairs={{0,4},{1,5},{2,6},{3,7},{4,0},{5,1},{6,2},{7,3},{8,12},{9,13},{10,... | collective-permute-start | bytes 2064392 | tf_op jit(solution)/shard_map/ppermute | solution.py:265
  305.9 30.5 %collective-permute-start.71 = (bf16[128,2688]{1,0:T(8,128)(2,1)S(1)}, bf16[128,2688]{1,0:T(8,128)(2,1)S(1)}, u32[]{:S(2)}, u32[]{:S(2)}) collective-permute-start(bf16[128,2688]{1,0:T(8,128)(2,1)S(1)} %fusion.5), channel_id=1, source_target_pairs={{0,8},{24,16},{1,9},{25,17},{2,10},{26,18},{3,11},{27,19},{4,12},{... | collective-permute-start | bytes 2064392 | tf_op jit(solution)/shard_map/ppermute | solution.py:589
  308.5 42.6 %collective-permute-start.74 = (bf16[128,2688]{1,0:T(8,128)(2,1)S(1)}, bf16[128,2688]{1,0:T(8,128)(2,1)S(1)}, u32[]{:S(2)}, u32[]{:S(2)}) collective-permute-start(bf16[128,2688]{1,0:T(8,128)(2,1)S(1)} %copy-done.54), channel_id=1, source_target_pairs={{0,8},{24,16},{1,9},{25,17},{2,10},{26,18},{3,11},{27,19},{4,12},{... | collective-permute-start | bytes 2064392 | tf_op jit(solution)/shard_map/ppermute | solution.py:589
  317.7 44.7 %collective-permute-start.52 = (bf16[128,2048]{1,0:T(8,128)(2,1)S(1)}, bf16[128,2048]{1,0:T(8,128)(2,1)S(1)}, u32[]{:S(2)}, u32[]{:S(2)}) collective-permute-start(bf16[128,2048]{1,0:T(8,128)(2,1)S(1)} %fusion.7), channel_id=1, source_target_pairs={{0,8},{24,16},{1,9},{25,17},{2,10},{26,18},{3,11},{27,19},{4,12},{... | collective-permute-start | bytes 1572872 | tf_op jit(solution)/shard_map/ppermute | solution.py:589
  320.2 52.3 %collective-permute-start.63 = (bf16[128,2048]{1,0:T(8,128)(2,1)S(1)}, bf16[128,2048]{1,0:T(8,128)(2,1)S(1)}, u32[]{:S(2)}, u32[]{:S(2)}) collective-permute-start(bf16[128,2048]{1,0:T(8,128)(2,1)S(1)} %fusion.6), channel_id=1, source_target_pairs={{0,8},{24,16},{1,9},{25,17},{2,10},{26,18},{3,11},{27,19},{4,12},{... | collective-permute-start | bytes 1572872 | tf_op jit(solution)/shard_map/ppermute | solution.py:589
  323.2 50.1 %collective-permute-start.68 = (bf16[128,2688]{1,0:T(8,128)(2,1)S(1)}, bf16[128,2688]{1,0:T(8,128)(2,1)S(1)}, u32[]{:S(2)}, u32[]{:S(2)}) collective-permute-start(bf16[128,2688]{1,0:T(8,128)(2,1)S(1)} %add_convert_fusion.5), channel_id=1, source_target_pairs={{8,16},{16,8},{9,17},{17,9},{10,18},{18,10},{11,19},{19,11},{12,20... | collective-permute-start | bytes 2064392 | tf_op jit(solution)/shard_map/ppermute | solution.py:591
  336.6 38.2 %collective-permute-start.72 = (bf16[128,2688]{1,0:T(8,128)(2,1)S(1)}, bf16[128,2688]{1,0:T(8,128)(2,1)S(1)}, u32[]{:S(2)}, u32[]{:S(2)}) collective-permute-start(bf16[128,2688]{1,0:T(8,128)(2,1)S(1)} %add_convert_fusion.3), channel_id=1, source_target_pairs={{8,16},{16,8},{9,17},{17,9},{10,18},{18,10},{11,19},{19,11},{12,20... | collective-permute-start | bytes 2064392 | tf_op jit(solution)/shard_map/ppermute | solution.py:591
  351.3 26.5 %collective-permute-start.75 = (bf16[128,2688]{1,0:T(8,128)(2,1)S(1)}, bf16[128,2688]{1,0:T(8,128)(2,1)S(1)}, u32[]{:S(2)}, u32[]{:S(2)}) collective-permute-start(bf16[128,2688]{1,0:T(8,128)(2,1)S(1)} %add_convert_fusion.1), channel_id=1, source_target_pairs={{8,16},{16,8},{9,17},{17,9},{10,18},{18,10},{11,19},{19,11},{12,20... | collective-permute-start | bytes 2064392 | tf_op jit(solution)/shard_map/ppermute | solution.py:591
  373.5 66.3 %collective-permute-start.69 = (bf16[128,2688]{1,0:T(8,128)(2,1)S(1)}, bf16[128,2688]{1,0:T(8,128)(2,1)}, u32[]{:S(2)}, u32[]{:S(2)}) collective-permute-start(bf16[128,2688]{1,0:T(8,128)(2,1)S(1)} %add_convert_fusion.4), channel_id=1, source_target_pairs={{8,0},{16,24},{9,1},{17,25},{10,2},{18,26},{11,3},{19,27},{12,4},{... | collective-permute-start | bytes 2064392 | tf_op jit(solution)/shard_map/ppermute | solution.py:593
  375.0 66.0 %collective-permute-start.73 = (bf16[128,2688]{1,0:T(8,128)(2,1)S(1)}, bf16[128,2688]{1,0:T(8,128)(2,1)}, u32[]{:S(2)}, u32[]{:S(2)}) collective-permute-start(bf16[128,2688]{1,0:T(8,128)(2,1)S(1)} %add_convert_fusion.2), channel_id=1, source_target_pairs={{8,0},{16,24},{9,1},{17,25},{10,2},{18,26},{11,3},{19,27},{12,4},{... | collective-permute-start | bytes 2064392 | tf_op jit(solution)/shard_map/ppermute | solution.py:593
  376.5 47.0 %collective-permute-start.54 = (bf16[128,2048]{1,0:T(8,128)(2,1)S(1)}, bf16[128,2048]{1,0:T(8,128)(2,1)S(1)}, u32[]{:S(2)}, u32[]{:S(2)}) collective-permute-start(bf16[128,2048]{1,0:T(8,128)(2,1)S(1)} %add_convert_fusion.8), channel_id=1, source_target_pairs={{8,0},{16,24},{9,1},{17,25},{10,2},{18,26},{11,3},{19,27},{12,4},{... | collective-permute-start | bytes 1572872 | tf_op jit(solution)/shard_map/ppermute | solution.py:593
  378.0 60.3 %collective-permute-start.76 = (bf16[128,2688]{1,0:T(8,128)(2,1)S(1)}, bf16[128,2688]{1,0:T(8,128)(2,1)S(1)}, u32[]{:S(2)}, u32[]{:S(2)}) collective-permute-start(bf16[128,2688]{1,0:T(8,128)(2,1)S(1)} %add_convert_fusion), channel_id=1, source_target_pairs={{8,0},{16,24},{9,1},{17,25},{10,2},{18,26},{11,3},{19,27},{12,4},{... | collective-permute-start | bytes 2064392 | tf_op jit(solution)/shard_map/ppermute | solution.py:593
  379.4 68.1 %collective-permute-start.65 = (bf16[128,2048]{1,0:T(8,128)(2,1)S(1)}, bf16[128,2048]{1,0:T(8,128)(2,1)}, u32[]{:S(2)}, u32[]{:S(2)}) collective-permute-start(bf16[128,2048]{1,0:T(8,128)(2,1)S(1)} %add_convert_fusion.6), channel_id=1, source_target_pairs={{8,0},{16,24},{9,1},{17,25},{10,2},{18,26},{11,3},{19,27},{12,4},{... | collective-permute-start | bytes 1572872 | tf_op jit(solution)/shard_map/ppermute | solution.py:593
  (105 other events, 1254.7 us)

commit v4 on v3

--- a/solution.py
+++ b/solution.py
@@ -265,15 +265,18 @@
     return lax.ppermute(value, PLANE, [(i, i ^ bit) for i in range(PLANE_SIZE)])
 
 
-def gather_pieces(own, after=None):
-    if after is not None:
-        own, _ = lax.optimization_barrier((own, after))
+def later(value, *others):
+    return lax.optimization_barrier((value, others))[0]
+
+
+def gather_pieces(own, after=()):
+    own = later(own, after)
     half = own.shape[0] // 2
     over_x = swap(own, X_BIT)
     over_y = swap(own, Y_BIT)
     first = [own, over_x, over_y, swap(over_x[:half], Y_BIT), swap(over_y[half:], X_BIT)]
     second = [swap(part, CORE_BIT) for part in first]
-    return (first + second, (over_x, over_y))
+    return (first + second, tuple(first[3:]))
 
 
 def fill(pieces, target, sems, me, columns=None):
@@ -298,13 +301,13 @@
 
 
 def pack(keep, send, left, right, gather_bit, sum_bit, me):
-    width = left.shape[1] // PLANE_SIZE
+    rows, width = (left.shape[0], left.shape[1] // PLANE_SIZE)
     for slot, offset in enumerate([0, CORE_BIT, sum_bit, CORE_BIT | sum_bit]):
         for target, flip in ((keep, 0), (send, gather_bit)):
             source = pl.multiple_of((me ^ (offset | flip)) * width, width)
-            target[:, slot * width : (slot + 1) * width] = left[:, pl.ds(source, width)]
-    keep[:, 4 * width :] = right
-    send[:, 4 * width :] = right
+            target[:rows, slot * width : (slot + 1) * width] = left[:, pl.ds(source, width)]
+    keep[:rows, 4 * width :] = right
+    send[:rows, 4 * width :] = right
 
 
 def turn(values, cosine, sine):
@@ -414,7 +417,7 @@
     pieces, (keep, send, slope_gate, active, weight, sems) = (refs[:PIECES], refs[PIECES:])
     me = place[0]
     cols = active.shape[1]
-    wait_all(fill(pieces, weight, sems, me))
+    wait_all(fill(pieces, weight, sems, me, pl.ds(0, 2 * cols)))
     gelu_input = dot_nn(xn2[...], weight[:, :cols])
     gate_part = dot_nn(xn2[...], weight[:, cols:])
     cdf_part = 0.5 * (1.0 + lax.erf(gelu_input * (1.0 / math.sqrt(2.0))))
@@ -429,7 +432,8 @@
     pieces, rest = (refs[:PIECES], refs[PIECES:])
     layer_out, keep_one, send_one, keep_two, send_two, weight, sems = rest
     me = place[0]
-    wait_all(fill(pieces, weight, sems, me))
+    cols = weight.shape[1]
+    wait_all(fill(pieces, weight, sems, me, pl.ds(2 * cols, cols)))
     d_gated = dot_nn(grad_out[...], weight[...])
     pack(keep_one, send_one, xn2, (d_gated * slope_gate[...]).astype(BF16), Y_BIT, X_BIT, me)
     pack(keep_two, send_two, xn2, (d_gated * active[...]).astype(BF16), X_BIT, Y_BIT, me)
@@ -442,7 +446,7 @@
     keep, send, d_hidden, d_attention, gain_grad, lift_weight, weight, sems, sems_three = refs[2 * PIECES :]
     me = place[0]
     width = hidden.shape[1]
-    copies = fill(first, lift_weight, sems, me)
+    copies = fill(first, lift_weight, sems, me, pl.ds(0, lift_weight.shape[1]))
     lasts = fill(third, weight, sems_three, me, pl.ds(3 * width, width))
     normed, scaled = norm_parts(hidden[...])
     wait_all(copies)
@@ -460,7 +464,7 @@
 
 
 def attend_back_kernel(
-    place, queries, keys_values, edge, bias, totals, d_attention, cosine, sine, xn1, keep, send, d_keys_values, d_edge, d_turned
+    place, queries, keys_values, edge, bias, totals, d_attention, cosine, sine, d_turned, d_keys_values, d_edge
 ):
     width = queries.shape[1]
     pair = 2 * HEAD_DIM
@@ -497,7 +501,6 @@
         d_keys_values[:, there] = d_val[:rows]
         d_edge[:, here] = d_key[rows:].astype(BF16)
         d_edge[:, there] = d_val[rows:].astype(BF16)
-    pack(keep, send, xn1, d_turned[...], X_BIT, Y_BIT, place[0])
 
 
 def keys_back_kernel(
@@ -517,34 +520,51 @@
     pack(keep_two, send_two, xn1, summed[:, width:].astype(BF16), X_BIT, Y_BIT, me)
 
 
-def tokens_back_kernel(place, pack_q, pack_k, pack_v, tokens, d_hidden, gains, *refs):
-    pieces, (input_grad, gain_grad, weight, sems) = (refs[:PIECES], refs[PIECES:])
+def tokens_back_kernel(place, d_queries, pack_k, pack_v, tokens, xn1, d_hidden, gains, mlp_term, *refs):
+    pieces, (keep, send, input_grad, weight, sems) = (refs[:PIECES], refs[PIECES:])
+    rows = tokens.shape[0]
     width = tokens.shape[1]
     copies = fill(pieces, weight, sems, place[0], pl.ds(0, 3 * width))
     normed, scaled = norm_parts(tokens[...].astype(F32))
     wait_all(copies)
-    d_xn1 = dot_nt(pack_q[:, width // 2 :], weight[:, :width])
+    d_xn1 = dot_nt(d_queries[...], weight[:, :width])
     d_xn1 = d_xn1 + dot_nt(pack_k[:, width // 2 :], weight[:, width : 2 * width])
     d_xn1 = d_xn1 + dot_nt(pack_v[:, width // 2 :], weight[:, 2 * width :])
     d_norm, gain_term = norm_back(d_xn1, normed, scaled, gains[0:1, :])
-    gain_grad[...] = gain_term
+    pack(keep, send, xn1, d_queries[...], X_BIT, Y_BIT, place[0])
+    extra = keep.shape[0] - rows
+    line = lax.broadcasted_iota(jnp.int32, (extra, width), 0)
+    terms = jnp.where(line == 0, mlp_term[...], jnp.where(line == 1, gain_term, 0.0)).astype(BF16)
+    for target in (keep, send):
+        target[rows:, : width // 2] = jnp.zeros((extra, width // 2), BF16)
+        target[rows:, width // 2 :] = terms
     input_grad[...] = (d_hidden[...] + d_norm).astype(BF16)
 
 
-def product_kernel(width, mine, over_link, core_mine, core_link, own, sent, joined, sems):
-    rows = mine.shape[0]
+def product_kernel(width, rows, mine, over_link, core_mine, core_link, own, sent, joined, *refs):
+    terms, sems = (refs[0] if len(refs) > 1 else None, refs[-1])
     copies = []
     for index, part in enumerate((mine, over_link, core_mine, core_link)):
-        copies.append(pltpu.make_async_copy(part, joined.at[pl.ds(index * rows, rows)], sems.at[index]))
+        source = part if terms is None else part.at[pl.ds(0, rows)]
+        copies.append(pltpu.make_async_copy(source, joined.at[pl.ds(index * rows, rows)], sems.at[index]))
+        if terms is not None:
+            extra = terms.shape[1]
+            copies.append(
+                pltpu.make_async_copy(part.at[pl.ds(rows, extra)], terms.at[index], sems.at[4 + index])
+            )
     for copy in copies:
         copy.start()
     wait_all(copies)
     block = lambda top, k: joined[2 * rows * top : 2 * rows * (top + 1), k * width : (k + 1) * width]
     right = joined[:, 4 * width :]
     left = jnp.concatenate([block(0, 2), block(1, 3)], axis=0)
-    sent[...] = dot_tt(left, right).astype(BF16)
+    sent[:width] = dot_tt(left, right).astype(BF16)
     left = jnp.concatenate([block(0, 0), block(1, 1)], axis=0)
-    own[...] = dot_tt(left, right)
+    own[:width] = dot_tt(left, right)
+    if terms is not None:
+        total = sum(terms[index, :, 4 * width :].astype(F32) for index in range(4))
+        own[width:] = total
+        sent[width:] = total.astype(BF16)
 
 
 def call(kernel, outs, operands, scratch=(), smem=1, anywhere=(), flops=0, size=0):
@@ -567,16 +587,22 @@
     )(*operands)
 
 
-def grad_rows(keep, send, gather_bit, sum_bit, width):
-    rows, cols = (keep.shape[0], keep.shape[1] - 4 * width)
+def grad_rows(keep, send, gather_bit, sum_bit, width, after=()):
+    rows = keep.shape[0] // 128 * 128
+    extra = keep.shape[0] - rows
+    cols = keep.shape[1] - 4 * width
     over_link = swap(send, gather_bit)
+    keep, over_link = later((keep, over_link), after)
     core_mine = swap(keep, CORE_BIT)
     core_link = swap(over_link, CORE_BIT)
+    scratch = [pltpu.VMEM((4 * rows, 4 * width + cols), BF16)]
+    if extra:
+        scratch.append(pltpu.VMEM((4, extra, 4 * width + cols), BF16))
     own, sent = call(
-        lambda *refs: product_kernel(width, *refs),
-        [((width, cols), F32), ((width, cols), BF16)],
+        lambda *refs: product_kernel(width, rows, *refs),
+        [((width + extra, cols), F32), ((width + extra, cols), BF16)],
         [keep, over_link, core_mine, core_link],
-        [pltpu.VMEM((4 * rows, 4 * width + cols), BF16), pltpu.SemaphoreType.DMA((4,))],
+        scratch + [pltpu.SemaphoreType.DMA((8,))],
         smem=0,
         anywhere=(0, 1, 2, 3),
         flops=16 * rows * width * cols,
@@ -596,12 +622,16 @@
     return jnp.where(middle, total, back).astype(F32)
 
 
-def sum_everywhere(values):
-    for bit in (CORE_BIT, X_BIT, Y_BIT):
-        values = values + swap(values, bit)
-    for bit in (1, 2):
-        values = values + lax.ppermute(values, "replica", [(i, i ^ bit) for i in range(4)])
-    return values
+def cross_sum(part):
+    half = part.shape[1] // 2
+    even = lax.axis_index("replica") % 2 == 0
+    step = lambda value, bit: lax.ppermute(value, "replica", [(i, i ^ bit) for i in range(4)])
+    low, high = (part[:, :half], part[:, half:])
+    got = step(jnp.where(even, high, low).astype(BF16), 1)
+    pair = (jnp.where(even, low, high) + got.astype(F32)).astype(BF16)
+    total = (pair.astype(F32) + step(pair, 2).astype(F32)).astype(BF16)
+    back = step(total, 1)
+    return jnp.concatenate([jnp.where(even, total, back), jnp.where(even, back, total)], axis=1).astype(F32)
 
 
 def body_plane(
@@ -629,12 +659,16 @@
     gains = jnp.pad(gains, ((0, 0), (0, 126)))
     front = jnp.concatenate([qkv_weight, output_weight, gains], axis=1)
     widened = lambda values: jnp.pad(values, ((0, 0), (0, fill_cols)))
-    lift = jnp.concatenate(
-        [widened(expand_weight[:, :true_width]), widened(expand_weight[:, true_width:])], axis=1
+    feed = jnp.concatenate(
+        [
+            widened(expand_weight[:, :true_width]),
+            widened(expand_weight[:, true_width:]),
+            widened(contract_weight),
+        ],
+        axis=1,
     )
     packed, arrived = gather_pieces(front)
-    lift_pieces, arrived = gather_pieces(lift, arrived)
-    contract_pieces, arrived = gather_pieces(widened(contract_weight), arrived)
+    feed_pieces, arrived = gather_pieces(feed, arrived)
     cosine, sine = rope_tables(positions[0], HEAD_DIM)
     cosine = jnp.concatenate([cosine[:, 0]] * 4, axis=1)
     sine = jnp.concatenate([-sine[:, 0], sine[:, 0]] * 2, axis=1)
@@ -667,45 +701,41 @@
     keep_c, send_c, slope_gate, active = call(
         lift_kernel,
         [((rows, half + ff_width), BF16)] * 2 + [((rows, ff_width), F32)] * 2,
-        [place, xn2, grad_out] + lift_pieces,
+        [place, xn2, grad_out] + feed_pieces,
         [pltpu.VMEM((width, 2 * ff_width), BF16), sems],
         anywhere=range(3, 3 + PIECES),
         flops=4 * rows * width * ff_width,
         size=4 * width * ff_width,
     )
-    contract_part, contract_sent = grad_rows(keep_c, send_c, X_BIT, Y_BIT, shard)
     layer_out, keep_g, send_g, keep_u, send_u = call(
         contract_kernel,
         [((rows, width), BF16)] + [((rows, half + ff_width), BF16)] * 4,
-        [place, keep_c, grad_out, xn2, hidden, slope_gate, active] + contract_pieces,
+        [place, keep_c, grad_out, xn2, hidden, slope_gate, active] + feed_pieces,
         [pltpu.VMEM((width, ff_width), BF16), sems],
         anywhere=range(7, 7 + PIECES),
         flops=4 * rows * width * ff_width,
         size=2 * width * ff_width,
     )
-    gelu_part, gelu_sent = grad_rows(keep_g, send_g, Y_BIT, X_BIT, shard)
-    gate_part, gate_sent = grad_rows(keep_u, send_u, X_BIT, Y_BIT, shard)
     keep_o, send_o, d_hidden, d_attention, mlp_term = call(
         hidden_back_kernel,
         [((rows, half + width), BF16)] * 2 + [((rows, width), F32), ((rows, width), BF16), ((1, width), F32)],
-        [place, keep_g, keep_u, grad_out, hidden, full_gains, attention] + lift_pieces + packed,
+        [place, keep_g, keep_u, grad_out, hidden, full_gains, attention] + feed_pieces + packed,
         [pltpu.VMEM((width, 2 * ff_width), BF16), pltpu.VMEM((width, width), BF16), sems, sems],
         anywhere=range(7, 7 + 2 * PIECES),
         flops=6 * rows * width * ff_width,
         size=6 * width * ff_width,
     )
-    output_part, output_sent = grad_rows(keep_o, send_o, Y_BIT, X_BIT, shard)
-    d_attention, _ = lax.optimization_barrier((d_attention, contract_sent))
-    keep_q, send_q, d_keys_values, d_edge = call(
+    contract_part, contract_sent = grad_rows(keep_c, send_c, X_BIT, Y_BIT, shard, d_attention)
+    d_attention = later(d_attention, contract_sent)
+    d_queries, d_keys_values, d_edge = call(
         attend_back_kernel,
-        [((rows, half + width), BF16)] * 2 + [((rows, 2 * width), F32), ((HALF, 2 * width), BF16)],
-        [place, queries, keys_values, edge, bias, totals, d_attention, cosine, sine, xn1],
-        [pltpu.VMEM((rows, width), BF16)],
+        [((rows, width), BF16), ((rows, 2 * width), F32), ((HALF, 2 * width), BF16)],
+        [place, queries, keys_values, edge, bias, totals, d_attention, cosine, sine],
         flops=20 * rows * width * width,
         size=4 * width * width,
     )
-    d_keys_values, _ = lax.optimization_barrier((d_keys_values, (gelu_sent, gate_sent)))
-    query_part, query_sent = grad_rows(keep_q, send_q, X_BIT, Y_BIT, shard)
+    gelu_part, gelu_sent = grad_rows(keep_g, send_g, Y_BIT, X_BIT, shard, d_edge)
+    gate_part, gate_sent = grad_rows(keep_u, send_u, X_BIT, Y_BIT, shard, d_edge)
     keep_k, send_k, keep_v, send_v = call(
         keys_back_kernel,
         [((rows, half + width), BF16)] * 4,
@@ -716,30 +746,32 @@
     )
     key_part, _ = grad_rows(keep_k, send_k, Y_BIT, X_BIT, shard)
     value_part, _ = grad_rows(keep_v, send_v, X_BIT, Y_BIT, shard)
-    d_hidden, _ = lax.optimization_barrier((d_hidden, (contract_part, output_sent)))
-    input_grad, input_term = call(
+    d_hidden = later(d_hidden, contract_part, gelu_sent, gate_sent)
+    keep_q, send_q, input_grad = call(
         tokens_back_kernel,
-        [((rows, width), BF16), ((1, width), F32)],
-        [place, keep_q, keep_k, keep_v, source, d_hidden, full_gains] + packed,
+        [((rows + 16, half + width), BF16)] * 2 + [((rows, width), BF16)],
+        [place, d_queries, keep_k, keep_v, source, xn1, d_hidden, full_gains, mlp_term] + packed,
         [pltpu.VMEM((width, 3 * width), BF16), sems],
-        anywhere=range(7, 7 + PIECES),
+        anywhere=range(9, 9 + PIECES),
         flops=6 * rows * width * width,
         size=6 * width * width,
     )
-    gain_sums = sum_everywhere(jnp.concatenate([input_term, mlp_term], axis=0))
-    gain_rows = lax.dynamic_slice_in_dim(gain_sums, me * shard, shard, axis=1)
+    output_part, _ = grad_rows(keep_o, send_o, Y_BIT, X_BIT, shard, keep_k)
+    query_part, _ = grad_rows(keep_q, send_q, X_BIT, Y_BIT, shard)
     contract_grad = line_sum(contract_part)
     gelu_grad = line_sum(gelu_part)
     gate_grad = line_sum(gate_part)
-    early_grad = line_sum(jnp.concatenate([output_part, query_part], axis=1))
-    late_grad = line_sum(jnp.concatenate([key_part, value_part], axis=1))
+    late_grad = cross_sum(jnp.concatenate([key_part, value_part], axis=1))
+    early_grad = line_sum(jnp.concatenate([output_part, query_part], axis=0))
+    query_grad = early_grad[shard : 2 * shard]
+    gain_rows = lax.dynamic_slice_in_dim(early_grad[2 * shard : 2 * shard + 2], me * shard, shard, axis=1)
     return (
         layer_out[None],
         input_grad[None],
+        gain_rows[1],
+        jnp.concatenate([query_grad, late_grad], axis=1),
+        early_grad[:shard],
         gain_rows[0],
-        jnp.concatenate([early_grad[:, width:], late_grad], axis=1),
-        early_grad[:, :width],
-        gain_rows[1],
         jnp.concatenate([gelu_grad[:, :true_width], gate_grad[:, :true_width]], axis=1),
         contract_grad[:, :true_width],
     )

time: 451 us -> 381 us (0.84)
  waiting for transfers between devices: 268 us -> 210 us
  local copies, waits for them, and re-layouts: 30.1 us -> 18.9 us
    ppermute x5 -> x4, waiting for transfers between devices: 45.8 us -> 4.25 us  [line_sum(): first = lax.ppermute(part.astype(BF16), 'replica', [(0, 1), (3, 2)])]
    ppermute x2 -> x3, waiting for transfers between devices: 0.42 us -> 27.6 us  [cross_sum(): lax.ppermute(value, 'replica', [(i, i ^ bit) for i in range(4)])]
    ppermute x60 -> x48, waiting for transfers between devices: 162 us -> 138 us  [swap(): return lax.ppermute(value, PLANE, [(i, i ^ bit) for i in range(PLANE_SIZE)])]
    ppermute x5 -> x4, waiting for transfers between devices: 59.9 us -> 39.7 us  [line_sum(): back = lax.ppermute(total, 'replica', [(1, 0), (2, 3)])]
    ppermute x60 -> x48, starting transfers between devices: 40.3 us -> 31.7 us  [swap(): return lax.ppermute(value, PLANE, [(i, i ^ bit) for i in range(PLANE_SIZE)])]
    ppermute x5 -> x4, starting transfers between devices: 8.13 us -> 16.7 us  [line_sum(): first = lax.ppermute(part.astype(BF16), 'replica', [(0, 1), (3, 2)])]
    unnamed x122 -> x92, local copies, waits for them, and re-layouts: 20.5 us -> 12.3 us
  transfers between devices with their start and end apart: 77 -> 63, of which waited for: 26 -> 26; matrix products, arithmetic and copies ran while one was open for 6% -> 7% of each run, Pallas kernels for 14% -> 16%
where the time goes in v4:
time: 381 us; the launch traced here: 380 us
  waiting for transfers between devices  210 us (55%)
  Pallas kernels  67.7 us (18%)
  starting transfers between devices  59.9 us (16%)
  other arithmetic  22.4 us (6%)
  local copies, waits for them, and re-layouts  18.9 us (5%)
    ppermute x48, waiting for transfers between devices, swap(): return lax.ppermute(value, PLANE, [(i, i ^ bit) for i in range(PLANE_SIZE)])  138 us
    pallas_call x15, Pallas kernels, call(): pl.pallas_call(kernel, out_shape=[jax.ShapeDtypeStruct(shape, kind) for s...  67.7 us
    ppermute x4, waiting for transfers between devices, line_sum(): back = lax.ppermute(total, 'replica', [(1, 0), (2, 3)])  39.7 us
    ppermute x48, starting transfers between devices, swap(): return lax.ppermute(value, PLANE, [(i, i ^ bit) for i in range(PLANE_SIZE)])  31.7 us
    ppermute x3, waiting for transfers between devices, cross_sum(): lax.ppermute(value, 'replica', [(i, i ^ bit) for i in range(4)])  27.6 us
    ppermute x4, starting transfers between devices, line_sum(): first = lax.ppermute(part.astype(BF16), 'replica', [(0, 1), (3, 2)])  16.7 us
    unnamed x92, local copies, waits for them, and re-layouts  12.3 us
  transfers between devices with their start and end apart: 63, of which 26 were waited for; matrix products, arithmetic and copies ran while one was open for 7% of the time, Pallas kernels for 16%

profile of v4, /device:TPU:0, one launch (start us, length us, event | category | flops | bytes accessed | tf_op | source)
XLA Modules:
  0.0 380.4 jit_solution(4622380507946231507)
XLA Ops:
  2.9 3.0 collective-permute-start
  10.0 19.9 %collective-permute-done.refs_1_.refs_11_ = bf16[128,4224]{1,0:T(8,128)(2,1)} collective-permute-done((bf16[128,4224]{1,0:T(8,128)(2,1)S(1)}, bf16[128,4224]{1,0:T(8,128)(2,1)}, u32[]{:S(2)}, u32[]{:S(2)}) %collective-permute-start) | collective-permute-done | bytes 1081376 | tf_op jit(solution)/shard_map/ppermute | solution.py:265
  36.9 7.6 %collective-permute-done.2.refs_3_.refs_13_ = bf16[64,4224]{1,0:T(8,128)(2,1)S(1)} collective-permute-done((bf16[64,4224]{1,0:T(8,128)(2,1)S(1)}, bf16[64,4224]{1,0:T(8,128)(2,1)S(1)}, u32[]{:S(2)}, u32[]{:S(2)}) %collective-permute-start.2) | collective-permute-done | bytes 540704 | tf_op jit(solution)/shard_map/ppermute | solution.py:265
  52.1 2.5 collective-permute-done.8.refs_9_.refs_19_
  55.8 4.6 %shard_map.161 = (bf16[128,1024]{1,0:T(8,128)(2,1)S(1)}, bf16[128,2048]{1,0:T(8,128)(2,1)S(1)}, bf16[64,2048]{1,0:T(8,128)(2,1)S(1)}, bf16[128,1024]{1,0:T(8,128)(2,1)S(1)}, f32[8,1024]{1,0:T(8,128)S(1)}) custom-call(s32[2]{0:T(128)S(1)} %pad_add_fusion.place, bf16[128,1024]{1,0:T(8,128)(2,1)S(1)} %bitcast.18, f32[128,128]{1,0:T(8,128)S(1)} %get-tuple-element.171.cosine, ...), custom_call_target="tpu_custom_call" | custom-call | flops 805306368 | bytes 8650752 | tf_op jit(solution)/shard_map/pallas_call | solution.py:579
  61.2 33.3 %collective-permute-done.10.refs_1_ = bf16[128,8064]{1,0:T(8,128)(2,1)} collective-permute-done((bf16[128,8064]{1,0:T(8,128)(2,1)}, bf16[128,8064]{1,0:T(8,128)(2,1)}, u32[]{:S(2)}, u32[]{:S(2)}) %collective-permute-start.10) | collective-permute-done | bytes 2064416 | tf_op jit(solution)/shard_map/ppermute | solution.py:265
  99.8 15.1 %collective-permute-done.12.refs_3_ = bf16[64,8064]{1,0:T(8,128)(2,1)S(1)} collective-permute-done((bf16[64,8064]{1,0:T(8,128)(2,1)S(1)}, bf16[64,8064]{1,0:T(8,128)(2,1)S(1)}, u32[]{:S(2)}, u32[]{:S(2)}) %collective-permute-start.12) | collective-permute-done | bytes 1032224 | tf_op jit(solution)/shard_map/ppermute | solution.py:265
  115.0 4.5 %collective-permute-done.13.refs_4_ = bf16[64,8064]{1,0:T(8,128)(2,1)} collective-permute-done((bf16[64,8064]{1,0:T(8,128)(2,1)S(1)}, bf16[64,8064]{1,0:T(8,128)(2,1)}, u32[]{:S(2)}, u32[]{:S(2)}) %collective-permute-start.13) | collective-permute-done | bytes 1032224 | tf_op jit(solution)/shard_map/ppermute | solution.py:265
  122.6 7.7 %shard_map.162 = (bf16[128,1024]{1,0:T(8,128)(2,1)S(1)}, f32[128,128]{1,0:T(8,128)S(1)}, f32[128,1024]{1,0:T(8,128)S(1)}, bf16[128,1024]{1,0:T(8,128)(2,1)S(1)}) custom-call(s32[2]{0:T(128)S(1)} %copy-done.33, bf16[128,1024]{1,0:T(8,128)(2,1)S(1)} %copy-done.27, bf16[128,2048]{1,0:T(8,128)(2,1)S(1)} %copy-done.16, bf16[64,2048]{1,0:T(8,128)(2,1)S(1)} %copy-done.30, ...), custom_call_target="tpu_custom_call" | custom-call | flops 1610612736 | bytes 4194304 | tf_op jit(solution)/shard_map/pallas_call | solution.py:579
  130.5 7.5 %shard_map.163 = (bf16[128,3200]{1,0:T(8,128)(2,1)S(1)}, bf16[128,3200]{1,0:T(8,128)(2,1)S(1)}, f32[128,2688]{1,0:T(8,128)}, f32[128,2688]{1,0:T(8,128)}) custom-call(s32[2]{0:T(128)S(1)} %copy-done.33, bf16[128,1024]{1,0:T(8,128)(2,1)S(1)} %get-tuple-element.76.xn2, bf16[128,1024]{1,0:T(8,128)(2,1)S(1)} %bitcast.15, bf16[128,8064]{1,0:T(8,128)(2,1)} %fusion.5.refs_0_, ...), custom_call_target="tpu_custom_call" | custom-call | flops 1409286144 | bytes 11010048 | tf_op jit(solution)/shard_map/pallas_call | solution.py:579
  140.4 8.3 %shard_map.164 = (bf16[128,1024]{1,0:T(8,128)(2,1)}, bf16[128,3200]{1,0:T(8,128)(2,1)S(1)}, bf16[128,3200]{1,0:T(8,128)(2,1)S(1)}, bf16[128,3200]{1,0:T(8,128)(2,1)S(1)}, bf16[128,3200]{1,0:T(8,128)(2,1)}) custom-call(s32[2]{0:T(128)S(1)} %copy-done.33, bf16[128,3200]{1,0:T(8,128)(2,1)} %copy-done.7, bf16[128,1024]{1,0:T(8,128)(2,1)S(1)} %bitcast.16, ...), custom_call_target="tpu_custom_call" | custom-call | flops 1409286144 | bytes 5505024 | tf_op jit(solution)/shard_map/pallas_call | solution.py:579
  150.5 10.8 %shard_map.165 = (bf16[128,1536]{1,0:T(8,128)(2,1)S(1)}, bf16[128,1536]{1,0:T(8,128)(2,1)S(1)}, f32[128,1024]{1,0:T(8,128)S(1)}, bf16[128,1024]{1,0:T(8,128)(2,1)S(1)}, f32[1,1024]{1,0:T(1,128)S(1)}) custom-call(s32[2]{0:T(128)S(1)} %copy-done.33, bf16[128,3200]{1,0:T(8,128)(2,1)} %copy-done.5, bf16[128,3200]{1,0:T(8,128)(2,1)} %copy-done.3, ...), custom_call_target="tpu_custom_call" | custom-call | flops 2113929216 | bytes 16515072 | tf_op jit(solution)/shard_map/pallas_call | solution.py:579
  164.9 2.5 shard_map.166
  167.4 6.3 %shard_map.167 = (bf16[128,1024]{1,0:T(8,128)(2,1)S(1)}, f32[128,2048]{1,0:T(8,128)S(1)}, bf16[64,2048]{1,0:T(8,128)(2,1)S(1)}) custom-call(s32[2]{0:T(128)S(1)} %copy-done.33, bf16[128,1024]{1,0:T(8,128)(2,1)S(1)} %copy-done.28, bf16[128,2048]{1,0:T(8,128)(2,1)S(1)} %copy-done.17, bf16[64,2048]{1,0:T(8,128)(2,1)S(1)} %copy-done.31, ...), custom_call_target="tpu_custom_call" | custom-call | flops 2684354560 | bytes 4194304 | tf_op jit(solution)/shard_map/pallas_call | solution.py:579
  175.9 12.3 %collective-permute-done.22.arrived = bf16[64,2048]{1,0:T(8,128)(2,1)S(1)} collective-permute-done((bf16[64,2048]{1,0:T(8,128)(2,1)S(1)}, bf16[64,2048]{1,0:T(8,128)(2,1)S(1)}, u32[]{:S(2)}, u32[]{:S(2)}) %collective-permute-start.22) | collective-permute-done | bytes 262176 | tf_op jit(solution)/shard_map/ppermute | solution.py:265
  192.1 7.4 %collective-permute-done.45.refs_1_ = bf16[128,1536]{1,0:T(8,128)(2,1)S(1)} collective-permute-done((bf16[128,1536]{1,0:T(8,128)(2,1)S(1)}, bf16[128,1536]{1,0:T(8,128)(2,1)S(1)}, u32[]{:S(2)}, u32[]{:S(2)}) %collective-permute-start.45) | collective-permute-done | bytes 393248 | tf_op jit(solution)/shard_map/ppermute | solution.py:265
  206.0 11.3 %collective-permute-done.23 = bf16[128,2688]{1,0:T(8,128)(2,1)S(1)} collective-permute-done((bf16[128,2688]{1,0:T(8,128)(2,1)S(1)}, bf16[128,2688]{1,0:T(8,128)(2,1)S(1)}, u32[]{:S(2)}, u32[]{:S(2)}) %collective-permute-start.23) | collective-permute-done | bytes 688160 | tf_op jit(solution)/shard_map/ppermute | solution.py:265
  218.4 2.8 fusion.12
  224.7 2.7 shard_map.170
  227.4 6.5 %shard_map.171 = (bf16[144,1536]{1,0:T(8,128)(2,1)S(1)}, bf16[144,1536]{1,0:T(8,128)(2,1)}, bf16[128,1024]{1,0:T(8,128)(2,1)}) custom-call(s32[2]{0:T(128)S(1)} %copy-done.33, bf16[128,1024]{1,0:T(8,128)(2,1)S(1)} %copy-done.25, bf16[128,1536]{1,0:T(8,128)(2,1)S(1)} %get-tuple-element.125.pack_k.refs_0_, ...), custom_call_target="tpu_custom_call" | custom-call | flops 805306368 | bytes 6291456 | tf_op jit(solution)/shard_map/pallas_call | solution.py:579
  235.0 4.5 %collective-permute-start.60 = (bf16[128,2688]{1,0:T(8,128)(2,1)}, bf16[128,2688]{1,0:T(8,128)(2,1)}, u32[]{:S(2)}, u32[]{:S(2)}) collective-permute-start(bf16[128,2688]{1,0:T(8,128)(2,1)} %get-tuple-element.160), channel_id=1, source_target_pairs={{0,8},{24,16},{1,9},{25,17},{2,10},{26,18},{3,11},{27,19},{4,12},{... | collective-permute-start | bytes 2064392 | tf_op jit(solution)/shard_map/ppermute | solution.py:615
  249.2 5.3 %collective-permute-done.44 = bf16[128,1024]{1,0:T(8,128)(2,1)} collective-permute-done((bf16[128,1024]{1,0:T(8,128)(2,1)}, bf16[128,1024]{1,0:T(8,128)(2,1)}, u32[]{:S(2)}, u32[]{:S(2)}) %collective-permute-start.44) | collective-permute-done | bytes 262176 | tf_op jit(solution)/shard_map/ppermute | solution.py:265
  257.1 10.0 %collective-permute-done.52 = bf16[128,2688]{1,0:T(8,128)(2,1)S(1)} collective-permute-done((bf16[128,2688]{1,0:T(8,128)(2,1)S(1)}, bf16[128,2688]{1,0:T(8,128)(2,1)S(1)}, u32[]{:S(2)}, u32[]{:S(2)}) %collective-permute-start.52) | collective-permute-done | bytes 688160 | tf_op jit(solution)/shard_map/ppermute | solution.py:265
  267.9 5.3 %collective-permute-start.53 = (bf16[128,2688]{1,0:T(8,128)(2,1)S(1)}, bf16[128,2688]{1,0:T(8,128)(2,1)S(1)}, u32[]{:S(2)}, u32[]{:S(2)}) collective-permute-start(bf16[128,2688]{1,0:T(8,128)(2,1)S(1)} %fusion.7), channel_id=1, source_target_pairs={{0,8},{24,16},{1,9},{25,17},{2,10},{26,18},{3,11},{27,19},{4,12},{... | collective-permute-start | bytes 2064392 | tf_op jit(solution)/shard_map/ppermute | solution.py:615
  277.9 3.8 %collective-permute-start.57 = (bf16[128,2688]{1,0:T(8,128)(2,1)S(1)}, bf16[128,2688]{1,0:T(8,128)(2,1)S(1)}, u32[]{:S(2)}, u32[]{:S(2)}) collective-permute-start(bf16[128,2688]{1,0:T(8,128)(2,1)S(1)} %fusion.8), channel_id=1, source_target_pairs={{0,8},{24,16},{1,9},{25,17},{2,10},{26,18},{3,11},{27,19},{4,12},{... | collective-permute-start | bytes 2064392 | tf_op jit(solution)/shard_map/ppermute | solution.py:615
  281.7 14.4 %collective-permute-done.50 = bf16[128,1024]{1,0:T(8,128)(2,1)S(1)} collective-permute-done((bf16[128,1024]{1,0:T(8,128)(2,1)S(1)}, bf16[128,1024]{1,0:T(8,128)(2,1)S(1)}, u32[]{:S(2)}, u32[]{:S(2)}) %collective-permute-start.50) | collective-permute-done | bytes 262176 | tf_op jit(solution)/shard_map/ppermute | solution.py:628
  297.4 3.0 collective-permute-start.38
  301.9 13.2 %collective-permute-done.51 = bf16[128,1024]{1,0:T(8,128)(2,1)S(1)} collective-permute-done((bf16[128,1024]{1,0:T(8,128)(2,1)S(1)}, bf16[128,1024]{1,0:T(8,128)(2,1)S(1)}, u32[]{:S(2)}, u32[]{:S(2)}) %collective-permute-start.51) | collective-permute-done | bytes 262176 | tf_op jit(solution)/shard_map/ppermute | solution.py:628
  320.4 4.2 %collective-permute-done.38 = bf16[272,1024]{1,0:T(8,128)(2,1)S(1)} collective-permute-done((bf16[272,1024]{1,0:T(8,128)(2,1)S(1)}, bf16[272,1024]{1,0:T(8,128)(2,1)S(1)}, u32[]{:S(2)}, u32[]{:S(2)}) %collective-permute-start.38) | collective-permute-done | bytes 557088 | tf_op jit(solution)/shard_map/ppermute | solution.py:615
  336.0 19.6 %collective-permute-done.55 = bf16[128,2688]{1,0:T(8,128)(2,1)S(1)} collective-permute-done((bf16[128,2688]{1,0:T(8,128)(2,1)S(1)}, bf16[128,2688]{1,0:T(8,128)(2,1)S(1)}, u32[]{:S(2)}, u32[]{:S(2)}) %collective-permute-start.55) | collective-permute-done | bytes 688160 | tf_op jit(solution)/shard_map/ppermute | solution.py:619
  355.7 16.0 %collective-permute-done.59 = bf16[128,2688]{1,0:T(8,128)(2,1)S(1)} collective-permute-done((bf16[128,2688]{1,0:T(8,128)(2,1)S(1)}, bf16[128,2688]{1,0:T(8,128)(2,1)S(1)}, u32[]{:S(2)}, u32[]{:S(2)}) %collective-permute-start.59) | collective-permute-done | bytes 688160 | tf_op jit(solution)/shard_map/ppermute | solution.py:619
  373.6 4.1 %collective-permute-done.40 = bf16[272,1024]{1,0:T(8,128)(2,1)S(1)} collective-permute-done((bf16[272,1024]{1,0:T(8,128)(2,1)S(1)}, bf16[272,1024]{1,0:T(8,128)(2,1)S(1)}, u32[]{:S(2)}, u32[]{:S(2)}) %collective-permute-start.40) | collective-permute-done | bytes 557088 | tf_op jit(solution)/shard_map/ppermute | solution.py:619
  (248 shorter events, 98.8 us)
Async XLA Ops:
  2.9 27.0 %collective-permute-start = (bf16[128,4224]{1,0:T(8,128)(2,1)S(1)}, bf16[128,4224]{1,0:T(8,128)(2,1)}, u32[]{:S(2)}, u32[]{:S(2)}) collective-permute-start(bf16[128,4224]{1,0:T(8,128)(2,1)S(1)} %fusion.6.refs_0_.refs_10_), channel_id=1, source_target_pairs={{0,1},{1,0},{2,3},{3,2},{4,5},{5,4},{6,7},{7,6},{8,9},{9,8},{10,11... | collective-permute-start | bytes 3244040 | tf_op jit(solution)/shard_map/ppermute | solution.py:265
  5.9 26.9 %collective-permute-start.1 = (bf16[128,4224]{1,0:T(8,128)(2,1)S(1)}, bf16[128,4224]{1,0:T(8,128)(2,1)}, u32[]{:S(2)}, u32[]{:S(2)}) collective-permute-start(bf16[128,4224]{1,0:T(8,128)(2,1)S(1)} %fusion.6.refs_0_.refs_10_), channel_id=1, source_target_pairs={{0,4},{1,5},{2,6},{3,7},{4,0},{5,1},{6,2},{7,3},{8,12},{9,13},{10,... | collective-permute-start | bytes 3244040 | tf_op jit(solution)/shard_map/ppermute | solution.py:265
  7.4 41.9 %collective-permute-start.4 = (bf16[128,4224]{1,0:T(8,128)(2,1)S(1)}, bf16[128,4224]{1,0:T(8,128)(2,1)}, u32[]{:S(2)}, u32[]{:S(2)}) collective-permute-start(bf16[128,4224]{1,0:T(8,128)(2,1)S(1)} %fusion.6.refs_0_.refs_10_), channel_id=1, source_target_pairs={{0,2},{1,3},{2,0},{3,1},{4,6},{5,7},{6,4},{7,5},{8,10},{9,11},{10,... | collective-permute-start | bytes 3244040 | tf_op jit(solution)/shard_map/ppermute | solution.py:265
  46.8 47.7 %collective-permute-start.10 = (bf16[128,8064]{1,0:T(8,128)(2,1)}, bf16[128,8064]{1,0:T(8,128)(2,1)}, u32[]{:S(2)}, u32[]{:S(2)}) collective-permute-start(bf16[128,8064]{1,0:T(8,128)(2,1)} %fusion.5.refs_0_), channel_id=1, source_target_pairs={{0,1},{1,0},{2,3},{3,2},{4,5},{5,4},{6,7},{7,6},{8,9},{9,8},{10,11... | collective-permute-start | bytes 6193160 | tf_op jit(solution)/shard_map/ppermute | solution.py:265
  48.3 48.5 %collective-permute-start.11 = (bf16[128,8064]{1,0:T(8,128)(2,1)}, bf16[128,8064]{1,0:T(8,128)(2,1)}, u32[]{:S(2)}, u32[]{:S(2)}) collective-permute-start(bf16[128,8064]{1,0:T(8,128)(2,1)} %fusion.5.refs_0_), channel_id=1, source_target_pairs={{0,4},{1,5},{2,6},{3,7},{4,0},{5,1},{6,2},{7,3},{8,12},{9,13},{10,... | collective-permute-start | bytes 6193160 | tf_op jit(solution)/shard_map/ppermute | solution.py:265
  60.5 39.0 %collective-permute-start.9 = (bf16[64,2048]{1,0:T(8,128)(2,1)S(1)}, bf16[64,2048]{1,0:T(8,128)(2,1)S(1)}, u32[]{:S(2)}, u32[]{:S(2)}) collective-permute-start(bf16[64,2048]{1,0:T(8,128)(2,1)S(1)} %get-tuple-element.74), channel_id=1, source_target_pairs={{0,1},{1,0},{2,3},{3,2},{4,5},{5,4},{6,7},{7,6},{8,9},{9,8},{10,11... | collective-permute-start | bytes 786440 | tf_op jit(solution)/shard_map/ppermute | solution.py:265
  61.2 69.2 %collective-permute-start.14 = (bf16[128,8064]{1,0:T(8,128)(2,1)}, bf16[128,8064]{1,0:T(8,128)(2,1)}, u32[]{:S(2)}, u32[]{:S(2)}) collective-permute-start(bf16[128,8064]{1,0:T(8,128)(2,1)} %fusion.5.refs_0_), channel_id=1, source_target_pairs={{0,2},{1,3},{2,0},{3,1},{4,6},{5,7},{6,4},{7,5},{8,10},{9,11},{10,... | collective-permute-start | bytes 6193160 | tf_op jit(solution)/shard_map/ppermute | solution.py:265
  98.1 21.3 %collective-permute-start.13 = (bf16[64,8064]{1,0:T(8,128)(2,1)S(1)}, bf16[64,8064]{1,0:T(8,128)(2,1)}, u32[]{:S(2)}, u32[]{:S(2)}) collective-permute-start(bf16[64,8064]{1,0:T(8,128)(2,1)S(1)} %slice.81), channel_id=1, source_target_pairs={{0,1},{1,0},{2,3},{3,2},{4,5},{5,4},{6,7},{7,6},{8,9},{9,8},{10,11... | collective-permute-start | bytes 3096584 | tf_op jit(solution)/shard_map/ppermute | solution.py:265
  99.3 31.1 %collective-permute-start.15 = (bf16[128,8064]{1,0:T(8,128)(2,1)}, bf16[128,8064]{1,0:T(8,128)(2,1)}, u32[]{:S(2)}, u32[]{:S(2)}) collective-permute-start(bf16[128,8064]{1,0:T(8,128)(2,1)} %collective-permute-done.10.refs_1_), channel_id=1, source_target_pairs={{0,2},{1,3},{2,0},{3,1},{4,6},{5,7},{6,4},{7,5},{8,10},{9,11},{10,... | collective-permute-start | bytes 6193160 | tf_op jit(solution)/shard_map/ppermute | solution.py:265
  99.5 30.9 %collective-permute-start.16 = (bf16[128,8064]{1,0:T(8,128)(2,1)}, bf16[128,8064]{1,0:T(8,128)(2,1)}, u32[]{:S(2)}, u32[]{:S(2)}) collective-permute-start(bf16[128,8064]{1,0:T(8,128)(2,1)} %collective-permute-done.11.refs_2_), channel_id=1, source_target_pairs={{0,2},{1,3},{2,0},{3,1},{4,6},{5,7},{6,4},{7,5},{8,10},{9,11},{10,... | collective-permute-start | bytes 6193160 | tf_op jit(solution)/shard_map/ppermute | solution.py:265
  138.9 22.5 %collective-permute-start.19 = (bf16[128,3200]{1,0:T(8,128)(2,1)S(1)}, bf16[128,3200]{1,0:T(8,128)(2,1)S(1)}, u32[]{:S(2)}, u32[]{:S(2)}) collective-permute-start(bf16[128,3200]{1,0:T(8,128)(2,1)S(1)} %get-tuple-element.88), channel_id=1, source_target_pairs={{0,1},{1,0},{2,3},{3,2},{4,5},{5,4},{6,7},{7,6},{8,9},{9,8},{10,11... | collective-permute-start | bytes 2457608 | tf_op jit(solution)/shard_map/ppermute | solution.py:265
  161.9 29.5 %collective-permute-start.24 = (bf16[128,3200]{1,0:T(8,128)(2,1)S(1)}, bf16[128,3200]{1,0:T(8,128)(2,1)S(1)}, u32[]{:S(2)}, u32[]{:S(2)}) collective-permute-start(bf16[128,3200]{1,0:T(8,128)(2,1)S(1)} %get-tuple-element.101), channel_id=1, source_target_pairs={{0,4},{1,5},{2,6},{3,7},{4,0},{5,1},{6,2},{7,3},{8,12},{9,13},{10,... | collective-permute-start | bytes 2457608 | tf_op jit(solution)/shard_map/ppermute | solution.py:265
  162.5 29.0 %collective-permute-start.27 = (bf16[128,3200]{1,0:T(8,128)(2,1)S(1)}, bf16[128,3200]{1,0:T(8,128)(2,1)S(1)}, u32[]{:S(2)}, u32[]{:S(2)}) collective-permute-start(bf16[128,3200]{1,0:T(8,128)(2,1)S(1)} %copy-done.43), channel_id=1, source_target_pairs={{0,1},{1,0},{2,3},{3,2},{4,5},{5,4},{6,7},{7,6},{8,9},{9,8},{10,11... | collective-permute-start | bytes 2457608 | tf_op jit(solution)/shard_map/ppermute | solution.py:265
  191.5 25.9 %collective-permute-start.25 = (bf16[128,3200]{1,0:T(8,128)(2,1)S(1)}, bf16[128,3200]{1,0:T(8,128)(2,1)S(1)}, u32[]{:S(2)}, u32[]{:S(2)}) collective-permute-start(bf16[128,3200]{1,0:T(8,128)(2,1)S(1)} %copy-done.6), channel_id=1, source_target_pairs={{0,2},{1,3},{2,0},{3,1},{4,6},{5,7},{6,4},{7,5},{8,10},{9,11},{10,... | collective-permute-start | bytes 2457608 | tf_op jit(solution)/shard_map/ppermute | solution.py:265
  191.5 26.4 %collective-permute-start.26 = (bf16[128,3200]{1,0:T(8,128)(2,1)S(1)}, bf16[128,3200]{1,0:T(8,128)(2,1)S(1)}, u32[]{:S(2)}, u32[]{:S(2)}) collective-permute-start(bf16[128,3200]{1,0:T(8,128)(2,1)S(1)} %collective-permute-done.24.refs_1_), channel_id=1, source_target_pairs={{0,2},{1,3},{2,0},{3,1},{4,6},{5,7},{6,4},{7,5},{8,10},{9,11},{10,... | collective-permute-start | bytes 2457608 | tf_op jit(solution)/shard_map/ppermute | solution.py:265
  192.0 25.9 %collective-permute-start.28 = (bf16[128,3200]{1,0:T(8,128)(2,1)S(1)}, bf16[128,3200]{1,0:T(8,128)(2,1)S(1)}, u32[]{:S(2)}, u32[]{:S(2)}) collective-permute-start(bf16[128,3200]{1,0:T(8,128)(2,1)S(1)} %copy-done.4), channel_id=1, source_target_pairs={{0,2},{1,3},{2,0},{3,1},{4,6},{5,7},{6,4},{7,5},{8,10},{9,11},{10,... | collective-permute-start | bytes 2457608 | tf_op jit(solution)/shard_map/ppermute | solution.py:265
  217.8 23.6 %collective-permute-start.42 = (bf16[128,1536]{1,0:T(8,128)(2,1)S(1)}, bf16[128,1536]{1,0:T(8,128)(2,1)S(1)}, u32[]{:S(2)}, u32[]{:S(2)}) collective-permute-start(bf16[128,1536]{1,0:T(8,128)(2,1)S(1)} %get-tuple-element.125.pack_k.refs_0_), channel_id=1, source_target_pairs={{0,2},{1,3},{2,0},{3,1},{4,6},{5,7},{6,4},{7,5},{8,10},{9,11},{10,... | collective-permute-start | bytes 1179656 | tf_op jit(solution)/shard_map/ppermute | solution.py:265
  217.9 25.1 %collective-permute-start.43 = (bf16[128,1536]{1,0:T(8,128)(2,1)S(1)}, bf16[128,1536]{1,0:T(8,128)(2,1)S(1)}, u32[]{:S(2)}, u32[]{:S(2)}) collective-permute-start(bf16[128,1536]{1,0:T(8,128)(2,1)S(1)} %collective-permute-done.41.refs_1_), channel_id=1, source_target_pairs={{0,2},{1,3},{2,0},{3,1},{4,6},{5,7},{6,4},{7,5},{8,10},{9,11},{10,... | collective-permute-start | bytes 1179656 | tf_op jit(solution)/shard_map/ppermute | solution.py:265
  223.6 21.8 %collective-permute-start.33 = (bf16[128,1024]{1,0:T(8,128)(2,1)}, bf16[128,1024]{1,0:T(8,128)(2,1)}, u32[]{:S(2)}, u32[]{:S(2)}) collective-permute-start(bf16[128,1024]{1,0:T(8,128)(2,1)} %get-tuple-element.117), channel_id=1, source_target_pairs={{0,1},{1,0},{2,3},{3,2},{4,5},{5,4},{6,7},{7,6},{8,9},{9,8},{10,11... | collective-permute-start | bytes 786440 | tf_op jit(solution)/shard_map/ppermute | solution.py:265
  245.5 21.6 %collective-permute-start.52 = (bf16[128,2688]{1,0:T(8,128)(2,1)S(1)}, bf16[128,2688]{1,0:T(8,128)(2,1)S(1)}, u32[]{:S(2)}, u32[]{:S(2)}) collective-permute-start(bf16[128,2688]{1,0:T(8,128)(2,1)S(1)} %get-tuple-element.104), channel_id=1, source_target_pairs={{0,1},{1,0},{2,3},{3,2},{4,5},{5,4},{6,7},{7,6},{8,9},{9,8},{10,11... | collective-permute-start | bytes 2064392 | tf_op jit(solution)/shard_map/ppermute | solution.py:265
  248.1 29.7 %collective-permute-start.56 = (bf16[128,2688]{1,0:T(8,128)(2,1)S(1)}, bf16[128,2688]{1,0:T(8,128)(2,1)S(1)}, u32[]{:S(2)}, u32[]{:S(2)}) collective-permute-start(bf16[128,2688]{1,0:T(8,128)(2,1)S(1)} %get-tuple-element.108), channel_id=1, source_target_pairs={{0,4},{1,5},{2,6},{3,7},{4,0},{5,1},{6,2},{7,3},{8,12},{9,13},{10,... | collective-permute-start | bytes 2064392 | tf_op jit(solution)/shard_map/ppermute | solution.py:265
  249.2 25.3 %collective-permute-start.35 = (bf16[144,1536]{1,0:T(8,128)(2,1)}, bf16[144,1536]{1,0:T(8,128)(2,1)S(1)}, u32[]{:S(2)}, u32[]{:S(2)}) collective-permute-start(bf16[144,1536]{1,0:T(8,128)(2,1)} %copy-done.20), channel_id=1, source_target_pairs={{0,2},{1,3},{2,0},{3,1},{4,6},{5,7},{6,4},{7,5},{8,10},{9,11},{10,... | collective-permute-start | bytes 1327112 | tf_op jit(solution)/shard_map/ppermute | solution.py:265
  267.1 33.3 %collective-permute-start.61 = (bf16[128,2688]{1,0:T(8,128)(2,1)S(1)}, bf16[128,2688]{1,0:T(8,128)(2,1)S(1)}, u32[]{:S(2)}, u32[]{:S(2)}) collective-permute-start(bf16[128,2688]{1,0:T(8,128)(2,1)S(1)} %add_convert_fusion.1), channel_id=1, source_target_pairs={{8,16},{16,8},{9,17},{17,9},{10,18},{18,10},{11,19},{19,11},{12,20... | collective-permute-start | bytes 2064392 | tf_op jit(solution)/shard_map/ppermute | solution.py:617
  267.9 47.3 %collective-permute-start.53 = (bf16[128,2688]{1,0:T(8,128)(2,1)S(1)}, bf16[128,2688]{1,0:T(8,128)(2,1)S(1)}, u32[]{:S(2)}, u32[]{:S(2)}) collective-permute-start(bf16[128,2688]{1,0:T(8,128)(2,1)S(1)} %fusion.7), channel_id=1, source_target_pairs={{0,8},{24,16},{1,9},{25,17},{2,10},{26,18},{3,11},{27,19},{4,12},{... | collective-permute-start | bytes 2064392 | tf_op jit(solution)/shard_map/ppermute | solution.py:615
  274.5 21.7 %collective-permute-start.50 = (bf16[128,1024]{1,0:T(8,128)(2,1)S(1)}, bf16[128,1024]{1,0:T(8,128)(2,1)S(1)}, u32[]{:S(2)}, u32[]{:S(2)}) collective-permute-start(bf16[128,1024]{1,0:T(8,128)(2,1)S(1)} %add_convert_fusion.9), channel_id=1, source_target_pairs={{0,16},{8,24},{16,0},{24,8},{1,17},{9,25},{17,1},{25,9},{2,18},{10... | collective-permute-start | bytes 786440 | tf_op jit(solution)/shard_map/ppermute | solution.py:628
  276.2 21.1 %collective-permute-start.37 = (bf16[144,1024]{1,0:T(8,128)(2,1)S(1)}, bf16[144,1024]{1,0:T(8,128)(2,1)S(1)}, u32[]{:S(2)}, u32[]{:S(2)}) collective-permute-start(bf16[144,1024]{1,0:T(8,128)(2,1)S(1)} %get-tuple-element.123), channel_id=1, source_target_pairs={{0,4},{1,5},{2,6},{3,7},{4,0},{5,1},{6,2},{7,3},{8,12},{9,13},{10,... | collective-permute-start | bytes 884744 | tf_op jit(solution)/shard_map/ppermute | solution.py:265
  277.9 39.9 %collective-permute-start.57 = (bf16[128,2688]{1,0:T(8,128)(2,1)S(1)}, bf16[128,2688]{1,0:T(8,128)(2,1)S(1)}, u32[]{:S(2)}, u32[]{:S(2)}) collective-permute-start(bf16[128,2688]{1,0:T(8,128)(2,1)S(1)} %fusion.8), channel_id=1, source_target_pairs={{0,8},{24,16},{1,9},{25,17},{2,10},{26,18},{3,11},{27,19},{4,12},{... | collective-permute-start | bytes 2064392 | tf_op jit(solution)/shard_map/ppermute | solution.py:615
  297.4 27.2 %collective-permute-start.38 = (bf16[272,1024]{1,0:T(8,128)(2,1)S(1)}, bf16[272,1024]{1,0:T(8,128)(2,1)S(1)}, u32[]{:S(2)}, u32[]{:S(2)}) collective-permute-start(bf16[272,1024]{1,0:T(8,128)(2,1)S(1)} %fusion.9), channel_id=1, source_target_pairs={{0,8},{24,16},{1,9},{25,17},{2,10},{26,18},{3,11},{27,19},{4,12},{... | collective-permute-start | bytes 1671176 | tf_op jit(solution)/shard_map/ppermute | solution.py:615
  300.6 25.6 %collective-permute-start.62 = (bf16[128,2688]{1,0:T(8,128)(2,1)S(1)}, bf16[128,2688]{1,0:T(8,128)(2,1)S(1)}, u32[]{:S(2)}, u32[]{:S(2)}) collective-permute-start(bf16[128,2688]{1,0:T(8,128)(2,1)S(1)} %add_convert_fusion), channel_id=1, source_target_pairs={{8,0},{16,24},{9,1},{17,25},{10,2},{18,26},{11,3},{19,27},{12,4},{... | collective-permute-start | bytes 2064392 | tf_op jit(solution)/shard_map/ppermute | solution.py:619
  329.3 26.3 %collective-permute-start.55 = (bf16[128,2688]{1,0:T(8,128)(2,1)S(1)}, bf16[128,2688]{1,0:T(8,128)(2,1)S(1)}, u32[]{:S(2)}, u32[]{:S(2)}) collective-permute-start(bf16[128,2688]{1,0:T(8,128)(2,1)S(1)} %add_convert_fusion.4), channel_id=1, source_target_pairs={{8,0},{16,24},{9,1},{17,25},{10,2},{18,26},{11,3},{19,27},{12,4},{... | collective-permute-start | bytes 2064392 | tf_op jit(solution)/shard_map/ppermute | solution.py:619
  332.1 39.6 %collective-permute-start.59 = (bf16[128,2688]{1,0:T(8,128)(2,1)S(1)}, bf16[128,2688]{1,0:T(8,128)(2,1)S(1)}, u32[]{:S(2)}, u32[]{:S(2)}) collective-permute-start(bf16[128,2688]{1,0:T(8,128)(2,1)S(1)} %add_convert_fusion.2), channel_id=1, source_target_pairs={{8,0},{16,24},{9,1},{17,25},{10,2},{18,26},{11,3},{19,27},{12,4},{... | collective-permute-start | bytes 2064392 | tf_op jit(solution)/shard_map/ppermute | solution.py:619
  334.7 43.0 %collective-permute-start.40 = (bf16[272,1024]{1,0:T(8,128)(2,1)S(1)}, bf16[272,1024]{1,0:T(8,128)(2,1)S(1)}, u32[]{:S(2)}, u32[]{:S(2)}) collective-permute-start(bf16[272,1024]{1,0:T(8,128)(2,1)S(1)} %add_convert_fusion.6), channel_id=1, source_target_pairs={{8,0},{16,24},{9,1},{17,25},{10,2},{18,26},{11,3},{19,27},{12,4},{... | collective-permute-start | bytes 1671176 | tf_op jit(solution)/shard_map/ppermute | solution.py:619
  (76 other events, 899.0 us)

commit v5 on v4

--- a/solution.py
+++ b/solution.py
@@ -269,14 +269,17 @@
     return lax.optimization_barrier((value, others))[0]
 
 
-def gather_pieces(own, after=()):
+def fetch_pieces(own, after=()):
     own = later(own, after)
     half = own.shape[0] // 2
     over_x = swap(own, X_BIT)
     over_y = swap(own, Y_BIT)
-    first = [own, over_x, over_y, swap(over_x[:half], Y_BIT), swap(over_y[half:], X_BIT)]
-    second = [swap(part, CORE_BIT) for part in first]
-    return (first + second, tuple(first[3:]))
+    return [own, over_x, over_y, swap(over_x[:half], Y_BIT), swap(over_y[half:], X_BIT)]
+
+
+def share_pieces(first, after=()):
+    corners = [swap(later(part, after), CORE_BIT) for part in first[3:]]
+    return first + [swap(part, CORE_BIT) for part in first[:3]] + corners
 
 
 def fill(pieces, target, sems, me, columns=None):
@@ -414,7 +417,8 @@
 
 
 def lift_kernel(place, xn2, grad_out, *refs):
-    pieces, (keep, send, slope_gate, active, weight, sems) = (refs[:PIECES], refs[PIECES:])
+    pieces, rest = (refs[:PIECES], refs[PIECES:])
+    keep_one, send_one, keep_two, send_two, slope_gate, active, weight, sems = rest
     me = place[0]
     cols = active.shape[1]
     wait_all(fill(pieces, weight, sems, me, pl.ds(0, 2 * cols)))
@@ -425,10 +429,13 @@
     activated = gelu_input * cdf_part
     active[...] = activated
     slope_gate[...] = gate_part * (cdf_part + gelu_input * density)
-    pack(keep, send, grad_out, (activated * gate_part).astype(BF16), X_BIT, Y_BIT, me)
-
-
-def contract_kernel(place, gated_pack, grad_out, xn2, hidden, slope_gate, active, *refs):
+    gated = (activated * gate_part).astype(BF16)
+    cut = keep_one.shape[1] - xn2.shape[1] // 2
+    pack(keep_one, send_one, grad_out, gated[:, :cut], X_BIT, Y_BIT, me)
+    pack(keep_two, send_two, grad_out, gated[:, cut:], Y_BIT, X_BIT, me)
+
+
+def contract_kernel(place, gated_one, gated_two, grad_out, xn2, hidden, slope_gate, active, *refs):
     pieces, rest = (refs[:PIECES], refs[PIECES:])
     layer_out, keep_one, send_one, keep_two, send_two, weight, sems = rest
     me = place[0]
@@ -437,13 +444,15 @@
     d_gated = dot_nn(grad_out[...], weight[...])
     pack(keep_one, send_one, xn2, (d_gated * slope_gate[...]).astype(BF16), Y_BIT, X_BIT, me)
     pack(keep_two, send_two, xn2, (d_gated * active[...]).astype(BF16), X_BIT, Y_BIT, me)
-    gated = gated_pack[:, xn2.shape[1] // 2 :]
-    layer_out[...] = (hidden[...] + dot_nt(gated, weight[...])).astype(BF16)
-
-
-def hidden_back_kernel(place, pack_one, pack_two, grad_out, hidden, gains, attention, *refs):
+    skip = xn2.shape[1] // 2
+    cut = gated_one.shape[1] - skip
+    down = dot_nt(gated_one[:, skip:], weight[:, :cut]) + dot_nt(gated_two[:, skip:], weight[:, cut:])
+    layer_out[...] = (hidden[...] + down).astype(BF16)
+
+
+def hidden_back_kernel(place, pack_one, pack_two, grad_out, hidden, gains, *refs):
     first, third = (refs[:PIECES], refs[PIECES : 2 * PIECES])
-    keep, send, d_hidden, d_attention, gain_grad, lift_weight, weight, sems, sems_three = refs[2 * PIECES :]
+    d_hidden, d_attention, gain_grad, lift_weight, weight, sems, sems_three = refs[2 * PIECES :]
     me = place[0]
     width = hidden.shape[1]
     copies = fill(first, lift_weight, sems, me, pl.ds(0, lift_weight.shape[1]))
@@ -460,7 +469,6 @@
     rounded = total.astype(BF16)
     wait_all(lasts)
     d_attention[...] = dot_nt(rounded, weight[...]).astype(BF16)
-    pack(keep, send, attention, rounded, Y_BIT, X_BIT, me)
 
 
 def attend_back_kernel(
@@ -504,7 +512,7 @@
 
 
 def keys_back_kernel(
-    place, d_keys_values, arrived, cosine, sine, xn1, keep_one, send_one, keep_two, send_two, summed, d_turned
+    place, d_queries, d_keys_values, arrived, cosine, sine, xn1, keep_one, send_one, keep_two, send_two, summed, d_turned
 ):
     me, along = (place[0], place[1])
     width = xn1.shape[1]
@@ -515,23 +523,27 @@
     summed[where, :] = summed[where, :] + arrived[...].astype(F32)
     for start in range(0, width, pair):
         here = slice(start, start + pair)
-        d_turned[:, here] = turn(summed[:, here], cosine[...], -sine[...]).astype(BF16)
-    pack(keep_one, send_one, xn1, d_turned[...], Y_BIT, X_BIT, me)
-    pack(keep_two, send_two, xn1, summed[:, width:].astype(BF16), X_BIT, Y_BIT, me)
-
-
-def tokens_back_kernel(place, d_queries, pack_k, pack_v, tokens, xn1, d_hidden, gains, mlp_term, *refs):
+        there = slice(width + start, width + start + pair)
+        d_turned[:, there] = turn(summed[:, here], cosine[...], -sine[...]).astype(BF16)
+    d_turned[:, :width] = d_queries[...]
+    d_turned[:, 2 * width :] = summed[:, width:].astype(BF16)
+    middle = d_turned.shape[1] // 2
+    pack(keep_one, send_one, xn1, d_turned[:, :middle], X_BIT, Y_BIT, me)
+    pack(keep_two, send_two, xn1, d_turned[:, middle:], Y_BIT, X_BIT, me)
+
+
+def tokens_back_kernel(place, pack_one, pack_two, tokens, attention, d_hidden, gains, mlp_term, *refs):
     pieces, (keep, send, input_grad, weight, sems) = (refs[:PIECES], refs[PIECES:])
     rows = tokens.shape[0]
     width = tokens.shape[1]
     copies = fill(pieces, weight, sems, place[0], pl.ds(0, 3 * width))
     normed, scaled = norm_parts(tokens[...].astype(F32))
     wait_all(copies)
-    d_xn1 = dot_nt(d_queries[...], weight[:, :width])
-    d_xn1 = d_xn1 + dot_nt(pack_k[:, width // 2 :], weight[:, width : 2 * width])
-    d_xn1 = d_xn1 + dot_nt(pack_v[:, width // 2 :], weight[:, 2 * width :])
+    middle = pack_one.shape[1] - width // 2
+    d_xn1 = dot_nt(pack_one[:, width // 2 :], weight[:, :middle])
+    d_xn1 = d_xn1 + dot_nt(pack_two[:, width // 2 :], weight[:, middle:])
     d_norm, gain_term = norm_back(d_xn1, normed, scaled, gains[0:1, :])
-    pack(keep, send, xn1, d_queries[...], X_BIT, Y_BIT, place[0])
+    pack(keep, send, attention, d_hidden[...].astype(BF16), Y_BIT, X_BIT, place[0])
     extra = keep.shape[0] - rows
     line = lax.broadcasted_iota(jnp.int32, (extra, width), 0)
     terms = jnp.where(line == 0, mlp_term[...], jnp.where(line == 1, gain_term, 0.0)).astype(BF16)
@@ -541,16 +553,17 @@
     input_grad[...] = (d_hidden[...] + d_norm).astype(BF16)
 
 
-def product_kernel(width, rows, mine, over_link, core_mine, core_link, own, sent, joined, *refs):
+def product_kernel(width, rows, chip, other, own, sent, joined, *refs):
     terms, sems = (refs[0] if len(refs) > 1 else None, refs[-1])
     copies = []
-    for index, part in enumerate((mine, over_link, core_mine, core_link)):
-        source = part if terms is None else part.at[pl.ds(0, rows)]
+    extra = 0 if terms is None else terms.shape[1]
+    for index in range(4):
+        part, start = ((chip, other)[index // 2], index % 2 * (rows + extra))
+        source = part.at[pl.ds(start, rows)]
         copies.append(pltpu.make_async_copy(source, joined.at[pl.ds(index * rows, rows)], sems.at[index]))
         if terms is not None:
-            extra = terms.shape[1]
             copies.append(
-                pltpu.make_async_copy(part.at[pl.ds(rows, extra)], terms.at[index], sems.at[4 + index])
+                pltpu.make_async_copy(part.at[pl.ds(start + rows, extra)], terms.at[index], sems.at[4 + index])
             )
     for copy in copies:
         copy.start()
@@ -587,51 +600,58 @@
     )(*operands)
 
 
-def grad_rows(keep, send, gather_bit, sum_bit, width, after=()):
-    rows = keep.shape[0] // 128 * 128
-    extra = keep.shape[0] - rows
-    cols = keep.shape[1] - 4 * width
-    over_link = swap(send, gather_bit)
-    keep, over_link = later((keep, over_link), after)
-    core_mine = swap(keep, CORE_BIT)
-    core_link = swap(over_link, CORE_BIT)
+def grad_rows(keep, over_link, width, before=(), after=()):
+    return products(share(keep, over_link, before), width, after)
+
+
+def share(keep, over_link, before=()):
+    return jnp.concatenate(later([keep, over_link], before), axis=0)
+
+
+def products(chip, width, after=()):
+    rows = chip.shape[0] // 256 * 128
+    extra = chip.shape[0] // 2 - rows
+    cols = chip.shape[1] - 4 * width
+    other = later(swap(chip, CORE_BIT), after)
     scratch = [pltpu.VMEM((4 * rows, 4 * width + cols), BF16)]
     if extra:
         scratch.append(pltpu.VMEM((4, extra, 4 * width + cols), BF16))
-    own, sent = call(
+    return call(
         lambda *refs: product_kernel(width, rows, *refs),
         [((width + extra, cols), F32), ((width + extra, cols), BF16)],
-        [keep, over_link, core_mine, core_link],
+        [chip, other],
         scratch + [pltpu.SemaphoreType.DMA((8,))],
         smem=0,
-        anywhere=(0, 1, 2, 3),
+        anywhere=(0, 1),
         flops=16 * rows * width * cols,
         size=4 * rows * (4 * width + cols) * 2 + 6 * width * cols,
     )
-    return (own + swap(sent, sum_bit).astype(F32), sent)
-
-
-def line_sum(part):
-    first = lax.ppermute(part.astype(BF16), "replica", [(0, 1), (3, 2)])
-    pair = (part + first.astype(F32)).astype(BF16)
-    other = lax.ppermute(pair, "replica", [(1, 2), (2, 1)])
-    total = (pair.astype(F32) + other.astype(F32)).astype(BF16)
-    back = lax.ppermute(total, "replica", [(1, 0), (2, 3)])
+
+
+def line_first(part):
+    return lax.ppermute(part.astype(BF16), "replica", [(0, 1), (3, 2)])
+
+
+def line_pair(part, first):
+    return (part + first.astype(F32)).astype(BF16)
+
+
+def line_middle(pair):
+    return lax.ppermute(pair, "replica", [(1, 2), (2, 1)])
+
+
+def line_total(pair, other):
+    return (pair.astype(F32) + other.astype(F32)).astype(BF16)
+
+
+def line_back(total):
+    return lax.ppermute(total, "replica", [(1, 0), (2, 3)])
+
+
+def line_end(total, back):
     place = lax.axis_index("replica")
     middle = (place == 1) | (place == 2)
     return jnp.where(middle, total, back).astype(F32)
-
-
-def cross_sum(part):
-    half = part.shape[1] // 2
-    even = lax.axis_index("replica") % 2 == 0
-    step = lambda value, bit: lax.ppermute(value, "replica", [(i, i ^ bit) for i in range(4)])
-    low, high = (part[:, :half], part[:, half:])
-    got = step(jnp.where(even, high, low).astype(BF16), 1)
-    pair = (jnp.where(even, low, high) + got.astype(F32)).astype(BF16)
-    total = (pair.astype(F32) + step(pair, 2).astype(F32)).astype(BF16)
-    back = step(total, 1)
-    return jnp.concatenate([jnp.where(even, total, back), jnp.where(even, back, total)], axis=1).astype(F32)
 
 
 def body_plane(
@@ -667,8 +687,9 @@
         ],
         axis=1,
     )
-    packed, arrived = gather_pieces(front)
-    feed_pieces, arrived = gather_pieces(feed, arrived)
+    fetched = fetch_pieces(front)
+    packed = share_pieces(fetched)
+    feed_fetched = fetch_pieces(feed, tuple(fetched[3:]))
     cosine, sine = rope_tables(positions[0], HEAD_DIM)
     cosine = jnp.concatenate([cosine[:, 0]] * 4, axis=1)
     sine = jnp.concatenate([-sine[:, 0], sine[:, 0]] * 2, axis=1)
@@ -697,10 +718,13 @@
         flops=12 * rows * width * width,
         size=4 * width * width,
     )
+    feed_pieces = share_pieces(feed_fetched, xn2)
     half = 4 * shard
-    keep_c, send_c, slope_gate, active = call(
+    cut = -(-ff_width // 256) * 128
+    cuts = [((rows, half + cut), BF16)] * 2 + [((rows, half + ff_width - cut), BF16)] * 2
+    keep_c, send_c, keep_d, send_d, slope_gate, active = call(
         lift_kernel,
-        [((rows, half + ff_width), BF16)] * 2 + [((rows, ff_width), F32)] * 2,
+        cuts + [((rows, ff_width), F32)] * 2,
         [place, xn2, grad_out] + feed_pieces,
         [pltpu.VMEM((width, 2 * ff_width), BF16), sems],
         anywhere=range(3, 3 + PIECES),
@@ -710,23 +734,25 @@
     layer_out, keep_g, send_g, keep_u, send_u = call(
         contract_kernel,
         [((rows, width), BF16)] + [((rows, half + ff_width), BF16)] * 4,
-        [place, keep_c, grad_out, xn2, hidden, slope_gate, active] + feed_pieces,
+        [place, keep_c, keep_d, grad_out, xn2, hidden, slope_gate, active] + feed_pieces,
         [pltpu.VMEM((width, ff_width), BF16), sems],
-        anywhere=range(7, 7 + PIECES),
+        anywhere=range(8, 8 + PIECES),
         flops=4 * rows * width * ff_width,
         size=2 * width * ff_width,
     )
-    keep_o, send_o, d_hidden, d_attention, mlp_term = call(
+    d_hidden, d_attention, mlp_term = call(
         hidden_back_kernel,
-        [((rows, half + width), BF16)] * 2 + [((rows, width), F32), ((rows, width), BF16), ((1, width), F32)],
-        [place, keep_g, keep_u, grad_out, hidden, full_gains, attention] + feed_pieces + packed,
+        [((rows, width), F32), ((rows, width), BF16), ((1, width), F32)],
+        [place, keep_g, keep_u, grad_out, hidden, full_gains] + feed_pieces + packed,
         [pltpu.VMEM((width, 2 * ff_width), BF16), pltpu.VMEM((width, width), BF16), sems, sems],
-        anywhere=range(7, 7 + 2 * PIECES),
+        anywhere=range(6, 6 + 2 * PIECES),
         flops=6 * rows * width * ff_width,
         size=6 * width * ff_width,
     )
-    contract_part, contract_sent = grad_rows(keep_c, send_c, X_BIT, Y_BIT, shard, d_attention)
-    d_attention = later(d_attention, contract_sent)
+    link_c = swap(send_c, X_BIT)
+    link_d = swap(send_d, Y_BIT)
+    link_g = swap(send_g, Y_BIT)
+    link_u = swap(send_u, X_BIT)
     d_queries, d_keys_values, d_edge = call(
         attend_back_kernel,
         [((rows, width), BF16), ((rows, 2 * width), F32), ((HALF, 2 * width), BF16)],
@@ -734,43 +760,97 @@
         flops=20 * rows * width * width,
         size=4 * width * width,
     )
-    gelu_part, gelu_sent = grad_rows(keep_g, send_g, Y_BIT, X_BIT, shard, d_edge)
-    gate_part, gate_sent = grad_rows(keep_u, send_u, X_BIT, Y_BIT, shard, d_edge)
-    keep_k, send_k, keep_v, send_v = call(
+    first_own, first_sent = grad_rows(keep_c, link_c, shard, keep_g, d_edge)
+    second_own, second_sent = grad_rows(keep_d, link_d, shard, keep_g, d_edge)
+    first_back = swap(first_sent, Y_BIT)
+    second_back = swap(second_sent, X_BIT)
+    chip_g = share(keep_g, link_g, (first_sent, second_sent))
+    chip_u = share(keep_u, link_u, (first_sent, second_sent))
+    first_back, second_back = later((first_back, second_back), chip_g, chip_u)
+    contract_part = jnp.concatenate(
+        [first_own + first_back.astype(F32), second_own + second_back.astype(F32)], axis=1
+    )
+    contract_first = line_first(contract_part)
+    gelu_own, gelu_sent = products(chip_g, shard, contract_part)
+    gelu_back = swap(gelu_sent, X_BIT)
+    gate_own, gate_sent = products(chip_u, shard, gelu_sent)
+    gate_back = swap(gate_sent, Y_BIT)
+    d_keys_values = later(d_keys_values, gate_sent)
+    keep_kv, send_kv, keep_vk, send_vk = call(
         keys_back_kernel,
-        [((rows, half + width), BF16)] * 4,
-        [place, d_keys_values, swap(d_edge, X_BIT), cosine, sine, xn1],
-        [pltpu.VMEM((rows, 2 * width), F32), pltpu.VMEM((rows, width), BF16)],
+        [((rows, half + 3 * width // 2), BF16)] * 4,
+        [place, d_queries, d_keys_values, swap(d_edge, X_BIT), cosine, sine, xn1],
+        [pltpu.VMEM((rows, 2 * width), F32), pltpu.VMEM((rows, 3 * width), BF16)],
         flops=rows * width,
         size=8 * rows * width,
     )
-    key_part, _ = grad_rows(keep_k, send_k, Y_BIT, X_BIT, shard)
-    value_part, _ = grad_rows(keep_v, send_v, X_BIT, Y_BIT, shard)
-    d_hidden = later(d_hidden, contract_part, gelu_sent, gate_sent)
-    keep_q, send_q, input_grad = call(
+    link_kv = swap(send_kv, X_BIT)
+    link_vk = swap(send_vk, Y_BIT)
+    contract_pair = line_pair(contract_part, later(contract_first, keep_kv))
+    contract_other = line_middle(contract_pair)
+    gelu_part = gelu_own + later(gelu_back, contract_pair).astype(F32)
+    gelu_first = line_first(gelu_part)
+    gate_part = gate_own + later(gate_back, gelu_part).astype(F32)
+    gate_first = line_first(gate_part)
+    contract_total = line_total(contract_pair, later(contract_other, gate_part))
+    contract_last = line_back(contract_total)
+    gelu_pair = line_pair(gelu_part, later(gelu_first, contract_total))
+    gelu_other = line_middle(gelu_pair)
+    chip_kv = share(keep_kv, link_kv, gelu_pair)
+    chip_vk = share(keep_vk, link_vk, gelu_pair)
+    d_hidden = later(d_hidden, chip_kv, chip_vk)
+    keep_o, send_o, input_grad = call(
         tokens_back_kernel,
         [((rows + 16, half + width), BF16)] * 2 + [((rows, width), BF16)],
-        [place, d_queries, keep_k, keep_v, source, xn1, d_hidden, full_gains, mlp_term] + packed,
+        [place, keep_kv, keep_vk, source, attention, d_hidden, full_gains, mlp_term] + packed,
         [pltpu.VMEM((width, 3 * width), BF16), sems],
-        anywhere=range(9, 9 + PIECES),
+        anywhere=range(8, 8 + PIECES),
         flops=6 * rows * width * width,
         size=6 * width * width,
     )
-    output_part, _ = grad_rows(keep_o, send_o, Y_BIT, X_BIT, shard, keep_k)
-    query_part, _ = grad_rows(keep_q, send_q, X_BIT, Y_BIT, shard)
-    contract_grad = line_sum(contract_part)
-    gelu_grad = line_sum(gelu_part)
-    gate_grad = line_sum(gate_part)
-    late_grad = cross_sum(jnp.concatenate([key_part, value_part], axis=1))
-    early_grad = line_sum(jnp.concatenate([output_part, query_part], axis=0))
-    query_grad = early_grad[shard : 2 * shard]
-    gain_rows = lax.dynamic_slice_in_dim(early_grad[2 * shard : 2 * shard + 2], me * shard, shard, axis=1)
+    link_o = swap(send_o, Y_BIT)
+    low_own, low_sent = products(chip_kv, shard, keep_o)
+    low_back = swap(low_sent, Y_BIT)
+    high_own, high_sent = products(chip_vk, shard, low_sent)
+    high_back = swap(high_sent, X_BIT)
+    gate_pair = line_pair(gate_part, later(gate_first, high_sent))
+    gate_other = line_middle(gate_pair)
+    out_own, out_sent = grad_rows(keep_o, link_o, shard, gate_pair)
+    out_back = swap(out_sent, X_BIT)
+    low_part = low_own + later(low_back, out_sent).astype(F32)
+    low_first = line_first(low_part)
+    high_part = high_own + later(high_back, low_part).astype(F32)
+    high_first = line_first(high_part)
+    gelu_total = line_total(gelu_pair, later(gelu_other, high_part))
+    gelu_last = line_back(gelu_total)
+    low_pair = line_pair(low_part, later(low_first, gelu_total))
+    low_other = line_middle(low_pair)
+    out_part = out_own + later(out_back, low_pair).astype(F32)
+    out_first = line_first(out_part)
+    gate_total = line_total(gate_pair, later(gate_other, out_part))
+    gate_last = line_back(gate_total)
+    high_pair = line_pair(high_part, later(high_first, gate_total))
+    high_other = line_middle(high_pair)
+    low_total = line_total(low_pair, later(low_other, high_pair))
+    low_last = line_back(low_total)
+    out_pair = line_pair(out_part, later(out_first, low_total))
+    out_other = line_middle(out_pair)
+    high_total = line_total(high_pair, later(high_other, out_pair))
+    high_last = line_back(high_total)
+    out_total = line_total(out_pair, later(out_other, high_total))
+    out_last = line_back(out_total)
+    contract_grad = line_end(contract_total, later(contract_last, high_pair))
+    gelu_grad = line_end(gelu_total, later(gelu_last, out_total))
+    gate_grad = line_end(gate_total, later(gate_last, out_total))
+    all_grad = jnp.concatenate([line_end(low_total, low_last), line_end(high_total, high_last)], axis=1)
+    out_grad = line_end(out_total, out_last)
+    gain_rows = lax.dynamic_slice_in_dim(out_grad[shard : shard + 2], me * shard, shard, axis=1)
     return (
         layer_out[None],
         input_grad[None],
         gain_rows[1],
-        jnp.concatenate([query_grad, late_grad], axis=1),
-        early_grad[:shard],
+        all_grad,
+        out_grad[:shard],
         gain_rows[0],
         jnp.concatenate([gelu_grad[:, :true_width], gate_grad[:, :true_width]], axis=1),
         contract_grad[:, :true_width],

time: 381 us -> 348 us (0.913)
  waiting for transfers between devices: 210 us -> 161 us
  starting transfers between devices: 59.9 us -> 77.8 us
    ppermute x48 -> x41, waiting for transfers between devices: 138 us -> 110 us  [swap(): return lax.ppermute(value, PLANE, [(i, i ^ bit) for i in range(PLANE_SIZE)])]
    ppermute x15 -> x18, waiting for transfers between devices: 71.6 us -> 51 us  [the longest x6 31 us: line_first(): return lax.ppermute(part.astype(BF16), 'replica', [(0, 1), (3, 2)])]
    ppermute x15 -> x18, starting transfers between devices: 28.2 us -> 47.2 us  [the longest x6 33.8 us: line_first(): return lax.ppermute(part.astype(BF16), 'replica', [(0, 1), (3, 2)])]
    unnamed x92 -> x99, local copies, waits for them, and re-layouts: 12.3 us -> 7.16 us
    ppermute x48 -> x41, starting transfers between devices: 31.7 us -> 30.6 us  [swap(): return lax.ppermute(value, PLANE, [(i, i ^ bit) for i in range(PLANE_SIZE)])]
    convert_element_type x17 -> x19, other arithmetic: 13.6 us -> 12.5 us  [the longest x6 4.68 us: line_total(): return (pair.astype(F32) + other.astype(F32)).astype(BF16)]
  transfers between devices with their start and end apart: 63 -> 59, of which waited for: 26 -> 30; matrix products, arithmetic and copies ran while one was open for 7% -> 9% of each run, Pallas kernels for 16% -> 17%
where the time goes in v5:
time: 348 us; the launch traced here: 347 us
  waiting for transfers between devices  161 us (46%)
  starting transfers between devices  77.8 us (22%)
  Pallas kernels  65.4 us (19%)
  other arithmetic  23.8 us (7%)
  local copies, waits for them, and re-layouts  17.2 us (5%)
    ppermute x41, waiting for transfers between devices, swap(): return lax.ppermute(value, PLANE, [(i, i ^ bit) for i in range(PLANE_SIZE)])  110 us
    pallas_call x15, Pallas kernels, call(): pl.pallas_call(kernel, out_shape=[jax.ShapeDtypeStruct(shape, kind) for s...  65.4 us
    ppermute x6, starting transfers between devices, line_first(): return lax.ppermute(part.astype(BF16), 'replica', [(0, 1), (3, 2)])  33.8 us
    ppermute x6, waiting for transfers between devices, line_first(): return lax.ppermute(part.astype(BF16), 'replica', [(0, 1), (3, 2)])  31 us
    ppermute x41, starting transfers between devices, swap(): return lax.ppermute(value, PLANE, [(i, i ^ bit) for i in range(PLANE_SIZE)])  30.6 us
    ppermute x6, waiting for transfers between devices, line_back(): return lax.ppermute(total, 'replica', [(1, 0), (2, 3)])  20 us
    ppermute x6, starting transfers between devices, line_back(): return lax.ppermute(total, 'replica', [(1, 0), (2, 3)])  7.72 us
    unnamed x99, local copies, waits for them, and re-layouts  7.16 us
  transfers between devices with their start and end apart: 59, of which 30 were waited for; matrix products, arithmetic and copies ran while one was open for 9% of the time, Pallas kernels for 17%

profile of v5, /device:TPU:0, one launch (start us, length us, event | category | flops | bytes accessed | tf_op | source)
XLA Modules:
  0.0 347.0 jit_solution(8049665588834035429)
XLA Ops:
  1.5 2.4 fusion.6.refs_0_.refs_10_
  3.9 3.0 collective-permute-start.1
  9.1 22.0 %collective-permute-done.1.refs_2_.refs_12_ = bf16[128,4224]{1,0:T(8,128)(2,1)} collective-permute-done((bf16[128,4224]{1,0:T(8,128)(2,1)}, bf16[128,4224]{1,0:T(8,128)(2,1)}, u32[]{:S(2)}, u32[]{:S(2)}) %collective-permute-start.1) | collective-permute-done | bytes 1081376 | tf_op jit(solution)/shard_map/ppermute | solution.py:265
  38.1 7.6 %collective-permute-done.3.refs_4_.refs_14_ = bf16[64,4224]{1,0:T(8,128)(2,1)S(1)} collective-permute-done((bf16[64,4224]{1,0:T(8,128)(2,1)S(1)}, bf16[64,4224]{1,0:T(8,128)(2,1)S(1)}, u32[]{:S(2)}, u32[]{:S(2)}) %collective-permute-start.3) | collective-permute-done | bytes 540704 | tf_op jit(solution)/shard_map/ppermute | solution.py:265
  55.8 4.7 %shard_map.161 = (bf16[128,1024]{1,0:T(8,128)(2,1)S(1)}, bf16[128,2048]{1,0:T(8,128)(2,1)S(1)}, bf16[64,2048]{1,0:T(8,128)(2,1)S(1)}, bf16[128,1024]{1,0:T(8,128)(2,1)S(1)}, f32[8,1024]{1,0:T(8,128)S(1)}) custom-call(s32[2]{0:T(128)S(1)} %pad_add_fusion.place, bf16[128,1024]{1,0:T(8,128)(2,1)S(1)} %bitcast.18, f32[128,128]{1,0:T(8,128)S(1)} %get-tuple-element.235.cosine, ...), custom_call_target="tpu_custom_call" | custom-call | flops 805306368 | bytes 8650752 | tf_op jit(solution)/shard_map/pallas_call | solution.py:592
  62.2 30.7 %collective-permute-done.11.refs_2_ = bf16[128,8064]{1,0:T(8,128)(2,1)} collective-permute-done((bf16[128,8064]{1,0:T(8,128)(2,1)}, bf16[128,8064]{1,0:T(8,128)(2,1)}, u32[]{:S(2)}, u32[]{:S(2)}) %collective-permute-start.11) | collective-permute-done | bytes 2064416 | tf_op jit(solution)/shard_map/ppermute | solution.py:265
  92.9 2.3 slice.77
  105.4 7.7 %shard_map.162 = (bf16[128,1024]{1,0:T(8,128)(2,1)S(1)}, f32[128,128]{1,0:T(8,128)S(1)}, f32[128,1024]{1,0:T(8,128)S(1)}, bf16[128,1024]{1,0:T(8,128)(2,1)S(1)}) custom-call(s32[2]{0:T(128)S(1)} %copy-done.28, bf16[128,1024]{1,0:T(8,128)(2,1)S(1)} %copy-done.23, bf16[128,2048]{1,0:T(8,128)(2,1)S(1)} %copy-done.16, ...), custom_call_target="tpu_custom_call" | custom-call | flops 1610612736 | bytes 4194304 | tf_op jit(solution)/shard_map/pallas_call | solution.py:592
  113.8 8.0 %collective-permute-done.13.refs_4_ = bf16[64,8064]{1,0:T(8,128)(2,1)} collective-permute-done((bf16[64,8064]{1,0:T(8,128)(2,1)}, bf16[64,8064]{1,0:T(8,128)(2,1)}, u32[]{:S(2)}, u32[]{:S(2)}) %collective-permute-start.13) | collective-permute-done | bytes 1032224 | tf_op jit(solution)/shard_map/ppermute | solution.py:265
  122.4 3.0 collective-permute-done.18.refs_9_
  127.0 7.5 %shard_map.163 = (bf16[128,1920]{1,0:T(8,128)(2,1)S(1)}, bf16[128,1920]{1,0:T(8,128)(2,1)S(1)}, bf16[128,1792]{1,0:T(8,128)(2,1)S(1)}, bf16[128,1792]{1,0:T(8,12...) custom-call(s32[2]{0:T(128)S(1)} %copy-done.28, bf16[128,1024]{1,0:T(8,128)(2,1)S(1)} %get-tuple-element.106.xn2, ...), custom_call_target="tpu_custom_call" | custom-call | flops 1409286144 | bytes 11010048 | tf_op jit(solution)/shard_map/pallas_call | solution.py:592
  136.0 8.3 %shard_map.164 = (bf16[128,1024]{1,0:T(8,128)(2,1)}, bf16[128,3200]{1,0:T(8,128)(2,1)S(1)}, bf16[128,3200]{1,0:T(8,128)(2,1)S(1)}, bf16[128,3200]{1,0:T(8,128)(2,1)}, bf16[128,3200]{1,0:T(8,128)(2,1)}) custom-call(s32[2]{0:T(128)S(1)} %copy-done.28, bf16[128,1920]{1,0:T(8,128)(2,1)S(1)} %get-tuple-element.124.gated_one, ...), custom_call_target="tpu_custom_call" | custom-call | flops 1409286144 | bytes 5505024 | tf_op jit(solution)/shard_map/pallas_call | solution.py:592
  144.3 2.8 collective-permute-done.22
  150.9 10.7 %shard_map.165 = (f32[128,1024]{1,0:T(8,128)S(1)}, bf16[128,1024]{1,0:T(8,128)(2,1)S(1)}, f32[1,1024]{1,0:T(1,128)S(1)}) custom-call(s32[2]{0:T(128)S(1)} %copy-done.28, bf16[128,3200]{1,0:T(8,128)(2,1)} %copy-done.5, bf16[128,3200]{1,0:T(8,128)(2,1)} %get-tuple-element.134.pack_two, bf16[128,1024]{1,0:T(8,128)(2,1)S(1)} %bitcast.17, ...), custom_call_target="tpu_custom_call" | custom-call | flops 2113929216 | bytes 16515072 | tf_op jit(solution)/shard_map/pallas_call | solution.py:592
  161.7 6.3 %shard_map.166 = (bf16[128,1024]{1,0:T(8,128)(2,1)S(1)}, f32[128,2048]{1,0:T(8,128)S(1)}, bf16[64,2048]{1,0:T(8,128)(2,1)S(1)}) custom-call(s32[2]{0:T(128)S(1)} %copy-done.28, bf16[128,1024]{1,0:T(8,128)(2,1)S(1)} %copy-done.24, bf16[128,2048]{1,0:T(8,128)(2,1)S(1)} %copy-done.17, bf16[64,2048]{1,0:T(8,128)(2,1)S(1)} %copy-done.26, ...), custom_call_target="tpu_custom_call" | custom-call | flops 2684354560 | bytes 4194304 | tf_op jit(solution)/shard_map/pallas_call | solution.py:592
  176.0 3.0 collective-permute-done.28
  179.0 3.9 %collective-permute-done.27 = bf16[128,1408]{1,0:T(8,128)(2,1)S(1)} collective-permute-done((bf16[128,1408]{1,0:T(8,128)(2,1)S(1)}, bf16[128,1408]{1,0:T(8,128)(2,1)S(1)}, u32[]{:S(2)}, u32[]{:S(2)}) %collective-permute-start.27) | collective-permute-done | bytes 360480 | tf_op jit(solution)/shard_map/ppermute | solution.py:265
  184.1 4.3 %collective-permute-start.32 = (bf16[128,2688]{1,0:T(8,128)(2,1)}, bf16[128,2688]{1,0:T(8,128)(2,1)}, u32[]{:S(2)}, u32[]{:S(2)}) collective-permute-start(bf16[128,2688]{1,0:T(8,128)(2,1)} %fusion.9), channel_id=1, source_target_pairs={{0,8},{24,16},{1,9},{25,17},{2,10},{26,18},{3,11},{27,19},{4,12},{... | collective-permute-start | bytes 2064392 | tf_op jit(solution)/shard_map/ppermute | solution.py:632
  188.9 2.6 shard_map.169
  194.3 2.6 shard_map.170
  204.0 8.4 %collective-permute-done.31 = bf16[128,2688]{1,0:T(8,128)(2,1)} collective-permute-done((bf16[128,2688]{1,0:T(8,128)(2,1)S(1)}, bf16[128,2688]{1,0:T(8,128)(2,1)}, u32[]{:S(2)}, u32[]{:S(2)}) %collective-permute-start.31) | collective-permute-done | bytes 688160 | tf_op jit(solution)/shard_map/ppermute | solution.py:265
  216.5 8.1 %collective-permute-done.33 = bf16[128,2688]{1,0:T(8,128)(2,1)S(1)} collective-permute-done((bf16[128,2688]{1,0:T(8,128)(2,1)S(1)}, bf16[128,2688]{1,0:T(8,128)(2,1)S(1)}, u32[]{:S(2)}, u32[]{:S(2)}) %collective-permute-start.33) | collective-permute-done | bytes 688160 | tf_op jit(solution)/shard_map/ppermute | solution.py:632
  226.4 4.4 %collective-permute-start.38 = (bf16[128,2688]{1,0:T(8,128)(2,1)S(1)}, bf16[128,2688]{1,0:T(8,128)(2,1)S(1)}, u32[]{:S(2)}, u32[]{:S(2)}) collective-permute-start(bf16[128,2688]{1,0:T(8,128)(2,1)S(1)} %get-tuple-element.226), channel_id=1, source_target_pairs={{0,8},{24,16},{1,9},{25,17},{2,10},{26,18},{3,11},{27,19},{4,12},{... | collective-permute-start | bytes 2064392 | tf_op jit(solution)/shard_map/ppermute | solution.py:632
  230.9 6.4 %shard_map.172 = (bf16[144,1536]{1,0:T(8,128)(2,1)S(1)}, bf16[144,1536]{1,0:T(8,128)(2,1)S(1)}, bf16[128,1024]{1,0:T(8,128)(2,1)}) custom-call(s32[2]{0:T(128)S(1)} %copy-done.28, bf16[128,2048]{1,0:T(8,128)(2,1)S(1)} %get-tuple-element.161.pack_one, bf16[128,2048]{1,0:T(8,128)(2,1)S(1)} %get-tuple-element.164.pack_two, bf16[128,1024]{1,0:T(8,128)(2,1)S(1)} %bitcast.20, ...), custom_call_target="tpu_custom_call" | custom-call | flops 805306368 | bytes 6291456 | tf_op jit(solution)/shard_map/pallas_call | solution.py:592
  240.4 5.3 %collective-permute-done.38 = bf16[128,2688]{1,0:T(8,128)(2,1)S(1)} collective-permute-done((bf16[128,2688]{1,0:T(8,128)(2,1)S(1)}, bf16[128,2688]{1,0:T(8,128)(2,1)S(1)}, u32[]{:S(2)}, u32[]{:S(2)}) %collective-permute-start.38) | collective-permute-done | bytes 688160 | tf_op jit(solution)/shard_map/ppermute | solution.py:632
  246.6 2.5 collective-permute-done.37
  255.9 5.1 %collective-permute-done.43 = bf16[128,1536]{1,0:T(8,128)(2,1)S(1)} collective-permute-done((bf16[128,1536]{1,0:T(8,128)(2,1)}, bf16[128,1536]{1,0:T(8,128)(2,1)S(1)}, u32[]{:S(2)}, u32[]{:S(2)}) %collective-permute-start.43) | collective-permute-done | bytes 393248 | tf_op jit(solution)/shard_map/ppermute | solution.py:265
  263.5 12.9 %collective-permute-start.49 = (bf16[128,1536]{1,0:T(8,128)(2,1)S(1)}, bf16[128,1536]{1,0:T(8,128)(2,1)S(1)}, u32[]{:S(2)}, u32[]{:S(2)}) collective-permute-start(bf16[128,1536]{1,0:T(8,128)(2,1)S(1)} %get-tuple-element.220), channel_id=1, source_target_pairs={{0,8},{24,16},{1,9},{25,17},{2,10},{26,18},{3,11},{27,19},{4,12},{... | collective-permute-start | bytes 1179656 | tf_op jit(solution)/shard_map/ppermute | solution.py:632
  277.9 13.3 %collective-permute-done.44 = bf16[128,1536]{1,0:T(8,128)(2,1)S(1)} collective-permute-done((bf16[128,1536]{1,0:T(8,128)(2,1)S(1)}, bf16[128,1536]{1,0:T(8,128)(2,1)S(1)}, u32[]{:S(2)}, u32[]{:S(2)}) %collective-permute-start.44) | collective-permute-done | bytes 393248 | tf_op jit(solution)/shard_map/ppermute | solution.py:632
  301.3 9.2 %collective-permute-start.47 = (bf16[144,1024]{1,0:T(8,128)(2,1)}, bf16[144,1024]{1,0:T(8,128)(2,1)S(1)}, u32[]{:S(2)}, u32[]{:S(2)}) collective-permute-start(bf16[144,1024]{1,0:T(8,128)(2,1)} %get-tuple-element.222), channel_id=1, source_target_pairs={{0,8},{24,16},{1,9},{25,17},{2,10},{26,18},{3,11},{27,19},{4,12},{... | collective-permute-start | bytes 884744 | tf_op jit(solution)/shard_map/ppermute | solution.py:632
  319.8 6.6 %collective-permute-done.57 = bf16[128,2688]{1,0:T(8,128)(2,1)} collective-permute-done((bf16[128,2688]{1,0:T(8,128)(2,1)}, bf16[128,2688]{1,0:T(8,128)(2,1)}, u32[]{:S(2)}, u32[]{:S(2)}) %collective-permute-start.57) | collective-permute-done | bytes 688160 | tf_op jit(solution)/shard_map/ppermute | solution.py:648
  330.8 11.6 %collective-permute-done.55 = bf16[128,1536]{1,0:T(8,128)(2,1)S(1)} collective-permute-done((bf16[128,1536]{1,0:T(8,128)(2,1)S(1)}, bf16[128,1536]{1,0:T(8,128)(2,1)S(1)}, u32[]{:S(2)}, u32[]{:S(2)}) %collective-permute-start.55) | collective-permute-done | bytes 393248 | tf_op jit(solution)/shard_map/ppermute | solution.py:648
  (257 shorter events, 107.9 us)
Async XLA Ops:
  3.9 27.1 %collective-permute-start.1 = (bf16[128,4224]{1,0:T(8,128)(2,1)}, bf16[128,4224]{1,0:T(8,128)(2,1)}, u32[]{:S(2)}, u32[]{:S(2)}) collective-permute-start(bf16[128,4224]{1,0:T(8,128)(2,1)} %fusion.6.refs_0_.refs_10_), channel_id=1, source_target_pairs={{0,4},{1,5},{2,6},{3,7},{4,0},{5,1},{6,2},{7,3},{8,12},{9,13},{10,... | collective-permute-start | bytes 3244040 | tf_op jit(solution)/shard_map/ppermute | solution.py:265
  6.9 27.0 %collective-permute-start = (bf16[128,4224]{1,0:T(8,128)(2,1)}, bf16[128,4224]{1,0:T(8,128)(2,1)}, u32[]{:S(2)}, u32[]{:S(2)}) collective-permute-start(bf16[128,4224]{1,0:T(8,128)(2,1)} %fusion.6.refs_0_.refs_10_), channel_id=1, source_target_pairs={{0,1},{1,0},{2,3},{3,2},{4,5},{5,4},{6,7},{7,6},{8,9},{9,8},{10,11... | collective-permute-start | bytes 3244040 | tf_op jit(solution)/shard_map/ppermute | solution.py:265
  8.4 42.2 %collective-permute-start.4 = (bf16[128,4224]{1,0:T(8,128)(2,1)}, bf16[128,4224]{1,0:T(8,128)(2,1)}, u32[]{:S(2)}, u32[]{:S(2)}) collective-permute-start(bf16[128,4224]{1,0:T(8,128)(2,1)} %fusion.6.refs_0_.refs_10_), channel_id=1, source_target_pairs={{0,2},{1,3},{2,0},{3,1},{4,6},{5,7},{6,4},{7,5},{8,10},{9,11},{10,... | collective-permute-start | bytes 3244040 | tf_op jit(solution)/shard_map/ppermute | solution.py:265
  48.0 44.9 %collective-permute-start.11 = (bf16[128,8064]{1,0:T(8,128)(2,1)}, bf16[128,8064]{1,0:T(8,128)(2,1)}, u32[]{:S(2)}, u32[]{:S(2)}) collective-permute-start(bf16[128,8064]{1,0:T(8,128)(2,1)} %fusion.5.refs_0_), channel_id=1, source_target_pairs={{0,4},{1,5},{2,6},{3,7},{4,0},{5,1},{6,2},{7,3},{8,12},{9,13},{10,... | collective-permute-start | bytes 6193160 | tf_op jit(solution)/shard_map/ppermute | solution.py:265
  49.5 48.2 %collective-permute-start.10 = (bf16[128,8064]{1,0:T(8,128)(2,1)}, bf16[128,8064]{1,0:T(8,128)(2,1)}, u32[]{:S(2)}, u32[]{:S(2)}) collective-permute-start(bf16[128,8064]{1,0:T(8,128)(2,1)} %fusion.5.refs_0_), channel_id=1, source_target_pairs={{0,1},{1,0},{2,3},{3,2},{4,5},{5,4},{6,7},{7,6},{8,9},{9,8},{10,11... | collective-permute-start | bytes 6193160 | tf_op jit(solution)/shard_map/ppermute | solution.py:265
  60.6 42.6 %collective-permute-start.9 = (bf16[64,2048]{1,0:T(8,128)(2,1)S(1)}, bf16[64,2048]{1,0:T(8,128)(2,1)S(1)}, u32[]{:S(2)}, u32[]{:S(2)}) collective-permute-start(bf16[64,2048]{1,0:T(8,128)(2,1)S(1)} %get-tuple-element.104), channel_id=1, source_target_pairs={{0,1},{1,0},{2,3},{3,2},{4,5},{5,4},{6,7},{7,6},{8,9},{9,8},{10,11... | collective-permute-start | bytes 786440 | tf_op jit(solution)/shard_map/ppermute | solution.py:265
  95.2 26.7 %collective-permute-start.13 = (bf16[64,8064]{1,0:T(8,128)(2,1)}, bf16[64,8064]{1,0:T(8,128)(2,1)}, u32[]{:S(2)}, u32[]{:S(2)}) collective-permute-start(bf16[64,8064]{1,0:T(8,128)(2,1)} %slice.77), channel_id=1, source_target_pairs={{0,1},{1,0},{2,3},{3,2},{4,5},{5,4},{6,7},{7,6},{8,9},{9,8},{10,11... | collective-permute-start | bytes 3096584 | tf_op jit(solution)/shard_map/ppermute | solution.py:265
  99.9 21.9 %collective-permute-start.12 = (bf16[64,8064]{1,0:T(8,128)(2,1)}, bf16[64,8064]{1,0:T(8,128)(2,1)S(1)}, u32[]{:S(2)}, u32[]{:S(2)}) collective-permute-start(bf16[64,8064]{1,0:T(8,128)(2,1)} %slice.76), channel_id=1, source_target_pairs={{0,4},{1,5},{2,6},{3,7},{4,0},{5,1},{6,2},{7,3},{8,12},{9,13},{10,... | collective-permute-start | bytes 3096584 | tf_op jit(solution)/shard_map/ppermute | solution.py:265
  100.5 21.9 %collective-permute-start.14 = (bf16[128,8064]{1,0:T(8,128)(2,1)}, bf16[128,8064]{1,0:T(8,128)(2,1)}, u32[]{:S(2)}, u32[]{:S(2)}) collective-permute-start(bf16[128,8064]{1,0:T(8,128)(2,1)} %fusion.5.refs_0_), channel_id=1, source_target_pairs={{0,2},{1,3},{2,0},{3,1},{4,6},{5,7},{6,4},{7,5},{8,10},{9,11},{10,... | collective-permute-start | bytes 6193160 | tf_op jit(solution)/shard_map/ppermute | solution.py:265
  100.5 24.9 %collective-permute-start.16 = (bf16[128,8064]{1,0:T(8,128)(2,1)}, bf16[128,8064]{1,0:T(8,128)(2,1)}, u32[]{:S(2)}, u32[]{:S(2)}) collective-permute-start(bf16[128,8064]{1,0:T(8,128)(2,1)} %collective-permute-done.11.refs_2_), channel_id=1, source_target_pairs={{0,2},{1,3},{2,0},{3,1},{4,6},{5,7},{6,4},{7,5},{8,10},{9,11},{10,... | collective-permute-start | bytes 6193160 | tf_op jit(solution)/shard_map/ppermute | solution.py:265
  103.2 22.8 %collective-permute-start.15 = (bf16[128,8064]{1,0:T(8,128)(2,1)}, bf16[128,8064]{1,0:T(8,128)(2,1)}, u32[]{:S(2)}, u32[]{:S(2)}) collective-permute-start(bf16[128,8064]{1,0:T(8,128)(2,1)} %collective-permute-done.10.refs_1_), channel_id=1, source_target_pairs={{0,2},{1,3},{2,0},{3,1},{4,6},{5,7},{6,4},{7,5},{8,10},{9,11},{10,... | collective-permute-start | bytes 6193160 | tf_op jit(solution)/shard_map/ppermute | solution.py:265
  148.2 23.2 %collective-permute-start.21 = (bf16[256,1920]{1,0:T(8,128)(2,1)S(1)}, bf16[256,1920]{1,0:T(8,128)(2,1)S(1)}, u32[]{:S(2)}, u32[]{:S(2)}) collective-permute-start(bf16[256,1920]{1,0:T(8,128)(2,1)S(1)} %constant_dynamic-update-slice_fusion.refs_0_), channel_id=1, source_target_pairs={{0,2},{1,3},{2,0},{3,1},{4,6},{5,7},{6,4},{7,5},{8,10},{9,11},{10,... | collective-permute-start | bytes 2949128 | tf_op jit(solution)/shard_map/ppermute | solution.py:265
  148.3 19.7 %collective-permute-start.23 = (bf16[256,1792]{1,0:T(8,128)(2,1)S(1)}, bf16[256,1792]{1,0:T(8,128)(2,1)S(1)}, u32[]{:S(2)}, u32[]{:S(2)}) collective-permute-start(bf16[256,1792]{1,0:T(8,128)(2,1)S(1)} %constant_dynamic-update-slice_fusion.2.refs_0_), channel_id=1, source_target_pairs={{0,2},{1,3},{2,0},{3,1},{4,6},{5,7},{6,4},{7,5},{8,10},{9,11},{10,... | collective-permute-start | bytes 2752520 | tf_op jit(solution)/shard_map/ppermute | solution.py:265
  148.9 25.0 %collective-permute-start.25 = (bf16[128,3200]{1,0:T(8,128)(2,1)S(1)}, bf16[128,3200]{1,0:T(8,128)(2,1)}, u32[]{:S(2)}, u32[]{:S(2)}) collective-permute-start(bf16[128,3200]{1,0:T(8,128)(2,1)S(1)} %get-tuple-element.136), channel_id=1, source_target_pairs={{0,4},{1,5},{2,6},{3,7},{4,0},{5,1},{6,2},{7,3},{8,12},{9,13},{10,... | collective-permute-start | bytes 2457608 | tf_op jit(solution)/shard_map/ppermute | solution.py:265
  150.4 23.5 %collective-permute-start.19 = (bf16[128,3200]{1,0:T(8,128)(2,1)}, bf16[128,3200]{1,0:T(8,128)(2,1)S(1)}, u32[]{:S(2)}, u32[]{:S(2)}) collective-permute-start(bf16[128,3200]{1,0:T(8,128)(2,1)} %get-tuple-element.122), channel_id=1, source_target_pairs={{0,1},{1,0},{2,3},{3,2},{4,5},{5,4},{6,7},{7,6},{8,9},{9,8},{10,11... | collective-permute-start | bytes 2457608 | tf_op jit(solution)/shard_map/ppermute | solution.py:265
  175.4 17.7 %collective-permute-start.24 = (bf16[256,3200]{1,0:T(8,128)(2,1)S(1)}, bf16[256,3200]{1,0:T(8,128)(2,1)S(1)}, u32[]{:S(2)}, u32[]{:S(2)}) collective-permute-start(bf16[256,3200]{1,0:T(8,128)(2,1)S(1)} %constant_dynamic-update-slice_fusion.4.refs_0_), channel_id=1, source_target_pairs={{0,2},{1,3},{2,0},{3,1},{4,6},{5,7},{6,4},{7,5},{8,10},{9,11},{10,... | collective-permute-start | bytes 4915208 | tf_op jit(solution)/shard_map/ppermute | solution.py:265
  191.6 20.8 %collective-permute-start.31 = (bf16[128,2688]{1,0:T(8,128)(2,1)S(1)}, bf16[128,2688]{1,0:T(8,128)(2,1)}, u32[]{:S(2)}, u32[]{:S(2)}) collective-permute-start(bf16[128,2688]{1,0:T(8,128)(2,1)S(1)} %get-tuple-element.144), channel_id=1, source_target_pairs={{0,1},{1,0},{2,3},{3,2},{4,5},{5,4},{6,7},{7,6},{8,9},{9,8},{10,11... | collective-permute-start | bytes 2064392 | tf_op jit(solution)/shard_map/ppermute | solution.py:265
  196.9 18.4 %collective-permute-start.35 = (bf16[128,2688]{1,0:T(8,128)(2,1)S(1)}, bf16[128,2688]{1,0:T(8,128)(2,1)S(1)}, u32[]{:S(2)}, u32[]{:S(2)}) collective-permute-start(bf16[128,2688]{1,0:T(8,128)(2,1)S(1)} %get-tuple-element.146), channel_id=1, source_target_pairs={{0,4},{1,5},{2,6},{3,7},{4,0},{5,1},{6,2},{7,3},{8,12},{9,13},{10,... | collective-permute-start | bytes 2064392 | tf_op jit(solution)/shard_map/ppermute | solution.py:265
  201.0 24.6 %collective-permute-start.30 = (bf16[128,2048]{1,0:T(8,128)(2,1)S(1)}, bf16[128,2048]{1,0:T(8,128)(2,1)S(1)}, u32[]{:S(2)}, u32[]{:S(2)}) collective-permute-start(bf16[128,2048]{1,0:T(8,128)(2,1)S(1)} %get-tuple-element.153), channel_id=1, source_target_pairs={{0,1},{1,0},{2,3},{3,2},{4,5},{5,4},{6,7},{7,6},{8,9},{9,8},{10,11... | collective-permute-start | bytes 1572872 | tf_op jit(solution)/shard_map/ppermute | solution.py:265
  201.6 24.0 %collective-permute-start.36 = (bf16[128,2048]{1,0:T(8,128)(2,1)S(1)}, bf16[128,2048]{1,0:T(8,128)(2,1)S(1)}, u32[]{:S(2)}, u32[]{:S(2)}) collective-permute-start(bf16[128,2048]{1,0:T(8,128)(2,1)S(1)} %get-tuple-element.163), channel_id=1, source_target_pairs={{0,4},{1,5},{2,6},{3,7},{4,0},{5,1},{6,2},{7,3},{8,12},{9,13},{10,... | collective-permute-start | bytes 1572872 | tf_op jit(solution)/shard_map/ppermute | solution.py:265
  226.4 19.2 %collective-permute-start.38 = (bf16[128,2688]{1,0:T(8,128)(2,1)S(1)}, bf16[128,2688]{1,0:T(8,128)(2,1)S(1)}, u32[]{:S(2)}, u32[]{:S(2)}) collective-permute-start(bf16[128,2688]{1,0:T(8,128)(2,1)S(1)} %get-tuple-element.226), channel_id=1, source_target_pairs={{0,8},{24,16},{1,9},{25,17},{2,10},{26,18},{3,11},{27,19},{4,12},{... | collective-permute-start | bytes 2064392 | tf_op jit(solution)/shard_map/ppermute | solution.py:632
  250.1 49.6 %collective-permute-start.58 = (bf16[128,2688]{1,0:T(8,128)(2,1)}, bf16[128,2688]{1,0:T(8,128)(2,1)S(1)}, u32[]{:S(2)}, u32[]{:S(2)}) collective-permute-start(bf16[128,2688]{1,0:T(8,128)(2,1)} %add_convert_fusion.4), channel_id=1, source_target_pairs={{8,0},{16,24},{9,1},{17,25},{10,2},{18,26},{11,3},{19,27},{12,4},{... | collective-permute-start | bytes 2064392 | tf_op jit(solution)/shard_map/ppermute | solution.py:648
  253.6 41.5 %collective-permute-start.50 = (bf16[128,2688]{1,0:T(8,128)(2,1)}, bf16[128,2688]{1,0:T(8,128)(2,1)S(1)}, u32[]{:S(2)}, u32[]{:S(2)}) collective-permute-start(bf16[128,2688]{1,0:T(8,128)(2,1)} %add_convert_fusion.2), channel_id=1, source_target_pairs={{8,16},{16,8},{9,17},{17,9},{10,18},{18,10},{11,19},{19,11},{12,20... | collective-permute-start | bytes 2064392 | tf_op jit(solution)/shard_map/ppermute | solution.py:640
  261.0 31.6 %collective-permute-start.42 = (bf16[144,1024]{1,0:T(8,128)(2,1)S(1)}, bf16[144,1024]{1,0:T(8,128)(2,1)S(1)}, u32[]{:S(2)}, u32[]{:S(2)}) collective-permute-start(bf16[144,1024]{1,0:T(8,128)(2,1)S(1)} %get-tuple-element.179), channel_id=1, source_target_pairs={{0,1},{1,0},{2,3},{3,2},{4,5},{5,4},{6,7},{7,6},{8,9},{9,8},{10,11... | collective-permute-start | bytes 884744 | tf_op jit(solution)/shard_map/ppermute | solution.py:265
  263.5 33.9 %collective-permute-start.49 = (bf16[128,1536]{1,0:T(8,128)(2,1)S(1)}, bf16[128,1536]{1,0:T(8,128)(2,1)S(1)}, u32[]{:S(2)}, u32[]{:S(2)}) collective-permute-start(bf16[128,1536]{1,0:T(8,128)(2,1)S(1)} %get-tuple-element.220), channel_id=1, source_target_pairs={{0,8},{24,16},{1,9},{25,17},{2,10},{26,18},{3,11},{27,19},{4,12},{... | collective-permute-start | bytes 1179656 | tf_op jit(solution)/shard_map/ppermute | solution.py:632
  291.3 36.5 %collective-permute-start.56 = (bf16[128,2688]{1,0:T(8,128)(2,1)S(1)}, bf16[128,2688]{1,0:T(8,128)(2,1)}, u32[]{:S(2)}, u32[]{:S(2)}) collective-permute-start(bf16[128,2688]{1,0:T(8,128)(2,1)S(1)} %add_convert_fusion.1), channel_id=1, source_target_pairs={{8,0},{16,24},{9,1},{17,25},{10,2},{18,26},{11,3},{19,27},{12,4},{... | collective-permute-start | bytes 2064392 | tf_op jit(solution)/shard_map/ppermute | solution.py:648
  292.7 17.9 %collective-permute-start.48 = (bf16[128,1536]{1,0:T(8,128)(2,1)S(1)}, bf16[128,1536]{1,0:T(8,128)(2,1)}, u32[]{:S(2)}, u32[]{:S(2)}) collective-permute-start(bf16[128,1536]{1,0:T(8,128)(2,1)S(1)} %add_convert_fusion.9), channel_id=1, source_target_pairs={{8,16},{16,8},{9,17},{17,9},{10,18},{18,10},{11,19},{19,11},{12,20... | collective-permute-start | bytes 1179656 | tf_op jit(solution)/shard_map/ppermute | solution.py:640
  296.1 30.2 %collective-permute-start.57 = (bf16[128,2688]{1,0:T(8,128)(2,1)}, bf16[128,2688]{1,0:T(8,128)(2,1)}, u32[]{:S(2)}, u32[]{:S(2)}) collective-permute-start(bf16[128,2688]{1,0:T(8,128)(2,1)} %add_convert_fusion), channel_id=1, source_target_pairs={{8,0},{16,24},{9,1},{17,25},{10,2},{18,26},{11,3},{19,27},{12,4},{... | collective-permute-start | bytes 2064392 | tf_op jit(solution)/shard_map/ppermute | solution.py:648
  298.3 17.6 %collective-permute-start.52 = (bf16[128,1536]{1,0:T(8,128)(2,1)}, bf16[128,1536]{1,0:T(8,128)(2,1)}, u32[]{:S(2)}, u32[]{:S(2)}) collective-permute-start(bf16[128,1536]{1,0:T(8,128)(2,1)} %add_convert_fusion.8), channel_id=1, source_target_pairs={{8,16},{16,8},{9,17},{17,9},{10,18},{18,10},{11,19},{19,11},{12,20... | collective-permute-start | bytes 1179656 | tf_op jit(solution)/shard_map/ppermute | solution.py:640
  311.8 30.7 %collective-permute-start.54 = (bf16[128,1536]{1,0:T(8,128)(2,1)S(1)}, bf16[128,1536]{1,0:T(8,128)(2,1)S(1)}, u32[]{:S(2)}, u32[]{:S(2)}) collective-permute-start(bf16[128,1536]{1,0:T(8,128)(2,1)S(1)} %add_convert_fusion.7), channel_id=1, source_target_pairs={{8,0},{16,24},{9,1},{17,25},{10,2},{18,26},{11,3},{19,27},{12,4},{... | collective-permute-start | bytes 1179656 | tf_op jit(solution)/shard_map/ppermute | solution.py:648
  317.1 25.3 %collective-permute-start.55 = (bf16[128,1536]{1,0:T(8,128)(2,1)S(1)}, bf16[128,1536]{1,0:T(8,128)(2,1)S(1)}, u32[]{:S(2)}, u32[]{:S(2)}) collective-permute-start(bf16[128,1536]{1,0:T(8,128)(2,1)S(1)} %add_convert_fusion.6), channel_id=1, source_target_pairs={{8,0},{16,24},{9,1},{17,25},{10,2},{18,26},{11,3},{19,27},{12,4},{... | collective-permute-start | bytes 1179656 | tf_op jit(solution)/shard_map/ppermute | solution.py:648
  318.5 27.1 %collective-permute-start.53 = (bf16[144,1024]{1,0:T(8,128)(2,1)S(1)}, bf16[144,1024]{1,0:T(8,128)(2,1)S(1)}, u32[]{:S(2)}, u32[]{:S(2)}) collective-permute-start(bf16[144,1024]{1,0:T(8,128)(2,1)S(1)} %add_convert_fusion.10), channel_id=1, source_target_pairs={{8,0},{16,24},{9,1},{17,25},{10,2},{18,26},{11,3},{19,27},{12,4},{... | collective-permute-start | bytes 884744 | tf_op jit(solution)/shard_map/ppermute | solution.py:648
  (72 other events, 754.6 us)

commit v6 on v5

--- a/solution.py
+++ b/solution.py
@@ -798,7 +798,11 @@
     gelu_other = line_middle(gelu_pair)
     chip_kv = share(keep_kv, link_kv, gelu_pair)
     chip_vk = share(keep_vk, link_vk, gelu_pair)
-    d_hidden = later(d_hidden, chip_kv, chip_vk)
+    low_own, low_sent = products(chip_kv, shard)
+    low_back = swap(low_sent, Y_BIT)
+    high_own, high_sent = products(chip_vk, shard, low_sent)
+    high_back = swap(high_sent, X_BIT)
+    d_hidden = later(d_hidden, high_sent)
     keep_o, send_o, input_grad = call(
         tokens_back_kernel,
         [((rows + 16, half + width), BF16)] * 2 + [((rows, width), BF16)],
@@ -809,39 +813,35 @@
         size=6 * width * width,
     )
     link_o = swap(send_o, Y_BIT)
-    low_own, low_sent = products(chip_kv, shard, keep_o)
-    low_back = swap(low_sent, Y_BIT)
-    high_own, high_sent = products(chip_vk, shard, low_sent)
-    high_back = swap(high_sent, X_BIT)
-    gate_pair = line_pair(gate_part, later(gate_first, high_sent))
+    gelu_total = line_total(gelu_pair, later(gelu_other, keep_o, contract_last))
+    gelu_last = line_back(gelu_total)
+    gate_pair = line_pair(gate_part, later(gate_first, gelu_total))
     gate_other = line_middle(gate_pair)
-    out_own, out_sent = grad_rows(keep_o, link_o, shard, gate_pair)
-    out_back = swap(out_sent, X_BIT)
-    low_part = low_own + later(low_back, out_sent).astype(F32)
+    low_part = low_own + later(low_back, gate_pair).astype(F32)
     low_first = line_first(low_part)
     high_part = high_own + later(high_back, low_part).astype(F32)
     high_first = line_first(high_part)
-    gelu_total = line_total(gelu_pair, later(gelu_other, high_part))
-    gelu_last = line_back(gelu_total)
-    low_pair = line_pair(low_part, later(low_first, gelu_total))
+    gate_total = line_total(gate_pair, later(gate_other, high_part))
+    gate_last = line_back(gate_total)
+    low_pair = line_pair(low_part, later(low_first, gate_total))
     low_other = line_middle(low_pair)
-    out_part = out_own + later(out_back, low_pair).astype(F32)
+    out_own, out_sent = grad_rows(keep_o, link_o, shard, low_pair)
+    out_back = swap(out_sent, X_BIT)
+    high_pair = line_pair(high_part, later(high_first, out_sent, gelu_last))
+    high_other = line_middle(high_pair)
+    out_part = out_own + later(out_back, high_pair).astype(F32)
     out_first = line_first(out_part)
-    gate_total = line_total(gate_pair, later(gate_other, out_part))
-    gate_last = line_back(gate_total)
-    high_pair = line_pair(high_part, later(high_first, gate_total))
-    high_other = line_middle(high_pair)
-    low_total = line_total(low_pair, later(low_other, high_pair))
+    low_total = line_total(low_pair, later(low_other, out_part))
     low_last = line_back(low_total)
     out_pair = line_pair(out_part, later(out_first, low_total))
     out_other = line_middle(out_pair)
-    high_total = line_total(high_pair, later(high_other, out_pair))
+    high_total = line_total(high_pair, later(high_other, out_pair, gate_last))
     high_last = line_back(high_total)
     out_total = line_total(out_pair, later(out_other, high_total))
     out_last = line_back(out_total)
-    contract_grad = line_end(contract_total, later(contract_last, high_pair))
-    gelu_grad = line_end(gelu_total, later(gelu_last, out_total))
-    gate_grad = line_end(gate_total, later(gate_last, out_total))
+    contract_grad = line_end(contract_total, later(contract_last, high_total))
+    gelu_grad = line_end(gelu_total, later(gelu_last, high_total))
+    gate_grad = line_end(gate_total, later(gate_last, high_total))
     all_grad = jnp.concatenate([line_end(low_total, low_last), line_end(high_total, high_last)], axis=1)
     out_grad = line_end(out_total, out_last)
     gain_rows = lax.dynamic_slice_in_dim(out_grad[shard : shard + 2], me * shard, shard, axis=1)

time: 348 us -> 330 us (0.948)
  waiting for transfers between devices: 161 us -> 144 us
    ppermute x6, waiting for transfers between devices: 31 us -> 20.6 us  [line_first(): return lax.ppermute(part.astype(BF16), 'replica', [(0, 1), (3, 2)])]
    ppermute x41, waiting for transfers between devices: 110 us -> 103 us  [swap(): return lax.ppermute(value, PLANE, [(i, i ^ bit) for i in range(PLANE_SIZE)])]
    unnamed x99 -> x89, local copies, waits for them, and re-layouts: 7.16 us -> 6.7 us
  transfers between devices with their start and end apart: 59 -> 59, of which waited for: 30 -> 28; matrix products, arithmetic and copies ran while one was open for 9% -> 10% of each run, Pallas kernels for 17% -> 18%
where the time goes in v6:
time: 330 us; the launch traced here: 328 us
  waiting for transfers between devices  144 us (44%)
  starting transfers between devices  76.3 us (23%)
  Pallas kernels  65.1 us (20%)
  other arithmetic  24.8 us (8%)
  local copies, waits for them, and re-layouts  16.8 us (5%)
    ppermute x41, waiting for transfers between devices, swap(): return lax.ppermute(value, PLANE, [(i, i ^ bit) for i in range(PLANE_SIZE)])  103 us
    pallas_call x15, Pallas kernels, call(): pl.pallas_call(kernel, out_shape=[jax.ShapeDtypeStruct(shape, kind) for s...  65.1 us
    ppermute x6, starting transfers between devices, line_first(): return lax.ppermute(part.astype(BF16), 'replica', [(0, 1), (3, 2)])  32.5 us
    ppermute x41, starting transfers between devices, swap(): return lax.ppermute(value, PLANE, [(i, i ^ bit) for i in range(PLANE_SIZE)])  30.3 us
    ppermute x6, waiting for transfers between devices, line_first(): return lax.ppermute(part.astype(BF16), 'replica', [(0, 1), (3, 2)])  20.6 us
    ppermute x6, waiting for transfers between devices, line_back(): return lax.ppermute(total, 'replica', [(1, 0), (2, 3)])  19.9 us
    ppermute x6, starting transfers between devices, line_back(): return lax.ppermute(total, 'replica', [(1, 0), (2, 3)])  7.85 us
    unnamed x89, local copies, waits for them, and re-layouts  6.7 us
  transfers between devices with their start and end apart: 59, of which 28 were waited for; matrix products, arithmetic and copies ran while one was open for 10% of the time, Pallas kernels for 18%

profile of v6, /device:TPU:0, one launch (start us, length us, event | category | flops | bytes accessed | tf_op | source)
XLA Modules:
  0.0 328.4 jit_solution(8309042116546364578)
XLA Ops:
  1.5 2.4 fusion.6.refs_0_.refs_10_
  3.9 3.0 collective-permute-start.1
  9.1 22.0 %collective-permute-done.1.refs_2_.refs_12_ = bf16[128,4224]{1,0:T(8,128)(2,1)} collective-permute-done((bf16[128,4224]{1,0:T(8,128)(2,1)}, bf16[128,4224]{1,0:T(8,128)(2,1)}, u32[]{:S(2)}, u32[]{:S(2)}) %collective-permute-start.1) | collective-permute-done | bytes 1081376 | tf_op jit(solution)/shard_map/ppermute | solution.py:265
  38.1 7.6 %collective-permute-done.3.refs_4_.refs_14_ = bf16[64,4224]{1,0:T(8,128)(2,1)S(1)} collective-permute-done((bf16[64,4224]{1,0:T(8,128)(2,1)S(1)}, bf16[64,4224]{1,0:T(8,128)(2,1)S(1)}, u32[]{:S(2)}, u32[]{:S(2)}) %collective-permute-start.3) | collective-permute-done | bytes 540704 | tf_op jit(solution)/shard_map/ppermute | solution.py:265
  55.8 4.7 %shard_map.161 = (bf16[128,1024]{1,0:T(8,128)(2,1)S(1)}, bf16[128,2048]{1,0:T(8,128)(2,1)S(1)}, bf16[64,2048]{1,0:T(8,128)(2,1)S(1)}, bf16[128,1024]{1,0:T(8,128)(2,1)S(1)}, f32[8,1024]{1,0:T(8,128)S(1)}) custom-call(s32[2]{0:T(128)S(1)} %pad_add_fusion.place, bf16[128,1024]{1,0:T(8,128)(2,1)S(1)} %bitcast.18, f32[128,128]{1,0:T(8,128)S(1)} %get-tuple-element.233.cosine, ...), custom_call_target="tpu_custom_call" | custom-call | flops 805306368 | bytes 8650752 | tf_op jit(solution)/shard_map/pallas_call | solution.py:592
  62.2 30.7 %collective-permute-done.11.refs_2_ = bf16[128,8064]{1,0:T(8,128)(2,1)} collective-permute-done((bf16[128,8064]{1,0:T(8,128)(2,1)}, bf16[128,8064]{1,0:T(8,128)(2,1)}, u32[]{:S(2)}, u32[]{:S(2)}) %collective-permute-start.11) | collective-permute-done | bytes 2064416 | tf_op jit(solution)/shard_map/ppermute | solution.py:265
  105.4 7.7 %shard_map.162 = (bf16[128,1024]{1,0:T(8,128)(2,1)S(1)}, f32[128,128]{1,0:T(8,128)S(1)}, f32[128,1024]{1,0:T(8,128)S(1)}, bf16[128,1024]{1,0:T(8,128)(2,1)S(1)}) custom-call(s32[2]{0:T(128)S(1)} %copy-done.24, bf16[128,1024]{1,0:T(8,128)(2,1)S(1)} %copy-done.19, bf16[128,2048]{1,0:T(8,128)(2,1)S(1)} %copy-done.12, ...), custom_call_target="tpu_custom_call" | custom-call | flops 1610612736 | bytes 4194304 | tf_op jit(solution)/shard_map/pallas_call | solution.py:592
  113.8 8.0 %collective-permute-done.13.refs_4_ = bf16[64,8064]{1,0:T(8,128)(2,1)} collective-permute-done((bf16[64,8064]{1,0:T(8,128)(2,1)}, bf16[64,8064]{1,0:T(8,128)(2,1)}, u32[]{:S(2)}, u32[]{:S(2)}) %collective-permute-start.13) | collective-permute-done | bytes 1032224 | tf_op jit(solution)/shard_map/ppermute | solution.py:265
  122.4 3.0 collective-permute-done.18.refs_9_
  127.0 7.5 %shard_map.163 = (bf16[128,1920]{1,0:T(8,128)(2,1)S(1)}, bf16[128,1920]{1,0:T(8,128)(2,1)S(1)}, bf16[128,1792]{1,0:T(8,128)(2,1)S(1)}, bf16[128,1792]{1,0:T(8,12...) custom-call(s32[2]{0:T(128)S(1)} %copy-done.24, bf16[128,1024]{1,0:T(8,128)(2,1)S(1)} %get-tuple-element.105.xn2, ...), custom_call_target="tpu_custom_call" | custom-call | flops 1409286144 | bytes 11010048 | tf_op jit(solution)/shard_map/pallas_call | solution.py:592
  136.0 8.5 %shard_map.164 = (bf16[128,1024]{1,0:T(8,128)(2,1)}, bf16[128,3200]{1,0:T(8,128)(2,1)S(1)}, bf16[128,3200]{1,0:T(8,128)(2,1)}, bf16[128,3200]{1,0:T(8,128)(2,1)}, bf16[128,3200]{1,0:T(8,128)(2,1)}) custom-call(s32[2]{0:T(128)S(1)} %copy-done.24, bf16[128,1920]{1,0:T(8,128)(2,1)S(1)} %get-tuple-element.123.gated_one, ...), custom_call_target="tpu_custom_call" | custom-call | flops 1409286144 | bytes 5505024 | tf_op jit(solution)/shard_map/pallas_call | solution.py:592
  144.5 2.5 collective-permute-done.22
  150.9 10.7 %shard_map.165 = (f32[128,1024]{1,0:T(8,128)S(1)}, bf16[128,1024]{1,0:T(8,128)(2,1)S(1)}, f32[1,1024]{1,0:T(1,128)S(1)}) custom-call(s32[2]{0:T(128)S(1)} %copy-done.24, bf16[128,3200]{1,0:T(8,128)(2,1)} %copy-done.5, bf16[128,3200]{1,0:T(8,128)(2,1)} %get-tuple-element.133.pack_two, bf16[128,1024]{1,0:T(8,128)(2,1)S(1)} %bitcast.17, ...), custom_call_target="tpu_custom_call" | custom-call | flops 2113929216 | bytes 16515072 | tf_op jit(solution)/shard_map/pallas_call | solution.py:592
  161.6 6.3 %shard_map.166 = (bf16[128,1024]{1,0:T(8,128)(2,1)S(1)}, f32[128,2048]{1,0:T(8,128)S(1)}, bf16[64,2048]{1,0:T(8,128)(2,1)S(1)}) custom-call(s32[2]{0:T(128)S(1)} %copy-done.24, bf16[128,1024]{1,0:T(8,128)(2,1)S(1)} %copy-done.20, bf16[128,2048]{1,0:T(8,128)(2,1)S(1)} %copy-done.13, bf16[64,2048]{1,0:T(8,128)(2,1)S(1)} %copy-done.22, ...), custom_call_target="tpu_custom_call" | custom-call | flops 2684354560 | bytes 4194304 | tf_op jit(solution)/shard_map/pallas_call | solution.py:592
  175.9 3.1 collective-permute-done.28
  179.0 3.8 %collective-permute-done.27 = bf16[128,1408]{1,0:T(8,128)(2,1)S(1)} collective-permute-done((bf16[128,1408]{1,0:T(8,128)(2,1)S(1)}, bf16[128,1408]{1,0:T(8,128)(2,1)S(1)}, u32[]{:S(2)}, u32[]{:S(2)}) %collective-permute-start.27) | collective-permute-done | bytes 360480 | tf_op jit(solution)/shard_map/ppermute | solution.py:265
  184.0 3.5 %collective-permute-start.32 = (bf16[128,2688]{1,0:T(8,128)(2,1)S(1)}, bf16[128,2688]{1,0:T(8,128)(2,1)S(1)}, u32[]{:S(2)}, u32[]{:S(2)}) collective-permute-start(bf16[128,2688]{1,0:T(8,128)(2,1)S(1)} %fusion.9), channel_id=1, source_target_pairs={{0,8},{24,16},{1,9},{25,17},{2,10},{26,18},{3,11},{27,19},{4,12},{... | collective-permute-start | bytes 2064392 | tf_op jit(solution)/shard_map/ppermute | solution.py:632
  188.1 2.6 shard_map.169
  192.3 2.6 shard_map.170
  198.0 2.7 collective-permute-done.32
  202.5 9.1 %collective-permute-done.31 = bf16[128,2688]{1,0:T(8,128)(2,1)} collective-permute-done((bf16[128,2688]{1,0:T(8,128)(2,1)S(1)}, bf16[128,2688]{1,0:T(8,128)(2,1)}, u32[]{:S(2)}, u32[]{:S(2)}) %collective-permute-start.31) | collective-permute-done | bytes 688160 | tf_op jit(solution)/shard_map/ppermute | solution.py:265
  216.7 7.0 %collective-permute-done.33 = bf16[128,2688]{1,0:T(8,128)(2,1)S(1)} collective-permute-done((bf16[128,2688]{1,0:T(8,128)(2,1)S(1)}, bf16[128,2688]{1,0:T(8,128)(2,1)S(1)}, u32[]{:S(2)}, u32[]{:S(2)}) %collective-permute-start.33) | collective-permute-done | bytes 688160 | tf_op jit(solution)/shard_map/ppermute | solution.py:632
  227.5 6.6 %collective-permute-start.41 = (bf16[128,2688]{1,0:T(8,128)(2,1)}, bf16[128,2688]{1,0:T(8,128)(2,1)S(1)}, u32[]{:S(2)}, u32[]{:S(2)}) collective-permute-start(bf16[128,2688]{1,0:T(8,128)(2,1)} %get-tuple-element.224), channel_id=1, source_target_pairs={{0,8},{24,16},{1,9},{25,17},{2,10},{26,18},{3,11},{27,19},{4,12},{... | collective-permute-start | bytes 2064392 | tf_op jit(solution)/shard_map/ppermute | solution.py:632
  238.0 6.3 %shard_map.174 = (bf16[144,1536]{1,0:T(8,128)(2,1)S(1)}, bf16[144,1536]{1,0:T(8,128)(2,1)S(1)}, bf16[128,1024]{1,0:T(8,128)(2,1)}) custom-call(s32[2]{0:T(128)S(1)} %copy-done.24, bf16[128,2048]{1,0:T(8,128)(2,1)S(1)} %get-tuple-element.163.pack_one, bf16[128,2048]{1,0:T(8,128)(2,1)S(1)} %get-tuple-element.160.pack_two, bf16[128,1024]{1,0:T(8,128)(2,1)S(1)} %bitcast.20, ...), custom_call_target="tpu_custom_call" | custom-call | flops 805306368 | bytes 6291456 | tf_op jit(solution)/shard_map/pallas_call | solution.py:592
  250.3 6.0 %collective-permute-start.44 = (bf16[128,1536]{1,0:T(8,128)(2,1)S(1)}, bf16[128,1536]{1,0:T(8,128)(2,1)S(1)}, u32[]{:S(2)}, u32[]{:S(2)}) collective-permute-start(bf16[128,1536]{1,0:T(8,128)(2,1)S(1)} %get-tuple-element.222), channel_id=1, source_target_pairs={{0,8},{24,16},{1,9},{25,17},{2,10},{26,18},{3,11},{27,19},{4,12},{... | collective-permute-start | bytes 1179656 | tf_op jit(solution)/shard_map/ppermute | solution.py:632
  258.2 5.0 %collective-permute-done.44 = bf16[128,1536]{1,0:T(8,128)(2,1)S(1)} collective-permute-done((bf16[128,1536]{1,0:T(8,128)(2,1)S(1)}, bf16[128,1536]{1,0:T(8,128)(2,1)S(1)}, u32[]{:S(2)}, u32[]{:S(2)}) %collective-permute-start.44) | collective-permute-done | bytes 393248 | tf_op jit(solution)/shard_map/ppermute | solution.py:632
  265.6 10.9 %collective-permute-start.49 = (bf16[128,1536]{1,0:T(8,128)(2,1)}, bf16[128,1536]{1,0:T(8,128)(2,1)}, u32[]{:S(2)}, u32[]{:S(2)}) collective-permute-start(bf16[128,1536]{1,0:T(8,128)(2,1)} %get-tuple-element.220), channel_id=1, source_target_pairs={{0,8},{24,16},{1,9},{25,17},{2,10},{26,18},{3,11},{27,19},{4,12},{... | collective-permute-start | bytes 1179656 | tf_op jit(solution)/shard_map/ppermute | solution.py:632
  281.6 7.9 %collective-permute-done.50 = bf16[128,2688]{1,0:T(8,128)(2,1)} collective-permute-done((bf16[128,2688]{1,0:T(8,128)(2,1)}, bf16[128,2688]{1,0:T(8,128)(2,1)}, u32[]{:S(2)}, u32[]{:S(2)}) %collective-permute-start.50) | collective-permute-done | bytes 688160 | tf_op jit(solution)/shard_map/ppermute | solution.py:648
  291.4 4.0 %collective-permute-start.51 = (bf16[144,1024]{1,0:T(8,128)(2,1)S(1)}, bf16[144,1024]{1,0:T(8,128)(2,1)S(1)}, u32[]{:S(2)}, u32[]{:S(2)}) collective-permute-start(bf16[144,1024]{1,0:T(8,128)(2,1)S(1)} %get-tuple-element.218), channel_id=1, source_target_pairs={{0,8},{24,16},{1,9},{25,17},{2,10},{26,18},{3,11},{27,19},{4,12},{... | collective-permute-start | bytes 884744 | tf_op jit(solution)/shard_map/ppermute | solution.py:632
  296.8 3.9 %collective-permute-done.51 = bf16[144,1024]{1,0:T(8,128)(2,1)S(1)} collective-permute-done((bf16[144,1024]{1,0:T(8,128)(2,1)S(1)}, bf16[144,1024]{1,0:T(8,128)(2,1)S(1)}, u32[]{:S(2)}, u32[]{:S(2)}) %collective-permute-start.51) | collective-permute-done | bytes 294944 | tf_op jit(solution)/shard_map/ppermute | solution.py:632
  315.0 6.1 %collective-permute-done.58 = bf16[128,1536]{1,0:T(8,128)(2,1)} collective-permute-done((bf16[128,1536]{1,0:T(8,128)(2,1)S(1)}, bf16[128,1536]{1,0:T(8,128)(2,1)}, u32[]{:S(2)}, u32[]{:S(2)}) %collective-permute-start.58) | collective-permute-done | bytes 393248 | tf_op jit(solution)/shard_map/ppermute | solution.py:648
  323.4 3.5 %collective-permute-done.56 = bf16[144,1024]{1,0:T(8,128)(2,1)S(1)} collective-permute-done((bf16[144,1024]{1,0:T(8,128)(2,1)S(1)}, bf16[144,1024]{1,0:T(8,128)(2,1)S(1)}, u32[]{:S(2)}, u32[]{:S(2)}) %collective-permute-start.56) | collective-permute-done | bytes 294944 | tf_op jit(solution)/shard_map/ppermute | solution.py:648
  (247 shorter events, 107.5 us)
Async XLA Ops:
  3.9 27.1 %collective-permute-start.1 = (bf16[128,4224]{1,0:T(8,128)(2,1)}, bf16[128,4224]{1,0:T(8,128)(2,1)}, u32[]{:S(2)}, u32[]{:S(2)}) collective-permute-start(bf16[128,4224]{1,0:T(8,128)(2,1)} %fusion.6.refs_0_.refs_10_), channel_id=1, source_target_pairs={{0,4},{1,5},{2,6},{3,7},{4,0},{5,1},{6,2},{7,3},{8,12},{9,13},{10,... | collective-permute-start | bytes 3244040 | tf_op jit(solution)/shard_map/ppermute | solution.py:265
  6.9 27.0 %collective-permute-start = (bf16[128,4224]{1,0:T(8,128)(2,1)}, bf16[128,4224]{1,0:T(8,128)(2,1)}, u32[]{:S(2)}, u32[]{:S(2)}) collective-permute-start(bf16[128,4224]{1,0:T(8,128)(2,1)} %fusion.6.refs_0_.refs_10_), channel_id=1, source_target_pairs={{0,1},{1,0},{2,3},{3,2},{4,5},{5,4},{6,7},{7,6},{8,9},{9,8},{10,11... | collective-permute-start | bytes 3244040 | tf_op jit(solution)/shard_map/ppermute | solution.py:265
  8.4 42.2 %collective-permute-start.4 = (bf16[128,4224]{1,0:T(8,128)(2,1)}, bf16[128,4224]{1,0:T(8,128)(2,1)}, u32[]{:S(2)}, u32[]{:S(2)}) collective-permute-start(bf16[128,4224]{1,0:T(8,128)(2,1)} %fusion.6.refs_0_.refs_10_), channel_id=1, source_target_pairs={{0,2},{1,3},{2,0},{3,1},{4,6},{5,7},{6,4},{7,5},{8,10},{9,11},{10,... | collective-permute-start | bytes 3244040 | tf_op jit(solution)/shard_map/ppermute | solution.py:265
  48.0 44.9 %collective-permute-start.11 = (bf16[128,8064]{1,0:T(8,128)(2,1)}, bf16[128,8064]{1,0:T(8,128)(2,1)}, u32[]{:S(2)}, u32[]{:S(2)}) collective-permute-start(bf16[128,8064]{1,0:T(8,128)(2,1)} %fusion.5.refs_0_), channel_id=1, source_target_pairs={{0,4},{1,5},{2,6},{3,7},{4,0},{5,1},{6,2},{7,3},{8,12},{9,13},{10,... | collective-permute-start | bytes 6193160 | tf_op jit(solution)/shard_map/ppermute | solution.py:265
  49.5 48.2 %collective-permute-start.10 = (bf16[128,8064]{1,0:T(8,128)(2,1)}, bf16[128,8064]{1,0:T(8,128)(2,1)}, u32[]{:S(2)}, u32[]{:S(2)}) collective-permute-start(bf16[128,8064]{1,0:T(8,128)(2,1)} %fusion.5.refs_0_), channel_id=1, source_target_pairs={{0,1},{1,0},{2,3},{3,2},{4,5},{5,4},{6,7},{7,6},{8,9},{9,8},{10,11... | collective-permute-start | bytes 6193160 | tf_op jit(solution)/shard_map/ppermute | solution.py:265
  60.6 42.5 %collective-permute-start.9 = (bf16[64,2048]{1,0:T(8,128)(2,1)S(1)}, bf16[64,2048]{1,0:T(8,128)(2,1)S(1)}, u32[]{:S(2)}, u32[]{:S(2)}) collective-permute-start(bf16[64,2048]{1,0:T(8,128)(2,1)S(1)} %get-tuple-element.103), channel_id=1, source_target_pairs={{0,1},{1,0},{2,3},{3,2},{4,5},{5,4},{6,7},{7,6},{8,9},{9,8},{10,11... | collective-permute-start | bytes 786440 | tf_op jit(solution)/shard_map/ppermute | solution.py:265
  95.2 26.7 %collective-permute-start.13 = (bf16[64,8064]{1,0:T(8,128)(2,1)}, bf16[64,8064]{1,0:T(8,128)(2,1)}, u32[]{:S(2)}, u32[]{:S(2)}) collective-permute-start(bf16[64,8064]{1,0:T(8,128)(2,1)} %slice.77), channel_id=1, source_target_pairs={{0,1},{1,0},{2,3},{3,2},{4,5},{5,4},{6,7},{7,6},{8,9},{9,8},{10,11... | collective-permute-start | bytes 3096584 | tf_op jit(solution)/shard_map/ppermute | solution.py:265
  99.9 21.9 %collective-permute-start.12 = (bf16[64,8064]{1,0:T(8,128)(2,1)}, bf16[64,8064]{1,0:T(8,128)(2,1)S(1)}, u32[]{:S(2)}, u32[]{:S(2)}) collective-permute-start(bf16[64,8064]{1,0:T(8,128)(2,1)} %slice.76), channel_id=1, source_target_pairs={{0,4},{1,5},{2,6},{3,7},{4,0},{5,1},{6,2},{7,3},{8,12},{9,13},{10,... | collective-permute-start | bytes 3096584 | tf_op jit(solution)/shard_map/ppermute | solution.py:265
  100.5 21.9 %collective-permute-start.14 = (bf16[128,8064]{1,0:T(8,128)(2,1)}, bf16[128,8064]{1,0:T(8,128)(2,1)}, u32[]{:S(2)}, u32[]{:S(2)}) collective-permute-start(bf16[128,8064]{1,0:T(8,128)(2,1)} %fusion.5.refs_0_), channel_id=1, source_target_pairs={{0,2},{1,3},{2,0},{3,1},{4,6},{5,7},{6,4},{7,5},{8,10},{9,11},{10,... | collective-permute-start | bytes 6193160 | tf_op jit(solution)/shard_map/ppermute | solution.py:265
  100.5 24.9 %collective-permute-start.16 = (bf16[128,8064]{1,0:T(8,128)(2,1)}, bf16[128,8064]{1,0:T(8,128)(2,1)}, u32[]{:S(2)}, u32[]{:S(2)}) collective-permute-start(bf16[128,8064]{1,0:T(8,128)(2,1)} %collective-permute-done.11.refs_2_), channel_id=1, source_target_pairs={{0,2},{1,3},{2,0},{3,1},{4,6},{5,7},{6,4},{7,5},{8,10},{9,11},{10,... | collective-permute-start | bytes 6193160 | tf_op jit(solution)/shard_map/ppermute | solution.py:265
  103.2 22.8 %collective-permute-start.15 = (bf16[128,8064]{1,0:T(8,128)(2,1)}, bf16[128,8064]{1,0:T(8,128)(2,1)}, u32[]{:S(2)}, u32[]{:S(2)}) collective-permute-start(bf16[128,8064]{1,0:T(8,128)(2,1)} %collective-permute-done.10.refs_1_), channel_id=1, source_target_pairs={{0,2},{1,3},{2,0},{3,1},{4,6},{5,7},{6,4},{7,5},{8,10},{9,11},{10,... | collective-permute-start | bytes 6193160 | tf_op jit(solution)/shard_map/ppermute | solution.py:265
  148.1 23.1 %collective-permute-start.21 = (bf16[256,1920]{1,0:T(8,128)(2,1)S(1)}, bf16[256,1920]{1,0:T(8,128)(2,1)S(1)}, u32[]{:S(2)}, u32[]{:S(2)}) collective-permute-start(bf16[256,1920]{1,0:T(8,128)(2,1)S(1)} %constant_dynamic-update-slice_fusion.refs_0_), channel_id=1, source_target_pairs={{0,2},{1,3},{2,0},{3,1},{4,6},{5,7},{6,4},{7,5},{8,10},{9,11},{10,... | collective-permute-start | bytes 2949128 | tf_op jit(solution)/shard_map/ppermute | solution.py:265
  148.2 19.7 %collective-permute-start.23 = (bf16[256,1792]{1,0:T(8,128)(2,1)S(1)}, bf16[256,1792]{1,0:T(8,128)(2,1)S(1)}, u32[]{:S(2)}, u32[]{:S(2)}) collective-permute-start(bf16[256,1792]{1,0:T(8,128)(2,1)S(1)} %constant_dynamic-update-slice_fusion.2.refs_0_), channel_id=1, source_target_pairs={{0,2},{1,3},{2,0},{3,1},{4,6},{5,7},{6,4},{7,5},{8,10},{9,11},{10,... | collective-permute-start | bytes 2752520 | tf_op jit(solution)/shard_map/ppermute | solution.py:265
  148.8 25.0 %collective-permute-start.25 = (bf16[128,3200]{1,0:T(8,128)(2,1)}, bf16[128,3200]{1,0:T(8,128)(2,1)}, u32[]{:S(2)}, u32[]{:S(2)}) collective-permute-start(bf16[128,3200]{1,0:T(8,128)(2,1)} %get-tuple-element.135), channel_id=1, source_target_pairs={{0,4},{1,5},{2,6},{3,7},{4,0},{5,1},{6,2},{7,3},{8,12},{9,13},{10,... | collective-permute-start | bytes 2457608 | tf_op jit(solution)/shard_map/ppermute | solution.py:265
  150.3 23.5 %collective-permute-start.19 = (bf16[128,3200]{1,0:T(8,128)(2,1)}, bf16[128,3200]{1,0:T(8,128)(2,1)S(1)}, u32[]{:S(2)}, u32[]{:S(2)}) collective-permute-start(bf16[128,3200]{1,0:T(8,128)(2,1)} %get-tuple-element.121), channel_id=1, source_target_pairs={{0,1},{1,0},{2,3},{3,2},{4,5},{5,4},{6,7},{7,6},{8,9},{9,8},{10,11... | collective-permute-start | bytes 2457608 | tf_op jit(solution)/shard_map/ppermute | solution.py:265
  175.3 17.0 %collective-permute-start.24 = (bf16[256,3200]{1,0:T(8,128)(2,1)S(1)}, bf16[256,3200]{1,0:T(8,128)(2,1)}, u32[]{:S(2)}, u32[]{:S(2)}) collective-permute-start(bf16[256,3200]{1,0:T(8,128)(2,1)S(1)} %constant_dynamic-update-slice_fusion.4.refs_0_), channel_id=1, source_target_pairs={{0,2},{1,3},{2,0},{3,1},{4,6},{5,7},{6,4},{7,5},{8,10},{9,11},{10,... | collective-permute-start | bytes 4915208 | tf_op jit(solution)/shard_map/ppermute | solution.py:265
  184.0 16.6 %collective-permute-start.32 = (bf16[128,2688]{1,0:T(8,128)(2,1)S(1)}, bf16[128,2688]{1,0:T(8,128)(2,1)S(1)}, u32[]{:S(2)}, u32[]{:S(2)}) collective-permute-start(bf16[128,2688]{1,0:T(8,128)(2,1)S(1)} %fusion.9), channel_id=1, source_target_pairs={{0,8},{24,16},{1,9},{25,17},{2,10},{26,18},{3,11},{27,19},{4,12},{... | collective-permute-start | bytes 2064392 | tf_op jit(solution)/shard_map/ppermute | solution.py:632
  190.7 20.9 %collective-permute-start.31 = (bf16[128,2688]{1,0:T(8,128)(2,1)S(1)}, bf16[128,2688]{1,0:T(8,128)(2,1)}, u32[]{:S(2)}, u32[]{:S(2)}) collective-permute-start(bf16[128,2688]{1,0:T(8,128)(2,1)S(1)} %get-tuple-element.143), channel_id=1, source_target_pairs={{0,1},{1,0},{2,3},{3,2},{4,5},{5,4},{6,7},{7,6},{8,9},{9,8},{10,11... | collective-permute-start | bytes 2064392 | tf_op jit(solution)/shard_map/ppermute | solution.py:265
  194.9 19.6 %collective-permute-start.35 = (bf16[128,2688]{1,0:T(8,128)(2,1)S(1)}, bf16[128,2688]{1,0:T(8,128)(2,1)}, u32[]{:S(2)}, u32[]{:S(2)}) collective-permute-start(bf16[128,2688]{1,0:T(8,128)(2,1)S(1)} %get-tuple-element.145), channel_id=1, source_target_pairs={{0,4},{1,5},{2,6},{3,7},{4,0},{5,1},{6,2},{7,3},{8,12},{9,13},{10,... | collective-permute-start | bytes 2064392 | tf_op jit(solution)/shard_map/ppermute | solution.py:265
  200.6 23.3 %collective-permute-start.30 = (bf16[128,2048]{1,0:T(8,128)(2,1)S(1)}, bf16[128,2048]{1,0:T(8,128)(2,1)S(1)}, u32[]{:S(2)}, u32[]{:S(2)}) collective-permute-start(bf16[128,2048]{1,0:T(8,128)(2,1)S(1)} %get-tuple-element.152), channel_id=1, source_target_pairs={{0,4},{1,5},{2,6},{3,7},{4,0},{5,1},{6,2},{7,3},{8,12},{9,13},{10,... | collective-permute-start | bytes 1572872 | tf_op jit(solution)/shard_map/ppermute | solution.py:265
  201.1 22.7 %collective-permute-start.37 = (bf16[128,2048]{1,0:T(8,128)(2,1)S(1)}, bf16[128,2048]{1,0:T(8,128)(2,1)S(1)}, u32[]{:S(2)}, u32[]{:S(2)}) collective-permute-start(bf16[128,2048]{1,0:T(8,128)(2,1)S(1)} %get-tuple-element.162), channel_id=1, source_target_pairs={{0,1},{1,0},{2,3},{3,2},{4,5},{5,4},{6,7},{7,6},{8,9},{9,8},{10,11... | collective-permute-start | bytes 1572872 | tf_op jit(solution)/shard_map/ppermute | solution.py:265
  224.7 19.6 %collective-permute-start.43 = (bf16[128,2688]{1,0:T(8,128)(2,1)S(1)}, bf16[128,2688]{1,0:T(8,128)(2,1)S(1)}, u32[]{:S(2)}, u32[]{:S(2)}) collective-permute-start(bf16[128,2688]{1,0:T(8,128)(2,1)S(1)} %add_convert_fusion.4), channel_id=1, source_target_pairs={{8,0},{16,24},{9,1},{17,25},{10,2},{18,26},{11,3},{19,27},{12,4},{... | collective-permute-start | bytes 2064392 | tf_op jit(solution)/shard_map/ppermute | solution.py:648
  226.0 18.4 %collective-permute-start.42 = (bf16[128,2688]{1,0:T(8,128)(2,1)S(1)}, bf16[128,2688]{1,0:T(8,128)(2,1)}, u32[]{:S(2)}, u32[]{:S(2)}) collective-permute-start(bf16[128,2688]{1,0:T(8,128)(2,1)S(1)} %add_convert_fusion.3), channel_id=1, source_target_pairs={{8,16},{16,8},{9,17},{17,9},{10,18},{18,10},{11,19},{19,11},{12,20... | collective-permute-start | bytes 2064392 | tf_op jit(solution)/shard_map/ppermute | solution.py:640
  227.5 21.3 %collective-permute-start.41 = (bf16[128,2688]{1,0:T(8,128)(2,1)}, bf16[128,2688]{1,0:T(8,128)(2,1)S(1)}, u32[]{:S(2)}, u32[]{:S(2)}) collective-permute-start(bf16[128,2688]{1,0:T(8,128)(2,1)} %get-tuple-element.224), channel_id=1, source_target_pairs={{0,8},{24,16},{1,9},{25,17},{2,10},{26,18},{3,11},{27,19},{4,12},{... | collective-permute-start | bytes 2064392 | tf_op jit(solution)/shard_map/ppermute | solution.py:632
  235.0 15.2 %collective-permute-start.40 = (bf16[128,1536]{1,0:T(8,128)(2,1)S(1)}, bf16[128,1536]{1,0:T(8,128)(2,1)S(1)}, u32[]{:S(2)}, u32[]{:S(2)}) collective-permute-start(bf16[128,1536]{1,0:T(8,128)(2,1)S(1)} %get-tuple-element.165), channel_id=1, source_target_pairs={{0,4},{1,5},{2,6},{3,7},{4,0},{5,1},{6,2},{7,3},{8,12},{9,13},{10,... | collective-permute-start | bytes 1179656 | tf_op jit(solution)/shard_map/ppermute | solution.py:265
  236.4 19.9 %collective-permute-start.46 = (bf16[128,1536]{1,0:T(8,128)(2,1)S(1)}, bf16[128,1536]{1,0:T(8,128)(2,1)S(1)}, u32[]{:S(2)}, u32[]{:S(2)}) collective-permute-start(bf16[128,1536]{1,0:T(8,128)(2,1)S(1)} %get-tuple-element.167), channel_id=1, source_target_pairs={{0,1},{1,0},{2,3},{3,2},{4,5},{5,4},{6,7},{7,6},{8,9},{9,8},{10,11... | collective-permute-start | bytes 1179656 | tf_op jit(solution)/shard_map/ppermute | solution.py:265
  248.8 15.1 %collective-permute-start.39 = (bf16[144,1536]{1,0:T(8,128)(2,1)S(1)}, bf16[144,1536]{1,0:T(8,128)(2,1)S(1)}, u32[]{:S(2)}, u32[]{:S(2)}) collective-permute-start(bf16[144,1536]{1,0:T(8,128)(2,1)S(1)} %get-tuple-element.172), channel_id=1, source_target_pairs={{0,4},{1,5},{2,6},{3,7},{4,0},{5,1},{6,2},{7,3},{8,12},{9,13},{10,... | collective-permute-start | bytes 1327112 | tf_op jit(solution)/shard_map/ppermute | solution.py:265
  264.1 25.4 %collective-permute-start.50 = (bf16[128,2688]{1,0:T(8,128)(2,1)}, bf16[128,2688]{1,0:T(8,128)(2,1)}, u32[]{:S(2)}, u32[]{:S(2)}) collective-permute-start(bf16[128,2688]{1,0:T(8,128)(2,1)} %add_convert_fusion.2), channel_id=1, source_target_pairs={{8,0},{16,24},{9,1},{17,25},{10,2},{18,26},{11,3},{19,27},{12,4},{... | collective-permute-start | bytes 2064392 | tf_op jit(solution)/shard_map/ppermute | solution.py:648
  265.6 23.9 %collective-permute-start.49 = (bf16[128,1536]{1,0:T(8,128)(2,1)}, bf16[128,1536]{1,0:T(8,128)(2,1)}, u32[]{:S(2)}, u32[]{:S(2)}) collective-permute-start(bf16[128,1536]{1,0:T(8,128)(2,1)} %get-tuple-element.220), channel_id=1, source_target_pairs={{0,8},{24,16},{1,9},{25,17},{2,10},{26,18},{3,11},{27,19},{4,12},{... | collective-permute-start | bytes 1179656 | tf_op jit(solution)/shard_map/ppermute | solution.py:632
  276.4 27.7 %collective-permute-start.55 = (bf16[128,2688]{1,0:T(8,128)(2,1)S(1)}, bf16[128,2688]{1,0:T(8,128)(2,1)S(1)}, u32[]{:S(2)}, u32[]{:S(2)}) collective-permute-start(bf16[128,2688]{1,0:T(8,128)(2,1)S(1)} %copy-done.30), channel_id=1, source_target_pairs={{8,0},{16,24},{9,1},{17,25},{10,2},{18,26},{11,3},{19,27},{12,4},{... | collective-permute-start | bytes 2064392 | tf_op jit(solution)/shard_map/ppermute | solution.py:648
  295.5 17.1 %collective-permute-start.57 = (bf16[128,1536]{1,0:T(8,128)(2,1)S(1)}, bf16[128,1536]{1,0:T(8,128)(2,1)S(1)}, u32[]{:S(2)}, u32[]{:S(2)}) collective-permute-start(bf16[128,1536]{1,0:T(8,128)(2,1)S(1)} %add_convert_fusion.7), channel_id=1, source_target_pairs={{8,0},{16,24},{9,1},{17,25},{10,2},{18,26},{11,3},{19,27},{12,4},{... | collective-permute-start | bytes 1179656 | tf_op jit(solution)/shard_map/ppermute | solution.py:648
  305.0 16.1 %collective-permute-start.58 = (bf16[128,1536]{1,0:T(8,128)(2,1)S(1)}, bf16[128,1536]{1,0:T(8,128)(2,1)}, u32[]{:S(2)}, u32[]{:S(2)}) collective-permute-start(bf16[128,1536]{1,0:T(8,128)(2,1)S(1)} %add_convert_fusion.6), channel_id=1, source_target_pairs={{8,0},{16,24},{9,1},{17,25},{10,2},{18,26},{11,3},{19,27},{12,4},{... | collective-permute-start | bytes 1179656 | tf_op jit(solution)/shard_map/ppermute | solution.py:648
  (67 other events, 721.4 us)

commit v7 on v6

--- a/solution.py
+++ b/solution.py
@@ -823,11 +823,11 @@
     high_first = line_first(high_part)
     gate_total = line_total(gate_pair, later(gate_other, high_part))
     gate_last = line_back(gate_total)
-    low_pair = line_pair(low_part, later(low_first, gate_total))
+    low_pair = line_pair(low_part, later(low_first, gate_total, gelu_last))
     low_other = line_middle(low_pair)
     out_own, out_sent = grad_rows(keep_o, link_o, shard, low_pair)
     out_back = swap(out_sent, X_BIT)
-    high_pair = line_pair(high_part, later(high_first, out_sent, gelu_last))
+    high_pair = line_pair(high_part, later(high_first, out_sent))
     high_other = line_middle(high_pair)
     out_part = out_own + later(out_back, high_pair).astype(F32)
     out_first = line_first(out_part)

time: 330 us -> 323 us (0.979)
  waiting for transfers between devices: 144 us -> 137 us
    ppermute x6, waiting for transfers between devices: 19.9 us -> 13.1 us  [line_back(): return lax.ppermute(total, 'replica', [(1, 0), (2, 3)])]
    unnamed x89 -> x97, local copies, waits for them, and re-layouts: 6.7 us -> 6.93 us
  transfers between devices with their start and end apart: 59 -> 59, of which waited for: 28 -> 27; matrix products, arithmetic and copies ran while one was open for 10% -> 10% of each run, Pallas kernels for 18% -> 18%
where the time goes in v7:
time: 323 us; the launch traced here: 321 us
  waiting for transfers between devices  137 us (42%)
  starting transfers between devices  77.1 us (24%)
  Pallas kernels  65.1 us (20%)
  other arithmetic  23.9 us (7%)
  local copies, waits for them, and re-layouts  17 us (5%)
    ppermute x41, waiting for transfers between devices, swap(): return lax.ppermute(value, PLANE, [(i, i ^ bit) for i in range(PLANE_SIZE)])  106 us
    pallas_call x15, Pallas kernels, call(): pl.pallas_call(kernel, out_shape=[jax.ShapeDtypeStruct(shape, kind) for s...  65.1 us
    ppermute x6, starting transfers between devices, line_first(): return lax.ppermute(part.astype(BF16), 'replica', [(0, 1), (3, 2)])  33.4 us
    ppermute x41, starting transfers between devices, swap(): return lax.ppermute(value, PLANE, [(i, i ^ bit) for i in range(PLANE_SIZE)])  30.3 us
    ppermute x6, waiting for transfers between devices, line_first(): return lax.ppermute(part.astype(BF16), 'replica', [(0, 1), (3, 2)])  17.9 us
    ppermute x6, waiting for transfers between devices, line_back(): return lax.ppermute(total, 'replica', [(1, 0), (2, 3)])  13.1 us
    ppermute x6, starting transfers between devices, line_back(): return lax.ppermute(total, 'replica', [(1, 0), (2, 3)])  7.72 us
    unnamed x97, local copies, waits for them, and re-layouts  6.93 us
  transfers between devices with their start and end apart: 59, of which 27 were waited for; matrix products, arithmetic and copies ran while one was open for 10% of the time, Pallas kernels for 18%

profile of v7, /device:TPU:0, one launch (start us, length us, event | category | flops | bytes accessed | tf_op | source)
XLA Modules:
  0.0 321.4 jit_solution(7537663342288410602)
XLA Ops:
  3.9 3.0 collective-permute-start.1
  9.1 22.0 %collective-permute-done.1.refs_2_.refs_12_ = bf16[128,4224]{1,0:T(8,128)(2,1)} collective-permute-done((bf16[128,4224]{1,0:T(8,128)(2,1)}, bf16[128,4224]{1,0:T(8,128)(2,1)}, u32[]{:S(2)}, u32[]{:S(2)}) %collective-permute-start.1) | collective-permute-done | bytes 1081376 | tf_op jit(solution)/shard_map/ppermute | solution.py:265
  38.1 7.6 %collective-permute-done.3.refs_4_.refs_14_ = bf16[64,4224]{1,0:T(8,128)(2,1)S(1)} collective-permute-done((bf16[64,4224]{1,0:T(8,128)(2,1)S(1)}, bf16[64,4224]{1,0:T(8,128)(2,1)S(1)}, u32[]{:S(2)}, u32[]{:S(2)}) %collective-permute-start.3) | collective-permute-done | bytes 540704 | tf_op jit(solution)/shard_map/ppermute | solution.py:265
  55.8 4.7 %shard_map.161 = (bf16[128,1024]{1,0:T(8,128)(2,1)S(1)}, bf16[128,2048]{1,0:T(8,128)(2,1)S(1)}, bf16[64,2048]{1,0:T(8,128)(2,1)S(1)}, bf16[128,1024]{1,0:T(8,128)(2,1)S(1)}, f32[8,1024]{1,0:T(8,128)S(1)}) custom-call(s32[2]{0:T(128)S(1)} %pad_add_fusion.place, bf16[128,1024]{1,0:T(8,128)(2,1)S(1)} %bitcast.18, f32[128,128]{1,0:T(8,128)S(1)} %get-tuple-element.233.cosine, ...), custom_call_target="tpu_custom_call" | custom-call | flops 805306368 | bytes 8650752 | tf_op jit(solution)/shard_map/pallas_call | solution.py:592
  62.2 30.7 %collective-permute-done.11.refs_2_ = bf16[128,8064]{1,0:T(8,128)(2,1)} collective-permute-done((bf16[128,8064]{1,0:T(8,128)(2,1)}, bf16[128,8064]{1,0:T(8,128)(2,1)}, u32[]{:S(2)}, u32[]{:S(2)}) %collective-permute-start.11) | collective-permute-done | bytes 2064416 | tf_op jit(solution)/shard_map/ppermute | solution.py:265
  105.4 7.7 %shard_map.162 = (bf16[128,1024]{1,0:T(8,128)(2,1)S(1)}, f32[128,128]{1,0:T(8,128)S(1)}, f32[128,1024]{1,0:T(8,128)S(1)}, bf16[128,1024]{1,0:T(8,128)(2,1)S(1)}) custom-call(s32[2]{0:T(128)S(1)} %copy-done.24, bf16[128,1024]{1,0:T(8,128)(2,1)S(1)} %copy-done.19, bf16[128,2048]{1,0:T(8,128)(2,1)S(1)} %copy-done.12, ...), custom_call_target="tpu_custom_call" | custom-call | flops 1610612736 | bytes 4194304 | tf_op jit(solution)/shard_map/pallas_call | solution.py:592
  113.8 8.0 %collective-permute-done.13.refs_4_ = bf16[64,8064]{1,0:T(8,128)(2,1)} collective-permute-done((bf16[64,8064]{1,0:T(8,128)(2,1)}, bf16[64,8064]{1,0:T(8,128)(2,1)}, u32[]{:S(2)}, u32[]{:S(2)}) %collective-permute-start.13) | collective-permute-done | bytes 1032224 | tf_op jit(solution)/shard_map/ppermute | solution.py:265
  122.4 3.0 collective-permute-done.18.refs_9_
  127.0 7.5 %shard_map.163 = (bf16[128,1920]{1,0:T(8,128)(2,1)S(1)}, bf16[128,1920]{1,0:T(8,128)(2,1)S(1)}, bf16[128,1792]{1,0:T(8,128)(2,1)S(1)}, bf16[128,1792]{1,0:T(8,12...) custom-call(s32[2]{0:T(128)S(1)} %copy-done.24, bf16[128,1024]{1,0:T(8,128)(2,1)S(1)} %get-tuple-element.105.xn2, ...), custom_call_target="tpu_custom_call" | custom-call | flops 1409286144 | bytes 11010048 | tf_op jit(solution)/shard_map/pallas_call | solution.py:592
  136.0 8.5 %shard_map.164 = (bf16[128,1024]{1,0:T(8,128)(2,1)}, bf16[128,3200]{1,0:T(8,128)(2,1)S(1)}, bf16[128,3200]{1,0:T(8,128)(2,1)}, bf16[128,3200]{1,0:T(8,128)(2,1)}, bf16[128,3200]{1,0:T(8,128)(2,1)}) custom-call(s32[2]{0:T(128)S(1)} %copy-done.24, bf16[128,1920]{1,0:T(8,128)(2,1)S(1)} %get-tuple-element.123.gated_one, ...), custom_call_target="tpu_custom_call" | custom-call | flops 1409286144 | bytes 5505024 | tf_op jit(solution)/shard_map/pallas_call | solution.py:592
  144.5 2.5 collective-permute-done.22
  150.9 10.7 %shard_map.165 = (f32[128,1024]{1,0:T(8,128)S(1)}, bf16[128,1024]{1,0:T(8,128)(2,1)S(1)}, f32[1,1024]{1,0:T(1,128)S(1)}) custom-call(s32[2]{0:T(128)S(1)} %copy-done.24, bf16[128,3200]{1,0:T(8,128)(2,1)} %copy-done.5, bf16[128,3200]{1,0:T(8,128)(2,1)} %get-tuple-element.133.pack_two, bf16[128,1024]{1,0:T(8,128)(2,1)S(1)} %bitcast.17, ...), custom_call_target="tpu_custom_call" | custom-call | flops 2113929216 | bytes 16515072 | tf_op jit(solution)/shard_map/pallas_call | solution.py:592
  161.7 6.3 %shard_map.166 = (bf16[128,1024]{1,0:T(8,128)(2,1)S(1)}, f32[128,2048]{1,0:T(8,128)S(1)}, bf16[64,2048]{1,0:T(8,128)(2,1)S(1)}) custom-call(s32[2]{0:T(128)S(1)} %copy-done.24, bf16[128,1024]{1,0:T(8,128)(2,1)S(1)} %copy-done.20, bf16[128,2048]{1,0:T(8,128)(2,1)S(1)} %copy-done.13, bf16[64,2048]{1,0:T(8,128)(2,1)S(1)} %copy-done.22, ...), custom_call_target="tpu_custom_call" | custom-call | flops 2684354560 | bytes 4194304 | tf_op jit(solution)/shard_map/pallas_call | solution.py:592
  175.9 3.1 collective-permute-done.28
  179.0 3.8 %collective-permute-done.27 = bf16[128,1408]{1,0:T(8,128)(2,1)S(1)} collective-permute-done((bf16[128,1408]{1,0:T(8,128)(2,1)S(1)}, bf16[128,1408]{1,0:T(8,128)(2,1)S(1)}, u32[]{:S(2)}, u32[]{:S(2)}) %collective-permute-start.27) | collective-permute-done | bytes 360480 | tf_op jit(solution)/shard_map/ppermute | solution.py:265
  184.0 3.5 %collective-permute-start.32 = (bf16[128,2688]{1,0:T(8,128)(2,1)S(1)}, bf16[128,2688]{1,0:T(8,128)(2,1)S(1)}, u32[]{:S(2)}, u32[]{:S(2)}) collective-permute-start(bf16[128,2688]{1,0:T(8,128)(2,1)S(1)} %fusion.9), channel_id=1, source_target_pairs={{0,8},{24,16},{1,9},{25,17},{2,10},{26,18},{3,11},{27,19},{4,12},{... | collective-permute-start | bytes 2064392 | tf_op jit(solution)/shard_map/ppermute | solution.py:632
  188.2 2.6 shard_map.169
  192.3 2.6 shard_map.170
  198.0 2.7 collective-permute-done.32
  202.6 9.1 %collective-permute-done.31 = bf16[128,2688]{1,0:T(8,128)(2,1)} collective-permute-done((bf16[128,2688]{1,0:T(8,128)(2,1)S(1)}, bf16[128,2688]{1,0:T(8,128)(2,1)}, u32[]{:S(2)}, u32[]{:S(2)}) %collective-permute-start.31) | collective-permute-done | bytes 688160 | tf_op jit(solution)/shard_map/ppermute | solution.py:265
  216.8 7.0 %collective-permute-done.33 = bf16[128,2688]{1,0:T(8,128)(2,1)S(1)} collective-permute-done((bf16[128,2688]{1,0:T(8,128)(2,1)S(1)}, bf16[128,2688]{1,0:T(8,128)(2,1)S(1)}, u32[]{:S(2)}, u32[]{:S(2)}) %collective-permute-start.33) | collective-permute-done | bytes 688160 | tf_op jit(solution)/shard_map/ppermute | solution.py:632
  227.5 6.6 %collective-permute-start.41 = (bf16[128,2688]{1,0:T(8,128)(2,1)}, bf16[128,2688]{1,0:T(8,128)(2,1)S(1)}, u32[]{:S(2)}, u32[]{:S(2)}) collective-permute-start(bf16[128,2688]{1,0:T(8,128)(2,1)} %get-tuple-element.224), channel_id=1, source_target_pairs={{0,8},{24,16},{1,9},{25,17},{2,10},{26,18},{3,11},{27,19},{4,12},{... | collective-permute-start | bytes 2064392 | tf_op jit(solution)/shard_map/ppermute | solution.py:632
  238.0 6.3 %shard_map.174 = (bf16[144,1536]{1,0:T(8,128)(2,1)S(1)}, bf16[144,1536]{1,0:T(8,128)(2,1)S(1)}, bf16[128,1024]{1,0:T(8,128)(2,1)}) custom-call(s32[2]{0:T(128)S(1)} %copy-done.24, bf16[128,2048]{1,0:T(8,128)(2,1)S(1)} %get-tuple-element.163.pack_one, bf16[128,2048]{1,0:T(8,128)(2,1)S(1)} %get-tuple-element.160.pack_two, bf16[128,1024]{1,0:T(8,128)(2,1)S(1)} %bitcast.20, ...), custom_call_target="tpu_custom_call" | custom-call | flops 805306368 | bytes 6291456 | tf_op jit(solution)/shard_map/pallas_call | solution.py:592
  251.4 6.5 %collective-permute-start.44 = (bf16[128,1536]{1,0:T(8,128)(2,1)S(1)}, bf16[128,1536]{1,0:T(8,128)(2,1)S(1)}, u32[]{:S(2)}, u32[]{:S(2)}) collective-permute-start(bf16[128,1536]{1,0:T(8,128)(2,1)S(1)} %get-tuple-element.222), channel_id=1, source_target_pairs={{0,8},{24,16},{1,9},{25,17},{2,10},{26,18},{3,11},{27,19},{4,12},{... | collective-permute-start | bytes 1179656 | tf_op jit(solution)/shard_map/ppermute | solution.py:632
  259.7 5.3 %collective-permute-done.47 = bf16[128,2688]{1,0:T(8,128)(2,1)S(1)} collective-permute-done((bf16[128,2688]{1,0:T(8,128)(2,1)S(1)}, bf16[128,2688]{1,0:T(8,128)(2,1)S(1)}, u32[]{:S(2)}, u32[]{:S(2)}) %collective-permute-start.47) | collective-permute-done | bytes 688160 | tf_op jit(solution)/shard_map/ppermute | solution.py:648
  266.2 8.3 %collective-permute-start.50 = (bf16[128,1536]{1,0:T(8,128)(2,1)}, bf16[128,1536]{1,0:T(8,128)(2,1)}, u32[]{:S(2)}, u32[]{:S(2)}) collective-permute-start(bf16[128,1536]{1,0:T(8,128)(2,1)} %get-tuple-element.220), channel_id=1, source_target_pairs={{0,8},{24,16},{1,9},{25,17},{2,10},{26,18},{3,11},{27,19},{4,12},{... | collective-permute-start | bytes 1179656 | tf_op jit(solution)/shard_map/ppermute | solution.py:632
  279.6 3.3 %collective-permute-done.50 = bf16[128,1536]{1,0:T(8,128)(2,1)} collective-permute-done((bf16[128,1536]{1,0:T(8,128)(2,1)}, bf16[128,1536]{1,0:T(8,128)(2,1)}, u32[]{:S(2)}, u32[]{:S(2)}) %collective-permute-start.50) | collective-permute-done | bytes 393248 | tf_op jit(solution)/shard_map/ppermute | solution.py:632
  284.7 2.4 collective-permute-done.49
  287.2 7.0 %collective-permute-start.51 = (bf16[144,1024]{1,0:T(8,128)(2,1)S(1)}, bf16[144,1024]{1,0:T(8,128)(2,1)S(1)}, u32[]{:S(2)}, u32[]{:S(2)}) collective-permute-start(bf16[144,1024]{1,0:T(8,128)(2,1)S(1)} %get-tuple-element.218), channel_id=1, source_target_pairs={{0,8},{24,16},{1,9},{25,17},{2,10},{26,18},{3,11},{27,19},{4,12},{... | collective-permute-start | bytes 884744 | tf_op jit(solution)/shard_map/ppermute | solution.py:632
  295.6 3.3 %collective-permute-done.51 = bf16[144,1024]{1,0:T(8,128)(2,1)S(1)} collective-permute-done((bf16[144,1024]{1,0:T(8,128)(2,1)S(1)}, bf16[144,1024]{1,0:T(8,128)(2,1)S(1)}, u32[]{:S(2)}, u32[]{:S(2)}) %collective-permute-start.51) | collective-permute-done | bytes 294944 | tf_op jit(solution)/shard_map/ppermute | solution.py:632
  309.9 4.9 %collective-permute-done.58 = bf16[128,1536]{1,0:T(8,128)(2,1)} collective-permute-done((bf16[128,1536]{1,0:T(8,128)(2,1)S(1)}, bf16[128,1536]{1,0:T(8,128)(2,1)}, u32[]{:S(2)}, u32[]{:S(2)}) %collective-permute-start.58) | collective-permute-done | bytes 393248 | tf_op jit(solution)/shard_map/ppermute | solution.py:648
  317.2 2.8 collective-permute-done.56
  (255 shorter events, 106.2 us)
Async XLA Ops:
  3.9 27.1 %collective-permute-start.1 = (bf16[128,4224]{1,0:T(8,128)(2,1)}, bf16[128,4224]{1,0:T(8,128)(2,1)}, u32[]{:S(2)}, u32[]{:S(2)}) collective-permute-start(bf16[128,4224]{1,0:T(8,128)(2,1)} %fusion.6.refs_0_.refs_10_), channel_id=1, source_target_pairs={{0,4},{1,5},{2,6},{3,7},{4,0},{5,1},{6,2},{7,3},{8,12},{9,13},{10,... | collective-permute-start | bytes 3244040 | tf_op jit(solution)/shard_map/ppermute | solution.py:265
  6.9 27.0 %collective-permute-start = (bf16[128,4224]{1,0:T(8,128)(2,1)}, bf16[128,4224]{1,0:T(8,128)(2,1)}, u32[]{:S(2)}, u32[]{:S(2)}) collective-permute-start(bf16[128,4224]{1,0:T(8,128)(2,1)} %fusion.6.refs_0_.refs_10_), channel_id=1, source_target_pairs={{0,1},{1,0},{2,3},{3,2},{4,5},{5,4},{6,7},{7,6},{8,9},{9,8},{10,11... | collective-permute-start | bytes 3244040 | tf_op jit(solution)/shard_map/ppermute | solution.py:265
  8.4 42.2 %collective-permute-start.4 = (bf16[128,4224]{1,0:T(8,128)(2,1)}, bf16[128,4224]{1,0:T(8,128)(2,1)}, u32[]{:S(2)}, u32[]{:S(2)}) collective-permute-start(bf16[128,4224]{1,0:T(8,128)(2,1)} %fusion.6.refs_0_.refs_10_), channel_id=1, source_target_pairs={{0,2},{1,3},{2,0},{3,1},{4,6},{5,7},{6,4},{7,5},{8,10},{9,11},{10,... | collective-permute-start | bytes 3244040 | tf_op jit(solution)/shard_map/ppermute | solution.py:265
  48.0 44.9 %collective-permute-start.11 = (bf16[128,8064]{1,0:T(8,128)(2,1)}, bf16[128,8064]{1,0:T(8,128)(2,1)}, u32[]{:S(2)}, u32[]{:S(2)}) collective-permute-start(bf16[128,8064]{1,0:T(8,128)(2,1)} %fusion.5.refs_0_), channel_id=1, source_target_pairs={{0,4},{1,5},{2,6},{3,7},{4,0},{5,1},{6,2},{7,3},{8,12},{9,13},{10,... | collective-permute-start | bytes 6193160 | tf_op jit(solution)/shard_map/ppermute | solution.py:265
  49.5 48.2 %collective-permute-start.10 = (bf16[128,8064]{1,0:T(8,128)(2,1)}, bf16[128,8064]{1,0:T(8,128)(2,1)}, u32[]{:S(2)}, u32[]{:S(2)}) collective-permute-start(bf16[128,8064]{1,0:T(8,128)(2,1)} %fusion.5.refs_0_), channel_id=1, source_target_pairs={{0,1},{1,0},{2,3},{3,2},{4,5},{5,4},{6,7},{7,6},{8,9},{9,8},{10,11... | collective-permute-start | bytes 6193160 | tf_op jit(solution)/shard_map/ppermute | solution.py:265
  60.6 42.5 %collective-permute-start.9 = (bf16[64,2048]{1,0:T(8,128)(2,1)S(1)}, bf16[64,2048]{1,0:T(8,128)(2,1)S(1)}, u32[]{:S(2)}, u32[]{:S(2)}) collective-permute-start(bf16[64,2048]{1,0:T(8,128)(2,1)S(1)} %get-tuple-element.103), channel_id=1, source_target_pairs={{0,1},{1,0},{2,3},{3,2},{4,5},{5,4},{6,7},{7,6},{8,9},{9,8},{10,11... | collective-permute-start | bytes 786440 | tf_op jit(solution)/shard_map/ppermute | solution.py:265
  95.2 26.6 %collective-permute-start.13 = (bf16[64,8064]{1,0:T(8,128)(2,1)}, bf16[64,8064]{1,0:T(8,128)(2,1)}, u32[]{:S(2)}, u32[]{:S(2)}) collective-permute-start(bf16[64,8064]{1,0:T(8,128)(2,1)} %slice.77), channel_id=1, source_target_pairs={{0,1},{1,0},{2,3},{3,2},{4,5},{5,4},{6,7},{7,6},{8,9},{9,8},{10,11... | collective-permute-start | bytes 3096584 | tf_op jit(solution)/shard_map/ppermute | solution.py:265
  99.9 21.9 %collective-permute-start.12 = (bf16[64,8064]{1,0:T(8,128)(2,1)}, bf16[64,8064]{1,0:T(8,128)(2,1)S(1)}, u32[]{:S(2)}, u32[]{:S(2)}) collective-permute-start(bf16[64,8064]{1,0:T(8,128)(2,1)} %slice.76), channel_id=1, source_target_pairs={{0,4},{1,5},{2,6},{3,7},{4,0},{5,1},{6,2},{7,3},{8,12},{9,13},{10,... | collective-permute-start | bytes 3096584 | tf_op jit(solution)/shard_map/ppermute | solution.py:265
  100.5 21.9 %collective-permute-start.14 = (bf16[128,8064]{1,0:T(8,128)(2,1)}, bf16[128,8064]{1,0:T(8,128)(2,1)}, u32[]{:S(2)}, u32[]{:S(2)}) collective-permute-start(bf16[128,8064]{1,0:T(8,128)(2,1)} %fusion.5.refs_0_), channel_id=1, source_target_pairs={{0,2},{1,3},{2,0},{3,1},{4,6},{5,7},{6,4},{7,5},{8,10},{9,11},{10,... | collective-permute-start | bytes 6193160 | tf_op jit(solution)/shard_map/ppermute | solution.py:265
  100.5 24.9 %collective-permute-start.16 = (bf16[128,8064]{1,0:T(8,128)(2,1)}, bf16[128,8064]{1,0:T(8,128)(2,1)}, u32[]{:S(2)}, u32[]{:S(2)}) collective-permute-start(bf16[128,8064]{1,0:T(8,128)(2,1)} %collective-permute-done.11.refs_2_), channel_id=1, source_target_pairs={{0,2},{1,3},{2,0},{3,1},{4,6},{5,7},{6,4},{7,5},{8,10},{9,11},{10,... | collective-permute-start | bytes 6193160 | tf_op jit(solution)/shard_map/ppermute | solution.py:265
  103.2 22.8 %collective-permute-start.15 = (bf16[128,8064]{1,0:T(8,128)(2,1)}, bf16[128,8064]{1,0:T(8,128)(2,1)}, u32[]{:S(2)}, u32[]{:S(2)}) collective-permute-start(bf16[128,8064]{1,0:T(8,128)(2,1)} %collective-permute-done.10.refs_1_), channel_id=1, source_target_pairs={{0,2},{1,3},{2,0},{3,1},{4,6},{5,7},{6,4},{7,5},{8,10},{9,11},{10,... | collective-permute-start | bytes 6193160 | tf_op jit(solution)/shard_map/ppermute | solution.py:265
  148.1 23.2 %collective-permute-start.21 = (bf16[256,1920]{1,0:T(8,128)(2,1)S(1)}, bf16[256,1920]{1,0:T(8,128)(2,1)S(1)}, u32[]{:S(2)}, u32[]{:S(2)}) collective-permute-start(bf16[256,1920]{1,0:T(8,128)(2,1)S(1)} %constant_dynamic-update-slice_fusion.refs_0_), channel_id=1, source_target_pairs={{0,2},{1,3},{2,0},{3,1},{4,6},{5,7},{6,4},{7,5},{8,10},{9,11},{10,... | collective-permute-start | bytes 2949128 | tf_op jit(solution)/shard_map/ppermute | solution.py:265
  148.2 19.7 %collective-permute-start.23 = (bf16[256,1792]{1,0:T(8,128)(2,1)S(1)}, bf16[256,1792]{1,0:T(8,128)(2,1)S(1)}, u32[]{:S(2)}, u32[]{:S(2)}) collective-permute-start(bf16[256,1792]{1,0:T(8,128)(2,1)S(1)} %constant_dynamic-update-slice_fusion.2.refs_0_), channel_id=1, source_target_pairs={{0,2},{1,3},{2,0},{3,1},{4,6},{5,7},{6,4},{7,5},{8,10},{9,11},{10,... | collective-permute-start | bytes 2752520 | tf_op jit(solution)/shard_map/ppermute | solution.py:265
  148.8 25.0 %collective-permute-start.25 = (bf16[128,3200]{1,0:T(8,128)(2,1)}, bf16[128,3200]{1,0:T(8,128)(2,1)}, u32[]{:S(2)}, u32[]{:S(2)}) collective-permute-start(bf16[128,3200]{1,0:T(8,128)(2,1)} %get-tuple-element.135), channel_id=1, source_target_pairs={{0,4},{1,5},{2,6},{3,7},{4,0},{5,1},{6,2},{7,3},{8,12},{9,13},{10,... | collective-permute-start | bytes 2457608 | tf_op jit(solution)/shard_map/ppermute | solution.py:265
  150.3 23.5 %collective-permute-start.19 = (bf16[128,3200]{1,0:T(8,128)(2,1)}, bf16[128,3200]{1,0:T(8,128)(2,1)S(1)}, u32[]{:S(2)}, u32[]{:S(2)}) collective-permute-start(bf16[128,3200]{1,0:T(8,128)(2,1)} %get-tuple-element.121), channel_id=1, source_target_pairs={{0,1},{1,0},{2,3},{3,2},{4,5},{5,4},{6,7},{7,6},{8,9},{9,8},{10,11... | collective-permute-start | bytes 2457608 | tf_op jit(solution)/shard_map/ppermute | solution.py:265
  175.4 17.0 %collective-permute-start.24 = (bf16[256,3200]{1,0:T(8,128)(2,1)S(1)}, bf16[256,3200]{1,0:T(8,128)(2,1)}, u32[]{:S(2)}, u32[]{:S(2)}) collective-permute-start(bf16[256,3200]{1,0:T(8,128)(2,1)S(1)} %constant_dynamic-update-slice_fusion.4.refs_0_), channel_id=1, source_target_pairs={{0,2},{1,3},{2,0},{3,1},{4,6},{5,7},{6,4},{7,5},{8,10},{9,11},{10,... | collective-permute-start | bytes 4915208 | tf_op jit(solution)/shard_map/ppermute | solution.py:265
  184.0 16.6 %collective-permute-start.32 = (bf16[128,2688]{1,0:T(8,128)(2,1)S(1)}, bf16[128,2688]{1,0:T(8,128)(2,1)S(1)}, u32[]{:S(2)}, u32[]{:S(2)}) collective-permute-start(bf16[128,2688]{1,0:T(8,128)(2,1)S(1)} %fusion.9), channel_id=1, source_target_pairs={{0,8},{24,16},{1,9},{25,17},{2,10},{26,18},{3,11},{27,19},{4,12},{... | collective-permute-start | bytes 2064392 | tf_op jit(solution)/shard_map/ppermute | solution.py:632
  190.8 20.9 %collective-permute-start.31 = (bf16[128,2688]{1,0:T(8,128)(2,1)S(1)}, bf16[128,2688]{1,0:T(8,128)(2,1)}, u32[]{:S(2)}, u32[]{:S(2)}) collective-permute-start(bf16[128,2688]{1,0:T(8,128)(2,1)S(1)} %get-tuple-element.143), channel_id=1, source_target_pairs={{0,1},{1,0},{2,3},{3,2},{4,5},{5,4},{6,7},{7,6},{8,9},{9,8},{10,11... | collective-permute-start | bytes 2064392 | tf_op jit(solution)/shard_map/ppermute | solution.py:265
  194.9 19.6 %collective-permute-start.35 = (bf16[128,2688]{1,0:T(8,128)(2,1)S(1)}, bf16[128,2688]{1,0:T(8,128)(2,1)}, u32[]{:S(2)}, u32[]{:S(2)}) collective-permute-start(bf16[128,2688]{1,0:T(8,128)(2,1)S(1)} %get-tuple-element.145), channel_id=1, source_target_pairs={{0,4},{1,5},{2,6},{3,7},{4,0},{5,1},{6,2},{7,3},{8,12},{9,13},{10,... | collective-permute-start | bytes 2064392 | tf_op jit(solution)/shard_map/ppermute | solution.py:265
  200.7 23.2 %collective-permute-start.30 = (bf16[128,2048]{1,0:T(8,128)(2,1)S(1)}, bf16[128,2048]{1,0:T(8,128)(2,1)S(1)}, u32[]{:S(2)}, u32[]{:S(2)}) collective-permute-start(bf16[128,2048]{1,0:T(8,128)(2,1)S(1)} %get-tuple-element.152), channel_id=1, source_target_pairs={{0,4},{1,5},{2,6},{3,7},{4,0},{5,1},{6,2},{7,3},{8,12},{9,13},{10,... | collective-permute-start | bytes 1572872 | tf_op jit(solution)/shard_map/ppermute | solution.py:265
  201.2 22.7 %collective-permute-start.37 = (bf16[128,2048]{1,0:T(8,128)(2,1)S(1)}, bf16[128,2048]{1,0:T(8,128)(2,1)S(1)}, u32[]{:S(2)}, u32[]{:S(2)}) collective-permute-start(bf16[128,2048]{1,0:T(8,128)(2,1)S(1)} %get-tuple-element.162), channel_id=1, source_target_pairs={{0,1},{1,0},{2,3},{3,2},{4,5},{5,4},{6,7},{7,6},{8,9},{9,8},{10,11... | collective-permute-start | bytes 1572872 | tf_op jit(solution)/shard_map/ppermute | solution.py:265
  201.8 14.8 %collective-permute-start.34 = (bf16[128,2688]{1,0:T(8,128)(2,1)S(1)}, bf16[128,2688]{1,0:T(8,128)(2,1)S(1)}, u32[]{:S(2)}, u32[]{:S(2)}) collective-permute-start(bf16[128,2688]{1,0:T(8,128)(2,1)S(1)} %add_convert_fusion.5), channel_id=1, source_target_pairs={{8,16},{16,8},{9,17},{17,9},{10,18},{18,10},{11,19},{19,11},{12,20... | collective-permute-start | bytes 2064392 | tf_op jit(solution)/shard_map/ppermute | solution.py:640
  224.7 19.7 %collective-permute-start.43 = (bf16[128,2688]{1,0:T(8,128)(2,1)S(1)}, bf16[128,2688]{1,0:T(8,128)(2,1)S(1)}, u32[]{:S(2)}, u32[]{:S(2)}) collective-permute-start(bf16[128,2688]{1,0:T(8,128)(2,1)S(1)} %add_convert_fusion.4), channel_id=1, source_target_pairs={{8,0},{16,24},{9,1},{17,25},{10,2},{18,26},{11,3},{19,27},{12,4},{... | collective-permute-start | bytes 2064392 | tf_op jit(solution)/shard_map/ppermute | solution.py:648
  226.0 18.4 %collective-permute-start.42 = (bf16[128,2688]{1,0:T(8,128)(2,1)S(1)}, bf16[128,2688]{1,0:T(8,128)(2,1)}, u32[]{:S(2)}, u32[]{:S(2)}) collective-permute-start(bf16[128,2688]{1,0:T(8,128)(2,1)S(1)} %add_convert_fusion.3), channel_id=1, source_target_pairs={{8,16},{16,8},{9,17},{17,9},{10,18},{18,10},{11,19},{19,11},{12,20... | collective-permute-start | bytes 2064392 | tf_op jit(solution)/shard_map/ppermute | solution.py:640
  227.5 21.3 %collective-permute-start.41 = (bf16[128,2688]{1,0:T(8,128)(2,1)}, bf16[128,2688]{1,0:T(8,128)(2,1)S(1)}, u32[]{:S(2)}, u32[]{:S(2)}) collective-permute-start(bf16[128,2688]{1,0:T(8,128)(2,1)} %get-tuple-element.224), channel_id=1, source_target_pairs={{0,8},{24,16},{1,9},{25,17},{2,10},{26,18},{3,11},{27,19},{4,12},{... | collective-permute-start | bytes 2064392 | tf_op jit(solution)/shard_map/ppermute | solution.py:632
  235.0 15.2 %collective-permute-start.40 = (bf16[128,1536]{1,0:T(8,128)(2,1)S(1)}, bf16[128,1536]{1,0:T(8,128)(2,1)}, u32[]{:S(2)}, u32[]{:S(2)}) collective-permute-start(bf16[128,1536]{1,0:T(8,128)(2,1)S(1)} %get-tuple-element.165), channel_id=1, source_target_pairs={{0,4},{1,5},{2,6},{3,7},{4,0},{5,1},{6,2},{7,3},{8,12},{9,13},{10,... | collective-permute-start | bytes 1179656 | tf_op jit(solution)/shard_map/ppermute | solution.py:265
  236.5 21.4 %collective-permute-start.46 = (bf16[128,1536]{1,0:T(8,128)(2,1)S(1)}, bf16[128,1536]{1,0:T(8,128)(2,1)S(1)}, u32[]{:S(2)}, u32[]{:S(2)}) collective-permute-start(bf16[128,1536]{1,0:T(8,128)(2,1)S(1)} %get-tuple-element.167), channel_id=1, source_target_pairs={{0,1},{1,0},{2,3},{3,2},{4,5},{5,4},{6,7},{7,6},{8,9},{9,8},{10,11... | collective-permute-start | bytes 1179656 | tf_op jit(solution)/shard_map/ppermute | solution.py:265
  245.9 19.1 %collective-permute-start.47 = (bf16[128,2688]{1,0:T(8,128)(2,1)S(1)}, bf16[128,2688]{1,0:T(8,128)(2,1)S(1)}, u32[]{:S(2)}, u32[]{:S(2)}) collective-permute-start(bf16[128,2688]{1,0:T(8,128)(2,1)S(1)} %add_convert_fusion.2), channel_id=1, source_target_pairs={{8,0},{16,24},{9,1},{17,25},{10,2},{18,26},{11,3},{19,27},{12,4},{... | collective-permute-start | bytes 2064392 | tf_op jit(solution)/shard_map/ppermute | solution.py:648
  248.9 17.1 %collective-permute-start.39 = (bf16[144,1536]{1,0:T(8,128)(2,1)S(1)}, bf16[144,1536]{1,0:T(8,128)(2,1)S(1)}, u32[]{:S(2)}, u32[]{:S(2)}) collective-permute-start(bf16[144,1536]{1,0:T(8,128)(2,1)S(1)} %get-tuple-element.172), channel_id=1, source_target_pairs={{0,4},{1,5},{2,6},{3,7},{4,0},{5,1},{6,2},{7,3},{8,12},{9,13},{10,... | collective-permute-start | bytes 1327112 | tf_op jit(solution)/shard_map/ppermute | solution.py:265
  266.2 16.7 %collective-permute-start.50 = (bf16[128,1536]{1,0:T(8,128)(2,1)}, bf16[128,1536]{1,0:T(8,128)(2,1)}, u32[]{:S(2)}, u32[]{:S(2)}) collective-permute-start(bf16[128,1536]{1,0:T(8,128)(2,1)} %get-tuple-element.220), channel_id=1, source_target_pairs={{0,8},{24,16},{1,9},{25,17},{2,10},{26,18},{3,11},{27,19},{4,12},{... | collective-permute-start | bytes 1179656 | tf_op jit(solution)/shard_map/ppermute | solution.py:632
  274.5 25.9 %collective-permute-start.55 = (bf16[128,2688]{1,0:T(8,128)(2,1)S(1)}, bf16[128,2688]{1,0:T(8,128)(2,1)S(1)}, u32[]{:S(2)}, u32[]{:S(2)}) collective-permute-start(bf16[128,2688]{1,0:T(8,128)(2,1)S(1)} %copy-done.32), channel_id=1, source_target_pairs={{8,0},{16,24},{9,1},{17,25},{10,2},{18,26},{11,3},{19,27},{12,4},{... | collective-permute-start | bytes 2064392 | tf_op jit(solution)/shard_map/ppermute | solution.py:648
  284.0 16.4 %collective-permute-start.54 = (bf16[128,1536]{1,0:T(8,128)(2,1)S(1)}, bf16[128,1536]{1,0:T(8,128)(2,1)S(1)}, u32[]{:S(2)}, u32[]{:S(2)}) collective-permute-start(bf16[128,1536]{1,0:T(8,128)(2,1)S(1)} %add_convert_fusion.8), channel_id=1, source_target_pairs={{8,16},{16,8},{9,17},{17,9},{10,18},{18,10},{11,19},{19,11},{12,20... | collective-permute-start | bytes 1179656 | tf_op jit(solution)/shard_map/ppermute | solution.py:640
  (71 other events, 718.0 us)

commit v8 on v7

--- a/solution.py
+++ b/solution.py
@@ -825,17 +825,17 @@
     gate_last = line_back(gate_total)
     low_pair = line_pair(low_part, later(low_first, gate_total, gelu_last))
     low_other = line_middle(low_pair)
-    out_own, out_sent = grad_rows(keep_o, link_o, shard, low_pair)
+    out_own, out_sent = grad_rows(keep_o, link_o, shard, high_part)
     out_back = swap(out_sent, X_BIT)
-    high_pair = line_pair(high_part, later(high_first, out_sent))
+    high_pair = line_pair(high_part, later(high_first, low_pair))
     high_other = line_middle(high_pair)
-    out_part = out_own + later(out_back, high_pair).astype(F32)
+    out_part = out_own + later(out_back, high_pair, gate_last).astype(F32)
     out_first = line_first(out_part)
     low_total = line_total(low_pair, later(low_other, out_part))
     low_last = line_back(low_total)
     out_pair = line_pair(out_part, later(out_first, low_total))
     out_other = line_middle(out_pair)
-    high_total = line_total(high_pair, later(high_other, out_pair, gate_last))
+    high_total = line_total(high_pair, later(high_other, out_pair))
     high_last = line_back(high_total)
     out_total = line_total(out_pair, later(out_other, high_total))
     out_last = line_back(out_total)

time: 323 us -> 322 us (level)
  starting transfers between devices: 77.1 us -> 67.7 us
    ppermute x6, starting transfers between devices: 33.4 us -> 24 us  [line_first(): return lax.ppermute(part.astype(BF16), 'replica', [(0, 1), (3, 2)])]
    ppermute x6, waiting for transfers between devices: 13.1 us -> 18.8 us  [line_back(): return lax.ppermute(total, 'replica', [(1, 0), (2, 3)])]
    unnamed x97 -> x93, local copies, waits for them, and re-layouts: 6.93 us -> 7.98 us
  transfers between devices with their start and end apart: 59 -> 59, of which waited for: 27 -> 28; matrix products, arithmetic and copies ran while one was open for 10% -> 10% of each run, Pallas kernels for 18% -> 19%
where the time goes in v8:
time: 322 us; the launch traced here: 320 us
  waiting for transfers between devices  140 us (43%)
  starting transfers between devices  67.7 us (21%)
  Pallas kernels  67.5 us (21%)
  other arithmetic  25.7 us (8%)
  local copies, waits for them, and re-layouts  17.7 us (5%)
    ppermute x41, waiting for transfers between devices, swap(): return lax.ppermute(value, PLANE, [(i, i ^ bit) for i in range(PLANE_SIZE)])  103 us
    pallas_call x15, Pallas kernels, call(): pl.pallas_call(kernel, out_shape=[jax.ShapeDtypeStruct(shape, kind) for s...  67.5 us
    ppermute x41, starting transfers between devices, swap(): return lax.ppermute(value, PLANE, [(i, i ^ bit) for i in range(PLANE_SIZE)])  30.3 us
    ppermute x6, starting transfers between devices, line_first(): return lax.ppermute(part.astype(BF16), 'replica', [(0, 1), (3, 2)])  24 us
    ppermute x6, waiting for transfers between devices, line_back(): return lax.ppermute(total, 'replica', [(1, 0), (2, 3)])  18.8 us
    ppermute x6, waiting for transfers between devices, line_first(): return lax.ppermute(part.astype(BF16), 'replica', [(0, 1), (3, 2)])  18 us
    unnamed x93, local copies, waits for them, and re-layouts  7.98 us
    ppermute x6, starting transfers between devices, line_back(): return lax.ppermute(total, 'replica', [(1, 0), (2, 3)])  7.74 us
  transfers between devices with their start and end apart: 59, of which 28 were waited for; matrix products, arithmetic and copies ran while one was open for 10% of the time, Pallas kernels for 19%

profile of v8, /device:TPU:0, one launch (start us, length us, event | category | flops | bytes accessed | tf_op | source)
XLA Modules:
  0.0 320.5 jit_solution(17969139061608465405)
XLA Ops:
  1.5 2.4 fusion.6.refs_0_.refs_10_
  3.9 3.0 collective-permute-start.1
  9.1 22.0 %collective-permute-done.1.refs_2_.refs_12_ = bf16[128,4224]{1,0:T(8,128)(2,1)} collective-permute-done((bf16[128,4224]{1,0:T(8,128)(2,1)}, bf16[128,4224]{1,0:T(8,128)(2,1)}, u32[]{:S(2)}, u32[]{:S(2)}) %collective-permute-start.1) | collective-permute-done | bytes 1081376 | tf_op jit(solution)/shard_map/ppermute | solution.py:265
  38.1 7.6 %collective-permute-done.3.refs_4_.refs_14_ = bf16[64,4224]{1,0:T(8,128)(2,1)S(1)} collective-permute-done((bf16[64,4224]{1,0:T(8,128)(2,1)S(1)}, bf16[64,4224]{1,0:T(8,128)(2,1)S(1)}, u32[]{:S(2)}, u32[]{:S(2)}) %collective-permute-start.3) | collective-permute-done | bytes 540704 | tf_op jit(solution)/shard_map/ppermute | solution.py:265
  45.7 2.3 collective-permute-done.2.refs_3_.refs_13_
  55.8 4.7 %shard_map.161 = (bf16[128,1024]{1,0:T(8,128)(2,1)S(1)}, bf16[128,2048]{1,0:T(8,128)(2,1)S(1)}, bf16[64,2048]{1,0:T(8,128)(2,1)S(1)}, bf16[128,1024]{1,0:T(8,128)(2,1)S(1)}, f32[8,1024]{1,0:T(8,128)S(1)}) custom-call(s32[2]{0:T(128)S(1)} %pad_add_fusion.place, bf16[128,1024]{1,0:T(8,128)(2,1)S(1)} %bitcast.18, f32[128,128]{1,0:T(8,128)S(1)} %get-tuple-element.233.cosine, ...), custom_call_target="tpu_custom_call" | custom-call | flops 805306368 | bytes 8650752 | tf_op jit(solution)/shard_map/pallas_call | solution.py:592
  62.2 30.7 %collective-permute-done.11.refs_2_ = bf16[128,8064]{1,0:T(8,128)(2,1)} collective-permute-done((bf16[128,8064]{1,0:T(8,128)(2,1)}, bf16[128,8064]{1,0:T(8,128)(2,1)}, u32[]{:S(2)}, u32[]{:S(2)}) %collective-permute-start.11) | collective-permute-done | bytes 2064416 | tf_op jit(solution)/shard_map/ppermute | solution.py:265
  92.9 2.3 slice.77
  105.4 7.7 %shard_map.162 = (bf16[128,1024]{1,0:T(8,128)(2,1)S(1)}, f32[128,128]{1,0:T(8,128)S(1)}, f32[128,1024]{1,0:T(8,128)S(1)}, bf16[128,1024]{1,0:T(8,128)(2,1)S(1)}) custom-call(s32[2]{0:T(128)S(1)} %copy-done.28, bf16[128,1024]{1,0:T(8,128)(2,1)S(1)} %copy-done.23, bf16[128,2048]{1,0:T(8,128)(2,1)S(1)} %copy-done.16, ...), custom_call_target="tpu_custom_call" | custom-call | flops 1610612736 | bytes 4194304 | tf_op jit(solution)/shard_map/pallas_call | solution.py:592
  113.9 8.0 %collective-permute-done.13.refs_4_ = bf16[64,8064]{1,0:T(8,128)(2,1)} collective-permute-done((bf16[64,8064]{1,0:T(8,128)(2,1)}, bf16[64,8064]{1,0:T(8,128)(2,1)}, u32[]{:S(2)}, u32[]{:S(2)}) %collective-permute-start.13) | collective-permute-done | bytes 1032224 | tf_op jit(solution)/shard_map/ppermute | solution.py:265
  122.4 3.0 collective-permute-done.18.refs_9_
  127.0 7.6 %shard_map.163 = (bf16[128,1920]{1,0:T(8,128)(2,1)S(1)}, bf16[128,1920]{1,0:T(8,128)(2,1)S(1)}, bf16[128,1792]{1,0:T(8,128)(2,1)S(1)}, bf16[128,1792]{1,0:T(8,12...) custom-call(s32[2]{0:T(128)S(1)} %copy-done.28, bf16[128,1024]{1,0:T(8,128)(2,1)S(1)} %get-tuple-element.105.xn2, ...), custom_call_target="tpu_custom_call" | custom-call | flops 1409286144 | bytes 11010048 | tf_op jit(solution)/shard_map/pallas_call | solution.py:592
  136.1 8.2 %shard_map.164 = (bf16[128,1024]{1,0:T(8,128)(2,1)}, bf16[128,3200]{1,0:T(8,128)(2,1)S(1)}, bf16[128,3200]{1,0:T(8,128)(2,1)S(1)}, bf16[128,3200]{1,0:T(8,128)(2,1)}, bf16[128,3200]{1,0:T(8,128)(2,1)}) custom-call(s32[2]{0:T(128)S(1)} %copy-done.28, bf16[128,1920]{1,0:T(8,128)(2,1)S(1)} %get-tuple-element.123.gated_one, ...), custom_call_target="tpu_custom_call" | custom-call | flops 1409286144 | bytes 5505024 | tf_op jit(solution)/shard_map/pallas_call | solution.py:592
  144.4 2.8 collective-permute-done.22
  151.0 10.8 %shard_map.165 = (f32[128,1024]{1,0:T(8,128)S(1)}, bf16[128,1024]{1,0:T(8,128)(2,1)S(1)}, f32[1,1024]{1,0:T(1,128)S(1)}) custom-call(s32[2]{0:T(128)S(1)} %copy-done.28, bf16[128,3200]{1,0:T(8,128)(2,1)} %copy-done.5, bf16[128,3200]{1,0:T(8,128)(2,1)} %get-tuple-element.133.pack_two, bf16[128,1024]{1,0:T(8,128)(2,1)S(1)} %bitcast.17, ...), custom_call_target="tpu_custom_call" | custom-call | flops 2113929216 | bytes 16515072 | tf_op jit(solution)/shard_map/pallas_call | solution.py:592
  161.9 6.3 %shard_map.166 = (bf16[128,1024]{1,0:T(8,128)(2,1)S(1)}, f32[128,2048]{1,0:T(8,128)S(1)}, bf16[64,2048]{1,0:T(8,128)(2,1)S(1)}) custom-call(s32[2]{0:T(128)S(1)} %copy-done.28, bf16[128,1024]{1,0:T(8,128)(2,1)S(1)} %copy-done.24, bf16[128,2048]{1,0:T(8,128)(2,1)S(1)} %copy-done.17, bf16[64,2048]{1,0:T(8,128)(2,1)S(1)} %copy-done.26, ...), custom_call_target="tpu_custom_call" | custom-call | flops 2684354560 | bytes 4194304 | tf_op jit(solution)/shard_map/pallas_call | solution.py:592
  175.0 4.2 %collective-permute-done.28 = bf16[128,1280]{1,0:T(8,128)(2,1)} collective-permute-done((bf16[128,1280]{1,0:T(8,128)(2,1)S(1)}, bf16[128,1280]{1,0:T(8,128)(2,1)}, u32[]{:S(2)}, u32[]{:S(2)}) %collective-permute-start.28) | collective-permute-done | bytes 327712 | tf_op jit(solution)/shard_map/ppermute | solution.py:265
  179.2 3.8 %collective-permute-done.27 = bf16[128,1408]{1,0:T(8,128)(2,1)S(1)} collective-permute-done((bf16[128,1408]{1,0:T(8,128)(2,1)S(1)}, bf16[128,1408]{1,0:T(8,128)(2,1)S(1)}, u32[]{:S(2)}, u32[]{:S(2)}) %collective-permute-start.27) | collective-permute-done | bytes 360480 | tf_op jit(solution)/shard_map/ppermute | solution.py:265
  185.1 4.3 %collective-permute-start.32 = (bf16[128,2688]{1,0:T(8,128)(2,1)}, bf16[128,2688]{1,0:T(8,128)(2,1)}, u32[]{:S(2)}, u32[]{:S(2)}) collective-permute-start(bf16[128,2688]{1,0:T(8,128)(2,1)} %fusion.9), channel_id=1, source_target_pairs={{0,8},{24,16},{1,9},{25,17},{2,10},{26,18},{3,11},{27,19},{4,12},{... | collective-permute-start | bytes 2064392 | tf_op jit(solution)/shard_map/ppermute | solution.py:632
  189.9 2.6 shard_map.169
  195.3 2.6 shard_map.170
  205.0 8.4 %collective-permute-done.31 = bf16[128,2688]{1,0:T(8,128)(2,1)} collective-permute-done((bf16[128,2688]{1,0:T(8,128)(2,1)S(1)}, bf16[128,2688]{1,0:T(8,128)(2,1)}, u32[]{:S(2)}, u32[]{:S(2)}) %collective-permute-start.31) | collective-permute-done | bytes 688160 | tf_op jit(solution)/shard_map/ppermute | solution.py:265
  218.8 6.8 %collective-permute-done.33 = bf16[128,2688]{1,0:T(8,128)(2,1)S(1)} collective-permute-done((bf16[128,2688]{1,0:T(8,128)(2,1)S(1)}, bf16[128,2688]{1,0:T(8,128)(2,1)S(1)}, u32[]{:S(2)}, u32[]{:S(2)}) %collective-permute-start.33) | collective-permute-done | bytes 688160 | tf_op jit(solution)/shard_map/ppermute | solution.py:632
  231.7 7.4 %collective-permute-start.42 = (bf16[128,2688]{1,0:T(8,128)(2,1)}, bf16[128,2688]{1,0:T(8,128)(2,1)S(1)}, u32[]{:S(2)}, u32[]{:S(2)}) collective-permute-start(bf16[128,2688]{1,0:T(8,128)(2,1)} %get-tuple-element.224), channel_id=1, source_target_pairs={{0,8},{24,16},{1,9},{25,17},{2,10},{26,18},{3,11},{27,19},{4,12},{... | collective-permute-start | bytes 2064392 | tf_op jit(solution)/shard_map/ppermute | solution.py:632
  245.5 6.4 %shard_map.174 = (bf16[144,1536]{1,0:T(8,128)(2,1)S(1)}, bf16[144,1536]{1,0:T(8,128)(2,1)S(1)}, bf16[128,1024]{1,0:T(8,128)(2,1)}) custom-call(s32[2]{0:T(128)S(1)} %copy-done.28, bf16[128,2048]{1,0:T(8,128)(2,1)S(1)} %get-tuple-element.163.pack_one, bf16[128,2048]{1,0:T(8,128)(2,1)S(1)} %copy-done.10, bf16[128,1024]{1,0:T(8,128)(2,1)S(1)} %bitcast.20, ...), custom_call_target="tpu_custom_call" | custom-call | flops 805306368 | bytes 6291456 | tf_op jit(solution)/shard_map/pallas_call | solution.py:592
  257.4 6.3 %collective-permute-start.48 = (bf16[128,1536]{1,0:T(8,128)(2,1)S(1)}, bf16[128,1536]{1,0:T(8,128)(2,1)S(1)}, u32[]{:S(2)}, u32[]{:S(2)}) collective-permute-start(bf16[128,1536]{1,0:T(8,128)(2,1)S(1)} %get-tuple-element.220), channel_id=1, source_target_pairs={{0,8},{24,16},{1,9},{25,17},{2,10},{26,18},{3,11},{27,19},{4,12},{... | collective-permute-start | bytes 1179656 | tf_op jit(solution)/shard_map/ppermute | solution.py:632
  267.4 4.2 %collective-permute-done.50 = bf16[128,2688]{1,0:T(8,128)(2,1)S(1)} collective-permute-done((bf16[128,2688]{1,0:T(8,128)(2,1)S(1)}, bf16[128,2688]{1,0:T(8,128)(2,1)S(1)}, u32[]{:S(2)}, u32[]{:S(2)}) %collective-permute-start.50) | collective-permute-done | bytes 688160 | tf_op jit(solution)/shard_map/ppermute | solution.py:648
  274.0 4.5 %collective-permute-done.47 = bf16[128,1536]{1,0:T(8,128)(2,1)S(1)} collective-permute-done((bf16[128,1536]{1,0:T(8,128)(2,1)S(1)}, bf16[128,1536]{1,0:T(8,128)(2,1)S(1)}, u32[]{:S(2)}, u32[]{:S(2)}) %collective-permute-start.47) | collective-permute-done | bytes 393248 | tf_op jit(solution)/shard_map/ppermute | solution.py:632
  281.5 9.5 %collective-permute-done.51 = bf16[128,2688]{1,0:T(8,128)(2,1)S(1)} collective-permute-done((bf16[128,2688]{1,0:T(8,128)(2,1)S(1)}, bf16[128,2688]{1,0:T(8,128)(2,1)S(1)}, u32[]{:S(2)}, u32[]{:S(2)}) %collective-permute-start.51) | collective-permute-done | bytes 688160 | tf_op jit(solution)/shard_map/ppermute | solution.py:648
  291.1 3.1 collective-permute-start.52
  295.6 2.8 collective-permute-done.52
  311.6 3.7 %collective-permute-done.58 = bf16[128,1536]{1,0:T(8,128)(2,1)} collective-permute-done((bf16[128,1536]{1,0:T(8,128)(2,1)S(1)}, bf16[128,1536]{1,0:T(8,128)(2,1)}, u32[]{:S(2)}, u32[]{:S(2)}) %collective-permute-start.58) | collective-permute-done | bytes 393248 | tf_op jit(solution)/shard_map/ppermute | solution.py:648
  (251 shorter events, 108.8 us)
Async XLA Ops:
  3.9 27.1 %collective-permute-start.1 = (bf16[128,4224]{1,0:T(8,128)(2,1)}, bf16[128,4224]{1,0:T(8,128)(2,1)}, u32[]{:S(2)}, u32[]{:S(2)}) collective-permute-start(bf16[128,4224]{1,0:T(8,128)(2,1)} %fusion.6.refs_0_.refs_10_), channel_id=1, source_target_pairs={{0,4},{1,5},{2,6},{3,7},{4,0},{5,1},{6,2},{7,3},{8,12},{9,13},{10,... | collective-permute-start | bytes 3244040 | tf_op jit(solution)/shard_map/ppermute | solution.py:265
  6.9 27.0 %collective-permute-start = (bf16[128,4224]{1,0:T(8,128)(2,1)}, bf16[128,4224]{1,0:T(8,128)(2,1)}, u32[]{:S(2)}, u32[]{:S(2)}) collective-permute-start(bf16[128,4224]{1,0:T(8,128)(2,1)} %fusion.6.refs_0_.refs_10_), channel_id=1, source_target_pairs={{0,1},{1,0},{2,3},{3,2},{4,5},{5,4},{6,7},{7,6},{8,9},{9,8},{10,11... | collective-permute-start | bytes 3244040 | tf_op jit(solution)/shard_map/ppermute | solution.py:265
  8.4 42.2 %collective-permute-start.4 = (bf16[128,4224]{1,0:T(8,128)(2,1)}, bf16[128,4224]{1,0:T(8,128)(2,1)}, u32[]{:S(2)}, u32[]{:S(2)}) collective-permute-start(bf16[128,4224]{1,0:T(8,128)(2,1)} %fusion.6.refs_0_.refs_10_), channel_id=1, source_target_pairs={{0,2},{1,3},{2,0},{3,1},{4,6},{5,7},{6,4},{7,5},{8,10},{9,11},{10,... | collective-permute-start | bytes 3244040 | tf_op jit(solution)/shard_map/ppermute | solution.py:265
  48.0 44.9 %collective-permute-start.11 = (bf16[128,8064]{1,0:T(8,128)(2,1)}, bf16[128,8064]{1,0:T(8,128)(2,1)}, u32[]{:S(2)}, u32[]{:S(2)}) collective-permute-start(bf16[128,8064]{1,0:T(8,128)(2,1)} %fusion.5.refs_0_), channel_id=1, source_target_pairs={{0,4},{1,5},{2,6},{3,7},{4,0},{5,1},{6,2},{7,3},{8,12},{9,13},{10,... | collective-permute-start | bytes 6193160 | tf_op jit(solution)/shard_map/ppermute | solution.py:265
  49.5 48.2 %collective-permute-start.10 = (bf16[128,8064]{1,0:T(8,128)(2,1)}, bf16[128,8064]{1,0:T(8,128)(2,1)}, u32[]{:S(2)}, u32[]{:S(2)}) collective-permute-start(bf16[128,8064]{1,0:T(8,128)(2,1)} %fusion.5.refs_0_), channel_id=1, source_target_pairs={{0,1},{1,0},{2,3},{3,2},{4,5},{5,4},{6,7},{7,6},{8,9},{9,8},{10,11... | collective-permute-start | bytes 6193160 | tf_op jit(solution)/shard_map/ppermute | solution.py:265
  60.6 42.5 %collective-permute-start.9 = (bf16[64,2048]{1,0:T(8,128)(2,1)S(1)}, bf16[64,2048]{1,0:T(8,128)(2,1)S(1)}, u32[]{:S(2)}, u32[]{:S(2)}) collective-permute-start(bf16[64,2048]{1,0:T(8,128)(2,1)S(1)} %get-tuple-element.103), channel_id=1, source_target_pairs={{0,1},{1,0},{2,3},{3,2},{4,5},{5,4},{6,7},{7,6},{8,9},{9,8},{10,11... | collective-permute-start | bytes 786440 | tf_op jit(solution)/shard_map/ppermute | solution.py:265
  95.2 26.7 %collective-permute-start.13 = (bf16[64,8064]{1,0:T(8,128)(2,1)}, bf16[64,8064]{1,0:T(8,128)(2,1)}, u32[]{:S(2)}, u32[]{:S(2)}) collective-permute-start(bf16[64,8064]{1,0:T(8,128)(2,1)} %slice.77), channel_id=1, source_target_pairs={{0,1},{1,0},{2,3},{3,2},{4,5},{5,4},{6,7},{7,6},{8,9},{9,8},{10,11... | collective-permute-start | bytes 3096584 | tf_op jit(solution)/shard_map/ppermute | solution.py:265
  99.9 21.9 %collective-permute-start.12 = (bf16[64,8064]{1,0:T(8,128)(2,1)}, bf16[64,8064]{1,0:T(8,128)(2,1)S(1)}, u32[]{:S(2)}, u32[]{:S(2)}) collective-permute-start(bf16[64,8064]{1,0:T(8,128)(2,1)} %slice.76), channel_id=1, source_target_pairs={{0,4},{1,5},{2,6},{3,7},{4,0},{5,1},{6,2},{7,3},{8,12},{9,13},{10,... | collective-permute-start | bytes 3096584 | tf_op jit(solution)/shard_map/ppermute | solution.py:265
  100.5 21.9 %collective-permute-start.14 = (bf16[128,8064]{1,0:T(8,128)(2,1)}, bf16[128,8064]{1,0:T(8,128)(2,1)}, u32[]{:S(2)}, u32[]{:S(2)}) collective-permute-start(bf16[128,8064]{1,0:T(8,128)(2,1)} %fusion.5.refs_0_), channel_id=1, source_target_pairs={{0,2},{1,3},{2,0},{3,1},{4,6},{5,7},{6,4},{7,5},{8,10},{9,11},{10,... | collective-permute-start | bytes 6193160 | tf_op jit(solution)/shard_map/ppermute | solution.py:265
  100.5 24.9 %collective-permute-start.16 = (bf16[128,8064]{1,0:T(8,128)(2,1)}, bf16[128,8064]{1,0:T(8,128)(2,1)}, u32[]{:S(2)}, u32[]{:S(2)}) collective-permute-start(bf16[128,8064]{1,0:T(8,128)(2,1)} %collective-permute-done.11.refs_2_), channel_id=1, source_target_pairs={{0,2},{1,3},{2,0},{3,1},{4,6},{5,7},{6,4},{7,5},{8,10},{9,11},{10,... | collective-permute-start | bytes 6193160 | tf_op jit(solution)/shard_map/ppermute | solution.py:265
  103.2 22.8 %collective-permute-start.15 = (bf16[128,8064]{1,0:T(8,128)(2,1)}, bf16[128,8064]{1,0:T(8,128)(2,1)}, u32[]{:S(2)}, u32[]{:S(2)}) collective-permute-start(bf16[128,8064]{1,0:T(8,128)(2,1)} %collective-permute-done.10.refs_1_), channel_id=1, source_target_pairs={{0,2},{1,3},{2,0},{3,1},{4,6},{5,7},{6,4},{7,5},{8,10},{9,11},{10,... | collective-permute-start | bytes 6193160 | tf_op jit(solution)/shard_map/ppermute | solution.py:265
  148.2 23.2 %collective-permute-start.21 = (bf16[256,1920]{1,0:T(8,128)(2,1)S(1)}, bf16[256,1920]{1,0:T(8,128)(2,1)S(1)}, u32[]{:S(2)}, u32[]{:S(2)}) collective-permute-start(bf16[256,1920]{1,0:T(8,128)(2,1)S(1)} %constant_dynamic-update-slice_fusion.refs_0_), channel_id=1, source_target_pairs={{0,2},{1,3},{2,0},{3,1},{4,6},{5,7},{6,4},{7,5},{8,10},{9,11},{10,... | collective-permute-start | bytes 2949128 | tf_op jit(solution)/shard_map/ppermute | solution.py:265
  148.4 19.8 %collective-permute-start.23 = (bf16[256,1792]{1,0:T(8,128)(2,1)S(1)}, bf16[256,1792]{1,0:T(8,128)(2,1)S(1)}, u32[]{:S(2)}, u32[]{:S(2)}) collective-permute-start(bf16[256,1792]{1,0:T(8,128)(2,1)S(1)} %constant_dynamic-update-slice_fusion.2.refs_0_), channel_id=1, source_target_pairs={{0,2},{1,3},{2,0},{3,1},{4,6},{5,7},{6,4},{7,5},{8,10},{9,11},{10,... | collective-permute-start | bytes 2752520 | tf_op jit(solution)/shard_map/ppermute | solution.py:265
  148.9 25.1 %collective-permute-start.25 = (bf16[128,3200]{1,0:T(8,128)(2,1)S(1)}, bf16[128,3200]{1,0:T(8,128)(2,1)S(1)}, u32[]{:S(2)}, u32[]{:S(2)}) collective-permute-start(bf16[128,3200]{1,0:T(8,128)(2,1)S(1)} %get-tuple-element.135), channel_id=1, source_target_pairs={{0,4},{1,5},{2,6},{3,7},{4,0},{5,1},{6,2},{7,3},{8,12},{9,13},{10,... | collective-permute-start | bytes 2457608 | tf_op jit(solution)/shard_map/ppermute | solution.py:265
  150.5 23.5 %collective-permute-start.19 = (bf16[128,3200]{1,0:T(8,128)(2,1)}, bf16[128,3200]{1,0:T(8,128)(2,1)S(1)}, u32[]{:S(2)}, u32[]{:S(2)}) collective-permute-start(bf16[128,3200]{1,0:T(8,128)(2,1)} %get-tuple-element.121), channel_id=1, source_target_pairs={{0,1},{1,0},{2,3},{3,2},{4,5},{5,4},{6,7},{7,6},{8,9},{9,8},{10,11... | collective-permute-start | bytes 2457608 | tf_op jit(solution)/shard_map/ppermute | solution.py:265
  174.3 15.7 %collective-permute-start.26 = (bf16[256,3200]{1,0:T(8,128)(2,1)S(1)}, bf16[256,3200]{1,0:T(8,128)(2,1)}, u32[]{:S(2)}, u32[]{:S(2)}) collective-permute-start(bf16[256,3200]{1,0:T(8,128)(2,1)S(1)} %constant_dynamic-update-slice_fusion.6.refs_0_), channel_id=1, source_target_pairs={{0,2},{1,3},{2,0},{3,1},{4,6},{5,7},{6,4},{7,5},{8,10},{9,11},{10,... | collective-permute-start | bytes 4915208 | tf_op jit(solution)/shard_map/ppermute | solution.py:265
  174.4 19.7 %collective-permute-start.24 = (bf16[256,3200]{1,0:T(8,128)(2,1)S(1)}, bf16[256,3200]{1,0:T(8,128)(2,1)S(1)}, u32[]{:S(2)}, u32[]{:S(2)}) collective-permute-start(bf16[256,3200]{1,0:T(8,128)(2,1)S(1)} %constant_dynamic-update-slice_fusion.4.refs_0_), channel_id=1, source_target_pairs={{0,2},{1,3},{2,0},{3,1},{4,6},{5,7},{6,4},{7,5},{8,10},{9,11},{10,... | collective-permute-start | bytes 4915208 | tf_op jit(solution)/shard_map/ppermute | solution.py:265
  185.1 17.0 %collective-permute-start.32 = (bf16[128,2688]{1,0:T(8,128)(2,1)}, bf16[128,2688]{1,0:T(8,128)(2,1)}, u32[]{:S(2)}, u32[]{:S(2)}) collective-permute-start(bf16[128,2688]{1,0:T(8,128)(2,1)} %fusion.9), channel_id=1, source_target_pairs={{0,8},{24,16},{1,9},{25,17},{2,10},{26,18},{3,11},{27,19},{4,12},{... | collective-permute-start | bytes 2064392 | tf_op jit(solution)/shard_map/ppermute | solution.py:632
  192.6 20.9 %collective-permute-start.31 = (bf16[128,2688]{1,0:T(8,128)(2,1)S(1)}, bf16[128,2688]{1,0:T(8,128)(2,1)}, u32[]{:S(2)}, u32[]{:S(2)}) collective-permute-start(bf16[128,2688]{1,0:T(8,128)(2,1)S(1)} %get-tuple-element.143), channel_id=1, source_target_pairs={{0,1},{1,0},{2,3},{3,2},{4,5},{5,4},{6,7},{7,6},{8,9},{9,8},{10,11... | collective-permute-start | bytes 2064392 | tf_op jit(solution)/shard_map/ppermute | solution.py:265
  197.9 18.4 %collective-permute-start.35 = (bf16[128,2688]{1,0:T(8,128)(2,1)S(1)}, bf16[128,2688]{1,0:T(8,128)(2,1)S(1)}, u32[]{:S(2)}, u32[]{:S(2)}) collective-permute-start(bf16[128,2688]{1,0:T(8,128)(2,1)S(1)} %get-tuple-element.145), channel_id=1, source_target_pairs={{0,4},{1,5},{2,6},{3,7},{4,0},{5,1},{6,2},{7,3},{8,12},{9,13},{10,... | collective-permute-start | bytes 2064392 | tf_op jit(solution)/shard_map/ppermute | solution.py:265
  202.0 24.6 %collective-permute-start.30 = (bf16[128,2048]{1,0:T(8,128)(2,1)S(1)}, bf16[128,2048]{1,0:T(8,128)(2,1)S(1)}, u32[]{:S(2)}, u32[]{:S(2)}) collective-permute-start(bf16[128,2048]{1,0:T(8,128)(2,1)S(1)} %get-tuple-element.152), channel_id=1, source_target_pairs={{0,4},{1,5},{2,6},{3,7},{4,0},{5,1},{6,2},{7,3},{8,12},{9,13},{10,... | collective-permute-start | bytes 1572872 | tf_op jit(solution)/shard_map/ppermute | solution.py:265
  202.5 24.0 %collective-permute-start.37 = (bf16[128,2048]{1,0:T(8,128)(2,1)S(1)}, bf16[128,2048]{1,0:T(8,128)(2,1)S(1)}, u32[]{:S(2)}, u32[]{:S(2)}) collective-permute-start(bf16[128,2048]{1,0:T(8,128)(2,1)S(1)} %get-tuple-element.162), channel_id=1, source_target_pairs={{0,1},{1,0},{2,3},{3,2},{4,5},{5,4},{6,7},{7,6},{8,9},{9,8},{10,11... | collective-permute-start | bytes 1572872 | tf_op jit(solution)/shard_map/ppermute | solution.py:265
  228.9 23.0 %collective-permute-start.44 = (bf16[128,2688]{1,0:T(8,128)(2,1)}, bf16[128,2688]{1,0:T(8,128)(2,1)}, u32[]{:S(2)}, u32[]{:S(2)}) collective-permute-start(bf16[128,2688]{1,0:T(8,128)(2,1)} %add_convert_fusion.4), channel_id=1, source_target_pairs={{8,0},{16,24},{9,1},{17,25},{10,2},{18,26},{11,3},{19,27},{12,4},{... | collective-permute-start | bytes 2064392 | tf_op jit(solution)/shard_map/ppermute | solution.py:648
  230.2 21.7 %collective-permute-start.43 = (bf16[128,2688]{1,0:T(8,128)(2,1)}, bf16[128,2688]{1,0:T(8,128)(2,1)}, u32[]{:S(2)}, u32[]{:S(2)}) collective-permute-start(bf16[128,2688]{1,0:T(8,128)(2,1)} %add_convert_fusion.3), channel_id=1, source_target_pairs={{8,16},{16,8},{9,17},{17,9},{10,18},{18,10},{11,19},{19,11},{12,20... | collective-permute-start | bytes 2064392 | tf_op jit(solution)/shard_map/ppermute | solution.py:640
  231.7 23.1 %collective-permute-start.42 = (bf16[128,2688]{1,0:T(8,128)(2,1)}, bf16[128,2688]{1,0:T(8,128)(2,1)S(1)}, u32[]{:S(2)}, u32[]{:S(2)}) collective-permute-start(bf16[128,2688]{1,0:T(8,128)(2,1)} %get-tuple-element.224), channel_id=1, source_target_pairs={{0,8},{24,16},{1,9},{25,17},{2,10},{26,18},{3,11},{27,19},{4,12},{... | collective-permute-start | bytes 2064392 | tf_op jit(solution)/shard_map/ppermute | solution.py:632
  241.4 15.9 %collective-permute-start.41 = (bf16[128,1536]{1,0:T(8,128)(2,1)S(1)}, bf16[128,1536]{1,0:T(8,128)(2,1)S(1)}, u32[]{:S(2)}, u32[]{:S(2)}) collective-permute-start(bf16[128,1536]{1,0:T(8,128)(2,1)S(1)} %get-tuple-element.165), channel_id=1, source_target_pairs={{0,4},{1,5},{2,6},{3,7},{4,0},{5,1},{6,2},{7,3},{8,12},{9,13},{10,... | collective-permute-start | bytes 1179656 | tf_op jit(solution)/shard_map/ppermute | solution.py:265
  244.0 19.7 %collective-permute-start.40 = (bf16[128,1536]{1,0:T(8,128)(2,1)S(1)}, bf16[128,1536]{1,0:T(8,128)(2,1)S(1)}, u32[]{:S(2)}, u32[]{:S(2)}) collective-permute-start(bf16[128,1536]{1,0:T(8,128)(2,1)S(1)} %get-tuple-element.167), channel_id=1, source_target_pairs={{0,1},{1,0},{2,3},{3,2},{4,5},{5,4},{6,7},{7,6},{8,9},{9,8},{10,11... | collective-permute-start | bytes 1179656 | tf_op jit(solution)/shard_map/ppermute | solution.py:265
  253.5 18.0 %collective-permute-start.50 = (bf16[128,2688]{1,0:T(8,128)(2,1)S(1)}, bf16[128,2688]{1,0:T(8,128)(2,1)S(1)}, u32[]{:S(2)}, u32[]{:S(2)}) collective-permute-start(bf16[128,2688]{1,0:T(8,128)(2,1)S(1)} %add_convert_fusion.2), channel_id=1, source_target_pairs={{8,0},{16,24},{9,1},{17,25},{10,2},{18,26},{11,3},{19,27},{12,4},{... | collective-permute-start | bytes 2064392 | tf_op jit(solution)/shard_map/ppermute | solution.py:648
  257.4 15.8 %collective-permute-start.48 = (bf16[128,1536]{1,0:T(8,128)(2,1)S(1)}, bf16[128,1536]{1,0:T(8,128)(2,1)S(1)}, u32[]{:S(2)}, u32[]{:S(2)}) collective-permute-start(bf16[128,1536]{1,0:T(8,128)(2,1)S(1)} %get-tuple-element.220), channel_id=1, source_target_pairs={{0,8},{24,16},{1,9},{25,17},{2,10},{26,18},{3,11},{27,19},{4,12},{... | collective-permute-start | bytes 1179656 | tf_op jit(solution)/shard_map/ppermute | solution.py:632
  266.1 24.9 %collective-permute-start.51 = (bf16[128,2688]{1,0:T(8,128)(2,1)S(1)}, bf16[128,2688]{1,0:T(8,128)(2,1)S(1)}, u32[]{:S(2)}, u32[]{:S(2)}) collective-permute-start(bf16[128,2688]{1,0:T(8,128)(2,1)S(1)} %add_convert_fusion), channel_id=1, source_target_pairs={{8,0},{16,24},{9,1},{17,25},{10,2},{18,26},{11,3},{19,27},{12,4},{... | collective-permute-start | bytes 2064392 | tf_op jit(solution)/shard_map/ppermute | solution.py:648
  273.3 17.8 %collective-permute-start.53 = (bf16[128,1536]{1,0:T(8,128)(2,1)S(1)}, bf16[128,1536]{1,0:T(8,128)(2,1)S(1)}, u32[]{:S(2)}, u32[]{:S(2)}) collective-permute-start(bf16[128,1536]{1,0:T(8,128)(2,1)S(1)} %add_convert_fusion.9), channel_id=1, source_target_pairs={{8,16},{16,8},{9,17},{17,9},{10,18},{18,10},{11,19},{19,11},{12,20... | collective-permute-start | bytes 1179656 | tf_op jit(solution)/shard_map/ppermute | solution.py:640
  280.8 19.8 %collective-permute-start.55 = (bf16[128,1536]{1,0:T(8,128)(2,1)S(1)}, bf16[128,1536]{1,0:T(8,128)(2,1)S(1)}, u32[]{:S(2)}, u32[]{:S(2)}) collective-permute-start(bf16[128,1536]{1,0:T(8,128)(2,1)S(1)} %add_convert_fusion.8), channel_id=1, source_target_pairs={{8,16},{16,8},{9,17},{17,9},{10,18},{18,10},{11,19},{19,11},{12,20... | collective-permute-start | bytes 1179656 | tf_op jit(solution)/shard_map/ppermute | solution.py:640
  (69 other events, 712.2 us)

commit v9 on v8

--- a/solution.py
+++ b/solution.py
@@ -829,10 +829,10 @@
     out_back = swap(out_sent, X_BIT)
     high_pair = line_pair(high_part, later(high_first, low_pair))
     high_other = line_middle(high_pair)
-    out_part = out_own + later(out_back, high_pair, gate_last).astype(F32)
+    low_total = line_total(low_pair, later(low_other, high_pair))
+    low_last = line_back(low_total)
+    out_part = out_own + later(out_back, low_total, gate_last).astype(F32)
     out_first = line_first(out_part)
-    low_total = line_total(low_pair, later(low_other, out_part))
-    low_last = line_back(low_total)
     out_pair = line_pair(out_part, later(out_first, low_total))
     out_other = line_middle(out_pair)
     high_total = line_total(high_pair, later(high_other, out_pair))

time: 322 us -> 322 us (level)
  starting transfers between devices: 67.7 us -> 72.2 us
    ppermute x6, starting transfers between devices: 24 us -> 28.4 us  [line_first(): return lax.ppermute(part.astype(BF16), 'replica', [(0, 1), (3, 2)])]
    unnamed x93 -> x87, local copies, waits for them, and re-layouts: 7.98 us -> 5.96 us
  transfers between devices with their start and end apart: 59 -> 59, of which waited for: 28 -> 29; matrix products, arithmetic and copies ran while one was open for 10% -> 9% of each run, Pallas kernels for 19% -> 18%
where the time goes in v9:
time: 322 us; the launch traced here: 321 us
  waiting for transfers between devices  143 us (44%)
  starting transfers between devices  72.2 us (22%)
  Pallas kernels  65 us (20%)
  other arithmetic  23.1 us (7%)
  local copies, waits for them, and re-layouts  16 us (5%)
    ppermute x41, waiting for transfers between devices, swap(): return lax.ppermute(value, PLANE, [(i, i ^ bit) for i in range(PLANE_SIZE)])  105 us
    pallas_call x15, Pallas kernels, call(): pl.pallas_call(kernel, out_shape=[jax.ShapeDtypeStruct(shape, kind) for s...  65 us
    ppermute x41, starting transfers between devices, swap(): return lax.ppermute(value, PLANE, [(i, i ^ bit) for i in range(PLANE_SIZE)])  30.3 us
    ppermute x6, starting transfers between devices, line_first(): return lax.ppermute(part.astype(BF16), 'replica', [(0, 1), (3, 2)])  28.4 us
    ppermute x6, waiting for transfers between devices, line_first(): return lax.ppermute(part.astype(BF16), 'replica', [(0, 1), (3, 2)])  20.8 us
    ppermute x6, waiting for transfers between devices, line_back(): return lax.ppermute(total, 'replica', [(1, 0), (2, 3)])  17.8 us
    ppermute x6, starting transfers between devices, line_back(): return lax.ppermute(total, 'replica', [(1, 0), (2, 3)])  7.74 us
  transfers between devices with their start and end apart: 59, of which 29 were waited for; matrix products, arithmetic and copies ran while one was open for 9% of the time, Pallas kernels for 18%

profile of v9, /device:TPU:0, one launch (start us, length us, event | category | flops | bytes accessed | tf_op | source)
XLA Modules:
  0.0 321.1 jit_solution(16523046364393287690)
XLA Ops:
  1.5 2.4 fusion.6.refs_0_.refs_10_
  3.9 3.0 collective-permute-start.1
  9.1 22.0 %collective-permute-done.1.refs_2_.refs_12_ = bf16[128,4224]{1,0:T(8,128)(2,1)} collective-permute-done((bf16[128,4224]{1,0:T(8,128)(2,1)}, bf16[128,4224]{1,0:T(8,128)(2,1)}, u32[]{:S(2)}, u32[]{:S(2)}) %collective-permute-start.1) | collective-permute-done | bytes 1081376 | tf_op jit(solution)/shard_map/ppermute | solution.py:265
  38.1 7.6 %collective-permute-done.3.refs_4_.refs_14_ = bf16[64,4224]{1,0:T(8,128)(2,1)S(1)} collective-permute-done((bf16[64,4224]{1,0:T(8,128)(2,1)S(1)}, bf16[64,4224]{1,0:T(8,128)(2,1)S(1)}, u32[]{:S(2)}, u32[]{:S(2)}) %collective-permute-start.3) | collective-permute-done | bytes 540704 | tf_op jit(solution)/shard_map/ppermute | solution.py:265
  55.8 4.7 %shard_map.161 = (bf16[128,1024]{1,0:T(8,128)(2,1)S(1)}, bf16[128,2048]{1,0:T(8,128)(2,1)S(1)}, bf16[64,2048]{1,0:T(8,128)(2,1)S(1)}, bf16[128,1024]{1,0:T(8,128)(2,1)S(1)}, f32[8,1024]{1,0:T(8,128)S(1)}) custom-call(s32[2]{0:T(128)S(1)} %pad_add_fusion.place, bf16[128,1024]{1,0:T(8,128)(2,1)S(1)} %bitcast.18, f32[128,128]{1,0:T(8,128)S(1)} %get-tuple-element.231.cosine, ...), custom_call_target="tpu_custom_call" | custom-call | flops 805306368 | bytes 8650752 | tf_op jit(solution)/shard_map/pallas_call | solution.py:592
  62.2 30.7 %collective-permute-done.11.refs_2_ = bf16[128,8064]{1,0:T(8,128)(2,1)} collective-permute-done((bf16[128,8064]{1,0:T(8,128)(2,1)}, bf16[128,8064]{1,0:T(8,128)(2,1)}, u32[]{:S(2)}, u32[]{:S(2)}) %collective-permute-start.11) | collective-permute-done | bytes 2064416 | tf_op jit(solution)/shard_map/ppermute | solution.py:265
  92.9 2.3 slice.77
  105.4 7.7 %shard_map.162 = (bf16[128,1024]{1,0:T(8,128)(2,1)S(1)}, f32[128,128]{1,0:T(8,128)S(1)}, f32[128,1024]{1,0:T(8,128)S(1)}, bf16[128,1024]{1,0:T(8,128)(2,1)S(1)}) custom-call(s32[2]{0:T(128)S(1)} %copy-done.24, bf16[128,1024]{1,0:T(8,128)(2,1)S(1)} %copy-done.19, bf16[128,2048]{1,0:T(8,128)(2,1)S(1)} %copy-done.12, ...), custom_call_target="tpu_custom_call" | custom-call | flops 1610612736 | bytes 4194304 | tf_op jit(solution)/shard_map/pallas_call | solution.py:592
  113.9 8.0 %collective-permute-done.13.refs_4_ = bf16[64,8064]{1,0:T(8,128)(2,1)} collective-permute-done((bf16[64,8064]{1,0:T(8,128)(2,1)}, bf16[64,8064]{1,0:T(8,128)(2,1)}, u32[]{:S(2)}, u32[]{:S(2)}) %collective-permute-start.13) | collective-permute-done | bytes 1032224 | tf_op jit(solution)/shard_map/ppermute | solution.py:265
  122.4 3.0 collective-permute-done.18.refs_9_
  127.0 7.5 %shard_map.163 = (bf16[128,1920]{1,0:T(8,128)(2,1)S(1)}, bf16[128,1920]{1,0:T(8,128)(2,1)S(1)}, bf16[128,1792]{1,0:T(8,128)(2,1)S(1)}, bf16[128,1792]{1,0:T(8,12...) custom-call(s32[2]{0:T(128)S(1)} %copy-done.24, bf16[128,1024]{1,0:T(8,128)(2,1)S(1)} %get-tuple-element.105.xn2, ...), custom_call_target="tpu_custom_call" | custom-call | flops 1409286144 | bytes 11010048 | tf_op jit(solution)/shard_map/pallas_call | solution.py:592
  136.0 8.5 %shard_map.164 = (bf16[128,1024]{1,0:T(8,128)(2,1)}, bf16[128,3200]{1,0:T(8,128)(2,1)S(1)}, bf16[128,3200]{1,0:T(8,128)(2,1)}, bf16[128,3200]{1,0:T(8,128)(2,1)}, bf16[128,3200]{1,0:T(8,128)(2,1)}) custom-call(s32[2]{0:T(128)S(1)} %copy-done.24, bf16[128,1920]{1,0:T(8,128)(2,1)S(1)} %get-tuple-element.123.gated_one, ...), custom_call_target="tpu_custom_call" | custom-call | flops 1409286144 | bytes 5505024 | tf_op jit(solution)/shard_map/pallas_call | solution.py:592
  144.5 2.5 collective-permute-done.22
  150.9 10.6 %shard_map.165 = (f32[128,1024]{1,0:T(8,128)S(1)}, bf16[128,1024]{1,0:T(8,128)(2,1)S(1)}, f32[1,1024]{1,0:T(1,128)S(1)}) custom-call(s32[2]{0:T(128)S(1)} %copy-done.24, bf16[128,3200]{1,0:T(8,128)(2,1)} %copy-done.5, bf16[128,3200]{1,0:T(8,128)(2,1)} %get-tuple-element.133.pack_two, bf16[128,1024]{1,0:T(8,128)(2,1)S(1)} %bitcast.17, ...), custom_call_target="tpu_custom_call" | custom-call | flops 2113929216 | bytes 16515072 | tf_op jit(solution)/shard_map/pallas_call | solution.py:592
  161.5 6.3 %shard_map.166 = (bf16[128,1024]{1,0:T(8,128)(2,1)S(1)}, f32[128,2048]{1,0:T(8,128)S(1)}, bf16[64,2048]{1,0:T(8,128)(2,1)S(1)}) custom-call(s32[2]{0:T(128)S(1)} %copy-done.24, bf16[128,1024]{1,0:T(8,128)(2,1)S(1)} %copy-done.20, bf16[128,2048]{1,0:T(8,128)(2,1)S(1)} %copy-done.13, bf16[64,2048]{1,0:T(8,128)(2,1)S(1)} %copy-done.22, ...), custom_call_target="tpu_custom_call" | custom-call | flops 2684354560 | bytes 4194304 | tf_op jit(solution)/shard_map/pallas_call | solution.py:592
  175.8 3.1 collective-permute-done.28
  178.9 3.8 %collective-permute-done.27 = bf16[128,1408]{1,0:T(8,128)(2,1)S(1)} collective-permute-done((bf16[128,1408]{1,0:T(8,128)(2,1)S(1)}, bf16[128,1408]{1,0:T(8,128)(2,1)S(1)}, u32[]{:S(2)}, u32[]{:S(2)}) %collective-permute-start.27) | collective-permute-done | bytes 360480 | tf_op jit(solution)/shard_map/ppermute | solution.py:265
  183.9 3.5 %collective-permute-start.32 = (bf16[128,2688]{1,0:T(8,128)(2,1)S(1)}, bf16[128,2688]{1,0:T(8,128)(2,1)S(1)}, u32[]{:S(2)}, u32[]{:S(2)}) collective-permute-start(bf16[128,2688]{1,0:T(8,128)(2,1)S(1)} %fusion.10), channel_id=1, source_target_pairs={{0,8},{24,16},{1,9},{25,17},{2,10},{26,18},{3,11},{27,19},{4,12},{... | collective-permute-start | bytes 2064392 | tf_op jit(solution)/shard_map/ppermute | solution.py:632
  188.0 2.6 shard_map.169
  192.2 2.6 shard_map.170
  197.9 2.7 collective-permute-done.32
  202.4 9.1 %collective-permute-done.31 = bf16[128,2688]{1,0:T(8,128)(2,1)} collective-permute-done((bf16[128,2688]{1,0:T(8,128)(2,1)S(1)}, bf16[128,2688]{1,0:T(8,128)(2,1)}, u32[]{:S(2)}, u32[]{:S(2)}) %collective-permute-start.31) | collective-permute-done | bytes 688160 | tf_op jit(solution)/shard_map/ppermute | solution.py:265
  216.7 7.0 %collective-permute-done.33 = bf16[128,2688]{1,0:T(8,128)(2,1)S(1)} collective-permute-done((bf16[128,2688]{1,0:T(8,128)(2,1)S(1)}, bf16[128,2688]{1,0:T(8,128)(2,1)S(1)}, u32[]{:S(2)}, u32[]{:S(2)}) %collective-permute-start.33) | collective-permute-done | bytes 688160 | tf_op jit(solution)/shard_map/ppermute | solution.py:632
  227.4 6.6 %collective-permute-start.42 = (bf16[128,2688]{1,0:T(8,128)(2,1)}, bf16[128,2688]{1,0:T(8,128)(2,1)S(1)}, u32[]{:S(2)}, u32[]{:S(2)}) collective-permute-start(bf16[128,2688]{1,0:T(8,128)(2,1)} %get-tuple-element.222), channel_id=1, source_target_pairs={{0,8},{24,16},{1,9},{25,17},{2,10},{26,18},{3,11},{27,19},{4,12},{... | collective-permute-start | bytes 2064392 | tf_op jit(solution)/shard_map/ppermute | solution.py:632
  237.9 6.3 %shard_map.174 = (bf16[144,1536]{1,0:T(8,128)(2,1)S(1)}, bf16[144,1536]{1,0:T(8,128)(2,1)S(1)}, bf16[128,1024]{1,0:T(8,128)(2,1)}) custom-call(s32[2]{0:T(128)S(1)} %copy-done.24, bf16[128,2048]{1,0:T(8,128)(2,1)S(1)} %get-tuple-element.163.pack_one, bf16[128,2048]{1,0:T(8,128)(2,1)S(1)} %get-tuple-element.160.pack_two, bf16[128,1024]{1,0:T(8,128)(2,1)S(1)} %bitcast.20, ...), custom_call_target="tpu_custom_call" | custom-call | flops 805306368 | bytes 6291456 | tf_op jit(solution)/shard_map/pallas_call | solution.py:592
  250.2 6.5 %collective-permute-start.47 = (bf16[128,1536]{1,0:T(8,128)(2,1)S(1)}, bf16[128,1536]{1,0:T(8,128)(2,1)S(1)}, u32[]{:S(2)}, u32[]{:S(2)}) collective-permute-start(bf16[128,1536]{1,0:T(8,128)(2,1)S(1)} %get-tuple-element.220), channel_id=1, source_target_pairs={{0,8},{24,16},{1,9},{25,17},{2,10},{26,18},{3,11},{27,19},{4,12},{... | collective-permute-start | bytes 1179656 | tf_op jit(solution)/shard_map/ppermute | solution.py:632
  261.1 3.8 %collective-permute-done.49 = bf16[128,2688]{1,0:T(8,128)(2,1)S(1)} collective-permute-done((bf16[128,2688]{1,0:T(8,128)(2,1)S(1)}, bf16[128,2688]{1,0:T(8,128)(2,1)S(1)}, u32[]{:S(2)}, u32[]{:S(2)}) %collective-permute-start.49) | collective-permute-done | bytes 688160 | tf_op jit(solution)/shard_map/ppermute | solution.py:648
  267.0 5.1 %collective-permute-done.51 = bf16[128,1536]{1,0:T(8,128)(2,1)S(1)} collective-permute-done((bf16[128,1536]{1,0:T(8,128)(2,1)S(1)}, bf16[128,1536]{1,0:T(8,128)(2,1)S(1)}, u32[]{:S(2)}, u32[]{:S(2)}) %collective-permute-start.51) | collective-permute-done | bytes 393248 | tf_op jit(solution)/shard_map/ppermute | solution.py:632
  277.4 6.6 %collective-permute-done.52 = bf16[128,2688]{1,0:T(8,128)(2,1)} collective-permute-done((bf16[128,2688]{1,0:T(8,128)(2,1)S(1)}, bf16[128,2688]{1,0:T(8,128)(2,1)}, u32[]{:S(2)}, u32[]{:S(2)}) %collective-permute-start.52) | collective-permute-done | bytes 688160 | tf_op jit(solution)/shard_map/ppermute | solution.py:648
  285.1 8.9 %collective-permute-start.53 = (bf16[144,1024]{1,0:T(8,128)(2,1)S(1)}, bf16[144,1024]{1,0:T(8,128)(2,1)S(1)}, u32[]{:S(2)}, u32[]{:S(2)}) collective-permute-start(bf16[144,1024]{1,0:T(8,128)(2,1)S(1)} %fusion.8), channel_id=1, source_target_pairs={{0,8},{24,16},{1,9},{25,17},{2,10},{26,18},{3,11},{27,19},{4,12},{... | collective-permute-start | bytes 884744 | tf_op jit(solution)/shard_map/ppermute | solution.py:632
  295.0 3.1 collective-permute-done.53
  310.0 5.3 %collective-permute-done.58 = bf16[128,1536]{1,0:T(8,128)(2,1)} collective-permute-done((bf16[128,1536]{1,0:T(8,128)(2,1)S(1)}, bf16[128,1536]{1,0:T(8,128)(2,1)}, u32[]{:S(2)}, u32[]{:S(2)}) %collective-permute-start.58) | collective-permute-done | bytes 393248 | tf_op jit(solution)/shard_map/ppermute | solution.py:648
  (245 shorter events, 106.0 us)
Async XLA Ops:
  3.9 27.1 %collective-permute-start.1 = (bf16[128,4224]{1,0:T(8,128)(2,1)}, bf16[128,4224]{1,0:T(8,128)(2,1)}, u32[]{:S(2)}, u32[]{:S(2)}) collective-permute-start(bf16[128,4224]{1,0:T(8,128)(2,1)} %fusion.6.refs_0_.refs_10_), channel_id=1, source_target_pairs={{0,4},{1,5},{2,6},{3,7},{4,0},{5,1},{6,2},{7,3},{8,12},{9,13},{10,... | collective-permute-start | bytes 3244040 | tf_op jit(solution)/shard_map/ppermute | solution.py:265
  6.9 27.0 %collective-permute-start = (bf16[128,4224]{1,0:T(8,128)(2,1)}, bf16[128,4224]{1,0:T(8,128)(2,1)}, u32[]{:S(2)}, u32[]{:S(2)}) collective-permute-start(bf16[128,4224]{1,0:T(8,128)(2,1)} %fusion.6.refs_0_.refs_10_), channel_id=1, source_target_pairs={{0,1},{1,0},{2,3},{3,2},{4,5},{5,4},{6,7},{7,6},{8,9},{9,8},{10,11... | collective-permute-start | bytes 3244040 | tf_op jit(solution)/shard_map/ppermute | solution.py:265
  8.4 42.2 %collective-permute-start.4 = (bf16[128,4224]{1,0:T(8,128)(2,1)}, bf16[128,4224]{1,0:T(8,128)(2,1)}, u32[]{:S(2)}, u32[]{:S(2)}) collective-permute-start(bf16[128,4224]{1,0:T(8,128)(2,1)} %fusion.6.refs_0_.refs_10_), channel_id=1, source_target_pairs={{0,2},{1,3},{2,0},{3,1},{4,6},{5,7},{6,4},{7,5},{8,10},{9,11},{10,... | collective-permute-start | bytes 3244040 | tf_op jit(solution)/shard_map/ppermute | solution.py:265
  48.0 44.9 %collective-permute-start.11 = (bf16[128,8064]{1,0:T(8,128)(2,1)}, bf16[128,8064]{1,0:T(8,128)(2,1)}, u32[]{:S(2)}, u32[]{:S(2)}) collective-permute-start(bf16[128,8064]{1,0:T(8,128)(2,1)} %fusion.5.refs_0_), channel_id=1, source_target_pairs={{0,4},{1,5},{2,6},{3,7},{4,0},{5,1},{6,2},{7,3},{8,12},{9,13},{10,... | collective-permute-start | bytes 6193160 | tf_op jit(solution)/shard_map/ppermute | solution.py:265
  49.5 48.2 %collective-permute-start.10 = (bf16[128,8064]{1,0:T(8,128)(2,1)}, bf16[128,8064]{1,0:T(8,128)(2,1)}, u32[]{:S(2)}, u32[]{:S(2)}) collective-permute-start(bf16[128,8064]{1,0:T(8,128)(2,1)} %fusion.5.refs_0_), channel_id=1, source_target_pairs={{0,1},{1,0},{2,3},{3,2},{4,5},{5,4},{6,7},{7,6},{8,9},{9,8},{10,11... | collective-permute-start | bytes 6193160 | tf_op jit(solution)/shard_map/ppermute | solution.py:265
  60.6 42.5 %collective-permute-start.9 = (bf16[64,2048]{1,0:T(8,128)(2,1)S(1)}, bf16[64,2048]{1,0:T(8,128)(2,1)S(1)}, u32[]{:S(2)}, u32[]{:S(2)}) collective-permute-start(bf16[64,2048]{1,0:T(8,128)(2,1)S(1)} %get-tuple-element.103), channel_id=1, source_target_pairs={{0,1},{1,0},{2,3},{3,2},{4,5},{5,4},{6,7},{7,6},{8,9},{9,8},{10,11... | collective-permute-start | bytes 786440 | tf_op jit(solution)/shard_map/ppermute | solution.py:265
  95.2 26.7 %collective-permute-start.13 = (bf16[64,8064]{1,0:T(8,128)(2,1)}, bf16[64,8064]{1,0:T(8,128)(2,1)}, u32[]{:S(2)}, u32[]{:S(2)}) collective-permute-start(bf16[64,8064]{1,0:T(8,128)(2,1)} %slice.77), channel_id=1, source_target_pairs={{0,1},{1,0},{2,3},{3,2},{4,5},{5,4},{6,7},{7,6},{8,9},{9,8},{10,11... | collective-permute-start | bytes 3096584 | tf_op jit(solution)/shard_map/ppermute | solution.py:265
  99.9 21.9 %collective-permute-start.12 = (bf16[64,8064]{1,0:T(8,128)(2,1)}, bf16[64,8064]{1,0:T(8,128)(2,1)S(1)}, u32[]{:S(2)}, u32[]{:S(2)}) collective-permute-start(bf16[64,8064]{1,0:T(8,128)(2,1)} %slice.76), channel_id=1, source_target_pairs={{0,4},{1,5},{2,6},{3,7},{4,0},{5,1},{6,2},{7,3},{8,12},{9,13},{10,... | collective-permute-start | bytes 3096584 | tf_op jit(solution)/shard_map/ppermute | solution.py:265
  100.5 21.9 %collective-permute-start.14 = (bf16[128,8064]{1,0:T(8,128)(2,1)}, bf16[128,8064]{1,0:T(8,128)(2,1)}, u32[]{:S(2)}, u32[]{:S(2)}) collective-permute-start(bf16[128,8064]{1,0:T(8,128)(2,1)} %fusion.5.refs_0_), channel_id=1, source_target_pairs={{0,2},{1,3},{2,0},{3,1},{4,6},{5,7},{6,4},{7,5},{8,10},{9,11},{10,... | collective-permute-start | bytes 6193160 | tf_op jit(solution)/shard_map/ppermute | solution.py:265
  100.5 24.9 %collective-permute-start.16 = (bf16[128,8064]{1,0:T(8,128)(2,1)}, bf16[128,8064]{1,0:T(8,128)(2,1)}, u32[]{:S(2)}, u32[]{:S(2)}) collective-permute-start(bf16[128,8064]{1,0:T(8,128)(2,1)} %collective-permute-done.11.refs_2_), channel_id=1, source_target_pairs={{0,2},{1,3},{2,0},{3,1},{4,6},{5,7},{6,4},{7,5},{8,10},{9,11},{10,... | collective-permute-start | bytes 6193160 | tf_op jit(solution)/shard_map/ppermute | solution.py:265
  103.2 22.8 %collective-permute-start.15 = (bf16[128,8064]{1,0:T(8,128)(2,1)}, bf16[128,8064]{1,0:T(8,128)(2,1)}, u32[]{:S(2)}, u32[]{:S(2)}) collective-permute-start(bf16[128,8064]{1,0:T(8,128)(2,1)} %collective-permute-done.10.refs_1_), channel_id=1, source_target_pairs={{0,2},{1,3},{2,0},{3,1},{4,6},{5,7},{6,4},{7,5},{8,10},{9,11},{10,... | collective-permute-start | bytes 6193160 | tf_op jit(solution)/shard_map/ppermute | solution.py:265
  148.1 23.1 %collective-permute-start.21 = (bf16[256,1920]{1,0:T(8,128)(2,1)S(1)}, bf16[256,1920]{1,0:T(8,128)(2,1)S(1)}, u32[]{:S(2)}, u32[]{:S(2)}) collective-permute-start(bf16[256,1920]{1,0:T(8,128)(2,1)S(1)} %constant_dynamic-update-slice_fusion.refs_0_), channel_id=1, source_target_pairs={{0,2},{1,3},{2,0},{3,1},{4,6},{5,7},{6,4},{7,5},{8,10},{9,11},{10,... | collective-permute-start | bytes 2949128 | tf_op jit(solution)/shard_map/ppermute | solution.py:265
  148.2 19.6 %collective-permute-start.23 = (bf16[256,1792]{1,0:T(8,128)(2,1)S(1)}, bf16[256,1792]{1,0:T(8,128)(2,1)S(1)}, u32[]{:S(2)}, u32[]{:S(2)}) collective-permute-start(bf16[256,1792]{1,0:T(8,128)(2,1)S(1)} %constant_dynamic-update-slice_fusion.2.refs_0_), channel_id=1, source_target_pairs={{0,2},{1,3},{2,0},{3,1},{4,6},{5,7},{6,4},{7,5},{8,10},{9,11},{10,... | collective-permute-start | bytes 2752520 | tf_op jit(solution)/shard_map/ppermute | solution.py:265
  148.8 24.9 %collective-permute-start.25 = (bf16[128,3200]{1,0:T(8,128)(2,1)}, bf16[128,3200]{1,0:T(8,128)(2,1)}, u32[]{:S(2)}, u32[]{:S(2)}) collective-permute-start(bf16[128,3200]{1,0:T(8,128)(2,1)} %get-tuple-element.135), channel_id=1, source_target_pairs={{0,4},{1,5},{2,6},{3,7},{4,0},{5,1},{6,2},{7,3},{8,12},{9,13},{10,... | collective-permute-start | bytes 2457608 | tf_op jit(solution)/shard_map/ppermute | solution.py:265
  150.3 23.4 %collective-permute-start.19 = (bf16[128,3200]{1,0:T(8,128)(2,1)}, bf16[128,3200]{1,0:T(8,128)(2,1)S(1)}, u32[]{:S(2)}, u32[]{:S(2)}) collective-permute-start(bf16[128,3200]{1,0:T(8,128)(2,1)} %get-tuple-element.121), channel_id=1, source_target_pairs={{0,1},{1,0},{2,3},{3,2},{4,5},{5,4},{6,7},{7,6},{8,9},{9,8},{10,11... | collective-permute-start | bytes 2457608 | tf_op jit(solution)/shard_map/ppermute | solution.py:265
  175.3 17.0 %collective-permute-start.24 = (bf16[256,3200]{1,0:T(8,128)(2,1)S(1)}, bf16[256,3200]{1,0:T(8,128)(2,1)}, u32[]{:S(2)}, u32[]{:S(2)}) collective-permute-start(bf16[256,3200]{1,0:T(8,128)(2,1)S(1)} %constant_dynamic-update-slice_fusion.4.refs_0_), channel_id=1, source_target_pairs={{0,2},{1,3},{2,0},{3,1},{4,6},{5,7},{6,4},{7,5},{8,10},{9,11},{10,... | collective-permute-start | bytes 4915208 | tf_op jit(solution)/shard_map/ppermute | solution.py:265
  183.9 16.6 %collective-permute-start.32 = (bf16[128,2688]{1,0:T(8,128)(2,1)S(1)}, bf16[128,2688]{1,0:T(8,128)(2,1)S(1)}, u32[]{:S(2)}, u32[]{:S(2)}) collective-permute-start(bf16[128,2688]{1,0:T(8,128)(2,1)S(1)} %fusion.10), channel_id=1, source_target_pairs={{0,8},{24,16},{1,9},{25,17},{2,10},{26,18},{3,11},{27,19},{4,12},{... | collective-permute-start | bytes 2064392 | tf_op jit(solution)/shard_map/ppermute | solution.py:632
  190.7 20.9 %collective-permute-start.31 = (bf16[128,2688]{1,0:T(8,128)(2,1)S(1)}, bf16[128,2688]{1,0:T(8,128)(2,1)}, u32[]{:S(2)}, u32[]{:S(2)}) collective-permute-start(bf16[128,2688]{1,0:T(8,128)(2,1)S(1)} %get-tuple-element.143), channel_id=1, source_target_pairs={{0,1},{1,0},{2,3},{3,2},{4,5},{5,4},{6,7},{7,6},{8,9},{9,8},{10,11... | collective-permute-start | bytes 2064392 | tf_op jit(solution)/shard_map/ppermute | solution.py:265
  194.8 19.6 %collective-permute-start.35 = (bf16[128,2688]{1,0:T(8,128)(2,1)S(1)}, bf16[128,2688]{1,0:T(8,128)(2,1)}, u32[]{:S(2)}, u32[]{:S(2)}) collective-permute-start(bf16[128,2688]{1,0:T(8,128)(2,1)S(1)} %get-tuple-element.145), channel_id=1, source_target_pairs={{0,4},{1,5},{2,6},{3,7},{4,0},{5,1},{6,2},{7,3},{8,12},{9,13},{10,... | collective-permute-start | bytes 2064392 | tf_op jit(solution)/shard_map/ppermute | solution.py:265
  200.5 23.3 %collective-permute-start.30 = (bf16[128,2048]{1,0:T(8,128)(2,1)S(1)}, bf16[128,2048]{1,0:T(8,128)(2,1)S(1)}, u32[]{:S(2)}, u32[]{:S(2)}) collective-permute-start(bf16[128,2048]{1,0:T(8,128)(2,1)S(1)} %get-tuple-element.152), channel_id=1, source_target_pairs={{0,4},{1,5},{2,6},{3,7},{4,0},{5,1},{6,2},{7,3},{8,12},{9,13},{10,... | collective-permute-start | bytes 1572872 | tf_op jit(solution)/shard_map/ppermute | solution.py:265
  201.0 22.7 %collective-permute-start.37 = (bf16[128,2048]{1,0:T(8,128)(2,1)S(1)}, bf16[128,2048]{1,0:T(8,128)(2,1)S(1)}, u32[]{:S(2)}, u32[]{:S(2)}) collective-permute-start(bf16[128,2048]{1,0:T(8,128)(2,1)S(1)} %get-tuple-element.162), channel_id=1, source_target_pairs={{0,1},{1,0},{2,3},{3,2},{4,5},{5,4},{6,7},{7,6},{8,9},{9,8},{10,11... | collective-permute-start | bytes 1572872 | tf_op jit(solution)/shard_map/ppermute | solution.py:265
  224.6 19.6 %collective-permute-start.44 = (bf16[128,2688]{1,0:T(8,128)(2,1)S(1)}, bf16[128,2688]{1,0:T(8,128)(2,1)S(1)}, u32[]{:S(2)}, u32[]{:S(2)}) collective-permute-start(bf16[128,2688]{1,0:T(8,128)(2,1)S(1)} %add_convert_fusion.4), channel_id=1, source_target_pairs={{8,0},{16,24},{9,1},{17,25},{10,2},{18,26},{11,3},{19,27},{12,4},{... | collective-permute-start | bytes 2064392 | tf_op jit(solution)/shard_map/ppermute | solution.py:648
  225.9 18.4 %collective-permute-start.43 = (bf16[128,2688]{1,0:T(8,128)(2,1)S(1)}, bf16[128,2688]{1,0:T(8,128)(2,1)}, u32[]{:S(2)}, u32[]{:S(2)}) collective-permute-start(bf16[128,2688]{1,0:T(8,128)(2,1)S(1)} %add_convert_fusion.3), channel_id=1, source_target_pairs={{8,16},{16,8},{9,17},{17,9},{10,18},{18,10},{11,19},{19,11},{12,20... | collective-permute-start | bytes 2064392 | tf_op jit(solution)/shard_map/ppermute | solution.py:640
  227.4 21.3 %collective-permute-start.42 = (bf16[128,2688]{1,0:T(8,128)(2,1)}, bf16[128,2688]{1,0:T(8,128)(2,1)S(1)}, u32[]{:S(2)}, u32[]{:S(2)}) collective-permute-start(bf16[128,2688]{1,0:T(8,128)(2,1)} %get-tuple-element.222), channel_id=1, source_target_pairs={{0,8},{24,16},{1,9},{25,17},{2,10},{26,18},{3,11},{27,19},{4,12},{... | collective-permute-start | bytes 2064392 | tf_op jit(solution)/shard_map/ppermute | solution.py:632
  234.9 15.2 %collective-permute-start.41 = (bf16[128,1536]{1,0:T(8,128)(2,1)S(1)}, bf16[128,1536]{1,0:T(8,128)(2,1)S(1)}, u32[]{:S(2)}, u32[]{:S(2)}) collective-permute-start(bf16[128,1536]{1,0:T(8,128)(2,1)S(1)} %get-tuple-element.165), channel_id=1, source_target_pairs={{0,4},{1,5},{2,6},{3,7},{4,0},{5,1},{6,2},{7,3},{8,12},{9,13},{10,... | collective-permute-start | bytes 1179656 | tf_op jit(solution)/shard_map/ppermute | solution.py:265
  236.3 20.3 %collective-permute-start.40 = (bf16[128,1536]{1,0:T(8,128)(2,1)S(1)}, bf16[128,1536]{1,0:T(8,128)(2,1)S(1)}, u32[]{:S(2)}, u32[]{:S(2)}) collective-permute-start(bf16[128,1536]{1,0:T(8,128)(2,1)S(1)} %get-tuple-element.167), channel_id=1, source_target_pairs={{0,1},{1,0},{2,3},{3,2},{4,5},{5,4},{6,7},{7,6},{8,9},{9,8},{10,11... | collective-permute-start | bytes 1179656 | tf_op jit(solution)/shard_map/ppermute | solution.py:265
  245.8 19.1 %collective-permute-start.49 = (bf16[128,2688]{1,0:T(8,128)(2,1)S(1)}, bf16[128,2688]{1,0:T(8,128)(2,1)S(1)}, u32[]{:S(2)}, u32[]{:S(2)}) collective-permute-start(bf16[128,2688]{1,0:T(8,128)(2,1)S(1)} %add_convert_fusion.2), channel_id=1, source_target_pairs={{8,0},{16,24},{9,1},{17,25},{10,2},{18,26},{11,3},{19,27},{12,4},{... | collective-permute-start | bytes 2064392 | tf_op jit(solution)/shard_map/ppermute | solution.py:648
  250.2 16.0 %collective-permute-start.47 = (bf16[128,1536]{1,0:T(8,128)(2,1)S(1)}, bf16[128,1536]{1,0:T(8,128)(2,1)S(1)}, u32[]{:S(2)}, u32[]{:S(2)}) collective-permute-start(bf16[128,1536]{1,0:T(8,128)(2,1)S(1)} %get-tuple-element.220), channel_id=1, source_target_pairs={{0,8},{24,16},{1,9},{25,17},{2,10},{26,18},{3,11},{27,19},{4,12},{... | collective-permute-start | bytes 1179656 | tf_op jit(solution)/shard_map/ppermute | solution.py:632
  256.8 15.2 %collective-permute-start.51 = (bf16[128,1536]{1,0:T(8,128)(2,1)S(1)}, bf16[128,1536]{1,0:T(8,128)(2,1)S(1)}, u32[]{:S(2)}, u32[]{:S(2)}) collective-permute-start(bf16[128,1536]{1,0:T(8,128)(2,1)S(1)} %get-tuple-element.218), channel_id=1, source_target_pairs={{0,8},{24,16},{1,9},{25,17},{2,10},{26,18},{3,11},{27,19},{4,12},{... | collective-permute-start | bytes 1179656 | tf_op jit(solution)/shard_map/ppermute | solution.py:632
  259.8 24.2 %collective-permute-start.52 = (bf16[128,2688]{1,0:T(8,128)(2,1)S(1)}, bf16[128,2688]{1,0:T(8,128)(2,1)}, u32[]{:S(2)}, u32[]{:S(2)}) collective-permute-start(bf16[128,2688]{1,0:T(8,128)(2,1)S(1)} %add_convert_fusion), channel_id=1, source_target_pairs={{8,0},{16,24},{9,1},{17,25},{10,2},{18,26},{11,3},{19,27},{12,4},{... | collective-permute-start | bytes 2064392 | tf_op jit(solution)/shard_map/ppermute | solution.py:648
  275.4 18.5 %collective-permute-start.57 = (bf16[128,1536]{1,0:T(8,128)(2,1)S(1)}, bf16[128,1536]{1,0:T(8,128)(2,1)}, u32[]{:S(2)}, u32[]{:S(2)}) collective-permute-start(bf16[128,1536]{1,0:T(8,128)(2,1)S(1)} %add_convert_fusion.7), channel_id=1, source_target_pairs={{8,0},{16,24},{9,1},{17,25},{10,2},{18,26},{11,3},{19,27},{12,4},{... | collective-permute-start | bytes 1179656 | tf_op jit(solution)/shard_map/ppermute | solution.py:648
  276.7 24.7 %collective-permute-start.55 = (bf16[128,1536]{1,0:T(8,128)(2,1)S(1)}, bf16[128,1536]{1,0:T(8,128)(2,1)S(1)}, u32[]{:S(2)}, u32[]{:S(2)}) collective-permute-start(bf16[128,1536]{1,0:T(8,128)(2,1)S(1)} %add_convert_fusion.8), channel_id=1, source_target_pairs={{8,16},{16,8},{9,17},{17,9},{10,18},{18,10},{11,19},{19,11},{12,20... | collective-permute-start | bytes 1179656 | tf_op jit(solution)/shard_map/ppermute | solution.py:640
  (66 other events, 664.3 us)
